TPU v7x, 256 devices: a whole 4x4x8 slice. The times are simulated.
256 devices in a mesh: node: 32 (over y, z), rep: 8 (over x, core).
Axes of the slice: x: 4, y: 4, z: 8, core: 2. Of those that a mesh axis runs over, the one named last changes fastest.
Arguments:
- memory: float32 [32768, 256], P('node'), may hold values from -3 to 3
- hot_memory: float32 [1024, 256], replicated, may hold values from -3 to 3
- cot_cold: float32 [32768, 256], P('node'), may hold values from -6 to 6
- cot_hot: float32 [1024, 256], replicated, may hold values from -6 to 6
- src_local: int32 [262144], P(('node', 'rep')), may hold values from 0 to 1023
- dst_ids: int32 [262144], P(('node', 'rep')), may hold values from 0 to 33791, as said below
- times: int32 [262144], P(('node', 'rep')), may hold values from 0 to 4095
- edge_feat: bfloat16 [262144, 128], P(('node', 'rep')), may hold values from -6 to 6
- cold_list: int32 [8192, 32], P(('node', 'rep')), may hold values from 0 to 1023, as said below
- cold_count: int32 [8192], P(('node', 'rep')), may hold values from 0 to 32, as said below
- hot_ids: int32 [1024], replicated, may hold values from 32768 to 33791, as said below
- time_freq: float32 [128], replicated, may hold values from 0.001 to 1
- time_phase: float32 [128], replicated, may hold values from -3.140625 to 3.140625
- w_msg: bfloat16 [512, 512], replicated, may hold values from -0.25 to 0.25
- b_msg: float32 [512], replicated, may hold values from -3 to 3
- w_in: bfloat16 [512, 768], replicated, may hold values from -0.25 to 0.25
- w_hid: bfloat16 [256, 768], replicated, may hold values from -0.375 to 0.375
Outputs:
- new_memory: float32 [32768, 256], P('node')
- new_hot: float32 [1024, 256], replicated
- grad_in: float32 [512, 768], replicated
- grad_hid: float32 [256, 768], replicated
Inputs may be any that keep to these rules, and one draw needn't show every extreme that they name: `dst_ids`: each device's events split into cold ones, each named in exactly one used slot of its owner's list, and hot ones whose destination is in hot_ids; cold destinations are node ids below 32768, hot ones 32768 or more. The hot destinations of device d are among the ids 32768 + ((d * 4 + j) mod 1024) for j below 16. `cold_list`: used slots hold distinct event indices of the device; unused slots hold 0. `cold_count`: some owner's list is full on every device. `hot_ids`: A permutation of the hot node ids 32768 to 33791.
All inputs are finite; a program needn't handle non-finite values.
Results may differ from a plain program's by a relative error of at most 0.0018.
The roundings to bfloat16 on the way count: a program that leaves them out, or rounds other values in their place, can miss the bound.
Values may be sent and summed in bfloat16 or wider, within the bound.
No kernel may reach another device: no remote copies, remote signals or barrier semaphores. Data moves between devices by JAX's collectives and lax.ppermute only.
A program may use at most 128 MiB of HBM per device.

v0:
```python
import jax
import jax.numpy as jnp
from jax import lax
from jax.sharding import PartitionSpec as P

GRAD_SCALE = 1.0 / 64.0


def gru_forward(agg, mem, w_in, w_hid):
    width = mem.shape[1]
    gate_in = jnp.dot(agg, w_in, preferred_element_type=jnp.float32)
    gate_hid = jnp.dot(mem.astype(jnp.bfloat16), w_hid, preferred_element_type=jnp.float32)
    reset = jax.nn.sigmoid(gate_in[:, :width] + gate_hid[:, :width])
    update = jax.nn.sigmoid(gate_in[:, width : 2 * width] + gate_hid[:, width : 2 * width])
    cand = jnp.tanh(gate_in[:, 2 * width :] + reset * gate_hid[:, 2 * width :])
    fresh = (1.0 - update) * cand + update * mem
    return (fresh, (reset, update, cand, gate_hid[:, 2 * width :]))


def gru_grads(agg, mem, saved, cot):
    reset, update, cand, hid_cand = saved
    d_cand = cot * (1.0 - update) * (1.0 - cand * cand)
    d_upd = cot * (mem - cand) * update * (1.0 - update)
    d_reset = d_cand * hid_cand * reset * (1.0 - reset)
    d_input = jnp.concatenate([d_reset, d_upd, d_cand], axis=1)
    d_hidden = jnp.concatenate([d_reset, d_upd, d_cand * reset], axis=1)
    mem_round = lax.optimization_barrier(mem.astype(jnp.bfloat16)).astype(jnp.float32)
    grad_a = jnp.dot(agg.astype(jnp.float32).T, d_input, precision=lax.Precision.HIGHEST)
    grad_b = jnp.dot(mem_round.T, d_hidden, precision=lax.Precision.HIGHEST)
    return (grad_a, grad_b)


def mean_rows(total, count):
    return (total / jnp.maximum(count, 1.0)[:, None]).astype(jnp.bfloat16)


def forward_rows(total, count, mem, w_in, w_hid):
    agg = mean_rows(total, count)
    fresh, saved = gru_forward(agg, mem, w_in, w_hid)
    live = (count > 0)[:, None]
    return (jnp.where(live, fresh, mem), agg, saved, live)


def on_device(
    memory,
    hot_memory,
    cot_cold,
    cot_hot,
    src_local,
    dst_ids,
    times,
    edge_feat,
    cold_list,
    cold_count,
    hot_ids,
    time_freq,
    time_phase,
    w_msg,
    b_msg,
    w_in,
    w_hid,
):
    n_node = lax.axis_size("node")
    n_rep = lax.axis_size("rep")
    rows_dev = memory.shape[0]
    slot_cap = cold_list.shape[1]
    hot_rows_all = hot_memory.shape[0]
    src_mem = jnp.take(memory, src_local, axis=0).astype(jnp.bfloat16)
    enc = jnp.cos(
        times.astype(jnp.float32)[:, None] * time_freq[None, :] + time_phase[None, :]
    ).astype(jnp.bfloat16)
    raw = jnp.concatenate([src_mem, edge_feat, enc], axis=1)
    messages = jax.nn.silu(
        jnp.dot(raw, w_msg, preferred_element_type=jnp.float32) + b_msg[None, :]
    ).astype(jnp.bfloat16)
    match = (dst_ids[:, None] == hot_ids[None, :]).astype(jnp.bfloat16)
    hot_total = lax.dot_general(
        match, messages, (((0,), (0,)), ((), ())), preferred_element_type=jnp.float32
    )
    hot_cnt = jnp.sum((dst_ids[:, None] == hot_ids[None, :]).astype(jnp.float32), axis=0)
    flat_list = cold_list.reshape(-1)
    slots = jnp.arange(slot_cap, dtype=jnp.int32)
    valid = (slots[None, :] < cold_count[:, None]).reshape(-1)
    owner = jnp.repeat(jnp.arange(n_node, dtype=jnp.int32), slot_cap)
    send_msg = jnp.take(messages, flat_list, axis=0)
    send_row = jnp.where(valid, jnp.take(dst_ids, flat_list) - owner * rows_dev, -1)
    recv_msg, recv_row = (
        lax.all_to_all(send_msg, "node", split_axis=0, concat_axis=0, tiled=True),
        lax.all_to_all(send_row, "node", split_axis=0, concat_axis=0, tiled=True),
    )
    share = rows_dev // n_rep
    first = lax.axis_index("rep") * share
    equal = jnp.arange(rows_dev, dtype=jnp.int32)[:, None] == recv_row[None, :]
    summed = jnp.dot(equal.astype(jnp.bfloat16), recv_msg, preferred_element_type=jnp.float32)
    cold_total, cold_cnt = lax.psum((summed, jnp.sum(equal.astype(jnp.float32), axis=1)), "rep")
    new_memory, agg_cold, saved_cold, live_cold = forward_rows(
        cold_total, cold_cnt, memory, w_in, w_hid
    )
    grad_a, grad_b = gru_grads(
        lax.dynamic_slice_in_dim(agg_cold, first, share, 0),
        lax.dynamic_slice_in_dim(memory, first, share, 0),
        tuple((lax.dynamic_slice_in_dim(item, first, share, 0) for item in saved_cold)),
        jnp.where(
            lax.dynamic_slice_in_dim(live_cold, first, share, 0),
            lax.dynamic_slice_in_dim(cot_cold, first, share, 0),
            0.0,
        ),
    )
    hot_share = hot_rows_all // (n_node * n_rep)
    hot_first = lax.axis_index(("node", "rep")) * hot_share
    hot_total, hot_cnt = lax.psum((hot_total, hot_cnt), ("node", "rep"))
    new_hot, agg_hot, saved_hot, live_hot = forward_rows(
        hot_total, hot_cnt, hot_memory, w_in, w_hid
    )
    hot_a, hot_b = gru_grads(
        lax.dynamic_slice_in_dim(agg_hot, hot_first, hot_share, 0),
        lax.dynamic_slice_in_dim(hot_memory, hot_first, hot_share, 0),
        tuple((lax.dynamic_slice_in_dim(item, hot_first, hot_share, 0) for item in saved_hot)),
        jnp.where(
            lax.dynamic_slice_in_dim(live_hot, hot_first, hot_share, 0),
            lax.dynamic_slice_in_dim(cot_hot, hot_first, hot_share, 0),
            0.0,
        ),
    )
    grad_in, grad_hid = lax.psum((grad_a + hot_a, grad_b + hot_b), ("node", "rep"))
    return (new_memory, new_hot, grad_in * GRAD_SCALE, grad_hid * GRAD_SCALE)


def solution(mesh):
    in_specs = (
        P("node", None),
        P(),
        P("node", None),
        P(),
        P(("node", "rep")),
        P(("node", "rep")),
        P(("node", "rep")),
        P(("node", "rep"), None),
        P(("node", "rep"), None),
        P(("node", "rep")),
        P(),
        P(),
        P(),
        P(),
        P(),
        P(),
        P(),
    )
    out_specs = (P("node", None), P(), P(), P())
    return jax.shard_map(
        on_device, mesh=mesh, in_specs=in_specs, out_specs=out_specs, check_vma=False
    )
```

profile of v0, /device:TPU:1, one launch (start us, length us, event | category | flops | bytes accessed | tf_op | source)
XLA Modules:
  0.0 659.8 jit_solution(15320068018080624457)
XLA Ops:
  8.0 0.0 copy-start
  8.0 0.9 reshape.105
  8.9 0.0 copy-start.10
  8.9 0.0 copy-start.14
  9.0 0.0 copy-start.11
  9.0 0.0 copy-start.13
  9.0 0.0 copy-start.2
  9.0 4.5 gather_fusion
  13.5 0.1 gather.17
  13.6 0.7 subtract_select_fusion
  14.3 12.0 %all-to-all-start = ((s32[32,32,1]{1,2,0:T(1,128)}), s32[32,32,1]{1,2,0:T(1,128)S(1)}, u32[]{:S(2)}, u32[]{:S(2)}) async-start(s32[32,32,1]{1,2,0:T(1,128)} %bitcast.1), calls=%async_computation | async-start | bytes 32768 | tf_op jit(solution)/shard_map/all_to_all | solution.py:89
  26.3 0.0 all-reduce.7.cloned.1.call-start
  26.4 0.0 copy-start.15
  26.5 0.0 copy-start.16
  26.5 0.0 copy-start.17
  26.5 0.0 copy-start.18
  26.5 3.5 gather_fusion.1
  30.0 0.2 select_convert_fusion
  30.2 2.0 cosine_convert_fusion
  32.2 0.0 copy-start.12
  32.3 1.9 multiply_convert_fusion
  34.2 3.0 fusion
  37.2 0.0 all-reduce.7.cloned.1.call-update
  37.2 5.1 gather_fusion.2
  42.3 0.5 fusion.2
  42.8 78.1 %psum.44 = f32[1024]{0:T(1024)S(1)} all-reduce(f32[1024]{0:T(1024)S(1)} %fusion.2), channel_id=1, replica_groups=mesh['node'=32,'rep'=8] {'node','rep'}, use_global_device_ids=true, to_apply=%region_4.5 | all-reduce | flops 1024 | bytes 8192 | tf_op jit(solution)/shard_map/psum | solution.py:111
  120.9 2.5 broadcast_select_fusion
  123.4 6.5 all-to-all-start.1
  129.9 0.0 all-reduce.5.cloned.1.call-start
  129.9 0.1 dynamic-slice.7
  130.0 2.2 fusion.32
  132.3 2.3 fusion.30
  134.5 0.5 broadcast.120
  135.0 0.7 reduce.3
  135.7 0.1 eq.15
  135.8 0.5 convert_reduce_fusion
  136.3 13.5 %psum.42 = f32[1024]{0:T(1024)S(1)} all-reduce(f32[1024]{0:T(1024)S(1)} %convert_reduce_fusion), channel_id=1, replica_groups=mesh['node'=32,'rep'=8] {'rep'}, use_global_device_ids=true, to_apply=%region_1.2 | all-reduce | flops 1024 | bytes 8192 | tf_op jit(solution)/shard_map/psum | solution.py:95
  149.8 0.1 dynamic-slice.6
  149.9 149.8 %all-reduce.7.cloned.1.call-done = f32[1024,512]{1,0:T(8,128)} async-done(((f32[1024,512]{1,0:T(8,128)}), f32[1024,512]{1,0:T(8,128)}) %all-reduce.7.cloned.1.call-update) | async-done | bytes 2097168 | tf_op jit(solution)/shard_map/psum | solution.py:111
  299.7 1.8 divide_convert_fusion
  301.5 0.0 all-to-all-done.1
  301.5 4.2 fusion.3
  305.7 0.0 all-reduce.5.cloned.1.call-update
  305.7 0.2 all-reduce.9.cloned.1.call-start
  306.0 0.0 copy-start.7
  306.0 1.0 fusion.63
  307.0 0.9 copy-done.4
  307.9 0.3 copy-done.7
  308.1 2.1 add_select_fusion
  310.2 0.8 fusion.48
  311.0 63.6 %all-reduce.5.cloned.1.call-done = f32[1024,512]{1,0:T(8,128)} async-done(((f32[1024,512]{1,0:T(8,128)}), f32[1024,512]{1,0:T(8,128)}) %all-reduce.5.cloned.1.call-update) | async-done | bytes 2097168 | tf_op jit(solution)/shard_map/psum | solution.py:95
  374.5 1.8 divide_convert_fusion.1
  376.4 1.0 fusion.62
  377.3 0.9 copy-done.3
  378.2 2.1 add_select_fusion.1
  380.3 1.0 dynamic-slice_multiply_fusion
  381.4 0.8 fusion.34
  382.2 0.5 fusion.37
  382.8 2.7 convolution_add_fusion
  385.4 1.4 convolution_add_fusion.1
  386.8 0.0 all-reduce.9.cloned.1.call-update
  386.9 261.8 %all-reduce.9.cloned.1.call-done = (f32[512,768]{1,0:T(8,128)}, f32[256,768]{1,0:T(8,128)}) async-done(((f32[512,768]{1,0:T(8,128)}, f32[256,768]{1,0:T(8,128)}), (f32[512,768]{1,0:T(8,128)}, f32[256,768]{1,0:T(8,128)})) %all-reduce.9.cloned.1.call-update) | async-done | bytes 2359312 | tf_op jit(solution)/shard_map/psum | solution.py:125
  648.7 2.7 broadcast_multiply_fusion
  651.4 0.9 broadcast_multiply_fusion.1
  (37 shorter events, 0.2 us)
Async XLA Ops:
  8.0 298.0 %copy-start = (bf16[512,768]{1,0:T(8,128)(2,1)S(1)}, bf16[512,768]{1,0:T(8,128)(2,1)}, u32[]{:S(2)}) copy-start(bf16[512,768]{1,0:T(8,128)(2,1)} %param.32) | copy-start | bytes 2359300
  8.0 0.9 copy-start.1
  8.9 4.7 copy-start.10
  8.9 4.7 copy-start.14
  9.0 17.4 %copy-start.11 = (s32[1024]{0:T(1024)S(1)}, s32[1024]{0:T(1024)}, u32[]{:S(2)}) copy-start(s32[1024]{0:T(1024)} %param.21) | copy-start | bytes 12292
  9.0 17.4 %copy-start.13 = (s32[1024]{0:T(1024)S(1)}, s32[1024]{0:T(1024)}, u32[]{:S(2)}) copy-start(s32[1024]{0:T(1024)} %param.23) | copy-start | bytes 12292
  9.0 17.5 %copy-start.2 = (f32[1024,256]{1,0:T(8,128)S(1)}, f32[1024,256]{1,0:T(8,128)}, u32[]{:S(2)}) copy-start(f32[1024,256]{1,0:T(8,128)} %param.17) | copy-start | bytes 3145732
  14.3 109.1 %all-to-all-start = ((s32[32,32,1]{1,2,0:T(1,128)}), s32[32,32,1]{1,2,0:T(1,128)S(1)}, u32[]{:S(2)}, u32[]{:S(2)}) async-start(s32[32,32,1]{1,2,0:T(1,128)} %bitcast.1), calls=%async_computation | async-start | bytes 32768 | tf_op jit(solution)/shard_map/all_to_all | solution.py:89
  26.3 273.3 %all-reduce.7.cloned.1.call-start = ((), (), s32[]{:S(2)}) async-start(), calls=%async_computation.3 | async-start | bytes 4194304 | tf_op jit(solution)/shard_map/psum | solution.py:111
  26.4 3.7 copy-start.15
  26.5 3.7 copy-start.16
  26.5 5.8 copy-start.17
  26.5 5.8 copy-start.18
  32.2 2.0 copy-start.12
  120.9 9.1 %copy-start.8 = (bf16[256,768]{1,0:T(8,128)(2,1)S(1)}, bf16[256,768]{1,0:T(8,128)(2,1)}, u32[]{:S(2)}) copy-start(bf16[256,768]{1,0:T(8,128)(2,1)} %param.33) | copy-start | bytes 1179652
  123.4 178.1 %all-to-all-start.1 = ((bf16[32,32,512]{2,1,0:T(8,128)(2,1)}), bf16[32,32,512]{2,1,0:T(8,128)(2,1)}, u32[]{:S(2)}, u32[]{:S(2)}) async-start(bf16[32,32,512]{2,1,0:T(8,128)(2,1)} %broadcast_select_fusion), calls=%async_computation.1 | async-start | bytes 2097152 | tf_op jit(solution)/shard_map/all_to_all | solution.py:88
  129.9 244.7 %all-reduce.5.cloned.1.call-start = ((), (), s32[]{:S(2)}) async-start(), calls=%async_computation.2 | async-start | bytes 4194304 | tf_op jit(solution)/shard_map/psum | solution.py:95
  130.0 2.2 copy-start.6
  301.5 4.5 copy-start.5
  305.7 342.9 %all-reduce.9.cloned.1.call-start = ((), (), s32[]{:S(2)}) async-start(), calls=%async_computation.4 | async-start | bytes 4718592 | tf_op jit(solution)/shard_map/psum | solution.py:125
  306.0 1.9 copy-start.4
  306.0 2.2 copy-start.7
  376.3 1.9 copy-start.3
  648.7 2.7 copy-start.9
Sparse Core Ops, SparseCore 0:
  37.3 262.2 all-reduce.6
  387.0 261.6 all-reduce.8
Sparse Core Ops, SparseCore 1:
  305.8 68.7 all-reduce.4
where the time goes:
time: 661 us; the launch traced here: 660 us
  waiting for transfers between devices  475 us (72%)
  blocking collectives  91.6 us (14%)
  matrix products  21 us (3%)
  other arithmetic  20.3 us (3%)
  starting transfers between devices  18.8 us (3%)
  local copies, waits for them, and re-layouts  16.9 us (3%)
  between operations  15.9 us (2%)
    psum x1, waiting for transfers between devices, on_device(): lax.psum((grad_a + hot_a, grad_b + hot_b), ('node', 'rep'))  262 us
    psum x1, waiting for transfers between devices, on_device(): hot_total, hot_cnt = lax.psum((hot_total, hot_cnt), ('node', 'rep'))  150 us
    psum x1, blocking collectives, on_device(): hot_total, hot_cnt = lax.psum((hot_total, hot_cnt), ('node', 'rep'))  78.1 us
    psum x1, waiting for transfers between devices, on_device(): lax.psum((summed, jnp.sum(equal.astype(jnp.float32), axis=1)), 'rep')  63.6 us
    psum x1, blocking collectives, on_device(): lax.psum((summed, jnp.sum(equal.astype(jnp.float32), axis=1)), 'rep')  13.5 us
  transfers between devices with their start and end apart: 5, of which 3 were waited for; matrix products, arithmetic and copies ran while one was open for 5% of the time, Pallas kernels for 0%

commit v1 on v0

v1 whole, which is shorter than its diff:
```python
import jax
import jax.numpy as jnp
from jax import lax
from jax.experimental import pallas as pl
from jax.experimental.pallas import tpu as pltpu
from jax.sharding import PartitionSpec as P

GRAD_SCALE = 1.0 / 64.0
DEAD = 2.0**100
F32, BF16, I32 = jnp.float32, jnp.bfloat16, jnp.int32
PARAMS = pltpu.CompilerParams(vmem_limit_bytes=48 * 1024 * 1024)
VM = pl.BlockSpec(memory_space=pltpu.VMEM)
SM = pl.BlockSpec(memory_space=pltpu.SMEM)


def iota(shape, dim):
    return lax.broadcasted_iota(I32, shape, dim)


def one_hot(mask):
    return jnp.where(mask, 1.0, 0.0).astype(BF16)


def mm(a, b, dims=((1,), (0,))):
    return lax.dot_general(a, b, (dims, ((), ())), preferred_element_type=F32)


def call(body, out_shape, n_smem, args, scratch=()):
    return pl.pallas_call(
        body,
        out_shape=out_shape,
        in_specs=[SM] * n_smem + [VM] * (len(args) - n_smem),
        out_specs=jax.tree.map(lambda _: VM, out_shape),
        scratch_shapes=list(scratch),
        compiler_params=PARAMS,
    )(*args)


def message_kernel(pos, idx, mem, edge, enc, w, b, send, hot, msgs, cols):
    cols[...] = idx[...].T
    mem16 = mem[...].astype(BF16)
    n_ev = idx.shape[1]
    step = 256
    for e in range(0, n_ev, step):
        src = cols[e : e + step, 0:1]
        src_mem = mm(one_hot(iota((step, mem.shape[0]), 1) == src), mem16).astype(BF16)
        raw = jnp.concatenate([src_mem, edge[e : e + step, :], enc[e : e + step, :]], axis=1)
        pre = mm(raw, w[...]) + b[...]
        msgs[e : e + step, 0:512] = (pre * jax.nn.sigmoid(pre)).astype(BF16)
        row = cols[e : e + step, 2:3] & 1023
        lane = iota((step, 128), 1)
        tail = jnp.where(lane == 0, row >> 5, jnp.where(lane == 1, row & 31, jnp.where(lane == 2, 1, 0)))
        msgs[e : e + step, 512:640] = tail.astype(F32).astype(BF16)
    for s in range(0, n_ev, step):
        pick = one_hot(iota((step, n_ev), 1) == cols[s : s + step, 3:4])
        send[s : s + step, :] = mm(pick, msgs[...]).astype(BF16)
    dst = idx[2:3, :]
    window = jnp.where(dst >= 32768, (dst - 32768 - 32 * pos[0] + 1024) & 1023, -1)
    q = iota((96, n_ev), 0)
    hit = one_hot(4 * (q >> 3) + (q & 3) == window)
    total = mm(hit, msgs[:, 0:512])
    count = jnp.sum(hit.astype(F32), axis=1, keepdims=True)
    hot[...] = jnp.where((iota((96, 512), 0) & 7) < 4, total, count)


def cold_kernel(pos, recv, keep, send):
    tail = recv[:, 512:640].astype(F32).T
    row = jnp.where(tail[2:3, :] > 0.5, tail[0:1, :] * 32.0 + tail[1:2, :], -1.0).astype(I32)
    ones = jnp.ones((8, recv.shape[0]), BF16)
    for out, core in ((send, 1 - pos[1]), (keep, pos[1])):
        q = iota((512, recv.shape[0]), 0)
        hit = one_hot(((q >> 7) * 256 + (q & 127) + core * 128) == row)
        total = mm(hit, recv[:, 0:512])
        count = mm(ones, hit, ((1,), (1,)))
        for j in range(4):
            out[j, 0:128, :] = total[128 * j : 128 * j + 128, :]
            out[j, 128:136, 0:128] = count[:, 128 * j : 128 * j + 128]
            out[j, 128:136, 128:512] = jnp.zeros((8, 384), F32)


def add_kernel(pos, keep, recv, o0, o1, o2, o3):
    for d, out in enumerate((o0, o1, o2, o3)):
        j = (pos[0] + d) & 3
        out[...] = keep[j] + recv[j]


def agg_kernel(p0, p1, p2, p3, hot, out):
    total = p0[...] + p1[...] + p2[...] + p3[...]
    count = total[128:129, 0:128]
    count = jnp.sum(jnp.where(iota((128, 128), 0) == iota((128, 128), 1), count, 0.0), axis=1, keepdims=True)
    agg = jnp.where(count > 0.0, total[0:128, :] / jnp.maximum(count, 1.0), DEAD)
    out[0:128, :] = agg.astype(BF16)
    out[128:144, :] = hot[...]


def gates(agg, mem, w_in, w_hid):
    gi = mm(agg, w_in)
    gh = mm(mem.astype(BF16), w_hid)
    reset = jax.nn.sigmoid(gi[:, 0:256] + gh[:, 0:256])
    update = jax.nn.sigmoid(gi[:, 256:512] + gh[:, 256:512])
    cand = jnp.tanh(gi[:, 512:768] + reset * gh[:, 512:768])
    return reset, update, cand, gh[:, 512:768]


def hot_kernel(parts, mem, w_in, w_hid, agg_out, new_out):
    total = parts[0]
    for k in range(1, 8):
        total = total + parts[k]
    count = total[4:8, :]
    agg = jnp.where(count > 0.0, total[0:4, :] / jnp.maximum(count, 1.0), DEAD)
    agg = jnp.concatenate([agg, jnp.full((12, 512), DEAD, F32)], axis=0).astype(BF16)
    agg_out[...] = agg
    live = agg[:, 0:256].astype(F32) < DEAD * 0.5
    mem = mem[...]
    wide = agg.astype(F32)
    agg = jnp.where(wide < DEAD * 0.5, wide, 0.0).astype(BF16)
    reset, update, cand, _ = gates(agg, mem, w_in[...], w_hid[...])
    new_out[...] = jnp.where(live, (1.0 - update) * cand + update * mem, mem)[0:8, :]


def update_kernel(pos, a0, a1, a2, a3, b0, b1, b2, b3, mem, cot, w_in, w_hid, new, grad, agg, acc):
    x, core, rep = pos[0], pos[1], pos[2]
    for group, c in (((a0, a1, a2, a3), core), ((b0, b1, b2, b3), 1 - core)):
        for d, part in enumerate(group):
            block = 2 * ((x - d + 4) & 3) + c
            agg[pl.ds(pl.multiple_of(block * 128, 128), 128), :] = part[0:128, :]
            agg[pl.ds(pl.multiple_of(1024 + block * 16, 16), 16), :] = part[128:144, :]
    k, q = iota((512, 128), 0), iota((512, 128), 1)
    sel_a = one_hot((k == 64 * rep + q) & (q < 64))
    k, q = iota((256, 128), 0), iota((256, 128), 1)
    sel_m = one_hot((k == 32 * rep + q - 64) & (q >= 64) & (q < 96))
    step = 384
    for s in range(0, 1152, step):
        wide = agg[s : s + step, :].astype(F32)
        live = wide[:, 0:1] < DEAD * 0.5
        a = jnp.where(live, wide, 0.0).astype(BF16)
        m = mem[s : s + step, :]
        reset, update, cand, hid_cand = gates(a, m, w_in[...], w_hid[...])
        fresh = jnp.where(live, (1.0 - update) * cand + update * m, m)
        rows = min(step, 1024 - s)
        new[s : s + rows, :] = fresh[0:rows, :]
        g = jnp.where(live, cot[s : s + step, :], 0.0)
        d_cand = g * (1.0 - update) * (1.0 - cand * cand)
        d_upd = g * (m - cand) * update * (1.0 - update)
        d_reset = d_cand * hid_cand * reset * (1.0 - reset)
        left = (mm(a, sel_a) + mm(m.astype(BF16), sel_m)).astype(BF16)
        for j, d in enumerate((d_reset, d_upd, d_cand, d_cand * reset)):
            hi = d.astype(BF16)
            rest = d - hi.astype(F32)
            mid = rest.astype(BF16)
            low = (rest - mid.astype(F32)).astype(BF16)
            dims = ((0,), (0,))
            part = mm(left, hi, dims) + (mm(left, mid, dims) + mm(left, low, dims))
            cols = slice(256 * j, 256 * j + 256)
            if s == 0:
                acc[:, cols] = part
            else:
                acc[:, cols] += part
    total = acc[...] * GRAD_SCALE
    third = jnp.where(iota((128, 256), 0) < 64, total[:, 512:768], total[:, 768:1024])
    total = jnp.concatenate([total[:, 0:512], third], axis=1)
    for p in range(32):
        i, j = p // 2, p % 2
        grad[p] = total[8 * i : 8 * i + 8, 384 * j : 384 * j + 384]


def piece_kernel(parts, out):
    total = parts[0]
    for k in range(1, 32):
        total = total + parts[k]
    for k in range(32):
        out[k] = total


def place_kernel(pos, a0, a1, a2, a3, b0, b1, b2, b3, g_in, g_hid):
    x, core = pos[0], pos[1]
    for group, c in (((a0, a1, a2, a3), core), ((b0, b1, b2, b3), 1 - core)):
        for d, part in enumerate(group):
            block = 2 * ((x - d + 4) & 3) + c
            for p in range(24):
                i, j = p // 2, p % 2
                cols = slice(384 * j, 384 * j + 384)
                if i < 8:
                    g_in[pl.ds(pl.multiple_of(block * 64 + 8 * i, 8), 8), cols] = part[p]
                else:
                    g_hid[pl.ds(pl.multiple_of(block * 32 + 8 * (i - 8), 8), 8), cols] = part[p]


def swap_core(v):
    return lax.ppermute(v, "rep", [(k, k ^ 1) for k in range(8)])


def shift_x(v, d):
    return lax.ppermute(v, "rep", [(k, (k + 2 * d) % 8) for k in range(8)])


def gather_rep(v):
    own = [v] + [shift_x(v, d) for d in (1, 2, 3)]
    return own + [swap_core(u) for u in own]


def on_device(
    memory,
    hot_memory,
    cot_cold,
    cot_hot,
    src_local,
    dst_ids,
    times,
    edge_feat,
    cold_list,
    cold_count,
    hot_ids,
    time_freq,
    time_phase,
    w_msg,
    b_msg,
    w_in,
    w_hid,
):
    node = lax.axis_index("node")
    rep = lax.axis_index("rep")
    pos = jnp.stack([rep // 2, rep % 2, rep]).astype(I32)
    sds = jax.ShapeDtypeStruct

    slots = jnp.arange(32, dtype=I32)
    listed = jnp.where(slots[None, :] < cold_count[:, None], cold_list, -1).reshape(-1)
    zero = jnp.zeros_like(listed)
    idx = jnp.stack([src_local, times, dst_ids, listed, zero, zero, zero, zero])
    enc = jnp.cos(times.astype(F32)[:, None] * time_freq[None, :] + time_phase[None, :]).astype(BF16)
    send, hot = call(
        message_kernel,
        (sds((1024, 640), BF16), sds((96, 512), F32)),
        1,
        (node.astype(I32)[None], idx, memory, edge_feat, enc, w_msg, b_msg[None, :]),
        (pltpu.VMEM((1024, 640), BF16), pltpu.VMEM((1024, 8), I32)),
    )
    recv = lax.all_to_all(send, "node", split_axis=0, concat_axis=0, tiled=True)

    spill = lax.ppermute(hot[64:96], "node", [(k, (k + 1) % 32) for k in range(32)])
    hot_main = jnp.concatenate([hot[0:32] + spill, hot[32:64]], axis=0)
    hot_parts = lax.all_to_all(hot_main, "rep", split_axis=0, concat_axis=0, tiled=True)
    k = jnp.arange(128, dtype=I32)
    want = 32768 + 32 * node + 4 * (k // 16) + k % 4
    at = jnp.sum(jnp.where(want[:, None] == hot_ids[None, :], jnp.arange(1024, dtype=I32)[None, :], 0), axis=1)
    hot_mem = jnp.take(hot_memory, at, axis=0)
    mem_all = jnp.concatenate([memory, hot_mem], axis=0)
    cot_all = jnp.concatenate([cot_cold, jnp.take(cot_hot, at, axis=0)], axis=0)
    own_mem = lax.dynamic_slice_in_dim(hot_mem, 16 * rep, 16, 0)
    hot_agg, hot_new = call(
        hot_kernel,
        (sds((16, 512), BF16), sds((8, 256), F32)),
        0,
        (hot_parts.reshape(8, 8, 512), own_mem, w_in, w_hid),
    )
    hot_all = lax.all_gather(hot_new[0:4], ("node", "rep"), axis=0, tiled=True)
    new_hot = jnp.take(hot_all, hot_ids - 32768, axis=0)

    block = sds((136, 512), F32)
    keep, give = call(cold_kernel, (sds((4, 136, 512), F32),) * 2, 1, (pos, recv))
    parts = call(add_kernel, (block,) * 4, 1, (pos, keep, swap_core(give)))
    parts = [parts[0]] + [shift_x(parts[d], d) for d in (1, 2, 3)]
    agg = call(agg_kernel, sds((144, 512), BF16), 0, (*parts, hot_agg))
    new_memory, grad = call(
        update_kernel,
        (sds((1024, 256), F32), sds((32, 8, 384), F32)),
        1,
        (pos, *gather_rep(agg), mem_all, cot_all, w_in, w_hid),
        (pltpu.VMEM((1152, 512), BF16), pltpu.VMEM((128, 1024), F32)),
    )

    grad = lax.all_to_all(grad, "node", split_axis=0, concat_axis=0, tiled=True)
    grad = call(piece_kernel, sds((32, 8, 384), F32), 0, (grad,))
    grad = lax.all_to_all(grad, "node", split_axis=0, concat_axis=0, tiled=True)
    grad_in, grad_hid = call(
        place_kernel,
        (sds((512, 768), F32), sds((256, 768), F32)),
        1,
        (pos, *gather_rep(grad[0:24])),
    )
    return (new_memory, new_hot, grad_in, grad_hid)


def solution(mesh):
    in_specs = (
        P("node", None),
        P(),
        P("node", None),
        P(),
        P(("node", "rep")),
        P(("node", "rep")),
        P(("node", "rep")),
        P(("node", "rep"), None),
        P(("node", "rep"), None),
        P(("node", "rep")),
        P(),
        P(),
        P(),
        P(),
        P(),
        P(),
        P(),
    )
    out_specs = (P("node", None), P(), P(), P())
    return jax.shard_map(
        on_device, mesh=mesh, in_specs=in_specs, out_specs=out_specs, check_vma=False
    )
```

time: 661 us -> 230 us (0.35)
  waiting for transfers between devices: 475 us -> 72.7 us
  blocking collectives: 91.6 us -> 33.5 us
  starting transfers between devices: 18.8 us -> 57.4 us
  matrix products: 21 us -> 0 us
  Pallas kernels: 0 us -> 18.6 us
  other arithmetic: 20.3 us -> 9.86 us
    psum x3 -> x0, waiting for transfers between devices: 475 us -> none  [the longest x1 262 us: on_device(): lax.psum((grad_a + hot_a, grad_b + hot_b), ('node', 'rep'))]
    psum x2 -> x0, blocking collectives: 91.6 us -> none  [the longest x1 78.1 us: on_device(): hot_total, hot_cnt = lax.psum((hot_total, hot_cnt), ('node', 'rep'))]
    ppermute x0 -> x19, starting transfers between devices: none -> 40.8 us  [the longest x9 26.4 us: swap_core(): return lax.ppermute(v, 'rep', [(k, k ^ 1) for k in range(8)])]
    all_gather x0 -> x1, waiting for transfers between devices: none -> 34.8 us  [on_device(): hot_all = lax.all_gather(hot_new[0:4], ('node', 'rep'), axis=0, tiled=True)]
    all_to_all x0 -> x2, blocking collectives: none -> 33.5 us  [on_device(): grad = lax.all_to_all(grad, 'node', split_axis=0, concat_axis=0, tiled=True)]
    all_to_all x2, waiting for transfers between devices: 0.01 us -> 28.1 us  [the longest x1 28.1 us: on_device(): recv = lax.all_to_all(send, 'node', split_axis=0, concat_axis=0, tiled=True)]
    dot_general x11 -> x0, matrix products: 21 us -> none  [the longest x2 4.47 us: gru_forward(): jnp.dot(mem.astype(jnp.bfloat16), w_hid, preferred_element_type=jnp.float32)]
    pallas_call x0 -> x8, Pallas kernels: none -> 18.6 us  [call(): pl.pallas_call(body, out_shape=out_shape, in_specs=[SM] * n_smem + [VM] *...]
  transfers between devices with their start and end apart: 5 -> 22, of which waited for: 3 -> 5; matrix products, arithmetic and copies ran while one was open for 5% -> 8% of each run, Pallas kernels for 0% -> 5%
where the time goes in v1:
time: 230 us; the launch traced here: 229 us
  waiting for transfers between devices  72.7 us (32%)
  starting transfers between devices  57.4 us (25%)
  blocking collectives  33.5 us (15%)
  local copies, waits for them, and re-layouts  22.6 us (10%)
  Pallas kernels  18.6 us (8%)
  between operations  14.3 us (6%)
  other arithmetic  9.86 us (4%)
    all_gather x1, waiting for transfers between devices, on_device(): hot_all = lax.all_gather(hot_new[0:4], ('node', 'rep'), axis=0, tiled=True)  34.8 us
    all_to_all x2, blocking collectives, on_device(): grad = lax.all_to_all(grad, 'node', split_axis=0, concat_axis=0, tiled=True)  33.5 us
    all_to_all x1, waiting for transfers between devices, on_device(): recv = lax.all_to_all(send, 'node', split_axis=0, concat_axis=0, tiled=True)  28.1 us
    ppermute x9, starting transfers between devices, swap_core(): return lax.ppermute(v, 'rep', [(k, k ^ 1) for k in range(8)])  26.4 us
    pallas_call x8, Pallas kernels, call(): pl.pallas_call(body, out_shape=out_shape, in_specs=[SM] * n_smem + [VM] *...  18.6 us
    ppermute x9, starting transfers between devices, shift_x(): return lax.ppermute(v, 'rep', [(k, (k + 2 * d) % 8) for k in range(8)])  13.1 us
    unnamed x36, local copies, waits for them, and re-layouts  13 us
    all_to_all x1, starting transfers between devices, on_device(): recv = lax.all_to_all(send, 'node', split_axis=0, concat_axis=0, tiled=True)  12.2 us
  transfers between devices with their start and end apart: 22, of which 5 were waited for; matrix products, arithmetic and copies ran while one was open for 8% of the time, Pallas kernels for 5%

profile of v1, /device:TPU:1, one launch (start us, length us, event | category | flops | bytes accessed | tf_op | source)
XLA Modules:
  0.0 229.0 jit_solution(5449354939367640907)
XLA Ops:
  7.2 0.8 convert_element_type.6
  8.0 0.8 fusion
  8.8 0.1 stack_reshape.3
  8.8 2.7 %cosine_convert_fusion.enc = bf16[1024,128]{1,0:T(8,128)(2,1)S(1)} fusion(f32[128]{0:T(128)} %param.31, f32[128]{0:T(128)} %param.30, f32[1024]{0:T(1024)S(1)} %convert_element_type.6), kind=kLoop, calls=%fused_computation.7 | loop fusion | flops 393216 | bytes 267264 | tf_op jit(solution)/shard_map/convert_element_type | solution.py:230
  11.5 0.8 stack.35.idx
  12.3 1.2 copy-done.1
  13.5 1.0 copy-done.10
  14.6 0.9 copy-done.13
  15.5 0.7 copy-done.14
  16.2 3.6 %shard_map.192 = (bf16[1024,640]{1,0:T(8,128)(2,1)S(1)}, f32[96,512]{1,0:T(8,128)S(1)}) custom-call(s32[1]{0:T(128)} %bitcast.3.pos, s32[8,1024]{1,0:T(8,128)S(1)} %stack.35.idx, f32[1024,256]{1,0:T(8,128)S(1)} %copy-done.1, bf16[1024,128]{1,0:T(8,128)(2,1)S(1)} %copy-done.13, bf16[1024,128]{1,0:T(8,128)(2,1)S(1)} %cosine_convert_fusion.enc, ...), custom_call_target="tpu_custom_call" | custom-call | tf_op jit(solution)/shard_map/pallas_call | solution.py:29
  19.9 1.0 copy-done.7
  20.9 12.2 %all-to-all-start = ((bf16[32,32,640]{2,1,0:T(8,128)(2,1)}), bf16[32,32,640]{2,1,0:T(8,128)(2,1)S(1)}, u32[]{:S(2)}, u32[]{:S(2)}) async-start(bf16[32,32,640]{2,1,0:T(8,128)(2,1)} %bitcast.15), calls=%async_computation | async-start | bytes 2621440 | tf_op jit(solution)/shard_map/all_to_all | solution.py:238
  33.1 1.3 collective-permute-start.4
  34.4 0.1 pad_add_fusion.pos
  34.5 0.2 select_reduce_fusion
  34.7 28.1 %all-to-all-done = bf16[32,32,640]{2,1,0:T(8,128)(2,1)S(1)} async-done(((bf16[32,32,640]{2,1,0:T(8,128)(2,1)}), bf16[32,32,640]{2,1,0:T(8,128)(2,1)S(1)}, u32[]{:S(2)}, u32[]{:S(2)}) %all-to-all-start) | async-done | bytes 1310752 | tf_op jit(solution)/shard_map/all_to_all | solution.py:238
  62.8 3.1 %shard_map.193 = (f32[4,136,512]{2,1,0:T(8,128)S(1)}, f32[4,136,512]{2,1,0:T(8,128)}) custom-call(s32[3]{0:T(128)S(1)} %pad_add_fusion.pos, bf16[1024,640]{1,0:T(8,128)(2,1)S(1)} %bitcast.14), custom_call_target="tpu_custom_call" | custom-call | tf_op jit(solution)/shard_map/pallas_call | solution.py:29
  65.9 1.0 copy-done.8
  67.0 6.6 %collective-permute-start = (f32[4,136,512]{2,1,0:T(8,128)}, f32[4,136,512]{2,1,0:T(8,128)}, u32[]{:S(2)}, u32[]{:S(2)}) collective-permute-start(f32[4,136,512]{2,1,0:T(8,128)} %get-tuple-element.21), channel_id=1, source_target_pairs={{0,1},{1,0},{2,3},{3,2},{4,5},{5,4},{6,7},{7,6},{8,9},{9,8},{10,11... | collective-permute-start | bytes 3342344 | tf_op jit(solution)/shard_map/ppermute | solution.py:190
  73.6 0.8 gather_fusion.1
  74.3 2.1 gather_fusion.2
  76.4 0.8 broadcast_select_fusion.1
  77.2 0.7 maximum_bitcast_fusion
  77.9 4.4 %all-to-all-start.1 = ((f32[8,8,512]{2,1,0:T(8,128)}), f32[8,8,512]{2,1,0:T(8,128)S(1)}, u32[]{:S(2)}, u32[]{:S(2)}) async-start(f32[8,8,512]{2,1,0:T(8,128)} %maximum_bitcast_fusion), calls=%async_computation.1 | async-start | bytes 262144 | tf_op jit(solution)/shard_map/all_to_all | solution.py:242
  82.3 2.3 %shard_map.194 = (f32[136,512]{1,0:T(8,128)S(1)}, f32[136,512]{1,0:T(8,128)}, f32[136,512]{1,0:T(8,128)}, f32[136,512]{1,0:T(8,128)}) custom-call(s32[3]{0:T(128)S(1)} %pad_add_fusion.pos, f32[4,136,512]{2,1,0:T(8,128)S(1)} %copy-done.9, f32[4,136,512]{2,1,0:T(8,128)} %collective-permute-done.recv), custom_call_target="tpu_custom_call" | custom-call | tf_op jit(solution)/shard_map/pallas_call | solution.py:29
  84.6 0.7 copy-done.11
  85.3 1.4 collective-permute-start.1
  86.7 2.4 %collective-permute-start.2 = (f32[136,512]{1,0:T(8,128)}, f32[136,512]{1,0:T(8,128)}, u32[]{:S(2)}, u32[]{:S(2)}) collective-permute-start(f32[136,512]{1,0:T(8,128)} %get-tuple-element.24), channel_id=1, source_target_pairs={{0,4},{1,5},{2,6},{3,7},{4,0},{5,1},{6,2},{7,3},{8,12},{9,13},{10,... | collective-permute-start | bytes 835592 | tf_op jit(solution)/shard_map/ppermute | solution.py:194
  89.1 1.2 collective-permute-start.3
  90.3 0.1 pad_maximum_fusion.mem
  90.4 1.1 copy-done.3
  91.5 1.0 copy-done.5
  92.5 0.3 shard_map.195
  92.8 2.3 collective-permute-done.1.p1
  95.1 6.7 %collective-permute-done.2.p2 = f32[136,512]{1,0:T(8,128)} collective-permute-done((f32[136,512]{1,0:T(8,128)}, f32[136,512]{1,0:T(8,128)}, u32[]{:S(2)}, u32[]{:S(2)}) %collective-permute-start.2) | collective-permute-done | bytes 278560 | tf_op jit(solution)/shard_map/ppermute | solution.py:194
  101.8 1.0 copy-done.12
  102.8 1.2 shard_map.196.a0
  104.0 2.2 collective-permute-start.6
  106.2 1.1 collective-permute-start.7
  107.3 0.4 collective-permute-start.5
  107.7 0.6 slice_bitcast_fusion
  108.3 2.4 %collective-permute-start.8 = (bf16[144,512]{1,0:T(8,128)(2,1)S(1)}, bf16[144,512]{1,0:T(8,128)(2,1)S(1)}, u32[]{:S(2)}, u32[]{:S(2)}) collective-permute-start(bf16[144,512]{1,0:T(8,128)(2,1)S(1)} %shard_map.196.a0), channel_id=1, source_target_pairs={{0,1},{1,0},{2,3},{3,2},{4,5},{5,4},{6,7},{7,6},{8,9},{9,8},{10,11... | collective-permute-start | bytes 442376 | tf_op jit(solution)/shard_map/ppermute | solution.py:190
  110.7 2.5 %collective-permute-start.10 = (bf16[144,512]{1,0:T(8,128)(2,1)S(1)}, bf16[144,512]{1,0:T(8,128)(2,1)S(1)}, u32[]{:S(2)}, u32[]{:S(2)}) collective-permute-start(bf16[144,512]{1,0:T(8,128)(2,1)S(1)} %collective-permute-done.6.a2), channel_id=1, source_target_pairs={{0,1},{1,0},{2,3},{3,2},{4,5},{5,4},{6,7},{7,6},{8,9},{9,8},{10,11... | collective-permute-start | bytes 442376 | tf_op jit(solution)/shard_map/ppermute | solution.py:190
  113.2 0.7 collective-permute-done.7.a3
  113.9 1.3 collective-permute-start.11
  115.2 0.3 collective-permute-start.9
  115.6 1.4 pad_maximum_fusion.1.cot
  117.0 0.1 copy-done.6
  117.1 5.8 %shard_map.197 = (f32[1024,256]{1,0:T(8,128)}, f32[32,8,384]{2,1,0:T(8,128)S(1)}) custom-call(s32[3]{0:T(128)S(1)} %pad_add_fusion.pos, bf16[144,512]{1,0:T(8,128)(2,1)S(1)} %shard_map.196.a0, bf16[144,512]{1,0:T(8,128)(2,1)S(1)} %collective-permute-done.5.a1, bf16[144,512]{1,0:T(8,128)(2,1)S(1)} %collective-permute-done.6.a2, ...), custom_call_target="tpu_custom_call" | custom-call | tf_op jit(solution)/shard_map/pallas_call | solution.py:29
  122.9 15.7 %all_to_all.30.parts = f32[32,8,384]{2,1,0:T(8,128)S(1)} all-to-all(f32[32,8,384]{2,1,0:T(8,128)S(1)} %get-tuple-element.30), channel_id=1, replica_groups=mesh['node'=32,'rep'=8] {'node'}, dimensions={0} | all-to-all | bytes 786432 | tf_op jit(solution)/shard_map/all_to_all | solution.py:272
  138.6 0.1 shard_map.198
  138.7 17.8 %all_to_all.31 = f32[32,8,384]{2,1,0:T(8,128)S(1)} all-to-all(f32[32,8,384]{2,1,0:T(8,128)S(1)} %shard_map.198), channel_id=1, replica_groups=mesh['node'=32,'rep'=8] {'node'}, dimensions={0} | all-to-all | bytes 786432 | tf_op jit(solution)/shard_map/all_to_all | solution.py:274
  156.5 0.3 collective-permute-start.12
  156.8 2.9 %collective-permute-start.13 = (f32[24,8,384]{2,1,0:T(8,128)S(1)}, f32[24,8,384]{2,1,0:T(8,128)S(1)}, u32[]{:S(2)}, u32[]{:S(2)}) collective-permute-start(f32[24,8,384]{2,1,0:T(8,128)S(1)} %slice.26.a0), channel_id=1, source_target_pairs={{0,4},{1,5},{2,6},{3,7},{4,0},{5,1},{6,2},{7,3},{8,12},{9,13},{10,... | collective-permute-start | bytes 884744 | tf_op jit(solution)/shard_map/ppermute | solution.py:194
  159.8 1.2 collective-permute-start.14
  161.0 5.1 %collective-permute-start.15 = (f32[24,8,384]{2,1,0:T(8,128)S(1)}, f32[24,8,384]{2,1,0:T(8,128)S(1)}, u32[]{:S(2)}, u32[]{:S(2)}) collective-permute-start(f32[24,8,384]{2,1,0:T(8,128)S(1)} %slice.26.a0), channel_id=1, source_target_pairs={{0,1},{1,0},{2,3},{3,2},{4,5},{5,4},{6,7},{7,6},{8,9},{9,8},{10,11... | collective-permute-start | bytes 884744 | tf_op jit(solution)/shard_map/ppermute | solution.py:190
  166.2 4.8 %collective-permute-start.16 = (f32[24,8,384]{2,1,0:T(8,128)S(1)}, f32[24,8,384]{2,1,0:T(8,128)S(1)}, u32[]{:S(2)}, u32[]{:S(2)}) collective-permute-start(f32[24,8,384]{2,1,0:T(8,128)S(1)} %collective-permute-done.12.a1), channel_id=1, source_target_pairs={{0,1},{1,0},{2,3},{3,2},{4,5},{5,4},{6,7},{7,6},{8,9},{9,8},{10,11... | collective-permute-start | bytes 884744 | tf_op jit(solution)/shard_map/ppermute | solution.py:190
  171.0 3.2 %collective-permute-start.17 = (f32[24,8,384]{2,1,0:T(8,128)S(1)}, f32[24,8,384]{2,1,0:T(8,128)S(1)}, u32[]{:S(2)}, u32[]{:S(2)}) collective-permute-start(f32[24,8,384]{2,1,0:T(8,128)S(1)} %collective-permute-done.13.a2), channel_id=1, source_target_pairs={{0,1},{1,0},{2,3},{3,2},{4,5},{5,4},{6,7},{7,6},{8,9},{9,8},{10,11... | collective-permute-start | bytes 884744 | tf_op jit(solution)/shard_map/ppermute | solution.py:190
  174.2 0.1 collective-permute-start.18
  174.3 34.8 %all-gather.3.cloned.1.call-done = f32[256,4,256]{2,1,0:T(4,128)} async-done(((f32[1,4,256]{2,1,0:T(4,128)}), f32[256,4,256]{2,1,0:T(4,128)}) %all-gather.3.cloned.1.call-update) | async-done | bytes 1048592 | tf_op jit(solution)/shard_map/all_gather | solution.py:256
  209.1 2.6 %reshape.80 = f32[1024,256]{1,0:T(8,128)} reshape(f32[256,4,256]{2,1,0:T(4,128)} %all-gather.3.cloned.1.call-done) | data formatting | bytes 2097152
  211.7 5.9 %gather_fusion = f32[1024,256]{1,0:T(8,128)} fusion(f32[1024,256]{1,0:T(8,128)} %reshape.80, s32[1024]{0:T(1024)S(1)} %fusion.1), kind=kCustom, calls=%fused_computation.2 | custom fusion | bytes 2101248 | tf_op jit(solution)/shard_map/jit(_take)/gather | solution.py:257
  217.6 2.4 %broadcast_select_fusion = f32[1024,256]{1,0:T(8,128)} fusion(f32[1024,256]{1,0:T(8,128)} %gather_fusion, pred[1024]{0:T(1024)(128)(4,1)S(1)} %compare_and_fusion), kind=kLoop, calls=%fused_computation.5 | loop fusion | flops 262144 | bytes 2098176 | tf_op jit(solution)/shard_map/jit(_take)/select_n | solution.py:257
  220.0 2.2 shard_map.199
  (53 shorter events, 0.2 us)
Async XLA Ops:
  7.2 66.4 %copy-start = (f32[1024,256]{1,0:T(8,128)S(1)}, f32[1024,256]{1,0:T(8,128)}, u32[]{:S(2)}) copy-start(f32[1024,256]{1,0:T(8,128)} %param.20) | copy-start | bytes 3145732
  12.3 1.2 copy-start.1
  13.5 1.0 copy-start.10
  14.6 0.9 copy-start.13
  15.5 0.7 copy-start.14
  19.8 1.1 copy-start.7
  20.9 13.6 %copy-start.16 = (s32[1024]{0:T(1024)S(1)}, s32[1024]{0:T(1024)}, u32[]{:S(2)}) copy-start(s32[1024]{0:T(1024)} %param.29) | copy-start | bytes 12292
  20.9 41.9 %all-to-all-start = ((bf16[32,32,640]{2,1,0:T(8,128)(2,1)}), bf16[32,32,640]{2,1,0:T(8,128)(2,1)S(1)}, u32[]{:S(2)}, u32[]{:S(2)}) async-start(bf16[32,32,640]{2,1,0:T(8,128)(2,1)} %bitcast.15), calls=%async_computation | async-start | bytes 2621440 | tf_op jit(solution)/shard_map/all_to_all | solution.py:238
  33.1 44.1 %collective-permute-start.4 = (f32[32,512]{1,0:T(8,128)S(1)}, f32[32,512]{1,0:T(8,128)S(1)}, u32[]{:S(2)}, u32[]{:S(2)}) collective-permute-start(f32[32,512]{1,0:T(8,128)S(1)} %slice.16), channel_id=1, source_target_pairs={{0,8},{8,16},{16,24},{24,32},{32,40},{40,48},{48,56},{56,64},{64,7... | collective-permute-start | bytes 196616 | tf_op jit(solution)/shard_map/ppermute | solution.py:240
  65.9 1.0 copy-start.8
  67.0 15.3 %collective-permute-start = (f32[4,136,512]{2,1,0:T(8,128)}, f32[4,136,512]{2,1,0:T(8,128)}, u32[]{:S(2)}, u32[]{:S(2)}) collective-permute-start(f32[4,136,512]{2,1,0:T(8,128)} %get-tuple-element.21), channel_id=1, source_target_pairs={{0,1},{1,0},{2,3},{3,2},{4,5},{5,4},{6,7},{7,6},{8,9},{9,8},{10,11... | collective-permute-start | bytes 3342344 | tf_op jit(solution)/shard_map/ppermute | solution.py:190
  74.3 7.9 %copy-start.9 = (f32[4,136,512]{2,1,0:T(8,128)S(1)}, f32[4,136,512]{2,1,0:T(8,128)}, u32[]{:S(2)}) copy-start(f32[4,136,512]{2,1,0:T(8,128)} %copy-done.8) | copy-start | bytes 3342340
  77.9 12.5 %all-to-all-start.1 = ((f32[8,8,512]{2,1,0:T(8,128)}), f32[8,8,512]{2,1,0:T(8,128)S(1)}, u32[]{:S(2)}, u32[]{:S(2)}) async-start(f32[8,8,512]{2,1,0:T(8,128)} %maximum_bitcast_fusion), calls=%async_computation.1 | async-start | bytes 262144 | tf_op jit(solution)/shard_map/all_to_all | solution.py:242
  82.3 8.0 %copy-start.2 = (f32[1024,256]{1,0:T(8,128)S(1)}, f32[1024,256]{1,0:T(8,128)}, u32[]{:S(2)}) copy-start(f32[1024,256]{1,0:T(8,128)} %mem.1) | copy-start | bytes 3145732
  82.3 126.8 %all-gather.3.cloned.1.call-start = ((), (), s32[]{:S(2)}) async-start(), calls=%async_computation.4 | async-start | bytes 1052672 | tf_op jit(solution)/shard_map/all_gather | solution.py:256
  84.6 0.7 copy-start.11
  85.3 9.8 %collective-permute-start.1 = (f32[136,512]{1,0:T(8,128)}, f32[136,512]{1,0:T(8,128)}, u32[]{:S(2)}, u32[]{:S(2)}) collective-permute-start(f32[136,512]{1,0:T(8,128)} %get-tuple-element.23), channel_id=1, source_target_pairs={{0,2},{1,3},{2,4},{3,5},{4,6},{5,7},{6,0},{7,1},{8,10},{9,11},{10,... | collective-permute-start | bytes 835592 | tf_op jit(solution)/shard_map/ppermute | solution.py:194
  86.7 15.1 %collective-permute-start.2 = (f32[136,512]{1,0:T(8,128)}, f32[136,512]{1,0:T(8,128)}, u32[]{:S(2)}, u32[]{:S(2)}) collective-permute-start(f32[136,512]{1,0:T(8,128)} %get-tuple-element.24), channel_id=1, source_target_pairs={{0,4},{1,5},{2,6},{3,7},{4,0},{5,1},{6,2},{7,3},{8,12},{9,13},{10,... | collective-permute-start | bytes 835592 | tf_op jit(solution)/shard_map/ppermute | solution.py:194
  89.1 12.7 %collective-permute-start.3 = (f32[136,512]{1,0:T(8,128)}, f32[136,512]{1,0:T(8,128)}, u32[]{:S(2)}, u32[]{:S(2)}) collective-permute-start(f32[136,512]{1,0:T(8,128)} %get-tuple-element.25), channel_id=1, source_target_pairs={{0,6},{1,7},{2,0},{3,1},{4,2},{5,3},{6,4},{7,5},{8,14},{9,15},{10,... | collective-permute-start | bytes 835592 | tf_op jit(solution)/shard_map/ppermute | solution.py:194
  90.4 1.1 copy-start.3
  91.5 1.0 copy-start.5
  92.5 23.0 %copy-start.15 = (f32[128,256]{1,0:T(8,128)S(1)}, f32[128,256]{1,0:T(8,128)}, u32[]{:S(2)}) copy-start(f32[128,256]{1,0:T(8,128)} %get-tuple-element.35) | copy-start | bytes 393220
  101.8 1.0 copy-start.12
  104.0 6.7 %collective-permute-start.6 = (bf16[144,512]{1,0:T(8,128)(2,1)S(1)}, bf16[144,512]{1,0:T(8,128)(2,1)S(1)}, u32[]{:S(2)}, u32[]{:S(2)}) collective-permute-start(bf16[144,512]{1,0:T(8,128)(2,1)S(1)} %shard_map.196.a0), channel_id=1, source_target_pairs={{0,4},{1,5},{2,6},{3,7},{4,0},{5,1},{6,2},{7,3},{8,12},{9,13},{10,... | collective-permute-start | bytes 442376 | tf_op jit(solution)/shard_map/ppermute | solution.py:194
  106.2 7.7 %collective-permute-start.7 = (bf16[144,512]{1,0:T(8,128)(2,1)S(1)}, bf16[144,512]{1,0:T(8,128)(2,1)S(1)}, u32[]{:S(2)}, u32[]{:S(2)}) collective-permute-start(bf16[144,512]{1,0:T(8,128)(2,1)S(1)} %shard_map.196.a0), channel_id=1, source_target_pairs={{0,6},{1,7},{2,0},{3,1},{4,2},{5,3},{6,4},{7,5},{8,14},{9,15},{10,... | collective-permute-start | bytes 442376 | tf_op jit(solution)/shard_map/ppermute | solution.py:194
  107.3 7.9 %collective-permute-start.5 = (bf16[144,512]{1,0:T(8,128)(2,1)S(1)}, bf16[144,512]{1,0:T(8,128)(2,1)S(1)}, u32[]{:S(2)}, u32[]{:S(2)}) collective-permute-start(bf16[144,512]{1,0:T(8,128)(2,1)S(1)} %shard_map.196.a0), channel_id=1, source_target_pairs={{0,2},{1,3},{2,4},{3,5},{4,6},{5,7},{6,0},{7,1},{8,10},{9,11},{10,... | collective-permute-start | bytes 442376 | tf_op jit(solution)/shard_map/ppermute | solution.py:194
  108.3 8.7 %collective-permute-start.8 = (bf16[144,512]{1,0:T(8,128)(2,1)S(1)}, bf16[144,512]{1,0:T(8,128)(2,1)S(1)}, u32[]{:S(2)}, u32[]{:S(2)}) collective-permute-start(bf16[144,512]{1,0:T(8,128)(2,1)S(1)} %shard_map.196.a0), channel_id=1, source_target_pairs={{0,1},{1,0},{2,3},{3,2},{4,5},{5,4},{6,7},{7,6},{8,9},{9,8},{10,11... | collective-permute-start | bytes 442376 | tf_op jit(solution)/shard_map/ppermute | solution.py:190
  110.7 6.3 %collective-permute-start.10 = (bf16[144,512]{1,0:T(8,128)(2,1)S(1)}, bf16[144,512]{1,0:T(8,128)(2,1)S(1)}, u32[]{:S(2)}, u32[]{:S(2)}) collective-permute-start(bf16[144,512]{1,0:T(8,128)(2,1)S(1)} %collective-permute-done.6.a2), channel_id=1, source_target_pairs={{0,1},{1,0},{2,3},{3,2},{4,5},{5,4},{6,7},{7,6},{8,9},{9,8},{10,11... | collective-permute-start | bytes 442376 | tf_op jit(solution)/shard_map/ppermute | solution.py:190
  113.9 3.1 %collective-permute-start.11 = (bf16[144,512]{1,0:T(8,128)(2,1)S(1)}, bf16[144,512]{1,0:T(8,128)(2,1)S(1)}, u32[]{:S(2)}, u32[]{:S(2)}) collective-permute-start(bf16[144,512]{1,0:T(8,128)(2,1)S(1)} %collective-permute-done.7.a3), channel_id=1, source_target_pairs={{0,1},{1,0},{2,3},{3,2},{4,5},{5,4},{6,7},{7,6},{8,9},{9,8},{10,11... | collective-permute-start | bytes 442376 | tf_op jit(solution)/shard_map/ppermute | solution.py:190
  115.2 1.8 collective-permute-start.9
  115.6 1.4 copy-start.4
  115.6 1.5 copy-start.6
  156.5 9.6 %collective-permute-start.12 = (f32[24,8,384]{2,1,0:T(8,128)S(1)}, f32[24,8,384]{2,1,0:T(8,128)S(1)}, u32[]{:S(2)}, u32[]{:S(2)}) collective-permute-start(f32[24,8,384]{2,1,0:T(8,128)S(1)} %slice.26.a0), channel_id=1, source_target_pairs={{0,2},{1,3},{2,4},{3,5},{4,6},{5,7},{6,0},{7,1},{8,10},{9,11},{10,... | collective-permute-start | bytes 884744 | tf_op jit(solution)/shard_map/ppermute | solution.py:194
  156.8 14.1 %collective-permute-start.13 = (f32[24,8,384]{2,1,0:T(8,128)S(1)}, f32[24,8,384]{2,1,0:T(8,128)S(1)}, u32[]{:S(2)}, u32[]{:S(2)}) collective-permute-start(f32[24,8,384]{2,1,0:T(8,128)S(1)} %slice.26.a0), channel_id=1, source_target_pairs={{0,4},{1,5},{2,6},{3,7},{4,0},{5,1},{6,2},{7,3},{8,12},{9,13},{10,... | collective-permute-start | bytes 884744 | tf_op jit(solution)/shard_map/ppermute | solution.py:194
  159.8 14.4 %collective-permute-start.14 = (f32[24,8,384]{2,1,0:T(8,128)S(1)}, f32[24,8,384]{2,1,0:T(8,128)S(1)}, u32[]{:S(2)}, u32[]{:S(2)}) collective-permute-start(f32[24,8,384]{2,1,0:T(8,128)S(1)} %slice.26.a0), channel_id=1, source_target_pairs={{0,6},{1,7},{2,0},{3,1},{4,2},{5,3},{6,4},{7,5},{8,14},{9,15},{10,... | collective-permute-start | bytes 884744 | tf_op jit(solution)/shard_map/ppermute | solution.py:194
  161.0 58.9 %collective-permute-start.15 = (f32[24,8,384]{2,1,0:T(8,128)S(1)}, f32[24,8,384]{2,1,0:T(8,128)S(1)}, u32[]{:S(2)}, u32[]{:S(2)}) collective-permute-start(f32[24,8,384]{2,1,0:T(8,128)S(1)} %slice.26.a0), channel_id=1, source_target_pairs={{0,1},{1,0},{2,3},{3,2},{4,5},{5,4},{6,7},{7,6},{8,9},{9,8},{10,11... | collective-permute-start | bytes 884744 | tf_op jit(solution)/shard_map/ppermute | solution.py:190
  166.2 53.8 %collective-permute-start.16 = (f32[24,8,384]{2,1,0:T(8,128)S(1)}, f32[24,8,384]{2,1,0:T(8,128)S(1)}, u32[]{:S(2)}, u32[]{:S(2)}) collective-permute-start(f32[24,8,384]{2,1,0:T(8,128)S(1)} %collective-permute-done.12.a1), channel_id=1, source_target_pairs={{0,1},{1,0},{2,3},{3,2},{4,5},{5,4},{6,7},{7,6},{8,9},{9,8},{10,11... | collective-permute-start | bytes 884744 | tf_op jit(solution)/shard_map/ppermute | solution.py:190
  171.0 49.0 %collective-permute-start.17 = (f32[24,8,384]{2,1,0:T(8,128)S(1)}, f32[24,8,384]{2,1,0:T(8,128)S(1)}, u32[]{:S(2)}, u32[]{:S(2)}) collective-permute-start(f32[24,8,384]{2,1,0:T(8,128)S(1)} %collective-permute-done.13.a2), channel_id=1, source_target_pairs={{0,1},{1,0},{2,3},{3,2},{4,5},{5,4},{6,7},{7,6},{8,9},{9,8},{10,11... | collective-permute-start | bytes 884744 | tf_op jit(solution)/shard_map/ppermute | solution.py:190
  174.2 45.8 %collective-permute-start.18 = (f32[24,8,384]{2,1,0:T(8,128)S(1)}, f32[24,8,384]{2,1,0:T(8,128)S(1)}, u32[]{:S(2)}, u32[]{:S(2)}) collective-permute-start(f32[24,8,384]{2,1,0:T(8,128)S(1)} %collective-permute-done.14.a3), channel_id=1, source_target_pairs={{0,1},{1,0},{2,3},{3,2},{4,5},{5,4},{6,7},{7,6},{8,9},{9,8},{10,11... | collective-permute-start | bytes 884744 | tf_op jit(solution)/shard_map/ppermute | solution.py:190
Sparse Core Ops, SparseCore 0:
  108.4 100.6 all-gather.2

commit v2 on v1

--- a/solution.py
+++ b/solution.py
@@ -11,6 +11,7 @@
 PARAMS = pltpu.CompilerParams(vmem_limit_bytes=48 * 1024 * 1024)
 VM = pl.BlockSpec(memory_space=pltpu.VMEM)
 SM = pl.BlockSpec(memory_space=pltpu.SMEM)
+HB = pl.BlockSpec(memory_space=pl.ANY)
 
 
 def iota(shape, dim):
@@ -25,72 +26,158 @@
     return lax.dot_general(a, b, (dims, ((), ())), preferred_element_type=F32)
 
 
-def call(body, out_shape, n_smem, args, scratch=()):
+def call(body, out_shape, places, args, scratch=(), out_places=None):
+    if out_places is None:
+        out_places = jax.tree.map(lambda _: VM, out_shape)
     return pl.pallas_call(
         body,
         out_shape=out_shape,
-        in_specs=[SM] * n_smem + [VM] * (len(args) - n_smem),
-        out_specs=jax.tree.map(lambda _: VM, out_shape),
+        in_specs=list(places) + [VM] * (len(args) - len(places)),
+        out_specs=out_places,
         scratch_shapes=list(scratch),
         compiler_params=PARAMS,
     )(*args)
 
 
-def message_kernel(pos, idx, mem, edge, enc, w, b, send, hot, msgs, cols):
-    cols[...] = idx[...].T
+def column(row):
+    return jnp.broadcast_to(row, (8, row.shape[1])).T[:, 0:1]
+
+
+def cosine(x):
+    k = jnp.round(x * 0.15915494309189535)
+    r = x - k * 6.28125
+    r = r - k * 0.0019350051879882812
+    r = r - k * 3.019916e-07
+    u = 1.5707963267948966 - jnp.abs(r)
+    u2 = u * u
+    p = 2.6083159809786593e-06
+    for c in (-0.00019810690719168633, 0.0083330785855650902, -0.16666659712791443, 1.0):
+        p = p * u2 + c
+    return u * p
+
+
+def message_kernel(
+    pos, mem_h, edge_h, w_h, src, times, dst_ref, listed, used, freq, phase, b, send_h, hot,
+    mem, edge, w, msgs, out, cols, sems,
+):
+    loads = [
+        pltpu.make_async_copy(h, v, sems.at[i])
+        for i, (h, v) in enumerate(((mem_h, mem), (edge_h, edge), (w_h, w)))
+    ]
+    for c in loads:
+        c.start()
+    n_ev, step = 1024, 256
+    dst = dst_ref[...]
+    line = iota((8, n_ev), 0)
+    packed = jnp.where(line == 0, src[...], jnp.where(line == 1, times[...], dst))
+    cols[...] = packed.T
+    slot = iota((32, 32), 0)
+    eye = one_hot(slot == iota((32, 32), 1))
+    names = listed[...]
+    hi = mm(eye, (names >> 5).astype(F32).astype(BF16), ((1,), (1,)))
+    lo = mm(eye, (names & 31).astype(F32).astype(BF16), ((1,), (1,)))
+    names = jnp.where(slot < used[...], (hi * 32.0 + lo).astype(I32), -1)
+    for c in loads:
+        c.wait()
     mem16 = mem[...].astype(BF16)
-    n_ev = idx.shape[1]
-    step = 256
     for e in range(0, n_ev, step):
-        src = cols[e : e + step, 0:1]
-        src_mem = mm(one_hot(iota((step, mem.shape[0]), 1) == src), mem16).astype(BF16)
-        raw = jnp.concatenate([src_mem, edge[e : e + step, :], enc[e : e + step, :]], axis=1)
+        at = cols[e : e + step, :]
+        src_mem = mm(one_hot(iota((step, 1024), 1) == at[:, 0:1]), mem16).astype(BF16)
+        enc = cosine(at[:, 1:2].astype(F32) * freq[...] + phase[...]).astype(BF16)
+        raw = jnp.concatenate([src_mem, edge[e : e + step, :], enc], axis=1)
         pre = mm(raw, w[...]) + b[...]
-        msgs[e : e + step, 0:512] = (pre * jax.nn.sigmoid(pre)).astype(BF16)
-        row = cols[e : e + step, 2:3] & 1023
-        lane = iota((step, 128), 1)
-        tail = jnp.where(lane == 0, row >> 5, jnp.where(lane == 1, row & 31, jnp.where(lane == 2, 1, 0)))
-        msgs[e : e + step, 512:640] = tail.astype(F32).astype(BF16)
-    for s in range(0, n_ev, step):
-        pick = one_hot(iota((step, n_ev), 1) == cols[s : s + step, 3:4])
-        send[s : s + step, :] = mm(pick, msgs[...]).astype(BF16)
-    dst = idx[2:3, :]
+        msgs[e : e + step, :] = (pre * jax.nn.sigmoid(pre)).astype(BF16)
+    row = dst & 1023
+    facts = jnp.where(line == 0, row >> 5, jnp.where(line == 1, row & 31, jnp.where(line == 2, 1, 0)))
+    facts = facts.astype(F32).astype(BF16)
+    lane = iota((8, 128), 1)
+    stores = []
+    for t in range(4):
+        pick = jnp.concatenate(
+            [one_hot(iota((32, n_ev), 1) == names[:, o : o + 1]) for o in range(8 * t, 8 * t + 8)], axis=0
+        )
+        moved = mm(pick, msgs[...]).astype(BF16)
+        tail = mm(facts, pick, ((1,), (1,)))
+        for i in range(8):
+            o = 8 * t + i
+            for q in range(4):
+                out[o, 32 * q : 32 * q + 32, :] = moved[32 * i : 32 * i + 32, 128 * q : 128 * q + 128]
+            k = o % 4
+            own = tail[:, 128 * (i // 4) : 128 * (i // 4) + 128]
+            own = jnp.where((lane >> 5) == k, own, 0.0)
+            own = pltpu.roll(own, ((pos[0] & 3) + 4 - k) * 32 & 127, 1)
+            out[o, 128:144, :] = jnp.concatenate([own, jnp.zeros((8, 128), F32)], axis=0).astype(BF16)
+        here = pl.ds(8 * t, 8)
+        stores.append(pltpu.make_async_copy(out.at[here], send_h.at[here], sems.at[3 + t]))
+        stores[-1].start()
     window = jnp.where(dst >= 32768, (dst - 32768 - 32 * pos[0] + 1024) & 1023, -1)
     q = iota((96, n_ev), 0)
-    hit = one_hot(4 * (q >> 3) + (q & 3) == window)
-    total = mm(hit, msgs[:, 0:512])
+    block = jnp.where(q < 64, 2 * ((q >> 3) & 3) + ((q >> 5) & 1), 8 + 2 * ((q >> 3) & 1) + ((q >> 4) & 1))
+    hit = one_hot(4 * block + (q & 3) == window)
+    total = mm(hit, msgs[...])
     count = jnp.sum(hit.astype(F32), axis=1, keepdims=True)
     hot[...] = jnp.where((iota((96, 512), 0) & 7) < 4, total, count)
-
-
-def cold_kernel(pos, recv, keep, send):
-    tail = recv[:, 512:640].astype(F32).T
-    row = jnp.where(tail[2:3, :] > 0.5, tail[0:1, :] * 32.0 + tail[1:2, :], -1.0).astype(I32)
-    ones = jnp.ones((8, recv.shape[0]), BF16)
-    for out, core in ((send, 1 - pos[1]), (keep, pos[1])):
-        q = iota((512, recv.shape[0]), 0)
-        hit = one_hot(((q >> 7) * 256 + (q & 127) + core * 128) == row)
-        total = mm(hit, recv[:, 0:512])
-        count = mm(ones, hit, ((1,), (1,)))
-        for j in range(4):
-            out[j, 0:128, :] = total[128 * j : 128 * j + 128, :]
-            out[j, 128:136, 0:128] = count[:, 128 * j : 128 * j + 128]
-            out[j, 128:136, 128:512] = jnp.zeros((8, 384), F32)
-
-
-def add_kernel(pos, keep, recv, o0, o1, o2, o3):
-    for d, out in enumerate((o0, o1, o2, o3)):
-        j = (pos[0] + d) & 3
-        out[...] = keep[j] + recv[j]
-
-
-def agg_kernel(p0, p1, p2, p3, hot, out):
-    total = p0[...] + p1[...] + p2[...] + p3[...]
-    count = total[128:129, 0:128]
-    count = jnp.sum(jnp.where(iota((128, 128), 0) == iota((128, 128), 1), count, 0.0), axis=1, keepdims=True)
+    for c in stores:
+        c.wait()
+
+
+def cold_kernel(pos, own_h, peer_h, tie, o0, o1_h, o2_h, o3_h, got, msgs, out, sems):
+    loads = [pltpu.make_async_copy(h, got.at[i], sems.at[i]) for i, h in enumerate((own_h, peer_h))]
+    for c in loads:
+        c.start()
+    q = iota((512, 128), 0)
+    want = (q & 127) + 256 * ((pos[0] + (q >> 7)) & 3) + 128 * pos[1]
+    hits = []
+    for h in range(2):
+        loads[h].wait()
+        for g in range(8):
+            tail = got[h, 4 * g, 128:144, :].astype(F32)
+            for i in range(1, 4):
+                tail = tail + got[h, 4 * g + i, 128:144, :].astype(F32)
+            row = jnp.where(tail[2:3, :] > 0.5, tail[0:1, :] * 32.0 + tail[1:2, :], -1.0).astype(I32)
+            hits.append(one_hot(want == row))
+        for s in range(32):
+            for k in range(4):
+                here = slice(1024 * h + 32 * s, 1024 * h + 32 * s + 32)
+                msgs[here, 128 * k : 128 * k + 128] = got[h, s, 32 * k : 32 * k + 32, :]
+    hit = jnp.concatenate(hits, axis=1)
+    count = mm(jnp.ones((8, 2048), BF16), hit, ((1,), (1,)))
+    stores = []
+    for n in range(2):
+        cols = slice(256 * n, 256 * n + 256)
+        total = mm(hit, msgs[:, cols])
+        for d in (2, 1, 3, 0):
+            here = slice(128 * d, 128 * d + 128)
+            to = o0 if d == 0 else out.at[d - 1]
+            to[0:128, cols] = total[here, :]
+            if n == 0:
+                to[128:136, 0:128] = count[:, here]
+                to[128:136, 128:256] = jnp.zeros((8, 128), F32)
+            else:
+                to[128:136, cols] = jnp.zeros((8, 256), F32)
+            if d > 0:
+                dst = (o1_h, o2_h, o3_h)[d - 1]
+                c = pltpu.make_async_copy(out.at[d - 1, :, cols], dst.at[:, cols], sems.at[2 + 3 * n + d - 1])
+                c.start()
+                stores.append(c)
+    for c in stores:
+        c.wait()
+
+
+def agg_kernel(p1_h, p2_h, p3_h, p0, hot, out_h, part, out, sems):
+    loads = [pltpu.make_async_copy(h, part.at[i], sems.at[i]) for i, h in enumerate((p1_h, p2_h, p3_h))]
+    for c in loads:
+        c.start()
+    out[128:144, :] = hot[...]
+    for c in loads:
+        c.wait()
+    total = p0[...] + part[0] + part[1] + part[2]
+    count = column(total[128:129, 0:128])
     agg = jnp.where(count > 0.0, total[0:128, :] / jnp.maximum(count, 1.0), DEAD)
     out[0:128, :] = agg.astype(BF16)
-    out[128:144, :] = hot[...]
+    store = pltpu.make_async_copy(out, out_h, sems.at[3])
+    store.start()
+    store.wait()
 
 
 def gates(agg, mem, w_in, w_hid):
@@ -102,10 +189,8 @@
     return reset, update, cand, gh[:, 512:768]
 
 
-def hot_kernel(parts, mem, w_in, w_hid, agg_out, new_out):
-    total = parts[0]
-    for k in range(1, 8):
-        total = total + parts[k]
+def hot_kernel(p0, p1, p2, p3, mem, w_in, w_hid, agg_out, new_out):
+    total = p0[...] + p1[...] + p2[...] + p3[...]
     count = total[4:8, :]
     agg = jnp.where(count > 0.0, total[0:4, :] / jnp.maximum(count, 1.0), DEAD)
     agg = jnp.concatenate([agg, jnp.full((12, 512), DEAD, F32)], axis=0).astype(BF16)
@@ -116,6 +201,19 @@
     agg = jnp.where(wide < DEAD * 0.5, wide, 0.0).astype(BF16)
     reset, update, cand, _ = gates(agg, mem, w_in[...], w_hid[...])
     new_out[...] = jnp.where(live, (1.0 - update) * cand + update * mem, mem)[0:8, :]
+
+
+def hot_place_kernel(ids, rows, out):
+    names = column(ids[...]) - 32768
+    at = 8 * (names >> 2) + (names & 3)
+    full = rows[...]
+    hi = full.astype(BF16)
+    rest = full - hi.astype(F32)
+    mid = rest.astype(BF16)
+    low = (rest - mid.astype(F32)).astype(BF16)
+    for h in range(0, 1024, 256):
+        pick = one_hot(iota((256, 2048), 1) == at[h : h + 256, :])
+        out[h : h + 256, :] = mm(pick, hi) + (mm(pick, mid) + mm(pick, low))
 
 
 def update_kernel(pos, a0, a1, a2, a3, b0, b1, b2, b3, mem, cot, w_in, w_hid, new, grad, agg, acc):
@@ -223,59 +321,85 @@
     pos = jnp.stack([rep // 2, rep % 2, rep]).astype(I32)
     sds = jax.ShapeDtypeStruct
 
-    slots = jnp.arange(32, dtype=I32)
-    listed = jnp.where(slots[None, :] < cold_count[:, None], cold_list, -1).reshape(-1)
-    zero = jnp.zeros_like(listed)
-    idx = jnp.stack([src_local, times, dst_ids, listed, zero, zero, zero, zero])
-    enc = jnp.cos(times.astype(F32)[:, None] * time_freq[None, :] + time_phase[None, :]).astype(BF16)
+    chip, core = rep // 2, rep % 2
     send, hot = call(
         message_kernel,
-        (sds((1024, 640), BF16), sds((96, 512), F32)),
-        1,
-        (node.astype(I32)[None], idx, memory, edge_feat, enc, w_msg, b_msg[None, :]),
-        (pltpu.VMEM((1024, 640), BF16), pltpu.VMEM((1024, 8), I32)),
+        (sds((32, 144, 128), BF16), sds((96, 512), F32)),
+        (SM, HB, HB, HB),
+        (
+            node.astype(I32)[None], memory, edge_feat, w_msg, src_local[None, :], times[None, :],
+            dst_ids[None, :], cold_list, cold_count[None, :], time_freq[None, :], time_phase[None, :],
+            b_msg[None, :],
+        ),
+        (
+            pltpu.VMEM((1024, 256), F32), pltpu.VMEM((1024, 128), BF16), pltpu.VMEM((512, 512), BF16),
+            pltpu.VMEM((1024, 512), BF16), pltpu.VMEM((32, 144, 128), BF16), pltpu.VMEM((1024, 8), I32),
+            pltpu.SemaphoreType.DMA((7,)),
+        ),
+        (HB, VM),
     )
     recv = lax.all_to_all(send, "node", split_axis=0, concat_axis=0, tiled=True)
 
-    spill = lax.ppermute(hot[64:96], "node", [(k, (k + 1) % 32) for k in range(32)])
-    hot_main = jnp.concatenate([hot[0:32] + spill, hot[32:64]], axis=0)
-    hot_parts = lax.all_to_all(hot_main, "rep", split_axis=0, concat_axis=0, tiled=True)
+    spill = lax.ppermute(hot[64:96], "node", [(k, (k + 1) % 32) for k in range(32)]).reshape(2, 2, 8, 512)
+    hot = hot[0:64].reshape(2, 4, 8, 512)
+    hot = jnp.concatenate([hot[:, 0:2] + spill, hot[:, 2:4]], axis=1)
+    got = swap_core(lax.dynamic_index_in_dim(hot, 1 - core, 0, False))
+    hot = lax.dynamic_index_in_dim(hot, core, 0, False) + got
+    hot = [lax.dynamic_index_in_dim(hot, (chip + d) % 4, 0, False) for d in range(4)]
+    hot = [hot[0]] + [shift_x(hot[d], d) for d in (1, 2, 3)]
     k = jnp.arange(128, dtype=I32)
     want = 32768 + 32 * node + 4 * (k // 16) + k % 4
     at = jnp.sum(jnp.where(want[:, None] == hot_ids[None, :], jnp.arange(1024, dtype=I32)[None, :], 0), axis=1)
-    hot_mem = jnp.take(hot_memory, at, axis=0)
+    hot_mem = jnp.take(hot_memory, at, axis=0, mode="clip")
     mem_all = jnp.concatenate([memory, hot_mem], axis=0)
-    cot_all = jnp.concatenate([cot_cold, jnp.take(cot_hot, at, axis=0)], axis=0)
+    cot_all = jnp.concatenate([cot_cold, jnp.take(cot_hot, at, axis=0, mode="clip")], axis=0)
     own_mem = lax.dynamic_slice_in_dim(hot_mem, 16 * rep, 16, 0)
     hot_agg, hot_new = call(
         hot_kernel,
         (sds((16, 512), BF16), sds((8, 256), F32)),
-        0,
-        (hot_parts.reshape(8, 8, 512), own_mem, w_in, w_hid),
-    )
-    hot_all = lax.all_gather(hot_new[0:4], ("node", "rep"), axis=0, tiled=True)
-    new_hot = jnp.take(hot_all, hot_ids - 32768, axis=0)
-
+        (),
+        (*hot, own_mem, w_in, w_hid),
+    )
+    hot_all = lax.all_gather(hot_new, ("node", "rep"), axis=0, tiled=True)
+    new_hot = call(hot_place_kernel, sds((1024, 256), F32), (), (hot_ids[None, :], hot_all))
+
+    recv, hot_agg, mem_all, cot_all = lax.optimization_barrier((recv, hot_agg, mem_all, cot_all))
     block = sds((136, 512), F32)
-    keep, give = call(cold_kernel, (sds((4, 136, 512), F32),) * 2, 1, (pos, recv))
-    parts = call(add_kernel, (block,) * 4, 1, (pos, keep, swap_core(give)))
+    parts = call(
+        cold_kernel,
+        (block,) * 4,
+        (SM, HB, HB, HB),
+        (pos, recv, swap_core(recv), hot_agg),
+        (
+            pltpu.VMEM((2, 32, 144, 128), BF16), pltpu.VMEM((2048, 512), BF16), pltpu.VMEM((3, 136, 512), F32),
+            pltpu.SemaphoreType.DMA((8,)),
+        ),
+        (VM, HB, HB, HB),
+    )
     parts = [parts[0]] + [shift_x(parts[d], d) for d in (1, 2, 3)]
-    agg = call(agg_kernel, sds((144, 512), BF16), 0, (*parts, hot_agg))
+    agg = call(
+        agg_kernel,
+        sds((144, 512), BF16),
+        (HB, HB, HB),
+        (*parts[1:], parts[0], hot_agg),
+        (pltpu.VMEM((3, 136, 512), F32), pltpu.VMEM((144, 512), BF16), pltpu.SemaphoreType.DMA((4,))),
+        HB,
+    )
     new_memory, grad = call(
         update_kernel,
         (sds((1024, 256), F32), sds((32, 8, 384), F32)),
-        1,
+        (SM,),
         (pos, *gather_rep(agg), mem_all, cot_all, w_in, w_hid),
         (pltpu.VMEM((1152, 512), BF16), pltpu.VMEM((128, 1024), F32)),
     )
 
     grad = lax.all_to_all(grad, "node", split_axis=0, concat_axis=0, tiled=True)
-    grad = call(piece_kernel, sds((32, 8, 384), F32), 0, (grad,))
+    grad = call(piece_kernel, sds((32, 8, 384), F32), (), (grad,))
     grad = lax.all_to_all(grad, "node", split_axis=0, concat_axis=0, tiled=True)
     grad_in, grad_hid = call(
         place_kernel,
         (sds((512, 768), F32), sds((256, 768), F32)),
-        1,
+        (SM,),
         (pos, *gather_rep(grad[0:24])),
     )
     return (new_memory, new_hot, grad_in, grad_hid)

time: 230 us -> 199 us (0.87)
  waiting for transfers between devices: 72.7 us -> 53.7 us
  local copies, waits for them, and re-layouts: 22.6 us -> 13.8 us
  starting transfers between devices: 57.4 us -> 50.6 us
  other arithmetic: 9.86 us -> 4.15 us
  Pallas kernels: 18.6 us -> 24.2 us
  blocking collectives: 33.5 us -> 36.8 us
    all_gather x1, waiting for transfers between devices: 34.8 us -> 0.01 us  [on_device(): hot_all = lax.all_gather(hot_new, ('node', 'rep'), axis=0, tiled=True)]
    ppermute x1, waiting for transfers between devices: 0.01 us -> 28.7 us  [on_device(): lax.ppermute(hot[64:96], 'node', [(k, (k + 1) % 32) for k in range(32)])]
    all_to_all x1, waiting for transfers between devices: 28.1 us -> 0.01 us  [on_device(): recv = lax.all_to_all(send, 'node', split_axis=0, concat_axis=0, tiled=True)]
    ppermute x9 -> x12, waiting for transfers between devices: 9.71 us -> 20.6 us  [shift_x(): return lax.ppermute(v, 'rep', [(k, (k + 2 * d) % 8) for k in range(8)])]
    pallas_call x8, Pallas kernels: 18.6 us -> 24.2 us  [call(): pl.pallas_call(body, out_shape=out_shape, in_specs=list(places) + [VM] *...]
    gather x3 -> x2, local copies, waits for them, and re-layouts: 8.72 us -> 3.38 us  [the longest x1 2.63 us: on_device(): jnp.take(cot_hot, at, axis=0, mode='clip')]
    ppermute x9 -> x10, starting transfers between devices: 26.4 us -> 21.4 us  [swap_core(): return lax.ppermute(v, 'rep', [(k, k ^ 1) for k in range(8)])]
    ppermute x9 -> x10, waiting for transfers between devices: 0.02 us -> 4.43 us  [swap_core(): return lax.ppermute(v, 'rep', [(k, k ^ 1) for k in range(8)])]
  transfers between devices with their start and end apart: 22 -> 25, of which waited for: 5 -> 12; matrix products, arithmetic and copies ran while one was open for 8% -> 4% of each run, Pallas kernels for 5% -> 9%
where the time goes in v2:
time: 199 us; the launch traced here: 198 us
  waiting for transfers between devices  53.7 us (27%)
  starting transfers between devices  50.6 us (25%)
  blocking collectives  36.8 us (18%)
  Pallas kernels  24.2 us (12%)
  between operations  14.4 us (7%)
  local copies, waits for them, and re-layouts  13.8 us (7%)
  other arithmetic  4.15 us (2%)
    all_to_all x2, blocking collectives, on_device(): grad = lax.all_to_all(grad, 'node', split_axis=0, concat_axis=0, tiled=True)  36.8 us
    ppermute x1, waiting for transfers between devices, on_device(): lax.ppermute(hot[64:96], 'node', [(k, (k + 1) % 32) for k in range(32)])  28.7 us
    pallas_call x8, Pallas kernels, call(): pl.pallas_call(body, out_shape=out_shape, in_specs=list(places) + [VM] *...  24.2 us
    ppermute x10, starting transfers between devices, swap_core(): return lax.ppermute(v, 'rep', [(k, k ^ 1) for k in range(8)])  21.4 us
    ppermute x12, waiting for transfers between devices, shift_x(): return lax.ppermute(v, 'rep', [(k, (k + 2 * d) % 8) for k in range(8)])  20.6 us
    ppermute x12, starting transfers between devices, shift_x(): return lax.ppermute(v, 'rep', [(k, (k + 2 * d) % 8) for k in range(8)])  15.8 us
    all_to_all x1, starting transfers between devices, on_device(): recv = lax.all_to_all(send, 'node', split_axis=0, concat_axis=0, tiled=True)  12.2 us
    unnamed x40, local copies, waits for them, and re-layouts  10.4 us
  transfers between devices with their start and end apart: 25, of which 12 were waited for; matrix products, arithmetic and copies ran while one was open for 4% of the time, Pallas kernels for 9%

profile of v2, /device:TPU:1, one launch (start us, length us, event | category | flops | bytes accessed | tf_op | source)
XLA Modules:
  0.0 197.7 jit_solution(10061557281517007365)
XLA Ops:
  7.2 1.3 copy-done.1
  8.5 1.0 copy-done.8
  9.5 0.9 copy-done.9
  10.5 0.7 copy-done.10
  11.2 0.7 copy-done.12
  11.9 0.7 copy-done.13
  12.6 0.7 copy-done.14
  13.3 0.7 copy-done.15
  14.0 0.7 copy-done.16
  14.6 0.7 copy-done.17
  15.3 0.7 copy-done.18
  15.9 4.5 %shard_map.192 = (bf16[32,144,128]{2,1,0:T(8,128)(2,1)}, f32[96,512]{1,0:T(8,128)S(1)}) custom-call(s32[1]{0:T(128)} %bitcast.3.pos, f32[1024,256]{1,0:T(8,128)S(1)} %copy-done.1, bf16[1024,128]{1,0:T(8,128)(2,1)S(1)} %copy-done.9, bf16[512,512]{1,0:T(8,128)(2,1)S(1)} %copy-done.8, s32[1,1024]{1,0:T(1,128)S(1)} %bitcast.29, s32[1,1024]{1,0:T(1,128)S(1)} %bitcast.30, ...), custom_call_target="tpu_custom_call" | custom-call | tf_op jit(solution)/shard_map/pallas_call | solution.py:32
  20.4 12.2 %all-to-all-start = ((bf16[32,144,128]{2,1,0:T(8,128)(2,1)}), bf16[32,144,128]{2,1,0:T(8,128)(2,1)}, u32[]{:S(2)}, u32[]{:S(2)}) async-start(bf16[32,144,128]{2,1,0:T(8,128)(2,1)} %get-tuple-element.20), calls=%async_computation | async-start | bytes 2359296 | tf_op jit(solution)/shard_map/all_to_all | solution.py:341
  32.6 0.0 all-gather.2.cloned.1.call-start
  32.6 1.2 collective-permute-start
  34.1 0.2 select_reduce_fusion
  34.3 28.7 %collective-permute-done = f32[32,512]{1,0:T(8,128)S(1)} collective-permute-done((f32[32,512]{1,0:T(8,128)S(1)}, f32[32,512]{1,0:T(8,128)S(1)}, u32[]{:S(2)}, u32[]{:S(2)}) %collective-permute-start) | collective-permute-done | bytes 65568 | tf_op jit(solution)/shard_map/ppermute | solution.py:343
  62.9 0.6 fusion.1
  63.6 2.2 %collective-permute-start.1 = (f32[4,8,512]{2,1,0:T(8,128)}, f32[4,8,512]{2,1,0:T(8,128)}, u32[]{:S(2)}, u32[]{:S(2)}) collective-permute-start(f32[4,8,512]{2,1,0:T(8,128)} %fusion.1), channel_id=1, source_target_pairs={{0,1},{1,0},{2,3},{3,2},{4,5},{5,4},{6,7},{7,6},{8,9},{9,8},{10,11... | collective-permute-start | bytes 196616 | tf_op jit(solution)/shard_map/ppermute | solution.py:288
  65.8 0.8 gather_fusion
  66.6 0.5 collective-permute-done.1
  67.0 0.8 fusion.4
  67.9 1.3 collective-permute-start.2
  69.2 2.5 %collective-permute-start.3 = (f32[8,512]{1,0:T(8,128)S(1)}, f32[8,512]{1,0:T(8,128)S(1)}, u32[]{:S(2)}, u32[]{:S(2)}) collective-permute-start(f32[8,512]{1,0:T(8,128)S(1)} %get-tuple-element.39), channel_id=1, source_target_pairs={{0,4},{1,5},{2,6},{3,7},{4,0},{5,1},{6,2},{7,3},{8,12},{9,13},{10,... | collective-permute-start | bytes 49160 | tf_op jit(solution)/shard_map/ppermute | solution.py:292
  71.6 1.2 collective-permute-start.4
  72.8 0.5 collective-permute-done.3.p2
  73.3 1.2 collective-permute-done.4.p3
  74.5 0.9 shard_map.193
  75.4 0.0 all-gather.2.cloned.1.call-update
  75.5 1.0 pad_maximum_fusion.mem
  76.5 2.6 %gather_fusion.1 = f32[128,256]{1,0:T(8,128)} fusion(f32[1024,256]{1,0:T(8,128)} %param.20, s32[1024]{0:T(1024)S(1)} %pad_clamp_fusion), kind=kCustom, calls=%fused_computation.1 | custom fusion | bytes 262656 | tf_op jit(solution)/shard_map/jit(_take)/gather | solution.py:355
  79.1 1.4 pad_maximum_fusion.1.cot
  80.5 1.9 collective-permute-start.5
  82.3 0.1 pad_add_fusion.pos
  82.4 2.6 %collective-permute-done.5.peer_h = bf16[32,144,128]{2,1,0:T(8,128)(2,1)S(1)} collective-permute-done((bf16[32,144,128]{2,1,0:T(8,128)(2,1)}, bf16[32,144,128]{2,1,0:T(8,128)(2,1)S(1)}, u32[]{:S(2)}, u32[]{:S(2)}) %collective-permute-start.5) | collective-permute-done | bytes 1179680 | tf_op jit(solution)/shard_map/ppermute | solution.py:288
  85.0 5.3 %shard_map.194 = (f32[136,512]{1,0:T(8,128)S(1)}, f32[136,512]{1,0:T(8,128)S(1)}, f32[136,512]{1,0:T(8,128)S(1)}, f32[136,512]{1,0:T(8,128)S(1)}) custom-call(s32[3]{0:T(128)S(1)} %pad_add_fusion.pos, bf16[32,144,128]{2,1,0:T(8,128)(2,1)} %all-to-all-done.own_h, bf16[32,144,128]{2,1,0:T(8,128)(2,1)S(1)} %collective-permute-done.5.peer_h, ...), custom_call_target="tpu_custom_call" | custom-call | tf_op jit(solution)/shard_map/pallas_call | solution.py:32
  90.4 0.3 collective-permute-start.6
  90.6 3.5 %collective-permute-start.7 = (f32[136,512]{1,0:T(8,128)S(1)}, f32[136,512]{1,0:T(8,128)S(1)}, u32[]{:S(2)}, u32[]{:S(2)}) collective-permute-start(f32[136,512]{1,0:T(8,128)S(1)} %get-tuple-element.26), channel_id=1, source_target_pairs={{0,4},{1,5},{2,6},{3,7},{4,0},{5,1},{6,2},{7,3},{8,12},{9,13},{10,... | collective-permute-start | bytes 835592 | tf_op jit(solution)/shard_map/ppermute | solution.py:292
  94.2 5.5 %collective-permute-done.6.p1_h = f32[136,512]{1,0:T(8,128)S(1)} collective-permute-done((f32[136,512]{1,0:T(8,128)S(1)}, f32[136,512]{1,0:T(8,128)S(1)}, u32[]{:S(2)}, u32[]{:S(2)}) %collective-permute-start.6) | collective-permute-done | bytes 278560 | tf_op jit(solution)/shard_map/ppermute | solution.py:292
  99.7 6.8 %collective-permute-done.7.p2_h = f32[136,512]{1,0:T(8,128)S(1)} collective-permute-done((f32[136,512]{1,0:T(8,128)S(1)}, f32[136,512]{1,0:T(8,128)S(1)}, u32[]{:S(2)}, u32[]{:S(2)}) %collective-permute-start.7) | collective-permute-done | bytes 278560 | tf_op jit(solution)/shard_map/ppermute | solution.py:292
  106.6 0.6 shard_map.195.a0
  107.1 1.1 collective-permute-start.9
  108.3 3.0 %collective-permute-start.10 = (bf16[144,512]{1,0:T(8,128)(2,1)S(1)}, bf16[144,512]{1,0:T(8,128)(2,1)S(1)}, u32[]{:S(2)}, u32[]{:S(2)}) collective-permute-start(bf16[144,512]{1,0:T(8,128)(2,1)S(1)} %shard_map.195.a0), channel_id=1, source_target_pairs={{0,4},{1,5},{2,6},{3,7},{4,0},{5,1},{6,2},{7,3},{8,12},{9,13},{10,... | collective-permute-start | bytes 442376 | tf_op jit(solution)/shard_map/ppermute | solution.py:292
  111.2 1.1 collective-permute-start.12
  112.3 0.3 collective-permute-done.9.a1
  112.6 2.3 %collective-permute-start.13 = (bf16[144,512]{1,0:T(8,128)(2,1)S(1)}, bf16[144,512]{1,0:T(8,128)(2,1)S(1)}, u32[]{:S(2)}, u32[]{:S(2)}) collective-permute-start(bf16[144,512]{1,0:T(8,128)(2,1)S(1)} %collective-permute-done.9.a1), channel_id=1, source_target_pairs={{0,1},{1,0},{2,3},{3,2},{4,5},{5,4},{6,7},{7,6},{8,9},{9,8},{10,11... | collective-permute-start | bytes 442376 | tf_op jit(solution)/shard_map/ppermute | solution.py:288
  114.8 3.0 %collective-permute-done.10.a2 = bf16[144,512]{1,0:T(8,128)(2,1)S(1)} collective-permute-done((bf16[144,512]{1,0:T(8,128)(2,1)S(1)}, bf16[144,512]{1,0:T(8,128)(2,1)S(1)}, u32[]{:S(2)}, u32[]{:S(2)}) %collective-permute-start.10) | collective-permute-done | bytes 147488 | tf_op jit(solution)/shard_map/ppermute | solution.py:292
  117.9 1.3 collective-permute-start.14
  119.2 1.0 collective-permute-done.14.b2
  120.2 0.4 collective-permute-done.15.b3
  120.6 6.0 %shard_map.196 = (f32[1024,256]{1,0:T(8,128)}, f32[32,8,384]{2,1,0:T(8,128)S(1)}) custom-call(s32[3]{0:T(128)S(1)} %pad_add_fusion.pos, bf16[144,512]{1,0:T(8,128)(2,1)S(1)} %shard_map.195.a0, bf16[144,512]{1,0:T(8,128)(2,1)S(1)} %collective-permute-done.9.a1, bf16[144,512]{1,0:T(8,128)(2,1)S(1)} %collective-permute-done.10.a2, ...), custom_call_target="tpu_custom_call" | custom-call | tf_op jit(solution)/shard_map/pallas_call | solution.py:32
  126.5 17.4 %all_to_all.15.parts = f32[32,8,384]{2,1,0:T(8,128)S(1)} all-to-all(f32[32,8,384]{2,1,0:T(8,128)S(1)} %get-tuple-element.33), channel_id=1, replica_groups=mesh['node'=32,'rep'=8] {'node'}, dimensions={0} | all-to-all | bytes 786432 | tf_op jit(solution)/shard_map/all_to_all | solution.py:396
  144.0 0.1 shard_map.198
  144.0 19.4 %all_to_all.16 = f32[32,8,384]{2,1,0:T(8,128)S(1)} all-to-all(f32[32,8,384]{2,1,0:T(8,128)S(1)} %shard_map.198), channel_id=1, replica_groups=mesh['node'=32,'rep'=8] {'node'}, dimensions={0} | all-to-all | bytes 786432 | tf_op jit(solution)/shard_map/all_to_all | solution.py:398
  163.4 0.3 collective-permute-start.16
  163.7 1.7 collective-permute-start.17
  165.4 1.0 collective-permute-start.18
  166.4 5.2 %collective-permute-start.19 = (f32[24,8,384]{2,1,0:T(8,128)S(1)}, f32[24,8,384]{2,1,0:T(8,128)S(1)}, u32[]{:S(2)}, u32[]{:S(2)}) collective-permute-start(f32[24,8,384]{2,1,0:T(8,128)S(1)} %slice.26.a0), channel_id=1, source_target_pairs={{0,1},{1,0},{2,3},{3,2},{4,5},{5,4},{6,7},{7,6},{8,9},{9,8},{10,11... | collective-permute-start | bytes 884744 | tf_op jit(solution)/shard_map/ppermute | solution.py:288
  171.6 3.1 %collective-permute-done.16.a1 = f32[24,8,384]{2,1,0:T(8,128)S(1)} collective-permute-done((f32[24,8,384]{2,1,0:T(8,128)S(1)}, f32[24,8,384]{2,1,0:T(8,128)S(1)}, u32[]{:S(2)}, u32[]{:S(2)}) %collective-permute-start.16) | collective-permute-done | bytes 294944 | tf_op jit(solution)/shard_map/ppermute | solution.py:292
  174.8 6.9 %collective-permute-start.20 = (f32[24,8,384]{2,1,0:T(8,128)S(1)}, f32[24,8,384]{2,1,0:T(8,128)S(1)}, u32[]{:S(2)}, u32[]{:S(2)}) collective-permute-start(f32[24,8,384]{2,1,0:T(8,128)S(1)} %collective-permute-done.16.a1), channel_id=1, source_target_pairs={{0,1},{1,0},{2,3},{3,2},{4,5},{5,4},{6,7},{7,6},{8,9},{9,8},{10,11... | collective-permute-start | bytes 884744 | tf_op jit(solution)/shard_map/ppermute | solution.py:288
  181.7 0.5 collective-permute-start.22
  182.3 1.6 copy-done.5
  183.8 4.8 %shard_map.197 = f32[1024,256]{1,0:T(8,128)} custom-call(s32[1,1024]{1,0:T(1,128)S(1)} %bitcast.28, f32[2048,256]{1,0:T(8,128)S(1)} %copy-done.5), custom_call_target="tpu_custom_call" | custom-call | tf_op jit(solution)/shard_map/pallas_call | solution.py:32
  188.7 2.2 %shard_map.199 = (f32[512,768]{1,0:T(8,128)}, f32[256,768]{1,0:T(8,128)}) custom-call(s32[3]{0:T(128)S(1)} %pad_add_fusion.pos, f32[24,8,384]{2,1,0:T(8,128)S(1)} %slice.26.a0, f32[24,8,384]{2,1,0:T(8,128)S(1)} %collective-permute-done.16.a1, f32[24,8,384]{2,1,0:T(8,128)S(1)} %collective-permute-done.17.a2, f32[24,8,384]{2,1,0:T(8,128)S(1)} %collective-permute-done.18.a3, ...), custom_call_target="tpu_custom_call" | custom-call | tf_op jit(solution)/shard_map/pallas_call | solution.py:32
  (53 shorter events, 0.2 us)
Async XLA Ops:
  7.2 58.6 %copy-start = (f32[1024,256]{1,0:T(8,128)S(1)}, f32[1024,256]{1,0:T(8,128)}, u32[]{:S(2)}) copy-start(f32[1024,256]{1,0:T(8,128)} %param.18) | copy-start | bytes 3145732
  7.2 1.3 copy-start.1
  8.5 1.0 copy-start.8
  9.5 0.9 copy-start.9
  10.5 0.7 copy-start.10
  11.2 0.7 copy-start.12
  11.9 0.7 copy-start.13
  12.6 0.7 copy-start.14
  13.3 0.7 copy-start.15
  14.0 0.7 copy-start.16
  14.6 0.7 copy-start.17
  15.3 0.7 copy-start.18
  20.4 13.7 %copy-start.11 = (s32[1024]{0:T(1024)S(1)}, s32[1024]{0:T(1024)}, u32[]{:S(2)}) copy-start(s32[1024]{0:T(1024)} %param.27) | copy-start | bytes 12292
  20.4 60.1 %all-to-all-start = ((bf16[32,144,128]{2,1,0:T(8,128)(2,1)}), bf16[32,144,128]{2,1,0:T(8,128)(2,1)}, u32[]{:S(2)}, u32[]{:S(2)}) async-start(bf16[32,144,128]{2,1,0:T(8,128)(2,1)} %get-tuple-element.20), calls=%async_computation | async-start | bytes 2359296 | tf_op jit(solution)/shard_map/all_to_all | solution.py:341
  32.6 149.7 %all-gather.2.cloned.1.call-start = ((), (), s32[]{:S(2)}) async-start(), calls=%async_computation.3 | async-start | bytes 2105344 | tf_op jit(solution)/shard_map/all_gather | solution.py:363
  32.6 30.3 %collective-permute-start = (f32[32,512]{1,0:T(8,128)S(1)}, f32[32,512]{1,0:T(8,128)S(1)}, u32[]{:S(2)}, u32[]{:S(2)}) collective-permute-start(f32[32,512]{1,0:T(8,128)S(1)} %slice.17), channel_id=1, source_target_pairs={{0,8},{8,16},{16,24},{24,32},{32,40},{40,48},{48,56},{56,64},{64,7... | collective-permute-start | bytes 196616 | tf_op jit(solution)/shard_map/ppermute | solution.py:343
  33.9 40.6 %copy-start.3 = (bf16[512,768]{1,0:T(8,128)(2,1)S(1)}, bf16[512,768]{1,0:T(8,128)(2,1)}, u32[]{:S(2)}) copy-start(bf16[512,768]{1,0:T(8,128)(2,1)} %w_in.3) | copy-start | bytes 2359300
  33.9 40.6 %copy-start.6 = (bf16[256,768]{1,0:T(8,128)(2,1)S(1)}, bf16[256,768]{1,0:T(8,128)(2,1)}, u32[]{:S(2)}) copy-start(bf16[256,768]{1,0:T(8,128)(2,1)} %w_hid.3) | copy-start | bytes 1179652
  63.6 3.4 %collective-permute-start.1 = (f32[4,8,512]{2,1,0:T(8,128)}, f32[4,8,512]{2,1,0:T(8,128)}, u32[]{:S(2)}, u32[]{:S(2)}) collective-permute-start(f32[4,8,512]{2,1,0:T(8,128)} %fusion.1), channel_id=1, source_target_pairs={{0,1},{1,0},{2,3},{3,2},{4,5},{5,4},{6,7},{7,6},{8,9},{9,8},{10,11... | collective-permute-start | bytes 196616 | tf_op jit(solution)/shard_map/ppermute | solution.py:288
  65.8 9.7 %copy-start.2 = (f32[1024,256]{1,0:T(8,128)S(1)}, f32[1024,256]{1,0:T(8,128)}, u32[]{:S(2)}) copy-start(f32[1024,256]{1,0:T(8,128)} %mem_h.1) | copy-start | bytes 3145732
  66.6 8.0 %copy-start.19 = (f32[128,256]{1,0:T(8,128)}, f32[128,256]{1,0:T(8,128)S(1)}, u32[]{:S(2)}) copy-start(f32[128,256]{1,0:T(8,128)S(1)} %gather_fusion) | copy-start | bytes 393220
  67.9 4.9 %collective-permute-start.2 = (f32[8,512]{1,0:T(8,128)S(1)}, f32[8,512]{1,0:T(8,128)S(1)}, u32[]{:S(2)}, u32[]{:S(2)}) collective-permute-start(f32[8,512]{1,0:T(8,128)S(1)} %get-tuple-element.40), channel_id=1, source_target_pairs={{0,2},{1,3},{2,4},{3,5},{4,6},{5,7},{6,0},{7,1},{8,10},{9,11},{10,... | collective-permute-start | bytes 49160 | tf_op jit(solution)/shard_map/ppermute | solution.py:292
  69.2 4.1 %collective-permute-start.3 = (f32[8,512]{1,0:T(8,128)S(1)}, f32[8,512]{1,0:T(8,128)S(1)}, u32[]{:S(2)}, u32[]{:S(2)}) collective-permute-start(f32[8,512]{1,0:T(8,128)S(1)} %get-tuple-element.39), channel_id=1, source_target_pairs={{0,4},{1,5},{2,6},{3,7},{4,0},{5,1},{6,2},{7,3},{8,12},{9,13},{10,... | collective-permute-start | bytes 49160 | tf_op jit(solution)/shard_map/ppermute | solution.py:292
  71.6 2.9 %collective-permute-start.4 = (f32[8,512]{1,0:T(8,128)S(1)}, f32[8,512]{1,0:T(8,128)S(1)}, u32[]{:S(2)}, u32[]{:S(2)}) collective-permute-start(f32[8,512]{1,0:T(8,128)S(1)} %get-tuple-element.38), channel_id=1, source_target_pairs={{0,6},{1,7},{2,0},{3,1},{4,2},{5,3},{6,4},{7,5},{8,14},{9,15},{10,... | collective-permute-start | bytes 49160 | tf_op jit(solution)/shard_map/ppermute | solution.py:292
  80.5 4.5 %collective-permute-start.5 = (bf16[32,144,128]{2,1,0:T(8,128)(2,1)}, bf16[32,144,128]{2,1,0:T(8,128)(2,1)S(1)}, u32[]{:S(2)}, u32[]{:S(2)}) collective-permute-start(bf16[32,144,128]{2,1,0:T(8,128)(2,1)} %all-to-all-done.own_h), channel_id=1, source_target_pairs={{0,1},{1,0},{2,3},{3,2},{4,5},{5,4},{6,7},{7,6},{8,9},{9,8},{10,11... | collective-permute-start | bytes 3538952 | tf_op jit(solution)/shard_map/ppermute | solution.py:288
  90.3 30.2 %copy-start.4 = (bf16[512,768]{1,0:T(8,128)(2,1)S(1)}, bf16[512,768]{1,0:T(8,128)(2,1)}, u32[]{:S(2)}) copy-start(bf16[512,768]{1,0:T(8,128)(2,1)} %w_in.3) | copy-start | bytes 2359300
  90.4 30.2 %copy-start.7 = (bf16[256,768]{1,0:T(8,128)(2,1)S(1)}, bf16[256,768]{1,0:T(8,128)(2,1)}, u32[]{:S(2)}) copy-start(bf16[256,768]{1,0:T(8,128)(2,1)} %w_hid.3) | copy-start | bytes 1179652
  90.4 9.4 %collective-permute-start.6 = (f32[136,512]{1,0:T(8,128)S(1)}, f32[136,512]{1,0:T(8,128)S(1)}, u32[]{:S(2)}, u32[]{:S(2)}) collective-permute-start(f32[136,512]{1,0:T(8,128)S(1)} %get-tuple-element.25), channel_id=1, source_target_pairs={{0,2},{1,3},{2,4},{3,5},{4,6},{5,7},{6,0},{7,1},{8,10},{9,11},{10,... | collective-permute-start | bytes 835592 | tf_op jit(solution)/shard_map/ppermute | solution.py:292
  90.6 15.9 %collective-permute-start.7 = (f32[136,512]{1,0:T(8,128)S(1)}, f32[136,512]{1,0:T(8,128)S(1)}, u32[]{:S(2)}, u32[]{:S(2)}) collective-permute-start(f32[136,512]{1,0:T(8,128)S(1)} %get-tuple-element.26), channel_id=1, source_target_pairs={{0,4},{1,5},{2,6},{3,7},{4,0},{5,1},{6,2},{7,3},{8,12},{9,13},{10,... | collective-permute-start | bytes 835592 | tf_op jit(solution)/shard_map/ppermute | solution.py:292
  94.2 12.4 %collective-permute-start.8 = (f32[136,512]{1,0:T(8,128)S(1)}, f32[136,512]{1,0:T(8,128)S(1)}, u32[]{:S(2)}, u32[]{:S(2)}) collective-permute-start(f32[136,512]{1,0:T(8,128)S(1)} %get-tuple-element.27), channel_id=1, source_target_pairs={{0,6},{1,7},{2,0},{3,1},{4,2},{5,3},{6,4},{7,5},{8,14},{9,15},{10,... | collective-permute-start | bytes 835592 | tf_op jit(solution)/shard_map/ppermute | solution.py:292
  107.1 5.4 %collective-permute-start.9 = (bf16[144,512]{1,0:T(8,128)(2,1)S(1)}, bf16[144,512]{1,0:T(8,128)(2,1)S(1)}, u32[]{:S(2)}, u32[]{:S(2)}) collective-permute-start(bf16[144,512]{1,0:T(8,128)(2,1)S(1)} %shard_map.195.a0), channel_id=1, source_target_pairs={{0,2},{1,3},{2,4},{3,5},{4,6},{5,7},{6,0},{7,1},{8,10},{9,11},{10,... | collective-permute-start | bytes 442376 | tf_op jit(solution)/shard_map/ppermute | solution.py:292
  108.3 9.6 %collective-permute-start.10 = (bf16[144,512]{1,0:T(8,128)(2,1)S(1)}, bf16[144,512]{1,0:T(8,128)(2,1)S(1)}, u32[]{:S(2)}, u32[]{:S(2)}) collective-permute-start(bf16[144,512]{1,0:T(8,128)(2,1)S(1)} %shard_map.195.a0), channel_id=1, source_target_pairs={{0,4},{1,5},{2,6},{3,7},{4,0},{5,1},{6,2},{7,3},{8,12},{9,13},{10,... | collective-permute-start | bytes 442376 | tf_op jit(solution)/shard_map/ppermute | solution.py:292
  111.2 8.0 %collective-permute-start.11 = (bf16[144,512]{1,0:T(8,128)(2,1)S(1)}, bf16[144,512]{1,0:T(8,128)(2,1)S(1)}, u32[]{:S(2)}, u32[]{:S(2)}) collective-permute-start(bf16[144,512]{1,0:T(8,128)(2,1)S(1)} %shard_map.195.a0), channel_id=1, source_target_pairs={{0,6},{1,7},{2,0},{3,1},{4,2},{5,3},{6,4},{7,5},{8,14},{9,15},{10,... | collective-permute-start | bytes 442376 | tf_op jit(solution)/shard_map/ppermute | solution.py:292
  111.2 8.0 %collective-permute-start.12 = (bf16[144,512]{1,0:T(8,128)(2,1)S(1)}, bf16[144,512]{1,0:T(8,128)(2,1)S(1)}, u32[]{:S(2)}, u32[]{:S(2)}) collective-permute-start(bf16[144,512]{1,0:T(8,128)(2,1)S(1)} %shard_map.195.a0), channel_id=1, source_target_pairs={{0,1},{1,0},{2,3},{3,2},{4,5},{5,4},{6,7},{7,6},{8,9},{9,8},{10,11... | collective-permute-start | bytes 442376 | tf_op jit(solution)/shard_map/ppermute | solution.py:288
  112.6 6.6 %collective-permute-start.13 = (bf16[144,512]{1,0:T(8,128)(2,1)S(1)}, bf16[144,512]{1,0:T(8,128)(2,1)S(1)}, u32[]{:S(2)}, u32[]{:S(2)}) collective-permute-start(bf16[144,512]{1,0:T(8,128)(2,1)S(1)} %collective-permute-done.9.a1), channel_id=1, source_target_pairs={{0,1},{1,0},{2,3},{3,2},{4,5},{5,4},{6,7},{7,6},{8,9},{9,8},{10,11... | collective-permute-start | bytes 442376 | tf_op jit(solution)/shard_map/ppermute | solution.py:288
  117.9 2.3 %collective-permute-start.14 = (bf16[144,512]{1,0:T(8,128)(2,1)S(1)}, bf16[144,512]{1,0:T(8,128)(2,1)S(1)}, u32[]{:S(2)}, u32[]{:S(2)}) collective-permute-start(bf16[144,512]{1,0:T(8,128)(2,1)S(1)} %collective-permute-done.10.a2), channel_id=1, source_target_pairs={{0,1},{1,0},{2,3},{3,2},{4,5},{5,4},{6,7},{7,6},{8,9},{9,8},{10,11... | collective-permute-start | bytes 442376 | tf_op jit(solution)/shard_map/ppermute | solution.py:288
  119.2 1.4 collective-permute-start.15
  163.4 11.4 %collective-permute-start.16 = (f32[24,8,384]{2,1,0:T(8,128)S(1)}, f32[24,8,384]{2,1,0:T(8,128)S(1)}, u32[]{:S(2)}, u32[]{:S(2)}) collective-permute-start(f32[24,8,384]{2,1,0:T(8,128)S(1)} %slice.26.a0), channel_id=1, source_target_pairs={{0,2},{1,3},{2,4},{3,5},{4,6},{5,7},{6,0},{7,1},{8,10},{9,11},{10,... | collective-permute-start | bytes 884744 | tf_op jit(solution)/shard_map/ppermute | solution.py:292
  163.7 18.0 %collective-permute-start.17 = (f32[24,8,384]{2,1,0:T(8,128)S(1)}, f32[24,8,384]{2,1,0:T(8,128)S(1)}, u32[]{:S(2)}, u32[]{:S(2)}) collective-permute-start(f32[24,8,384]{2,1,0:T(8,128)S(1)} %slice.26.a0), channel_id=1, source_target_pairs={{0,4},{1,5},{2,6},{3,7},{4,0},{5,1},{6,2},{7,3},{8,12},{9,13},{10,... | collective-permute-start | bytes 884744 | tf_op jit(solution)/shard_map/ppermute | solution.py:292
  165.4 16.3 %collective-permute-start.18 = (f32[24,8,384]{2,1,0:T(8,128)S(1)}, f32[24,8,384]{2,1,0:T(8,128)S(1)}, u32[]{:S(2)}, u32[]{:S(2)}) collective-permute-start(f32[24,8,384]{2,1,0:T(8,128)S(1)} %slice.26.a0), channel_id=1, source_target_pairs={{0,6},{1,7},{2,0},{3,1},{4,2},{5,3},{6,4},{7,5},{8,14},{9,15},{10,... | collective-permute-start | bytes 884744 | tf_op jit(solution)/shard_map/ppermute | solution.py:292
  166.4 22.2 %collective-permute-start.19 = (f32[24,8,384]{2,1,0:T(8,128)S(1)}, f32[24,8,384]{2,1,0:T(8,128)S(1)}, u32[]{:S(2)}, u32[]{:S(2)}) collective-permute-start(f32[24,8,384]{2,1,0:T(8,128)S(1)} %slice.26.a0), channel_id=1, source_target_pairs={{0,1},{1,0},{2,3},{3,2},{4,5},{5,4},{6,7},{7,6},{8,9},{9,8},{10,11... | collective-permute-start | bytes 884744 | tf_op jit(solution)/shard_map/ppermute | solution.py:288
  174.8 13.9 %collective-permute-start.20 = (f32[24,8,384]{2,1,0:T(8,128)S(1)}, f32[24,8,384]{2,1,0:T(8,128)S(1)}, u32[]{:S(2)}, u32[]{:S(2)}) collective-permute-start(f32[24,8,384]{2,1,0:T(8,128)S(1)} %collective-permute-done.16.a1), channel_id=1, source_target_pairs={{0,1},{1,0},{2,3},{3,2},{4,5},{5,4},{6,7},{7,6},{8,9},{9,8},{10,11... | collective-permute-start | bytes 884744 | tf_op jit(solution)/shard_map/ppermute | solution.py:288
  181.7 6.9 %collective-permute-start.21 = (f32[24,8,384]{2,1,0:T(8,128)S(1)}, f32[24,8,384]{2,1,0:T(8,128)S(1)}, u32[]{:S(2)}, u32[]{:S(2)}) collective-permute-start(f32[24,8,384]{2,1,0:T(8,128)S(1)} %collective-permute-done.17.a2), channel_id=1, source_target_pairs={{0,1},{1,0},{2,3},{3,2},{4,5},{5,4},{6,7},{7,6},{8,9},{9,8},{10,11... | collective-permute-start | bytes 884744 | tf_op jit(solution)/shard_map/ppermute | solution.py:288
  181.7 6.9 %collective-permute-start.22 = (f32[24,8,384]{2,1,0:T(8,128)S(1)}, f32[24,8,384]{2,1,0:T(8,128)S(1)}, u32[]{:S(2)}, u32[]{:S(2)}) collective-permute-start(f32[24,8,384]{2,1,0:T(8,128)S(1)} %collective-permute-done.18.a3), channel_id=1, source_target_pairs={{0,1},{1,0},{2,3},{3,2},{4,5},{5,4},{6,7},{7,6},{8,9},{9,8},{10,11... | collective-permute-start | bytes 884744 | tf_op jit(solution)/shard_map/ppermute | solution.py:288
  182.3 1.6 copy-start.5
Sparse Core Ops, SparseCore 0:
  75.6 106.6 all-gather.1

commit v3 on v2

--- a/solution.py
+++ b/solution.py
@@ -8,10 +8,10 @@
 GRAD_SCALE = 1.0 / 64.0
 DEAD = 2.0**100
 F32, BF16, I32 = jnp.float32, jnp.bfloat16, jnp.int32
-PARAMS = pltpu.CompilerParams(vmem_limit_bytes=48 * 1024 * 1024)
 VM = pl.BlockSpec(memory_space=pltpu.VMEM)
 SM = pl.BlockSpec(memory_space=pltpu.SMEM)
-HB = pl.BlockSpec(memory_space=pl.ANY)
+HB = pl.BlockSpec(memory_space=pltpu.HBM)
+ANY = pl.BlockSpec(memory_space=pl.ANY)
 
 
 def iota(shape, dim):
@@ -26,7 +26,7 @@
     return lax.dot_general(a, b, (dims, ((), ())), preferred_element_type=F32)
 
 
-def call(body, out_shape, places, args, scratch=(), out_places=None):
+def call(body, out_shape, places, args, scratch=(), out_places=None, mib=48):
     if out_places is None:
         out_places = jax.tree.map(lambda _: VM, out_shape)
     return pl.pallas_call(
@@ -35,7 +35,7 @@
         in_specs=list(places) + [VM] * (len(args) - len(places)),
         out_specs=out_places,
         scratch_shapes=list(scratch),
-        compiler_params=PARAMS,
+        compiler_params=pltpu.CompilerParams(vmem_limit_bytes=mib * 1024 * 1024),
     )(*args)
 
 
@@ -57,17 +57,24 @@
 
 
 def message_kernel(
-    pos, mem_h, edge_h, w_h, src, times, dst_ref, listed, used, freq, phase, b, send_h, hot,
-    mem, edge, w, msgs, out, cols, sems,
+    pos, mem_h, edge_h, w_h, src_h, times_h, dst_h, listed_h, used_h, freq_h, phase_h, b_h, send_h, hot,
+    mem, edge, w, src, times, dst_v, listed, used, freq, phase, b, msgs, out, cols, sems,
 ):
     loads = [
         pltpu.make_async_copy(h, v, sems.at[i])
-        for i, (h, v) in enumerate(((mem_h, mem), (edge_h, edge), (w_h, w)))
+        for i, (h, v) in enumerate(
+            (
+                (src_h, src), (times_h, times), (dst_h, dst_v), (listed_h, listed), (used_h, used),
+                (freq_h, freq), (phase_h, phase), (b_h, b), (mem_h, mem), (edge_h, edge), (w_h, w),
+            )
+        )
     ]
     for c in loads:
         c.start()
+    for c in loads[:8]:
+        c.wait()
     n_ev, step = 1024, 256
-    dst = dst_ref[...]
+    dst = dst_v[...]
     line = iota((8, n_ev), 0)
     packed = jnp.where(line == 0, src[...], jnp.where(line == 1, times[...], dst))
     cols[...] = packed.T
@@ -77,7 +84,7 @@
     hi = mm(eye, (names >> 5).astype(F32).astype(BF16), ((1,), (1,)))
     lo = mm(eye, (names & 31).astype(F32).astype(BF16), ((1,), (1,)))
     names = jnp.where(slot < used[...], (hi * 32.0 + lo).astype(I32), -1)
-    for c in loads:
+    for c in loads[8:]:
         c.wait()
     mem16 = mem[...].astype(BF16)
     for e in range(0, n_ev, step):
@@ -108,7 +115,7 @@
             own = pltpu.roll(own, ((pos[0] & 3) + 4 - k) * 32 & 127, 1)
             out[o, 128:144, :] = jnp.concatenate([own, jnp.zeros((8, 128), F32)], axis=0).astype(BF16)
         here = pl.ds(8 * t, 8)
-        stores.append(pltpu.make_async_copy(out.at[here], send_h.at[here], sems.at[3 + t]))
+        stores.append(pltpu.make_async_copy(out.at[here], send_h.at[here], sems.at[11 + t]))
         stores[-1].start()
     window = jnp.where(dst >= 32768, (dst - 32768 - 32 * pos[0] + 1024) & 1023, -1)
     q = iota((96, n_ev), 0)
@@ -121,25 +128,22 @@
         c.wait()
 
 
-def cold_kernel(pos, own_h, peer_h, tie, o0, o1_h, o2_h, o3_h, got, msgs, out, sems):
-    loads = [pltpu.make_async_copy(h, got.at[i], sems.at[i]) for i, h in enumerate((own_h, peer_h))]
-    for c in loads:
-        c.start()
+def cold_kernel(pos, own, peer, hot, spill, o0, o1_h, o2_h, o3_h, msgs, out, sems):
+    got = (own, peer)
     q = iota((512, 128), 0)
     want = (q & 127) + 256 * ((pos[0] + (q >> 7)) & 3) + 128 * pos[1]
     hits = []
     for h in range(2):
-        loads[h].wait()
         for g in range(8):
-            tail = got[h, 4 * g, 128:144, :].astype(F32)
+            tail = got[h][4 * g, 128:144, :].astype(F32)
             for i in range(1, 4):
-                tail = tail + got[h, 4 * g + i, 128:144, :].astype(F32)
+                tail = tail + got[h][4 * g + i, 128:144, :].astype(F32)
             row = jnp.where(tail[2:3, :] > 0.5, tail[0:1, :] * 32.0 + tail[1:2, :], -1.0).astype(I32)
             hits.append(one_hot(want == row))
         for s in range(32):
             for k in range(4):
                 here = slice(1024 * h + 32 * s, 1024 * h + 32 * s + 32)
-                msgs[here, 128 * k : 128 * k + 128] = got[h, s, 32 * k : 32 * k + 32, :]
+                msgs[here, 128 * k : 128 * k + 128] = got[h][s, 32 * k : 32 * k + 32, :]
     hit = jnp.concatenate(hits, axis=1)
     count = mm(jnp.ones((8, 2048), BF16), hit, ((1,), (1,)))
     stores = []
@@ -150,31 +154,34 @@
             here = slice(128 * d, 128 * d + 128)
             to = o0 if d == 0 else out.at[d - 1]
             to[0:128, cols] = total[here, :]
+            j = (pos[0] + d) & 3
+            tile = hot[j, :, cols] + jnp.where(j < 2, 1.0, 0.0) * spill[j & 1, :, cols]
             if n == 0:
-                to[128:136, 0:128] = count[:, here]
-                to[128:136, 128:256] = jnp.zeros((8, 128), F32)
-            else:
-                to[128:136, cols] = jnp.zeros((8, 256), F32)
+                rows = jnp.concatenate([count[:, here], tile[:, 128:256]], axis=1)
+                tile = jnp.where((iota((8, 256), 0) >= 4) & (iota((8, 256), 1) < 128), rows, tile)
+            to[128:136, cols] = tile
             if d > 0:
                 dst = (o1_h, o2_h, o3_h)[d - 1]
-                c = pltpu.make_async_copy(out.at[d - 1, :, cols], dst.at[:, cols], sems.at[2 + 3 * n + d - 1])
+                c = pltpu.make_async_copy(out.at[d - 1, :, cols], dst.at[:, cols], sems.at[3 * n + d - 1])
                 c.start()
                 stores.append(c)
     for c in stores:
         c.wait()
 
 
-def agg_kernel(p1_h, p2_h, p3_h, p0, hot, out_h, part, out, sems):
+def agg_kernel(p1_h, p2_h, p3_h, p0, out_h, part, out, sems):
     loads = [pltpu.make_async_copy(h, part.at[i], sems.at[i]) for i, h in enumerate((p1_h, p2_h, p3_h))]
     for c in loads:
         c.start()
-    out[128:144, :] = hot[...]
     for c in loads:
         c.wait()
     total = p0[...] + part[0] + part[1] + part[2]
-    count = column(total[128:129, 0:128])
+    count = column(total[132:133, 0:128])
     agg = jnp.where(count > 0.0, total[0:128, :] / jnp.maximum(count, 1.0), DEAD)
     out[0:128, :] = agg.astype(BF16)
+    count = total[132:136, 128:129]
+    agg = jnp.where(count > 0.0, total[128:132, :] / jnp.maximum(count, 1.0), DEAD)
+    out[128:144, :] = jnp.concatenate([agg, jnp.full((12, 512), DEAD, F32)], axis=0).astype(BF16)
     store = pltpu.make_async_copy(out, out_h, sems.at[3])
     store.start()
     store.wait()
@@ -189,34 +196,27 @@
     return reset, update, cand, gh[:, 512:768]
 
 
-def hot_kernel(p0, p1, p2, p3, mem, w_in, w_hid, agg_out, new_out):
-    total = p0[...] + p1[...] + p2[...] + p3[...]
-    count = total[4:8, :]
-    agg = jnp.where(count > 0.0, total[0:4, :] / jnp.maximum(count, 1.0), DEAD)
-    agg = jnp.concatenate([agg, jnp.full((12, 512), DEAD, F32)], axis=0).astype(BF16)
-    agg_out[...] = agg
-    live = agg[:, 0:256].astype(F32) < DEAD * 0.5
-    mem = mem[...]
-    wide = agg.astype(F32)
-    agg = jnp.where(wide < DEAD * 0.5, wide, 0.0).astype(BF16)
-    reset, update, cand, _ = gates(agg, mem, w_in[...], w_hid[...])
-    new_out[...] = jnp.where(live, (1.0 - update) * cand + update * mem, mem)[0:8, :]
-
-
-def hot_place_kernel(ids, rows, out):
-    names = column(ids[...]) - 32768
-    at = 8 * (names >> 2) + (names & 3)
-    full = rows[...]
+def hot_place_kernel(pos, ids, a0, a1, a2, a3, b0, b1, b2, b3, out, rows):
+    x, core = pos[0], pos[1]
+    for group, c in (((a0, a1, a2, a3), core), ((b0, b1, b2, b3), 1 - core)):
+        for d, part in enumerate(group):
+            block = 2 * ((x - d + 4) & 3) + c
+            for n in range(32):
+                rows[block, 4 * n : 4 * n + 4, 0:128] = part[n, 0:4, :]
+                rows[block, 4 * n : 4 * n + 4, 128:256] = part[n, 4:8, :]
+    name = column(ids[...]) - 32768
+    at = 128 * ((name >> 2) & 7) + 4 * (name >> 5) + (name & 3)
+    full = rows[...].reshape(1024, 256)
     hi = full.astype(BF16)
     rest = full - hi.astype(F32)
     mid = rest.astype(BF16)
     low = (rest - mid.astype(F32)).astype(BF16)
     for h in range(0, 1024, 256):
-        pick = one_hot(iota((256, 2048), 1) == at[h : h + 256, :])
+        pick = one_hot(iota((256, 1024), 1) == at[h : h + 256, :])
         out[h : h + 256, :] = mm(pick, hi) + (mm(pick, mid) + mm(pick, low))
 
 
-def update_kernel(pos, a0, a1, a2, a3, b0, b1, b2, b3, mem, cot, w_in, w_hid, new, grad, agg, acc):
+def update_kernel(pos, a0, a1, a2, a3, b0, b1, b2, b3, mem, cot, w_in, w_hid, new, grad, agg, acc, hot):
     x, core, rep = pos[0], pos[1], pos[2]
     for group, c in (((a0, a1, a2, a3), core), ((b0, b1, b2, b3), 1 - core)):
         for d, part in enumerate(group):
@@ -237,6 +237,8 @@
         fresh = jnp.where(live, (1.0 - update) * cand + update * m, m)
         rows = min(step, 1024 - s)
         new[s : s + rows, :] = fresh[0:rows, :]
+        if rows < step:
+            hot[...] = fresh[rows:step, :]
         g = jnp.where(live, cot[s : s + step, :], 0.0)
         d_cand = g * (1.0 - update) * (1.0 - cand * cand)
         d_upd = g * (m - cand) * update * (1.0 - update)
@@ -257,17 +259,21 @@
     total = acc[...] * GRAD_SCALE
     third = jnp.where(iota((128, 256), 0) < 64, total[:, 512:768], total[:, 768:1024])
     total = jnp.concatenate([total[:, 0:512], third], axis=1)
+    own = hot[pl.ds(pl.multiple_of(16 * rep, 16), 8), :]
+    own = jnp.concatenate([own[0:4, 0:128], own[0:4, 128:256]], axis=0)
     for p in range(32):
         i, j = p // 2, p % 2
-        grad[p] = total[8 * i : 8 * i + 8, 384 * j : 384 * j + 384]
-
-
-def piece_kernel(parts, out):
-    total = parts[0]
+        grad[p, :, 0:384] = total[8 * i : 8 * i + 8, 384 * j : 384 * j + 384]
+        grad[p, :, 384:512] = own
+
+
+def piece_kernel(parts, out, hot):
+    total = parts[0, :, 0:384]
     for k in range(1, 32):
-        total = total + parts[k]
+        total = total + parts[k, :, 0:384]
     for k in range(32):
         out[k] = total
+        hot[k] = parts[k, :, 384:512]
 
 
 def place_kernel(pos, a0, a1, a2, a3, b0, b1, b2, b3, g_in, g_hid):
@@ -325,7 +331,7 @@
     send, hot = call(
         message_kernel,
         (sds((32, 144, 128), BF16), sds((96, 512), F32)),
-        (SM, HB, HB, HB),
+        (SM,) + (HB,) * 11,
         (
             node.astype(I32)[None], memory, edge_feat, w_msg, src_local[None, :], times[None, :],
             dst_ids[None, :], cold_list, cold_count[None, :], time_freq[None, :], time_phase[None, :],
@@ -333,69 +339,66 @@
         ),
         (
             pltpu.VMEM((1024, 256), F32), pltpu.VMEM((1024, 128), BF16), pltpu.VMEM((512, 512), BF16),
+            pltpu.VMEM((1, 1024), I32), pltpu.VMEM((1, 1024), I32), pltpu.VMEM((1, 1024), I32),
+            pltpu.VMEM((32, 32), I32), pltpu.VMEM((1, 32), I32), pltpu.VMEM((1, 128), F32),
+            pltpu.VMEM((1, 128), F32), pltpu.VMEM((1, 512), F32),
             pltpu.VMEM((1024, 512), BF16), pltpu.VMEM((32, 144, 128), BF16), pltpu.VMEM((1024, 8), I32),
-            pltpu.SemaphoreType.DMA((7,)),
+            pltpu.SemaphoreType.DMA((15,)),
         ),
-        (HB, VM),
+        (ANY, VM),
+        63,
     )
     recv = lax.all_to_all(send, "node", split_axis=0, concat_axis=0, tiled=True)
 
-    spill = lax.ppermute(hot[64:96], "node", [(k, (k + 1) % 32) for k in range(32)]).reshape(2, 2, 8, 512)
-    hot = hot[0:64].reshape(2, 4, 8, 512)
-    hot = jnp.concatenate([hot[:, 0:2] + spill, hot[:, 2:4]], axis=1)
-    got = swap_core(lax.dynamic_index_in_dim(hot, 1 - core, 0, False))
-    hot = lax.dynamic_index_in_dim(hot, core, 0, False) + got
-    hot = [lax.dynamic_index_in_dim(hot, (chip + d) % 4, 0, False) for d in range(4)]
-    hot = [hot[0]] + [shift_x(hot[d], d) for d in (1, 2, 3)]
+    hot = hot + swap_core(hot)
+    spill = lax.dynamic_slice_in_dim(hot, 64 + 16 * core, 16, 0)
+    spill = lax.ppermute(spill, "node", [(k, (k + 1) % 32) for k in range(32)])
+    hot = lax.dynamic_slice_in_dim(hot, 32 * core, 32, 0)
     k = jnp.arange(128, dtype=I32)
     want = 32768 + 32 * node + 4 * (k // 16) + k % 4
     at = jnp.sum(jnp.where(want[:, None] == hot_ids[None, :], jnp.arange(1024, dtype=I32)[None, :], 0), axis=1)
-    hot_mem = jnp.take(hot_memory, at, axis=0, mode="clip")
-    mem_all = jnp.concatenate([memory, hot_mem], axis=0)
+    mem_all = jnp.concatenate([memory, jnp.take(hot_memory, at, axis=0, mode="clip")], axis=0)
     cot_all = jnp.concatenate([cot_cold, jnp.take(cot_hot, at, axis=0, mode="clip")], axis=0)
-    own_mem = lax.dynamic_slice_in_dim(hot_mem, 16 * rep, 16, 0)
-    hot_agg, hot_new = call(
-        hot_kernel,
-        (sds((16, 512), BF16), sds((8, 256), F32)),
-        (),
-        (*hot, own_mem, w_in, w_hid),
-    )
-    hot_all = lax.all_gather(hot_new, ("node", "rep"), axis=0, tiled=True)
-    new_hot = call(hot_place_kernel, sds((1024, 256), F32), (), (hot_ids[None, :], hot_all))
-
-    recv, hot_agg, mem_all, cot_all = lax.optimization_barrier((recv, hot_agg, mem_all, cot_all))
+
+    recv, spill, mem_all, cot_all = lax.optimization_barrier((recv, spill, mem_all, cot_all))
     block = sds((136, 512), F32)
     parts = call(
         cold_kernel,
         (block,) * 4,
-        (SM, HB, HB, HB),
-        (pos, recv, swap_core(recv), hot_agg),
-        (
-            pltpu.VMEM((2, 32, 144, 128), BF16), pltpu.VMEM((2048, 512), BF16), pltpu.VMEM((3, 136, 512), F32),
-            pltpu.SemaphoreType.DMA((8,)),
-        ),
-        (VM, HB, HB, HB),
+        (SM,),
+        (pos, recv, swap_core(recv), hot.reshape(4, 8, 512), spill.reshape(2, 8, 512)),
+        (pltpu.VMEM((2048, 512), BF16), pltpu.VMEM((3, 136, 512), F32), pltpu.SemaphoreType.DMA((6,))),
+        (VM, ANY, ANY, ANY),
     )
     parts = [parts[0]] + [shift_x(parts[d], d) for d in (1, 2, 3)]
     agg = call(
         agg_kernel,
         sds((144, 512), BF16),
-        (HB, HB, HB),
-        (*parts[1:], parts[0], hot_agg),
+        (ANY, ANY, ANY),
+        (*parts[1:], parts[0]),
         (pltpu.VMEM((3, 136, 512), F32), pltpu.VMEM((144, 512), BF16), pltpu.SemaphoreType.DMA((4,))),
-        HB,
+        ANY,
     )
     new_memory, grad = call(
         update_kernel,
-        (sds((1024, 256), F32), sds((32, 8, 384), F32)),
+        (sds((1024, 256), F32), sds((32, 8, 512), F32)),
         (SM,),
         (pos, *gather_rep(agg), mem_all, cot_all, w_in, w_hid),
-        (pltpu.VMEM((1152, 512), BF16), pltpu.VMEM((128, 1024), F32)),
+        (pltpu.VMEM((1152, 512), BF16), pltpu.VMEM((128, 1024), F32), pltpu.VMEM((128, 256), F32)),
     )
 
     grad = lax.all_to_all(grad, "node", split_axis=0, concat_axis=0, tiled=True)
-    grad = call(piece_kernel, sds((32, 8, 384), F32), (), (grad,))
+    grad, hot_new = call(piece_kernel, (sds((32, 8, 384), F32), sds((32, 8, 128), F32)), (), (grad,))
     grad = lax.all_to_all(grad, "node", split_axis=0, concat_axis=0, tiled=True)
+    hot_parts = gather_rep(hot_new)
+    grad, hot_parts = lax.optimization_barrier((grad, hot_parts))
+    new_hot = call(
+        hot_place_kernel,
+        sds((1024, 256), F32),
+        (SM,),
+        (pos, hot_ids[None, :], *hot_parts),
+        (pltpu.VMEM((8, 128, 256), F32),),
+    )
     grad_in, grad_hid = call(
         place_kernel,
         (sds((512, 768), F32), sds((256, 768), F32)),

time: 199 us -> 162 us (0.81)
  blocking collectives: 36.8 us -> 18.8 us
  starting transfers between devices: 50.6 us -> 66.7 us
  between operations: 14.4 us -> 0.86 us
  waiting for transfers between devices: 53.7 us -> 42.5 us
  local copies, waits for them, and re-layouts: 13.8 us -> 6.33 us
  other arithmetic: 4.15 us -> 1.56 us
    all_to_all x2 -> x1, blocking collectives: 36.8 us -> 18.8 us  [on_device(): grad = lax.all_to_all(grad, 'node', split_axis=0, concat_axis=0, tiled=True)]
    ppermute x10 -> x14, starting transfers between devices: 21.4 us -> 33.3 us  [swap_core(): return lax.ppermute(v, 'rep', [(k, k ^ 1) for k in range(8)])]
    unnamed x40 -> x20, local copies, waits for them, and re-layouts: 10.4 us -> 2.07 us
    all_to_all x0 -> x1, starting transfers between devices: none -> 8.13 us  [on_device(): grad = lax.all_to_all(grad, 'node', split_axis=0, concat_axis=0, tiled=True)]
    ppermute x1, waiting for transfers between devices: 28.7 us -> 21.2 us  [on_device(): spill = lax.ppermute(spill, 'node', [(k, (k + 1) % 32) for k in range(32)])]
    ppermute x12, starting transfers between devices: 15.8 us -> 11.6 us  [shift_x(): return lax.ppermute(v, 'rep', [(k, (k + 2 * d) % 8) for k in range(8)])]
    ppermute x12, waiting for transfers between devices: 20.6 us -> 17.6 us  [shift_x(): return lax.ppermute(v, 'rep', [(k, (k + 2 * d) % 8) for k in range(8)])]
    ppermute x10 -> x14, waiting for transfers between devices: 4.43 us -> 3.68 us  [swap_core(): return lax.ppermute(v, 'rep', [(k, k ^ 1) for k in range(8)])]
  transfers between devices with their start and end apart: 25 -> 29, of which waited for: 12 -> 10; matrix products, arithmetic and copies ran while one was open for 4% -> 4% of each run, Pallas kernels for 9% -> 2%
where the time goes in v3:
time: 162 us; the launch traced here: 161 us
  starting transfers between devices  66.7 us (41%)
  waiting for transfers between devices  42.5 us (26%)
  Pallas kernels  24.6 us (15%)
  blocking collectives  18.8 us (12%)
  local copies, waits for them, and re-layouts  6.33 us (4%)
    ppermute x14, starting transfers between devices, swap_core(): return lax.ppermute(v, 'rep', [(k, k ^ 1) for k in range(8)])  33.3 us
    pallas_call x7, Pallas kernels, call(): pl.pallas_call(body, out_shape=out_shape, in_specs=list(places) + [VM] *...  24.6 us
    ppermute x1, waiting for transfers between devices, on_device(): spill = lax.ppermute(spill, 'node', [(k, (k + 1) % 32) for k in range(32)])  21.2 us
    all_to_all x1, blocking collectives, on_device(): grad = lax.all_to_all(grad, 'node', split_axis=0, concat_axis=0, tiled=True)  18.8 us
    ppermute x12, waiting for transfers between devices, shift_x(): return lax.ppermute(v, 'rep', [(k, (k + 2 * d) % 8) for k in range(8)])  17.6 us
    all_to_all x1, starting transfers between devices, on_device(): recv = lax.all_to_all(send, 'node', split_axis=0, concat_axis=0, tiled=True)  12.2 us
    ppermute x12, starting transfers between devices, shift_x(): return lax.ppermute(v, 'rep', [(k, (k + 2 * d) % 8) for k in range(8)])  11.6 us
    all_to_all x1, starting transfers between devices, on_device(): grad = lax.all_to_all(grad, 'node', split_axis=0, concat_axis=0, tiled=True)  8.13 us
  transfers between devices with their start and end apart: 29, of which 10 were waited for; matrix products, arithmetic and copies ran while one was open for 4% of the time, Pallas kernels for 2%

profile of v3, /device:TPU:1, one launch (start us, length us, event | category | flops | bytes accessed | tf_op | source)
XLA Modules:
  0.0 161.4 jit_solution(14927605119580535546)
XLA Ops:
  0.6 6.4 %shard_map.192 = (bf16[32,144,128]{2,1,0:T(8,128)(2,1)}, f32[96,512]{1,0:T(8,128)}) custom-call(s32[1]{0:T(128)} %bitcast.3.pos, f32[1024,256]{1,0:T(8,128)} %mem_h.1, bf16[1024,128]{1,0:T(8,128)(2,1)} %edge_h.1, bf16[512,512]{1,0:T(8,128)(2,1)} %w_h.1, s32[1,1024]{1,0:T(1,128)} %bitcast.17, s32[1,1024]{1,0:T(1,128)} %bitcast.18, s32[1,1024]{1,0:T(1,128)} %bitcast.19, ...), custom_call_target="tpu_custom_call" | custom-call | tf_op jit(solution)/shard_map/pallas_call | solution.py:32
  7.1 0.0 copy-start.4
  7.1 0.0 copy-start.6
  7.1 12.2 %all-to-all-start = ((bf16[32,144,128]{2,1,0:T(8,128)(2,1)}), bf16[32,144,128]{2,1,0:T(8,128)(2,1)S(1)}, u32[]{:S(2)}, u32[]{:S(2)}) async-start(bf16[32,144,128]{2,1,0:T(8,128)(2,1)} %get-tuple-element.29), calls=%async_computation | async-start | bytes 2359296 | tf_op jit(solution)/shard_map/all_to_all | solution.py:351
  19.3 1.0 collective-permute-start
  20.4 0.2 select_reduce_fusion
  20.6 1.4 gather_fusion.1
  22.0 2.0 %gather_fusion = f32[128,256]{1,0:T(8,128)S(1)} fusion(f32[1024,256]{1,0:T(8,128)} %param.18, s32[1024]{0:T(1024)S(1)} %pad_clamp_fusion), kind=kCustom, calls=%fused_computation | custom fusion | bytes 262656 | tf_op jit(solution)/shard_map/jit(_take)/gather | solution.py:360
  24.0 0.0 copy-start.7
  24.0 0.1 pad_maximum_fusion.mem
  24.1 1.1 add.50
  25.2 0.0 copy-start.9
  25.3 0.6 copy-done.9
  25.9 1.5 collective-permute-start.1
  27.4 0.1 pad_maximum_fusion.1.cot
  27.5 21.2 %collective-permute-done.1 = f32[16,512]{1,0:T(8,128)S(1)} collective-permute-done((f32[16,512]{1,0:T(8,128)S(1)}, f32[16,512]{1,0:T(8,128)S(1)}, u32[]{:S(2)}, u32[]{:S(2)}) %collective-permute-start.1) | collective-permute-done | bytes 32800 | tf_op jit(solution)/shard_map/ppermute | solution.py:355
  48.7 0.6 copy-done.2
  49.3 3.0 %collective-permute-start.2 = (bf16[32,144,128]{2,1,0:T(8,128)(2,1)S(1)}, bf16[32,144,128]{2,1,0:T(8,128)(2,1)}, u32[]{:S(2)}, u32[]{:S(2)}) collective-permute-start(bf16[32,144,128]{2,1,0:T(8,128)(2,1)S(1)} %all-to-all-done.own), channel_id=1, source_target_pairs={{0,1},{1,0},{2,3},{3,2},{4,5},{5,4},{6,7},{7,6},{8,9},{9,8},{10,11... | collective-permute-start | bytes 3538952 | tf_op jit(solution)/shard_map/ppermute | solution.py:294
  52.3 0.1 pad_add_fusion.pos
  52.3 0.8 dynamic-slice_bitcast_fusion.hot
  53.2 1.7 %collective-permute-done.2.peer = bf16[32,144,128]{2,1,0:T(8,128)(2,1)} collective-permute-done((bf16[32,144,128]{2,1,0:T(8,128)(2,1)S(1)}, bf16[32,144,128]{2,1,0:T(8,128)(2,1)}, u32[]{:S(2)}, u32[]{:S(2)}) %collective-permute-start.2) | collective-permute-done | bytes 1179680 | tf_op jit(solution)/shard_map/ppermute | solution.py:294
  54.9 0.8 copy-done.3
  55.6 4.8 %shard_map.193 = (f32[136,512]{1,0:T(8,128)S(1)}, f32[136,512]{1,0:T(8,128)S(1)}, f32[136,512]{1,0:T(8,128)S(1)}, f32[136,512]{1,0:T(8,128)S(1)}) custom-call(s32[3]{0:T(128)S(1)} %pad_add_fusion.pos, bf16[32,144,128]{2,1,0:T(8,128)(2,1)S(1)} %all-to-all-done.own, bf16[32,144,128]{2,1,0:T(8,128)(2,1)} %collective-permute-done.2.peer, ...), custom_call_target="tpu_custom_call" | custom-call | tf_op jit(solution)/shard_map/pallas_call | solution.py:32
  60.4 0.0 copy-start
  60.5 1.3 collective-permute-start.3
  61.7 2.5 %collective-permute-start.4 = (f32[136,512]{1,0:T(8,128)S(1)}, f32[136,512]{1,0:T(8,128)S(1)}, u32[]{:S(2)}, u32[]{:S(2)}) collective-permute-start(f32[136,512]{1,0:T(8,128)S(1)} %get-tuple-element.34), channel_id=1, source_target_pairs={{0,4},{1,5},{2,6},{3,7},{4,0},{5,1},{6,2},{7,3},{8,12},{9,13},{10,... | collective-permute-start | bytes 835592 | tf_op jit(solution)/shard_map/ppermute | solution.py:298
  64.2 1.2 collective-permute-start.5
  65.4 4.3 %collective-permute-done.3.p1_h = f32[136,512]{1,0:T(8,128)S(1)} collective-permute-done((f32[136,512]{1,0:T(8,128)S(1)}, f32[136,512]{1,0:T(8,128)S(1)}, u32[]{:S(2)}, u32[]{:S(2)}) %collective-permute-start.3) | collective-permute-done | bytes 278560 | tf_op jit(solution)/shard_map/ppermute | solution.py:298
  69.6 7.0 %collective-permute-done.4.p2_h = f32[136,512]{1,0:T(8,128)S(1)} collective-permute-done((f32[136,512]{1,0:T(8,128)S(1)}, f32[136,512]{1,0:T(8,128)S(1)}, u32[]{:S(2)}, u32[]{:S(2)}) %collective-permute-start.4) | collective-permute-done | bytes 278560 | tf_op jit(solution)/shard_map/ppermute | solution.py:298
  76.6 0.6 shard_map.194.a0
  77.1 2.8 %collective-permute-start.8 = (bf16[144,512]{1,0:T(8,128)(2,1)S(1)}, bf16[144,512]{1,0:T(8,128)(2,1)S(1)}, u32[]{:S(2)}, u32[]{:S(2)}) collective-permute-start(bf16[144,512]{1,0:T(8,128)(2,1)S(1)} %shard_map.194.a0), channel_id=1, source_target_pairs={{0,6},{1,7},{2,0},{3,1},{4,2},{5,3},{6,4},{7,5},{8,14},{9,15},{10,... | collective-permute-start | bytes 442376 | tf_op jit(solution)/shard_map/ppermute | solution.py:298
  79.9 0.1 collective-permute-start.7
  80.0 0.7 collective-permute-start.6
  80.8 1.7 %collective-permute-start.9 = (bf16[144,512]{1,0:T(8,128)(2,1)S(1)}, bf16[144,512]{1,0:T(8,128)(2,1)S(1)}, u32[]{:S(2)}, u32[]{:S(2)}) collective-permute-start(bf16[144,512]{1,0:T(8,128)(2,1)S(1)} %shard_map.194.a0), channel_id=1, source_target_pairs={{0,1},{1,0},{2,3},{3,2},{4,5},{5,4},{6,7},{7,6},{8,9},{9,8},{10,11... | collective-permute-start | bytes 442376 | tf_op jit(solution)/shard_map/ppermute | solution.py:294
  82.5 3.4 %collective-permute-done.8.a3 = bf16[144,512]{1,0:T(8,128)(2,1)S(1)} collective-permute-done((bf16[144,512]{1,0:T(8,128)(2,1)S(1)}, bf16[144,512]{1,0:T(8,128)(2,1)S(1)}, u32[]{:S(2)}, u32[]{:S(2)}) %collective-permute-start.8) | collective-permute-done | bytes 147488 | tf_op jit(solution)/shard_map/ppermute | solution.py:298
  85.9 1.2 collective-permute-start.12
  87.1 1.8 %collective-permute-start.11 = (bf16[144,512]{1,0:T(8,128)(2,1)S(1)}, bf16[144,512]{1,0:T(8,128)(2,1)S(1)}, u32[]{:S(2)}, u32[]{:S(2)}) collective-permute-start(bf16[144,512]{1,0:T(8,128)(2,1)S(1)} %collective-permute-done.7.a2), channel_id=1, source_target_pairs={{0,1},{1,0},{2,3},{3,2},{4,5},{5,4},{6,7},{7,6},{8,9},{9,8},{10,11... | collective-permute-start | bytes 442376 | tf_op jit(solution)/shard_map/ppermute | solution.py:294
  88.9 1.1 collective-permute-done.6.a1
  90.0 0.7 collective-permute-start.10
  90.7 1.0 collective-permute-done.10.b1
  91.7 6.0 %shard_map.195 = (f32[1024,256]{1,0:T(8,128)}, f32[32,8,512]{2,1,0:T(8,128)S(1)}) custom-call(s32[3]{0:T(128)S(1)} %pad_add_fusion.pos, bf16[144,512]{1,0:T(8,128)(2,1)S(1)} %shard_map.194.a0, bf16[144,512]{1,0:T(8,128)(2,1)S(1)} %collective-permute-done.6.a1, bf16[144,512]{1,0:T(8,128)(2,1)S(1)} %collective-permute-done.7.a2, ...), custom_call_target="tpu_custom_call" | custom-call | tf_op jit(solution)/shard_map/pallas_call | solution.py:32
  97.7 18.8 %all_to_all.15.parts = f32[32,8,512]{2,1,0:T(8,128)S(1)} all-to-all(f32[32,8,512]{2,1,0:T(8,128)S(1)} %get-tuple-element.40), channel_id=1, replica_groups=mesh['node'=32,'rep'=8] {'node'}, dimensions={0} | all-to-all | bytes 1048576 | tf_op jit(solution)/shard_map/all_to_all | solution.py:390
  116.5 0.8 shard_map.196
  117.3 8.1 %all-to-all-start.2 = ((f32[32,8,384]{2,1,0:T(8,128)}), f32[32,8,384]{2,1,0:T(8,128)S(1)}, u32[]{:S(2)}, u32[]{:S(2)}) async-start(f32[32,8,384]{2,1,0:T(8,128)} %get-tuple-element.41), calls=%async_computation.2 | async-start | bytes 786432 | tf_op jit(solution)/shard_map/all_to_all | solution.py:392
  125.4 0.6 collective-permute-start.15
  126.0 0.1 collective-permute-start.14
  126.1 0.9 collective-permute-start.13
  127.0 1.7 %collective-permute-start.16 = (f32[32,8,128]{2,1,0:T(8,128)S(1)}, f32[32,8,128]{2,1,0:T(8,128)S(1)}, u32[]{:S(2)}, u32[]{:S(2)}) collective-permute-start(f32[32,8,128]{2,1,0:T(8,128)S(1)} %get-tuple-element.43.a0), channel_id=1, source_target_pairs={{0,1},{1,0},{2,3},{3,2},{4,5},{5,4},{6,7},{7,6},{8,9},{9,8},{10,11... | collective-permute-start | bytes 393224 | tf_op jit(solution)/shard_map/ppermute | solution.py:294
  128.7 0.6 collective-permute-done.15.a3
  129.3 3.5 %collective-permute-start.19 = (f32[32,8,128]{2,1,0:T(8,128)S(1)}, f32[32,8,128]{2,1,0:T(8,128)S(1)}, u32[]{:S(2)}, u32[]{:S(2)}) collective-permute-start(f32[32,8,128]{2,1,0:T(8,128)S(1)} %collective-permute-done.15.a3), channel_id=1, source_target_pairs={{0,1},{1,0},{2,3},{3,2},{4,5},{5,4},{6,7},{7,6},{8,9},{9,8},{10,11... | collective-permute-start | bytes 393224 | tf_op jit(solution)/shard_map/ppermute | solution.py:294
  132.8 2.2 %collective-permute-start.18 = (f32[32,8,128]{2,1,0:T(8,128)S(1)}, f32[32,8,128]{2,1,0:T(8,128)S(1)}, u32[]{:S(2)}, u32[]{:S(2)}) collective-permute-start(f32[32,8,128]{2,1,0:T(8,128)S(1)} %collective-permute-done.14.a2), channel_id=1, source_target_pairs={{0,1},{1,0},{2,3},{3,2},{4,5},{5,4},{6,7},{7,6},{8,9},{9,8},{10,11... | collective-permute-start | bytes 393224 | tf_op jit(solution)/shard_map/ppermute | solution.py:294
  135.0 0.0 collective-permute-done.13.a1
  135.0 1.2 collective-permute-start.17
  136.2 1.0 collective-permute-done.17.b1
  137.2 0.8 collective-permute-start.22
  138.1 0.1 collective-permute-start.21
  138.1 0.6 collective-permute-start.20
  138.8 4.3 %collective-permute-start.23 = (f32[24,8,384]{2,1,0:T(8,128)S(1)}, f32[24,8,384]{2,1,0:T(8,128)S(1)}, u32[]{:S(2)}, u32[]{:S(2)}) collective-permute-start(f32[24,8,384]{2,1,0:T(8,128)S(1)} %slice.3.a0), channel_id=1, source_target_pairs={{0,1},{1,0},{2,3},{3,2},{4,5},{5,4},{6,7},{7,6},{8,9},{9,8},{10,11... | collective-permute-start | bytes 884744 | tf_op jit(solution)/shard_map/ppermute | solution.py:294
  143.1 6.8 %collective-permute-start.26 = (f32[24,8,384]{2,1,0:T(8,128)S(1)}, f32[24,8,384]{2,1,0:T(8,128)S(1)}, u32[]{:S(2)}, u32[]{:S(2)}) collective-permute-start(f32[24,8,384]{2,1,0:T(8,128)S(1)} %collective-permute-done.22.a3), channel_id=1, source_target_pairs={{0,1},{1,0},{2,3},{3,2},{4,5},{5,4},{6,7},{7,6},{8,9},{9,8},{10,11... | collective-permute-start | bytes 884744 | tf_op jit(solution)/shard_map/ppermute | solution.py:294
  149.9 2.4 %collective-permute-start.25 = (f32[24,8,384]{2,1,0:T(8,128)S(1)}, f32[24,8,384]{2,1,0:T(8,128)S(1)}, u32[]{:S(2)}, u32[]{:S(2)}) collective-permute-start(f32[24,8,384]{2,1,0:T(8,128)S(1)} %collective-permute-done.21.a2), channel_id=1, source_target_pairs={{0,1},{1,0},{2,3},{3,2},{4,5},{5,4},{6,7},{7,6},{8,9},{9,8},{10,11... | collective-permute-start | bytes 884744 | tf_op jit(solution)/shard_map/ppermute | solution.py:294
  152.3 1.3 collective-permute-done.20.a1
  153.6 1.7 %collective-permute-start.24 = (f32[24,8,384]{2,1,0:T(8,128)S(1)}, f32[24,8,384]{2,1,0:T(8,128)S(1)}, u32[]{:S(2)}, u32[]{:S(2)}) collective-permute-start(f32[24,8,384]{2,1,0:T(8,128)S(1)} %collective-permute-done.20.a1), channel_id=1, source_target_pairs={{0,1},{1,0},{2,3},{3,2},{4,5},{5,4},{6,7},{7,6},{8,9},{9,8},{10,11... | collective-permute-start | bytes 884744 | tf_op jit(solution)/shard_map/ppermute | solution.py:294
  155.3 3.9 %shard_map.197 = f32[1024,256]{1,0:T(8,128)} custom-call(s32[3]{0:T(128)S(1)} %pad_add_fusion.pos, s32[1,1024]{1,0:T(1,128)S(1)} %bitcast.16, f32[32,8,128]{2,1,0:T(8,128)S(1)} %get-tuple-element.43.a0, f32[32,8,128]{2,1,0:T(8,128)S(1)} %collective-permute-done.13.a1, f32[32,8,128]{2,1,0:T(8,128)S(1)} %collective-permute-done.14.a2, ...), custom_call_target="tpu_custom_call" | custom-call | tf_op jit(solution)/shard_map/pallas_call | solution.py:32
  159.2 2.2 %shard_map.198 = (f32[512,768]{1,0:T(8,128)}, f32[256,768]{1,0:T(8,128)}) custom-call(s32[3]{0:T(128)S(1)} %pad_add_fusion.pos, f32[24,8,384]{2,1,0:T(8,128)S(1)} %slice.3.a0, f32[24,8,384]{2,1,0:T(8,128)S(1)} %collective-permute-done.20.a1, f32[24,8,384]{2,1,0:T(8,128)S(1)} %collective-permute-done.21.a2, f32[24,8,384]{2,1,0:T(8,128)S(1)} %collective-permute-done.22.a3, ...), custom_call_target="tpu_custom_call" | custom-call | tf_op jit(solution)/shard_map/pallas_call | solution.py:32
  (34 shorter events, 0.1 us)
Async XLA Ops:
  7.1 13.3 %copy-start.4 = (s32[1024]{0:T(1024)S(1)}, s32[1024]{0:T(1024)}, u32[]{:S(2)}) copy-start(s32[1024]{0:T(1024)} %param.27) | copy-start | bytes 12292
  7.1 13.5 %copy-start.6 = (f32[1024,256]{1,0:T(8,128)S(1)}, f32[1024,256]{1,0:T(8,128)}, u32[]{:S(2)}) copy-start(f32[1024,256]{1,0:T(8,128)} %param.20) | copy-start | bytes 3145732
  7.1 42.2 %all-to-all-start = ((bf16[32,144,128]{2,1,0:T(8,128)(2,1)}), bf16[32,144,128]{2,1,0:T(8,128)(2,1)S(1)}, u32[]{:S(2)}, u32[]{:S(2)}) async-start(bf16[32,144,128]{2,1,0:T(8,128)(2,1)} %get-tuple-element.29), calls=%async_computation | async-start | bytes 2359296 | tf_op jit(solution)/shard_map/all_to_all | solution.py:351
  19.3 4.8 %collective-permute-start = (f32[96,512]{1,0:T(8,128)}, f32[96,512]{1,0:T(8,128)}, u32[]{:S(2)}, u32[]{:S(2)}) collective-permute-start(f32[96,512]{1,0:T(8,128)} %get-tuple-element.30), channel_id=1, source_target_pairs={{0,1},{1,0},{2,3},{3,2},{4,5},{5,4},{6,7},{7,6},{8,9},{9,8},{10,11... | collective-permute-start | bytes 589832 | tf_op jit(solution)/shard_map/ppermute | solution.py:294
  20.6 3.4 %copy-start.5 = (f32[1024,256]{1,0:T(8,128)S(1)}, f32[1024,256]{1,0:T(8,128)}, u32[]{:S(2)}) copy-start(f32[1024,256]{1,0:T(8,128)} %mem_h.1) | copy-start | bytes 3145732
  24.0 3.4 %copy-start.7 = (f32[1024,256]{1,0:T(8,128)S(1)}, f32[1024,256]{1,0:T(8,128)}, u32[]{:S(2)}) copy-start(f32[1024,256]{1,0:T(8,128)} %param.19) | copy-start | bytes 3145732
  24.0 3.4 %copy-start.8 = (f32[128,256]{1,0:T(8,128)S(1)}, f32[128,256]{1,0:T(8,128)}, u32[]{:S(2)}) copy-start(f32[128,256]{1,0:T(8,128)} %gather_fusion.1) | copy-start | bytes 393220
  25.2 0.7 copy-start.9
  25.9 22.8 %collective-permute-start.1 = (f32[16,512]{1,0:T(8,128)S(1)}, f32[16,512]{1,0:T(8,128)S(1)}, u32[]{:S(2)}, u32[]{:S(2)}) collective-permute-start(f32[16,512]{1,0:T(8,128)S(1)} %constant_dynamic-slice_fusion), channel_id=1, source_target_pairs={{0,8},{8,16},{16,24},{24,32},{32,40},{40,48},{48,56},{56,64},{64,7... | collective-permute-start | bytes 98312 | tf_op jit(solution)/shard_map/ppermute | solution.py:355
  48.7 0.6 copy-start.2
  49.3 5.6 %collective-permute-start.2 = (bf16[32,144,128]{2,1,0:T(8,128)(2,1)S(1)}, bf16[32,144,128]{2,1,0:T(8,128)(2,1)}, u32[]{:S(2)}, u32[]{:S(2)}) collective-permute-start(bf16[32,144,128]{2,1,0:T(8,128)(2,1)S(1)} %all-to-all-done.own), channel_id=1, source_target_pairs={{0,1},{1,0},{2,3},{3,2},{4,5},{5,4},{6,7},{7,6},{8,9},{9,8},{10,11... | collective-permute-start | bytes 3538952 | tf_op jit(solution)/shard_map/ppermute | solution.py:294
  54.9 0.8 copy-start.3
  60.4 31.2 %copy-start = (bf16[512,768]{1,0:T(8,128)(2,1)S(1)}, bf16[512,768]{1,0:T(8,128)(2,1)}, u32[]{:S(2)}) copy-start(bf16[512,768]{1,0:T(8,128)(2,1)} %w_in.1) | copy-start | bytes 2359300
  60.4 31.2 %copy-start.1 = (bf16[256,768]{1,0:T(8,128)(2,1)S(1)}, bf16[256,768]{1,0:T(8,128)(2,1)}, u32[]{:S(2)}) copy-start(bf16[256,768]{1,0:T(8,128)(2,1)} %w_hid.1) | copy-start | bytes 1179652
  60.5 9.2 %collective-permute-start.3 = (f32[136,512]{1,0:T(8,128)S(1)}, f32[136,512]{1,0:T(8,128)S(1)}, u32[]{:S(2)}, u32[]{:S(2)}) collective-permute-start(f32[136,512]{1,0:T(8,128)S(1)} %get-tuple-element.33), channel_id=1, source_target_pairs={{0,2},{1,3},{2,4},{3,5},{4,6},{5,7},{6,0},{7,1},{8,10},{9,11},{10,... | collective-permute-start | bytes 835592 | tf_op jit(solution)/shard_map/ppermute | solution.py:298
  61.7 14.8 %collective-permute-start.4 = (f32[136,512]{1,0:T(8,128)S(1)}, f32[136,512]{1,0:T(8,128)S(1)}, u32[]{:S(2)}, u32[]{:S(2)}) collective-permute-start(f32[136,512]{1,0:T(8,128)S(1)} %get-tuple-element.34), channel_id=1, source_target_pairs={{0,4},{1,5},{2,6},{3,7},{4,0},{5,1},{6,2},{7,3},{8,12},{9,13},{10,... | collective-permute-start | bytes 835592 | tf_op jit(solution)/shard_map/ppermute | solution.py:298
  64.2 12.4 %collective-permute-start.5 = (f32[136,512]{1,0:T(8,128)S(1)}, f32[136,512]{1,0:T(8,128)S(1)}, u32[]{:S(2)}, u32[]{:S(2)}) collective-permute-start(f32[136,512]{1,0:T(8,128)S(1)} %get-tuple-element.35), channel_id=1, source_target_pairs={{0,6},{1,7},{2,0},{3,1},{4,2},{5,3},{6,4},{7,5},{8,14},{9,15},{10,... | collective-permute-start | bytes 835592 | tf_op jit(solution)/shard_map/ppermute | solution.py:298
  77.1 8.7 %collective-permute-start.8 = (bf16[144,512]{1,0:T(8,128)(2,1)S(1)}, bf16[144,512]{1,0:T(8,128)(2,1)S(1)}, u32[]{:S(2)}, u32[]{:S(2)}) collective-permute-start(bf16[144,512]{1,0:T(8,128)(2,1)S(1)} %shard_map.194.a0), channel_id=1, source_target_pairs={{0,6},{1,7},{2,0},{3,1},{4,2},{5,3},{6,4},{7,5},{8,14},{9,15},{10,... | collective-permute-start | bytes 442376 | tf_op jit(solution)/shard_map/ppermute | solution.py:298
  79.9 7.2 %collective-permute-start.7 = (bf16[144,512]{1,0:T(8,128)(2,1)S(1)}, bf16[144,512]{1,0:T(8,128)(2,1)S(1)}, u32[]{:S(2)}, u32[]{:S(2)}) collective-permute-start(bf16[144,512]{1,0:T(8,128)(2,1)S(1)} %shard_map.194.a0), channel_id=1, source_target_pairs={{0,4},{1,5},{2,6},{3,7},{4,0},{5,1},{6,2},{7,3},{8,12},{9,13},{10,... | collective-permute-start | bytes 442376 | tf_op jit(solution)/shard_map/ppermute | solution.py:298
  80.0 10.0 %collective-permute-start.6 = (bf16[144,512]{1,0:T(8,128)(2,1)S(1)}, bf16[144,512]{1,0:T(8,128)(2,1)S(1)}, u32[]{:S(2)}, u32[]{:S(2)}) collective-permute-start(bf16[144,512]{1,0:T(8,128)(2,1)S(1)} %shard_map.194.a0), channel_id=1, source_target_pairs={{0,2},{1,3},{2,4},{3,5},{4,6},{5,7},{6,0},{7,1},{8,10},{9,11},{10,... | collective-permute-start | bytes 442376 | tf_op jit(solution)/shard_map/ppermute | solution.py:298
  80.8 9.9 %collective-permute-start.9 = (bf16[144,512]{1,0:T(8,128)(2,1)S(1)}, bf16[144,512]{1,0:T(8,128)(2,1)S(1)}, u32[]{:S(2)}, u32[]{:S(2)}) collective-permute-start(bf16[144,512]{1,0:T(8,128)(2,1)S(1)} %shard_map.194.a0), channel_id=1, source_target_pairs={{0,1},{1,0},{2,3},{3,2},{4,5},{5,4},{6,7},{7,6},{8,9},{9,8},{10,11... | collective-permute-start | bytes 442376 | tf_op jit(solution)/shard_map/ppermute | solution.py:294
  85.9 4.8 %collective-permute-start.12 = (bf16[144,512]{1,0:T(8,128)(2,1)S(1)}, bf16[144,512]{1,0:T(8,128)(2,1)S(1)}, u32[]{:S(2)}, u32[]{:S(2)}) collective-permute-start(bf16[144,512]{1,0:T(8,128)(2,1)S(1)} %collective-permute-done.8.a3), channel_id=1, source_target_pairs={{0,1},{1,0},{2,3},{3,2},{4,5},{5,4},{6,7},{7,6},{8,9},{9,8},{10,11... | collective-permute-start | bytes 442376 | tf_op jit(solution)/shard_map/ppermute | solution.py:294
  87.1 3.5 %collective-permute-start.11 = (bf16[144,512]{1,0:T(8,128)(2,1)S(1)}, bf16[144,512]{1,0:T(8,128)(2,1)S(1)}, u32[]{:S(2)}, u32[]{:S(2)}) collective-permute-start(bf16[144,512]{1,0:T(8,128)(2,1)S(1)} %collective-permute-done.7.a2), channel_id=1, source_target_pairs={{0,1},{1,0},{2,3},{3,2},{4,5},{5,4},{6,7},{7,6},{8,9},{9,8},{10,11... | collective-permute-start | bytes 442376 | tf_op jit(solution)/shard_map/ppermute | solution.py:294
  90.0 1.7 %collective-permute-start.10 = (bf16[144,512]{1,0:T(8,128)(2,1)S(1)}, bf16[144,512]{1,0:T(8,128)(2,1)S(1)}, u32[]{:S(2)}, u32[]{:S(2)}) collective-permute-start(bf16[144,512]{1,0:T(8,128)(2,1)S(1)} %collective-permute-done.6.a1), channel_id=1, source_target_pairs={{0,1},{1,0},{2,3},{3,2},{4,5},{5,4},{6,7},{7,6},{8,9},{9,8},{10,11... | collective-permute-start | bytes 442376 | tf_op jit(solution)/shard_map/ppermute | solution.py:294
  117.3 19.9 %all-to-all-start.2 = ((f32[32,8,384]{2,1,0:T(8,128)}), f32[32,8,384]{2,1,0:T(8,128)S(1)}, u32[]{:S(2)}, u32[]{:S(2)}) async-start(f32[32,8,384]{2,1,0:T(8,128)} %get-tuple-element.41), calls=%async_computation.2 | async-start | bytes 786432 | tf_op jit(solution)/shard_map/all_to_all | solution.py:392
  125.4 3.9 %collective-permute-start.15 = (f32[32,8,128]{2,1,0:T(8,128)S(1)}, f32[32,8,128]{2,1,0:T(8,128)S(1)}, u32[]{:S(2)}, u32[]{:S(2)}) collective-permute-start(f32[32,8,128]{2,1,0:T(8,128)S(1)} %get-tuple-element.43.a0), channel_id=1, source_target_pairs={{0,6},{1,7},{2,0},{3,1},{4,2},{5,3},{6,4},{7,5},{8,14},{9,15},{10,... | collective-permute-start | bytes 393224 | tf_op jit(solution)/shard_map/ppermute | solution.py:298
  126.0 6.8 %collective-permute-start.14 = (f32[32,8,128]{2,1,0:T(8,128)S(1)}, f32[32,8,128]{2,1,0:T(8,128)S(1)}, u32[]{:S(2)}, u32[]{:S(2)}) collective-permute-start(f32[32,8,128]{2,1,0:T(8,128)S(1)} %get-tuple-element.43.a0), channel_id=1, source_target_pairs={{0,4},{1,5},{2,6},{3,7},{4,0},{5,1},{6,2},{7,3},{8,12},{9,13},{10,... | collective-permute-start | bytes 393224 | tf_op jit(solution)/shard_map/ppermute | solution.py:298
  126.1 9.0 %collective-permute-start.13 = (f32[32,8,128]{2,1,0:T(8,128)S(1)}, f32[32,8,128]{2,1,0:T(8,128)S(1)}, u32[]{:S(2)}, u32[]{:S(2)}) collective-permute-start(f32[32,8,128]{2,1,0:T(8,128)S(1)} %get-tuple-element.43.a0), channel_id=1, source_target_pairs={{0,2},{1,3},{2,4},{3,5},{4,6},{5,7},{6,0},{7,1},{8,10},{9,11},{10,... | collective-permute-start | bytes 393224 | tf_op jit(solution)/shard_map/ppermute | solution.py:298
  127.0 9.2 %collective-permute-start.16 = (f32[32,8,128]{2,1,0:T(8,128)S(1)}, f32[32,8,128]{2,1,0:T(8,128)S(1)}, u32[]{:S(2)}, u32[]{:S(2)}) collective-permute-start(f32[32,8,128]{2,1,0:T(8,128)S(1)} %get-tuple-element.43.a0), channel_id=1, source_target_pairs={{0,1},{1,0},{2,3},{3,2},{4,5},{5,4},{6,7},{7,6},{8,9},{9,8},{10,11... | collective-permute-start | bytes 393224 | tf_op jit(solution)/shard_map/ppermute | solution.py:294
  129.3 6.9 %collective-permute-start.19 = (f32[32,8,128]{2,1,0:T(8,128)S(1)}, f32[32,8,128]{2,1,0:T(8,128)S(1)}, u32[]{:S(2)}, u32[]{:S(2)}) collective-permute-start(f32[32,8,128]{2,1,0:T(8,128)S(1)} %collective-permute-done.15.a3), channel_id=1, source_target_pairs={{0,1},{1,0},{2,3},{3,2},{4,5},{5,4},{6,7},{7,6},{8,9},{9,8},{10,11... | collective-permute-start | bytes 393224 | tf_op jit(solution)/shard_map/ppermute | solution.py:294
  132.8 3.4 %collective-permute-start.18 = (f32[32,8,128]{2,1,0:T(8,128)S(1)}, f32[32,8,128]{2,1,0:T(8,128)S(1)}, u32[]{:S(2)}, u32[]{:S(2)}) collective-permute-start(f32[32,8,128]{2,1,0:T(8,128)S(1)} %collective-permute-done.14.a2), channel_id=1, source_target_pairs={{0,1},{1,0},{2,3},{3,2},{4,5},{5,4},{6,7},{7,6},{8,9},{9,8},{10,11... | collective-permute-start | bytes 393224 | tf_op jit(solution)/shard_map/ppermute | solution.py:294
  135.0 2.2 %collective-permute-start.17 = (f32[32,8,128]{2,1,0:T(8,128)S(1)}, f32[32,8,128]{2,1,0:T(8,128)S(1)}, u32[]{:S(2)}, u32[]{:S(2)}) collective-permute-start(f32[32,8,128]{2,1,0:T(8,128)S(1)} %collective-permute-done.13.a1), channel_id=1, source_target_pairs={{0,1},{1,0},{2,3},{3,2},{4,5},{5,4},{6,7},{7,6},{8,9},{9,8},{10,11... | collective-permute-start | bytes 393224 | tf_op jit(solution)/shard_map/ppermute | solution.py:294
  137.2 5.9 %collective-permute-start.22 = (f32[24,8,384]{2,1,0:T(8,128)S(1)}, f32[24,8,384]{2,1,0:T(8,128)S(1)}, u32[]{:S(2)}, u32[]{:S(2)}) collective-permute-start(f32[24,8,384]{2,1,0:T(8,128)S(1)} %slice.3.a0), channel_id=1, source_target_pairs={{0,6},{1,7},{2,0},{3,1},{4,2},{5,3},{6,4},{7,5},{8,14},{9,15},{10,... | collective-permute-start | bytes 884744 | tf_op jit(solution)/shard_map/ppermute | solution.py:298
  138.1 11.8 %collective-permute-start.21 = (f32[24,8,384]{2,1,0:T(8,128)S(1)}, f32[24,8,384]{2,1,0:T(8,128)S(1)}, u32[]{:S(2)}, u32[]{:S(2)}) collective-permute-start(f32[24,8,384]{2,1,0:T(8,128)S(1)} %slice.3.a0), channel_id=1, source_target_pairs={{0,4},{1,5},{2,6},{3,7},{4,0},{5,1},{6,2},{7,3},{8,12},{9,13},{10,... | collective-permute-start | bytes 884744 | tf_op jit(solution)/shard_map/ppermute | solution.py:298
  138.1 15.4 %collective-permute-start.20 = (f32[24,8,384]{2,1,0:T(8,128)S(1)}, f32[24,8,384]{2,1,0:T(8,128)S(1)}, u32[]{:S(2)}, u32[]{:S(2)}) collective-permute-start(f32[24,8,384]{2,1,0:T(8,128)S(1)} %slice.3.a0), channel_id=1, source_target_pairs={{0,2},{1,3},{2,4},{3,5},{4,6},{5,7},{6,0},{7,1},{8,10},{9,11},{10,... | collective-permute-start | bytes 884744 | tf_op jit(solution)/shard_map/ppermute | solution.py:298
  138.8 20.4 %collective-permute-start.23 = (f32[24,8,384]{2,1,0:T(8,128)S(1)}, f32[24,8,384]{2,1,0:T(8,128)S(1)}, u32[]{:S(2)}, u32[]{:S(2)}) collective-permute-start(f32[24,8,384]{2,1,0:T(8,128)S(1)} %slice.3.a0), channel_id=1, source_target_pairs={{0,1},{1,0},{2,3},{3,2},{4,5},{5,4},{6,7},{7,6},{8,9},{9,8},{10,11... | collective-permute-start | bytes 884744 | tf_op jit(solution)/shard_map/ppermute | solution.py:294
  143.1 16.1 %collective-permute-start.26 = (f32[24,8,384]{2,1,0:T(8,128)S(1)}, f32[24,8,384]{2,1,0:T(8,128)S(1)}, u32[]{:S(2)}, u32[]{:S(2)}) collective-permute-start(f32[24,8,384]{2,1,0:T(8,128)S(1)} %collective-permute-done.22.a3), channel_id=1, source_target_pairs={{0,1},{1,0},{2,3},{3,2},{4,5},{5,4},{6,7},{7,6},{8,9},{9,8},{10,11... | collective-permute-start | bytes 884744 | tf_op jit(solution)/shard_map/ppermute | solution.py:294
  149.9 9.3 %collective-permute-start.25 = (f32[24,8,384]{2,1,0:T(8,128)S(1)}, f32[24,8,384]{2,1,0:T(8,128)S(1)}, u32[]{:S(2)}, u32[]{:S(2)}) collective-permute-start(f32[24,8,384]{2,1,0:T(8,128)S(1)} %collective-permute-done.21.a2), channel_id=1, source_target_pairs={{0,1},{1,0},{2,3},{3,2},{4,5},{5,4},{6,7},{7,6},{8,9},{9,8},{10,11... | collective-permute-start | bytes 884744 | tf_op jit(solution)/shard_map/ppermute | solution.py:294
  153.6 5.6 %collective-permute-start.24 = (f32[24,8,384]{2,1,0:T(8,128)S(1)}, f32[24,8,384]{2,1,0:T(8,128)S(1)}, u32[]{:S(2)}, u32[]{:S(2)}) collective-permute-start(f32[24,8,384]{2,1,0:T(8,128)S(1)} %collective-permute-done.20.a1), channel_id=1, source_target_pairs={{0,1},{1,0},{2,3},{3,2},{4,5},{5,4},{6,7},{7,6},{8,9},{9,8},{10,11... | collective-permute-start | bytes 884744 | tf_op jit(solution)/shard_map/ppermute | solution.py:294

commit v4 on v3

--- a/solution.py
+++ b/solution.py
@@ -1,3 +1,5 @@
+import functools
+
 import jax
 import jax.numpy as jnp
 from jax import lax
@@ -58,7 +60,7 @@
 
 def message_kernel(
     pos, mem_h, edge_h, w_h, src_h, times_h, dst_h, listed_h, used_h, freq_h, phase_h, b_h, send_h, hot,
-    mem, edge, w, src, times, dst_v, listed, used, freq, phase, b, msgs, out, cols, sems,
+    mem, edge, w, src, times, dst_v, listed, used, freq, phase, b, encs, msgs, out, cols, sems,
 ):
     loads = [
         pltpu.make_async_copy(h, v, sems.at[i])
@@ -84,14 +86,14 @@
     hi = mm(eye, (names >> 5).astype(F32).astype(BF16), ((1,), (1,)))
     lo = mm(eye, (names & 31).astype(F32).astype(BF16), ((1,), (1,)))
     names = jnp.where(slot < used[...], (hi * 32.0 + lo).astype(I32), -1)
+    encs[...] = cosine(cols[:, 1:2].astype(F32) * freq[...] + phase[...]).astype(BF16)
     for c in loads[8:]:
         c.wait()
     mem16 = mem[...].astype(BF16)
     for e in range(0, n_ev, step):
         at = cols[e : e + step, :]
         src_mem = mm(one_hot(iota((step, 1024), 1) == at[:, 0:1]), mem16).astype(BF16)
-        enc = cosine(at[:, 1:2].astype(F32) * freq[...] + phase[...]).astype(BF16)
-        raw = jnp.concatenate([src_mem, edge[e : e + step, :], enc], axis=1)
+        raw = jnp.concatenate([src_mem, edge[e : e + step, :], encs[e : e + step, :]], axis=1)
         pre = mm(raw, w[...]) + b[...]
         msgs[e : e + step, :] = (pre * jax.nn.sigmoid(pre)).astype(BF16)
     row = dst & 1023
@@ -128,45 +130,40 @@
         c.wait()
 
 
-def cold_kernel(pos, own, peer, hot, spill, o0, o1_h, o2_h, o3_h, msgs, out, sems):
-    got = (own, peer)
+def cold_kernel(pos, own, peer, hot, spill, o0, o1, o2, o3):
     q = iota((512, 128), 0)
     want = (q & 127) + 256 * ((pos[0] + (q >> 7)) & 3) + 128 * pos[1]
     hits = []
-    for h in range(2):
+    for got in (own, peer):
         for g in range(8):
-            tail = got[h][4 * g, 128:144, :].astype(F32)
+            tail = got[4 * g, 128:144, :].astype(F32)
             for i in range(1, 4):
-                tail = tail + got[h][4 * g + i, 128:144, :].astype(F32)
+                tail = tail + got[4 * g + i, 128:144, :].astype(F32)
             row = jnp.where(tail[2:3, :] > 0.5, tail[0:1, :] * 32.0 + tail[1:2, :], -1.0).astype(I32)
             hits.append(one_hot(want == row))
-        for s in range(32):
-            for k in range(4):
-                here = slice(1024 * h + 32 * s, 1024 * h + 32 * s + 32)
-                msgs[here, 128 * k : 128 * k + 128] = got[h][s, 32 * k : 32 * k + 32, :]
     hit = jnp.concatenate(hits, axis=1)
     count = mm(jnp.ones((8, 2048), BF16), hit, ((1,), (1,)))
-    stores = []
     for n in range(2):
         cols = slice(256 * n, 256 * n + 256)
-        total = mm(hit, msgs[:, cols])
-        for d in (2, 1, 3, 0):
+        msgs = jnp.concatenate(
+            [
+                jnp.concatenate(
+                    [got[:, 32 * k : 32 * k + 32, :].reshape(1024, 128) for k in (2 * n, 2 * n + 1)], axis=1
+                )
+                for got in (own, peer)
+            ],
+            axis=0,
+        )
+        total = mm(hit, msgs)
+        for d, to in enumerate((o0, o1, o2, o3)):
             here = slice(128 * d, 128 * d + 128)
-            to = o0 if d == 0 else out.at[d - 1]
             to[0:128, cols] = total[here, :]
             j = (pos[0] + d) & 3
-            tile = hot[j, :, cols] + jnp.where(j < 2, 1.0, 0.0) * spill[j & 1, :, cols]
+            tile = hot[4 * pos[1] + j, :, cols] + jnp.where(j < 2, 1.0, 0.0) * spill[j & 1, :, cols]
             if n == 0:
                 rows = jnp.concatenate([count[:, here], tile[:, 128:256]], axis=1)
                 tile = jnp.where((iota((8, 256), 0) >= 4) & (iota((8, 256), 1) < 128), rows, tile)
             to[128:136, cols] = tile
-            if d > 0:
-                dst = (o1_h, o2_h, o3_h)[d - 1]
-                c = pltpu.make_async_copy(out.at[d - 1, :, cols], dst.at[:, cols], sems.at[3 * n + d - 1])
-                c.start()
-                stores.append(c)
-    for c in stores:
-        c.wait()
 
 
 def agg_kernel(p1_h, p2_h, p3_h, p0, out_h, part, out, sems):
@@ -216,55 +213,61 @@
         out[h : h + 256, :] = mm(pick, hi) + (mm(pick, mid) + mm(pick, low))
 
 
-def update_kernel(pos, a0, a1, a2, a3, b0, b1, b2, b3, mem, cot, w_in, w_hid, new, grad, agg, acc, hot):
+def update_kernel(ds, last, pos, *refs):
+    parts, refs = refs[: 2 * len(ds)], refs[2 * len(ds) :]
+    mem, cot, hot_mem, hot_cot, w_in, w_hid = refs[:6]
+    if last:
+        own_new, own_hot, own_acc, new, grad, acc = refs[6:]
+        acc[...] = own_acc[...]
+        new[pl.ds(pl.multiple_of(256 * pos[0], 256), 256), :] = own_new[...]
+    else:
+        new, hot, acc = refs[6:]
     x, core, rep = pos[0], pos[1], pos[2]
-    for group, c in (((a0, a1, a2, a3), core), ((b0, b1, b2, b3), 1 - core)):
-        for d, part in enumerate(group):
-            block = 2 * ((x - d + 4) & 3) + c
-            agg[pl.ds(pl.multiple_of(block * 128, 128), 128), :] = part[0:128, :]
-            agg[pl.ds(pl.multiple_of(1024 + block * 16, 16), 16), :] = part[128:144, :]
     k, q = iota((512, 128), 0), iota((512, 128), 1)
     sel_a = one_hot((k == 64 * rep + q) & (q < 64))
     k, q = iota((256, 128), 0), iota((256, 128), 1)
     sel_m = one_hot((k == 32 * rep + q - 64) & (q >= 64) & (q < 96))
-    step = 384
-    for s in range(0, 1152, step):
-        wide = agg[s : s + step, :].astype(F32)
+    for i, d in enumerate(ds):
+        chip = (x - d + 4) & 3
+        at = pl.ds(pl.multiple_of(256 * chip, 256), 256)
+        hot_at = pl.ds(pl.multiple_of(32 * chip, 32), 32)
+        mine, other = parts[2 * i][...], parts[2 * i + 1][...]
+        low = jnp.where(core == 0, mine, other)
+        high = jnp.where(core == 0, other, mine)
+        wide = jnp.concatenate([low[0:128], high[0:128], low[128:144], high[128:144]], axis=0).astype(F32)
         live = wide[:, 0:1] < DEAD * 0.5
         a = jnp.where(live, wide, 0.0).astype(BF16)
-        m = mem[s : s + step, :]
+        m = jnp.concatenate([mem[at, :], hot_mem[hot_at, :]], axis=0)
         reset, update, cand, hid_cand = gates(a, m, w_in[...], w_hid[...])
         fresh = jnp.where(live, (1.0 - update) * cand + update * m, m)
-        rows = min(step, 1024 - s)
-        new[s : s + rows, :] = fresh[0:rows, :]
-        if rows < step:
-            hot[...] = fresh[rows:step, :]
-        g = jnp.where(live, cot[s : s + step, :], 0.0)
+        if last:
+            new[at, :] = fresh[0:256, :]
+        else:
+            new[...] = fresh[0:256, :]
+            own = jnp.where(core == 0, fresh[256:264, :], fresh[272:280, :])
+            hot[...] = jnp.concatenate([own[0:4, 0:128], own[0:4, 128:256]], axis=0)
+        g = jnp.where(live, jnp.concatenate([cot[at, :], hot_cot[hot_at, :]], axis=0), 0.0)
         d_cand = g * (1.0 - update) * (1.0 - cand * cand)
         d_upd = g * (m - cand) * update * (1.0 - update)
         d_reset = d_cand * hid_cand * reset * (1.0 - reset)
         left = (mm(a, sel_a) + mm(m.astype(BF16), sel_m)).astype(BF16)
-        for j, d in enumerate((d_reset, d_upd, d_cand, d_cand * reset)):
-            hi = d.astype(BF16)
-            rest = d - hi.astype(F32)
-            mid = rest.astype(BF16)
-            low = (rest - mid.astype(F32)).astype(BF16)
-            dims = ((0,), (0,))
-            part = mm(left, hi, dims) + (mm(left, mid, dims) + mm(left, low, dims))
+        for j, v in enumerate((d_reset, d_upd, d_cand, d_cand * reset)):
+            hi = v.astype(BF16)
+            low = (v - hi.astype(F32)).astype(BF16)
+            part = mm(left, hi, ((0,), (0,))) + mm(left, low, ((0,), (0,)))
             cols = slice(256 * j, 256 * j + 256)
-            if s == 0:
+            if i == 0 and not last:
                 acc[:, cols] = part
             else:
                 acc[:, cols] += part
-    total = acc[...] * GRAD_SCALE
-    third = jnp.where(iota((128, 256), 0) < 64, total[:, 512:768], total[:, 768:1024])
-    total = jnp.concatenate([total[:, 0:512], third], axis=1)
-    own = hot[pl.ds(pl.multiple_of(16 * rep, 16), 8), :]
-    own = jnp.concatenate([own[0:4, 0:128], own[0:4, 128:256]], axis=0)
-    for p in range(32):
-        i, j = p // 2, p % 2
-        grad[p, :, 0:384] = total[8 * i : 8 * i + 8, 384 * j : 384 * j + 384]
-        grad[p, :, 384:512] = own
+    if last:
+        total = acc[...] * GRAD_SCALE
+        third = jnp.where(iota((128, 256), 0) < 64, total[:, 512:768], total[:, 768:1024])
+        total = jnp.concatenate([total[:, 0:512], third], axis=1)
+        for p in range(32):
+            i, j = p // 2, p % 2
+            grad[p, :, 0:384] = total[8 * i : 8 * i + 8, 384 * j : 384 * j + 384]
+            grad[p, :, 384:512] = own_hot[...]
 
 
 def piece_kernel(parts, out, hot):
@@ -276,18 +279,24 @@
         hot[k] = parts[k, :, 384:512]
 
 
-def place_kernel(pos, a0, a1, a2, a3, b0, b1, b2, b3, g_in, g_hid):
+def place_kernel(pos, a0, a1, a2, a3, b0, b1, b2, b3, g_in, g_hid, both, sems):
     x, core = pos[0], pos[1]
+    stores = []
     for group, c in (((a0, a1, a2, a3), core), ((b0, b1, b2, b3), 1 - core)):
         for d, part in enumerate(group):
             block = 2 * ((x - d + 4) & 3) + c
+            k = len(stores)
             for p in range(24):
                 i, j = p // 2, p % 2
-                cols = slice(384 * j, 384 * j + 384)
-                if i < 8:
-                    g_in[pl.ds(pl.multiple_of(block * 64 + 8 * i, 8), 8), cols] = part[p]
-                else:
-                    g_hid[pl.ds(pl.multiple_of(block * 32 + 8 * (i - 8), 8), 8), cols] = part[p]
+                both[96 * (k // 2) + 8 * i : 96 * (k // 2) + 8 * i + 8, 384 * j : 384 * j + 384] = part[p]
+            for rows, at, dst in (
+                (64, 96 * (k // 2), g_in.at[pl.ds(pl.multiple_of(block * 64, 64), 64)]),
+                (32, 96 * (k // 2) + 64, g_hid.at[pl.ds(pl.multiple_of(block * 32, 32), 32)]),
+            ):
+                stores.append(pltpu.make_async_copy(both.at[at : at + rows], dst, sems.at[len(stores)]))
+                stores[-1].start()
+    for c in stores:
+        c.wait()
 
 
 def swap_core(v):
@@ -342,7 +351,8 @@
             pltpu.VMEM((1, 1024), I32), pltpu.VMEM((1, 1024), I32), pltpu.VMEM((1, 1024), I32),
             pltpu.VMEM((32, 32), I32), pltpu.VMEM((1, 32), I32), pltpu.VMEM((1, 128), F32),
             pltpu.VMEM((1, 128), F32), pltpu.VMEM((1, 512), F32),
-            pltpu.VMEM((1024, 512), BF16), pltpu.VMEM((32, 144, 128), BF16), pltpu.VMEM((1024, 8), I32),
+            pltpu.VMEM((1024, 128), BF16), pltpu.VMEM((1024, 512), BF16), pltpu.VMEM((32, 144, 128), BF16),
+            pltpu.VMEM((1024, 8), I32),
             pltpu.SemaphoreType.DMA((15,)),
         ),
         (ANY, VM),
@@ -353,22 +363,19 @@
     hot = hot + swap_core(hot)
     spill = lax.dynamic_slice_in_dim(hot, 64 + 16 * core, 16, 0)
     spill = lax.ppermute(spill, "node", [(k, (k + 1) % 32) for k in range(32)])
-    hot = lax.dynamic_slice_in_dim(hot, 32 * core, 32, 0)
     k = jnp.arange(128, dtype=I32)
     want = 32768 + 32 * node + 4 * (k // 16) + k % 4
     at = jnp.sum(jnp.where(want[:, None] == hot_ids[None, :], jnp.arange(1024, dtype=I32)[None, :], 0), axis=1)
-    mem_all = jnp.concatenate([memory, jnp.take(hot_memory, at, axis=0, mode="clip")], axis=0)
-    cot_all = jnp.concatenate([cot_cold, jnp.take(cot_hot, at, axis=0, mode="clip")], axis=0)
-
-    recv, spill, mem_all, cot_all = lax.optimization_barrier((recv, spill, mem_all, cot_all))
+    hot_mem = jnp.take(hot_memory, at, axis=0, mode="clip")
+    hot_cot = jnp.take(cot_hot, at, axis=0, mode="clip")
+
+    recv, hot_mem, hot_cot, _ = lax.optimization_barrier((recv, hot_mem, hot_cot, spill))
     block = sds((136, 512), F32)
     parts = call(
         cold_kernel,
         (block,) * 4,
         (SM,),
-        (pos, recv, swap_core(recv), hot.reshape(4, 8, 512), spill.reshape(2, 8, 512)),
-        (pltpu.VMEM((2048, 512), BF16), pltpu.VMEM((3, 136, 512), F32), pltpu.SemaphoreType.DMA((6,))),
-        (VM, ANY, ANY, ANY),
+        (pos, recv, swap_core(recv), hot.reshape(12, 8, 512), spill.reshape(2, 8, 512)),
     )
     parts = [parts[0]] + [shift_x(parts[d], d) for d in (1, 2, 3)]
     agg = call(
@@ -379,31 +386,40 @@
         (pltpu.VMEM((3, 136, 512), F32), pltpu.VMEM((144, 512), BF16), pltpu.SemaphoreType.DMA((4,))),
         ANY,
     )
+    parts = gather_rep(agg)
+    shared = (memory, cot_cold, hot_mem, hot_cot, w_in, w_hid)
+    own = call(
+        functools.partial(update_kernel, (0,), False),
+        (sds((256, 256), F32), sds((8, 128), F32), sds((128, 1024), F32)),
+        (SM,),
+        (pos, parts[0], parts[4], *shared),
+    )
     new_memory, grad = call(
-        update_kernel,
+        functools.partial(update_kernel, (3, 2, 1), True),
         (sds((1024, 256), F32), sds((32, 8, 512), F32)),
         (SM,),
-        (pos, *gather_rep(agg), mem_all, cot_all, w_in, w_hid),
-        (pltpu.VMEM((1152, 512), BF16), pltpu.VMEM((128, 1024), F32), pltpu.VMEM((128, 256), F32)),
+        (pos, parts[3], parts[7], parts[2], parts[6], parts[1], parts[5], *shared, *own),
+        (pltpu.VMEM((128, 1024), F32),),
     )
 
     grad = lax.all_to_all(grad, "node", split_axis=0, concat_axis=0, tiled=True)
     grad, hot_new = call(piece_kernel, (sds((32, 8, 384), F32), sds((32, 8, 128), F32)), (), (grad,))
     grad = lax.all_to_all(grad, "node", split_axis=0, concat_axis=0, tiled=True)
-    hot_parts = gather_rep(hot_new)
-    grad, hot_parts = lax.optimization_barrier((grad, hot_parts))
     new_hot = call(
         hot_place_kernel,
         sds((1024, 256), F32),
         (SM,),
-        (pos, hot_ids[None, :], *hot_parts),
+        (pos, hot_ids[None, :], *gather_rep(hot_new)),
         (pltpu.VMEM((8, 128, 256), F32),),
     )
+    grad, new_hot = lax.optimization_barrier((grad, new_hot))
     grad_in, grad_hid = call(
         place_kernel,
         (sds((512, 768), F32), sds((256, 768), F32)),
         (SM,),
         (pos, *gather_rep(grad[0:24])),
+        (pltpu.VMEM((768, 768), F32), pltpu.SemaphoreType.DMA((16,))),
+        (ANY, ANY),
     )
     return (new_memory, new_hot, grad_in, grad_hid)
 

time: 162 us -> 159 us (0.981)
  waiting for transfers between devices: 42.5 us -> 53.9 us
  starting transfers between devices: 66.7 us -> 58.8 us
  local copies, waits for them, and re-layouts: 6.33 us -> 2.8 us
    ppermute x14, starting transfers between devices: 33.3 us -> 23.4 us  [swap_core(): return lax.ppermute(v, 'rep', [(k, k ^ 1) for k in range(8)])]
    ppermute x12, waiting for transfers between devices: 17.6 us -> 25.6 us  [shift_x(): return lax.ppermute(v, 'rep', [(k, (k + 2 * d) % 8) for k in range(8)])]
    ppermute x12, starting transfers between devices: 11.6 us -> 13.9 us  [shift_x(): return lax.ppermute(v, 'rep', [(k, (k + 2 * d) % 8) for k in range(8)])]
    unnamed x20 -> x14, local copies, waits for them, and re-layouts: 2.07 us -> 0.04 us
    ppermute x14, waiting for transfers between devices: 3.68 us -> 5.46 us  [swap_core(): return lax.ppermute(v, 'rep', [(k, k ^ 1) for k in range(8)])]
    ppermute x1, waiting for transfers between devices: 21.2 us -> 22.9 us  [on_device(): spill = lax.ppermute(spill, 'node', [(k, (k + 1) % 32) for k in range(32)])]
    pallas_call x7 -> x8, Pallas kernels: 24.6 us -> 23.4 us  [call(): pl.pallas_call(body, out_shape=out_shape, in_specs=list(places) + [VM] *...]
  transfers between devices with their start and end apart: 29 -> 29, of which waited for: 10 -> 11; matrix products, arithmetic and copies ran while one was open for 4% -> 2% of each run, Pallas kernels for 2% -> 4%
where the time goes in v4:
time: 159 us; the launch traced here: 158 us
  starting transfers between devices  58.8 us (37%)
  waiting for transfers between devices  53.9 us (34%)
  Pallas kernels  23.4 us (15%)
  blocking collectives  18.2 us (11%)
  local copies, waits for them, and re-layouts  2.8 us (2%)
    ppermute x12, waiting for transfers between devices, shift_x(): return lax.ppermute(v, 'rep', [(k, (k + 2 * d) % 8) for k in range(8)])  25.6 us
    ppermute x14, starting transfers between devices, swap_core(): return lax.ppermute(v, 'rep', [(k, k ^ 1) for k in range(8)])  23.4 us
    pallas_call x8, Pallas kernels, call(): pl.pallas_call(body, out_shape=out_shape, in_specs=list(places) + [VM] *...  23.4 us
    ppermute x1, waiting for transfers between devices, on_device(): spill = lax.ppermute(spill, 'node', [(k, (k + 1) % 32) for k in range(32)])  22.9 us
    all_to_all x1, blocking collectives, on_device(): grad = lax.all_to_all(grad, 'node', split_axis=0, concat_axis=0, tiled=True)  18.2 us
    ppermute x12, starting transfers between devices, shift_x(): return lax.ppermute(v, 'rep', [(k, (k + 2 * d) % 8) for k in range(8)])  13.9 us
    all_to_all x1, starting transfers between devices, on_device(): recv = lax.all_to_all(send, 'node', split_axis=0, concat_axis=0, tiled=True)  12.2 us
    all_to_all x1, starting transfers between devices, on_device(): grad = lax.all_to_all(grad, 'node', split_axis=0, concat_axis=0, tiled=True)  7.68 us
  transfers between devices with their start and end apart: 29, of which 11 were waited for; matrix products, arithmetic and copies ran while one was open for 2% of the time, Pallas kernels for 4%

profile of v4, /device:TPU:1, one launch (start us, length us, event | category | flops | bytes accessed | tf_op | source)
XLA Modules:
  0.0 158.4 jit_solution(10707947590237811032)
XLA Ops:
  0.6 6.3 %shard_map.192 = (bf16[32,144,128]{2,1,0:T(8,128)(2,1)}, f32[96,512]{1,0:T(8,128)}) custom-call(s32[1]{0:T(128)} %bitcast.3.pos, f32[1024,256]{1,0:T(8,128)} %refs_6_.3, bf16[1024,128]{1,0:T(8,128)(2,1)} %edge_h.1, bf16[512,512]{1,0:T(8,128)(2,1)} %w_h.1, s32[1,1024]{1,0:T(1,128)} %bitcast.17, s32[1,1024]{1,0:T(1,128)} %bitcast.18, s32[1,1024]{1,0:T(1,128)} %bitcast.19, ...), custom_call_target="tpu_custom_call" | custom-call | tf_op jit(solution)/shard_map/pallas_call | solution.py:34
  7.0 0.0 copy-start.6
  7.0 0.0 copy-start.4
  7.0 0.0 copy-start.5
  7.0 12.2 %all-to-all-start = ((bf16[32,144,128]{2,1,0:T(8,128)(2,1)}), bf16[32,144,128]{2,1,0:T(8,128)(2,1)S(1)}, u32[]{:S(2)}, u32[]{:S(2)}) async-start(bf16[32,144,128]{2,1,0:T(8,128)(2,1)} %get-tuple-element.24), calls=%async_computation | async-start | bytes 2359296 | tf_op jit(solution)/shard_map/all_to_all | solution.py:361
  19.2 1.0 collective-permute-start
  20.3 0.2 select_reduce_fusion
  20.5 0.9 collective-permute-done
  21.4 1.6 %collective-permute-start.1 = (f32[16,512]{1,0:T(8,128)S(1)}, f32[16,512]{1,0:T(8,128)S(1)}, u32[]{:S(2)}, u32[]{:S(2)}) collective-permute-start(f32[16,512]{1,0:T(8,128)S(1)} %constant_dynamic-slice_fusion), channel_id=1, source_target_pairs={{0,8},{8,16},{16,24},{24,32},{32,40},{40,48},{48,56},{56,64},{64,7... | collective-permute-start | bytes 98312 | tf_op jit(solution)/shard_map/ppermute | solution.py:365
  23.0 0.8 gather_fusion.1
  23.7 2.0 %gather_fusion = f32[128,256]{1,0:T(8,128)S(1)} fusion(f32[1024,256]{1,0:T(8,128)} %param.18, s32[1024]{0:T(1024)S(1)} %pad_clamp_fusion), kind=kCustom, calls=%fused_computation | custom fusion | bytes 262656 | tf_op jit(solution)/shard_map/jit(_take)/gather | solution.py:369
  25.7 22.9 %collective-permute-done.1 = f32[16,512]{1,0:T(8,128)S(1)} collective-permute-done((f32[16,512]{1,0:T(8,128)S(1)}, f32[16,512]{1,0:T(8,128)S(1)}, u32[]{:S(2)}, u32[]{:S(2)}) %collective-permute-start.1) | collective-permute-done | bytes 32800 | tf_op jit(solution)/shard_map/ppermute | solution.py:365
  48.6 0.0 all-to-all-done.own
  48.6 3.6 %collective-permute-start.2 = (bf16[32,144,128]{2,1,0:T(8,128)(2,1)S(1)}, bf16[32,144,128]{2,1,0:T(8,128)(2,1)S(1)}, u32[]{:S(2)}, u32[]{:S(2)}) collective-permute-start(bf16[32,144,128]{2,1,0:T(8,128)(2,1)S(1)} %all-to-all-done.own), channel_id=1, source_target_pairs={{0,1},{1,0},{2,3},{3,2},{4,5},{5,4},{6,7},{7,6},{8,9},{9,8},{10,11... | collective-permute-start | bytes 3538952 | tf_op jit(solution)/shard_map/ppermute | solution.py:303
  52.2 0.1 pad_add_fusion.pos
  52.2 2.4 %collective-permute-done.2.peer = bf16[32,144,128]{2,1,0:T(8,128)(2,1)S(1)} collective-permute-done((bf16[32,144,128]{2,1,0:T(8,128)(2,1)S(1)}, bf16[32,144,128]{2,1,0:T(8,128)(2,1)S(1)}, u32[]{:S(2)}, u32[]{:S(2)}) %collective-permute-start.2) | collective-permute-done | bytes 1179680 | tf_op jit(solution)/shard_map/ppermute | solution.py:303
  54.6 2.4 %shard_map.193 = (f32[136,512]{1,0:T(8,128)S(1)}, f32[136,512]{1,0:T(8,128)S(1)}, f32[136,512]{1,0:T(8,128)S(1)}, f32[136,512]{1,0:T(8,128)S(1)}) custom-call(s32[3]{0:T(128)S(1)} %pad_add_fusion.pos, bf16[32,144,128]{2,1,0:T(8,128)(2,1)S(1)} %all-to-all-done.own, bf16[32,144,128]{2,1,0:T(8,128)(2,1)S(1)} %collective-permute-done.2.peer, ...), custom_call_target="tpu_custom_call" | custom-call | tf_op jit(solution)/shard_map/pallas_call | solution.py:34
  57.0 0.0 copy-start
  57.0 1.3 collective-permute-start.3
  58.3 2.5 %collective-permute-start.4 = (f32[136,512]{1,0:T(8,128)S(1)}, f32[136,512]{1,0:T(8,128)S(1)}, u32[]{:S(2)}, u32[]{:S(2)}) collective-permute-start(f32[136,512]{1,0:T(8,128)S(1)} %get-tuple-element.28), channel_id=1, source_target_pairs={{0,4},{1,5},{2,6},{3,7},{4,0},{5,1},{6,2},{7,3},{8,12},{9,13},{10,... | collective-permute-start | bytes 835592 | tf_op jit(solution)/shard_map/ppermute | solution.py:307
  60.8 1.1 collective-permute-start.5
  61.9 4.3 %collective-permute-done.3.p1_h = f32[136,512]{1,0:T(8,128)S(1)} collective-permute-done((f32[136,512]{1,0:T(8,128)S(1)}, f32[136,512]{1,0:T(8,128)S(1)}, u32[]{:S(2)}, u32[]{:S(2)}) %collective-permute-start.3) | collective-permute-done | bytes 278560 | tf_op jit(solution)/shard_map/ppermute | solution.py:307
  66.2 7.0 %collective-permute-done.4.p2_h = f32[136,512]{1,0:T(8,128)S(1)} collective-permute-done((f32[136,512]{1,0:T(8,128)S(1)}, f32[136,512]{1,0:T(8,128)S(1)}, u32[]{:S(2)}, u32[]{:S(2)}) %collective-permute-start.4) | collective-permute-done | bytes 278560 | tf_op jit(solution)/shard_map/ppermute | solution.py:307
  73.1 0.0 collective-permute-done.5.p3_h
  73.1 0.6 shard_map.194.refs_0_
  73.7 1.1 collective-permute-start.10
  74.8 2.8 %collective-permute-start.8 = (bf16[144,512]{1,0:T(8,128)(2,1)S(1)}, bf16[144,512]{1,0:T(8,128)(2,1)S(1)}, u32[]{:S(2)}, u32[]{:S(2)}) collective-permute-start(bf16[144,512]{1,0:T(8,128)(2,1)S(1)} %shard_map.194.refs_0_), channel_id=1, source_target_pairs={{0,4},{1,5},{2,6},{3,7},{4,0},{5,1},{6,2},{7,3},{8,12},{9,13},{10,... | collective-permute-start | bytes 442376 | tf_op jit(solution)/shard_map/ppermute | solution.py:307
  77.7 0.3 collective-permute-start.6
  78.0 2.3 %collective-permute-start.12 = (bf16[144,512]{1,0:T(8,128)(2,1)S(1)}, bf16[144,512]{1,0:T(8,128)(2,1)S(1)}, u32[]{:S(2)}, u32[]{:S(2)}) collective-permute-start(bf16[144,512]{1,0:T(8,128)(2,1)S(1)} %shard_map.194.refs_0_), channel_id=1, source_target_pairs={{0,1},{1,0},{2,3},{3,2},{4,5},{5,4},{6,7},{7,6},{8,9},{9,8},{10,11... | collective-permute-start | bytes 442376 | tf_op jit(solution)/shard_map/ppermute | solution.py:303
  80.3 1.1 collective-permute-start.11
  81.3 2.9 %collective-permute-done.8.refs_2_ = bf16[144,512]{1,0:T(8,128)(2,1)S(1)} collective-permute-done((bf16[144,512]{1,0:T(8,128)(2,1)S(1)}, bf16[144,512]{1,0:T(8,128)(2,1)S(1)}, u32[]{:S(2)}, u32[]{:S(2)}) %collective-permute-start.8) | collective-permute-done | bytes 147488 | tf_op jit(solution)/shard_map/ppermute | solution.py:307
  84.3 1.3 collective-permute-start.9
  85.6 0.0 collective-permute-done.6.refs_0_
  85.6 0.0 collective-permute-start.7
  85.7 2.1 %shard_map.195 = (f32[256,256]{1,0:T(8,128)S(1)}, f32[8,128]{1,0:T(8,128)S(1)}, f32[128,1024]{1,0:T(8,128)S(1)}) custom-call(s32[3]{0:T(128)S(1)} %pad_add_fusion.pos, bf16[144,512]{1,0:T(8,128)(2,1)S(1)} %shard_map.194.refs_0_, bf16[144,512]{1,0:T(8,128)(2,1)S(1)} %collective-permute-done.12.refs_1_, f32[1024,256]{1,0:T(8,128)S(1)} %copy-done, ...), custom_call_target="tpu_custom_call" | custom-call | tf_op jit(solution)/shard_map/pallas_call | solution.py:34
  87.8 0.0 collective-permute-done.7.refs_1_
  87.8 5.2 %shard_map.196 = (f32[1024,256]{1,0:T(8,128)}, f32[32,8,512]{2,1,0:T(8,128)S(1)}) custom-call(s32[3]{0:T(128)S(1)} %pad_add_fusion.pos, bf16[144,512]{1,0:T(8,128)(2,1)S(1)} %collective-permute-done.6.refs_0_, bf16[144,512]{1,0:T(8,128)(2,1)S(1)} %collective-permute-done.7.refs_1_, bf16[144,512]{1,0:T(8,128)(2,1)S(1)} %collective-permute-done.8.refs_2_, ...), custom_call_target="tpu_custom_call" | custom-call | tf_op jit(solution)/shard_map/pallas_call | solution.py:34
  93.1 18.2 %all_to_all.15.parts = f32[32,8,512]{2,1,0:T(8,128)S(1)} all-to-all(f32[32,8,512]{2,1,0:T(8,128)S(1)} %get-tuple-element.37), channel_id=1, replica_groups=mesh['node'=32,'rep'=8] {'node'}, dimensions={0} | all-to-all | bytes 1048576 | tf_op jit(solution)/shard_map/all_to_all | solution.py:405
  111.2 0.8 shard_map.197
  112.0 7.7 %all-to-all-start.2 = ((f32[32,8,384]{2,1,0:T(8,128)}), f32[32,8,384]{2,1,0:T(8,128)S(1)}, u32[]{:S(2)}, u32[]{:S(2)}) async-start(f32[32,8,384]{2,1,0:T(8,128)} %get-tuple-element.38), calls=%async_computation.2 | async-start | bytes 786432 | tf_op jit(solution)/shard_map/all_to_all | solution.py:407
  119.7 2.4 %collective-permute-start.15 = (f32[32,8,128]{2,1,0:T(8,128)S(1)}, f32[32,8,128]{2,1,0:T(8,128)S(1)}, u32[]{:S(2)}, u32[]{:S(2)}) collective-permute-start(f32[32,8,128]{2,1,0:T(8,128)S(1)} %get-tuple-element.39.a0), channel_id=1, source_target_pairs={{0,6},{1,7},{2,0},{3,1},{4,2},{5,3},{6,4},{7,5},{8,14},{9,15},{10,... | collective-permute-start | bytes 393224 | tf_op jit(solution)/shard_map/ppermute | solution.py:307
  122.1 0.7 collective-permute-start.14
  122.9 1.8 %collective-permute-start.16 = (f32[32,8,128]{2,1,0:T(8,128)S(1)}, f32[32,8,128]{2,1,0:T(8,128)S(1)}, u32[]{:S(2)}, u32[]{:S(2)}) collective-permute-start(f32[32,8,128]{2,1,0:T(8,128)S(1)} %get-tuple-element.39.a0), channel_id=1, source_target_pairs={{0,1},{1,0},{2,3},{3,2},{4,5},{5,4},{6,7},{7,6},{8,9},{9,8},{10,11... | collective-permute-start | bytes 393224 | tf_op jit(solution)/shard_map/ppermute | solution.py:303
  124.6 1.2 collective-permute-done.15.a3
  125.9 2.8 %collective-permute-start.19 = (f32[32,8,128]{2,1,0:T(8,128)S(1)}, f32[32,8,128]{2,1,0:T(8,128)S(1)}, u32[]{:S(2)}, u32[]{:S(2)}) collective-permute-start(f32[32,8,128]{2,1,0:T(8,128)S(1)} %collective-permute-done.15.a3), channel_id=1, source_target_pairs={{0,1},{1,0},{2,3},{3,2},{4,5},{5,4},{6,7},{7,6},{8,9},{9,8},{10,11... | collective-permute-start | bytes 393224 | tf_op jit(solution)/shard_map/ppermute | solution.py:303
  128.7 2.3 %collective-permute-start.18 = (f32[32,8,128]{2,1,0:T(8,128)S(1)}, f32[32,8,128]{2,1,0:T(8,128)S(1)}, u32[]{:S(2)}, u32[]{:S(2)}) collective-permute-start(f32[32,8,128]{2,1,0:T(8,128)S(1)} %collective-permute-done.14.a2), channel_id=1, source_target_pairs={{0,1},{1,0},{2,3},{3,2},{4,5},{5,4},{6,7},{7,6},{8,9},{9,8},{10,11... | collective-permute-start | bytes 393224 | tf_op jit(solution)/shard_map/ppermute | solution.py:303
  131.0 1.3 collective-permute-start.17
  132.3 0.0 collective-permute-done.18.b2
  132.3 1.0 collective-permute-done.17.b1
  133.3 3.9 %shard_map.198 = f32[1024,256]{1,0:T(8,128)} custom-call(s32[3]{0:T(128)S(1)} %pad_add_fusion.pos, s32[1,1024]{1,0:T(1,128)S(1)} %bitcast.16, f32[32,8,128]{2,1,0:T(8,128)S(1)} %get-tuple-element.39.a0, f32[32,8,128]{2,1,0:T(8,128)S(1)} %collective-permute-done.13.a1, f32[32,8,128]{2,1,0:T(8,128)S(1)} %collective-permute-done.14.a2, ...), custom_call_target="tpu_custom_call" | custom-call | tf_op jit(solution)/shard_map/pallas_call | solution.py:34
  137.2 0.0 all-to-all-done.2
  137.2 0.5 collective-permute-start.22
  137.7 0.6 collective-permute-start.21
  138.3 0.6 collective-permute-start.20
  138.9 1.2 collective-permute-start.23
  140.1 5.4 %collective-permute-done.22.a3 = f32[24,8,384]{2,1,0:T(8,128)S(1)} collective-permute-done((f32[24,8,384]{2,1,0:T(8,128)S(1)}, f32[24,8,384]{2,1,0:T(8,128)S(1)}, u32[]{:S(2)}, u32[]{:S(2)}) %collective-permute-start.22) | collective-permute-done | bytes 294944 | tf_op jit(solution)/shard_map/ppermute | solution.py:307
  145.5 2.0 %collective-permute-start.26 = (f32[24,8,384]{2,1,0:T(8,128)S(1)}, f32[24,8,384]{2,1,0:T(8,128)S(1)}, u32[]{:S(2)}, u32[]{:S(2)}) collective-permute-start(f32[24,8,384]{2,1,0:T(8,128)S(1)} %collective-permute-done.22.a3), channel_id=1, source_target_pairs={{0,1},{1,0},{2,3},{3,2},{4,5},{5,4},{6,7},{7,6},{8,9},{9,8},{10,11... | collective-permute-start | bytes 884744 | tf_op jit(solution)/shard_map/ppermute | solution.py:303
  147.5 2.1 %collective-permute-start.25 = (f32[24,8,384]{2,1,0:T(8,128)S(1)}, f32[24,8,384]{2,1,0:T(8,128)S(1)}, u32[]{:S(2)}, u32[]{:S(2)}) collective-permute-start(f32[24,8,384]{2,1,0:T(8,128)S(1)} %collective-permute-done.21.a2), channel_id=1, source_target_pairs={{0,1},{1,0},{2,3},{3,2},{4,5},{5,4},{6,7},{7,6},{8,9},{9,8},{10,11... | collective-permute-start | bytes 884744 | tf_op jit(solution)/shard_map/ppermute | solution.py:303
  149.6 4.8 %collective-permute-done.20.a1 = f32[24,8,384]{2,1,0:T(8,128)S(1)} collective-permute-done((f32[24,8,384]{2,1,0:T(8,128)S(1)}, f32[24,8,384]{2,1,0:T(8,128)S(1)}, u32[]{:S(2)}, u32[]{:S(2)}) %collective-permute-start.20) | collective-permute-done | bytes 294944 | tf_op jit(solution)/shard_map/ppermute | solution.py:307
  154.4 0.5 collective-permute-start.24
  154.9 0.0 collective-permute-done.23.b0
  154.9 0.0 collective-permute-done.26.b3
  154.9 1.2 collective-permute-done.24.b1
  156.1 2.1 %shard_map.199 = (f32[512,768]{1,0:T(8,128)}, f32[256,768]{1,0:T(8,128)}) custom-call(s32[3]{0:T(128)S(1)} %pad_add_fusion.pos, f32[24,8,384]{2,1,0:T(8,128)S(1)} %slice.3.a0, f32[24,8,384]{2,1,0:T(8,128)S(1)} %collective-permute-done.20.a1, f32[24,8,384]{2,1,0:T(8,128)S(1)} %collective-permute-done.21.a2, f32[24,8,384]{2,1,0:T(8,128)S(1)} %collective-permute-done.22.a3, ...), custom_call_target="tpu_custom_call" | custom-call | tf_op jit(solution)/shard_map/pallas_call | solution.py:34
  (26 shorter events, 0.1 us)
Async XLA Ops:
  7.0 12.2 %copy-start.6 = (f32[96,512]{1,0:T(8,128)S(1)}, f32[96,512]{1,0:T(8,128)}, u32[]{:S(2)}) copy-start(f32[96,512]{1,0:T(8,128)} %get-tuple-element.25) | copy-start | bytes 589828
  7.0 13.3 %copy-start.4 = (s32[1024]{0:T(1024)S(1)}, s32[1024]{0:T(1024)}, u32[]{:S(2)}) copy-start(s32[1024]{0:T(1024)} %param.27) | copy-start | bytes 12292
  7.0 16.0 %copy-start.5 = (f32[1024,256]{1,0:T(8,128)S(1)}, f32[1024,256]{1,0:T(8,128)}, u32[]{:S(2)}) copy-start(f32[1024,256]{1,0:T(8,128)} %param.20) | copy-start | bytes 3145732
  7.0 41.6 %all-to-all-start = ((bf16[32,144,128]{2,1,0:T(8,128)(2,1)}), bf16[32,144,128]{2,1,0:T(8,128)(2,1)S(1)}, u32[]{:S(2)}, u32[]{:S(2)}) async-start(bf16[32,144,128]{2,1,0:T(8,128)(2,1)} %get-tuple-element.24), calls=%async_computation | async-start | bytes 2359296 | tf_op jit(solution)/shard_map/all_to_all | solution.py:361
  19.2 2.1 %collective-permute-start = (f32[96,512]{1,0:T(8,128)S(1)}, f32[96,512]{1,0:T(8,128)S(1)}, u32[]{:S(2)}, u32[]{:S(2)}) collective-permute-start(f32[96,512]{1,0:T(8,128)S(1)} %copy-done.6), channel_id=1, source_target_pairs={{0,1},{1,0},{2,3},{3,2},{4,5},{5,4},{6,7},{7,6},{8,9},{9,8},{10,11... | collective-permute-start | bytes 589832 | tf_op jit(solution)/shard_map/ppermute | solution.py:303
  21.4 27.2 %collective-permute-start.1 = (f32[16,512]{1,0:T(8,128)S(1)}, f32[16,512]{1,0:T(8,128)S(1)}, u32[]{:S(2)}, u32[]{:S(2)}) collective-permute-start(f32[16,512]{1,0:T(8,128)S(1)} %constant_dynamic-slice_fusion), channel_id=1, source_target_pairs={{0,8},{8,16},{16,24},{24,32},{32,40},{40,48},{48,56},{56,64},{64,7... | collective-permute-start | bytes 98312 | tf_op jit(solution)/shard_map/ppermute | solution.py:365
  48.6 6.1 %collective-permute-start.2 = (bf16[32,144,128]{2,1,0:T(8,128)(2,1)S(1)}, bf16[32,144,128]{2,1,0:T(8,128)(2,1)S(1)}, u32[]{:S(2)}, u32[]{:S(2)}) collective-permute-start(bf16[32,144,128]{2,1,0:T(8,128)(2,1)S(1)} %all-to-all-done.own), channel_id=1, source_target_pairs={{0,1},{1,0},{2,3},{3,2},{4,5},{5,4},{6,7},{7,6},{8,9},{9,8},{10,11... | collective-permute-start | bytes 3538952 | tf_op jit(solution)/shard_map/ppermute | solution.py:303
  54.6 31.0 %copy-start.1 = (f32[1024,256]{1,0:T(8,128)S(1)}, f32[1024,256]{1,0:T(8,128)}, u32[]{:S(2)}) copy-start(f32[1024,256]{1,0:T(8,128)} %refs_7_.3) | copy-start | bytes 3145732
  54.6 31.0 %copy-start.2 = (bf16[512,768]{1,0:T(8,128)(2,1)S(1)}, bf16[512,768]{1,0:T(8,128)(2,1)}, u32[]{:S(2)}) copy-start(bf16[512,768]{1,0:T(8,128)(2,1)} %refs_10_.1) | copy-start | bytes 2359300
  54.6 31.0 %copy-start.3 = (bf16[256,768]{1,0:T(8,128)(2,1)S(1)}, bf16[256,768]{1,0:T(8,128)(2,1)}, u32[]{:S(2)}) copy-start(bf16[256,768]{1,0:T(8,128)(2,1)} %refs_11_.1) | copy-start | bytes 1179652
  57.0 28.6 %copy-start = (f32[1024,256]{1,0:T(8,128)S(1)}, f32[1024,256]{1,0:T(8,128)}, u32[]{:S(2)}) copy-start(f32[1024,256]{1,0:T(8,128)} %refs_6_.3) | copy-start | bytes 3145732
  57.0 9.2 %collective-permute-start.3 = (f32[136,512]{1,0:T(8,128)S(1)}, f32[136,512]{1,0:T(8,128)S(1)}, u32[]{:S(2)}, u32[]{:S(2)}) collective-permute-start(f32[136,512]{1,0:T(8,128)S(1)} %get-tuple-element.27), channel_id=1, source_target_pairs={{0,2},{1,3},{2,4},{3,5},{4,6},{5,7},{6,0},{7,1},{8,10},{9,11},{10,... | collective-permute-start | bytes 835592 | tf_op jit(solution)/shard_map/ppermute | solution.py:307
  58.3 14.8 %collective-permute-start.4 = (f32[136,512]{1,0:T(8,128)S(1)}, f32[136,512]{1,0:T(8,128)S(1)}, u32[]{:S(2)}, u32[]{:S(2)}) collective-permute-start(f32[136,512]{1,0:T(8,128)S(1)} %get-tuple-element.28), channel_id=1, source_target_pairs={{0,4},{1,5},{2,6},{3,7},{4,0},{5,1},{6,2},{7,3},{8,12},{9,13},{10,... | collective-permute-start | bytes 835592 | tf_op jit(solution)/shard_map/ppermute | solution.py:307
  60.8 12.4 %collective-permute-start.5 = (f32[136,512]{1,0:T(8,128)S(1)}, f32[136,512]{1,0:T(8,128)S(1)}, u32[]{:S(2)}, u32[]{:S(2)}) collective-permute-start(f32[136,512]{1,0:T(8,128)S(1)} %get-tuple-element.29), channel_id=1, source_target_pairs={{0,6},{1,7},{2,0},{3,1},{4,2},{5,3},{6,4},{7,5},{8,14},{9,15},{10,... | collective-permute-start | bytes 835592 | tf_op jit(solution)/shard_map/ppermute | solution.py:307
  73.7 6.6 %collective-permute-start.10 = (bf16[144,512]{1,0:T(8,128)(2,1)S(1)}, bf16[144,512]{1,0:T(8,128)(2,1)S(1)}, u32[]{:S(2)}, u32[]{:S(2)}) collective-permute-start(bf16[144,512]{1,0:T(8,128)(2,1)S(1)} %shard_map.194.refs_0_), channel_id=1, source_target_pairs={{0,2},{1,3},{2,4},{3,5},{4,6},{5,7},{6,0},{7,1},{8,10},{9,11},{10,... | collective-permute-start | bytes 442376 | tf_op jit(solution)/shard_map/ppermute | solution.py:307
  74.8 9.5 %collective-permute-start.8 = (bf16[144,512]{1,0:T(8,128)(2,1)S(1)}, bf16[144,512]{1,0:T(8,128)(2,1)S(1)}, u32[]{:S(2)}, u32[]{:S(2)}) collective-permute-start(bf16[144,512]{1,0:T(8,128)(2,1)S(1)} %shard_map.194.refs_0_), channel_id=1, source_target_pairs={{0,4},{1,5},{2,6},{3,7},{4,0},{5,1},{6,2},{7,3},{8,12},{9,13},{10,... | collective-permute-start | bytes 442376 | tf_op jit(solution)/shard_map/ppermute | solution.py:307
  77.7 8.0 %collective-permute-start.6 = (bf16[144,512]{1,0:T(8,128)(2,1)S(1)}, bf16[144,512]{1,0:T(8,128)(2,1)S(1)}, u32[]{:S(2)}, u32[]{:S(2)}) collective-permute-start(bf16[144,512]{1,0:T(8,128)(2,1)S(1)} %shard_map.194.refs_0_), channel_id=1, source_target_pairs={{0,6},{1,7},{2,0},{3,1},{4,2},{5,3},{6,4},{7,5},{8,14},{9,15},{10,... | collective-permute-start | bytes 442376 | tf_op jit(solution)/shard_map/ppermute | solution.py:307
  78.0 7.7 %collective-permute-start.12 = (bf16[144,512]{1,0:T(8,128)(2,1)S(1)}, bf16[144,512]{1,0:T(8,128)(2,1)S(1)}, u32[]{:S(2)}, u32[]{:S(2)}) collective-permute-start(bf16[144,512]{1,0:T(8,128)(2,1)S(1)} %shard_map.194.refs_0_), channel_id=1, source_target_pairs={{0,1},{1,0},{2,3},{3,2},{4,5},{5,4},{6,7},{7,6},{8,9},{9,8},{10,11... | collective-permute-start | bytes 442376 | tf_op jit(solution)/shard_map/ppermute | solution.py:303
  80.3 7.5 %collective-permute-start.11 = (bf16[144,512]{1,0:T(8,128)(2,1)S(1)}, bf16[144,512]{1,0:T(8,128)(2,1)S(1)}, u32[]{:S(2)}, u32[]{:S(2)}) collective-permute-start(bf16[144,512]{1,0:T(8,128)(2,1)S(1)} %collective-permute-done.10.refs_4_), channel_id=1, source_target_pairs={{0,1},{1,0},{2,3},{3,2},{4,5},{5,4},{6,7},{7,6},{8,9},{9,8},{10,11... | collective-permute-start | bytes 442376 | tf_op jit(solution)/shard_map/ppermute | solution.py:303
  84.3 3.5 %collective-permute-start.9 = (bf16[144,512]{1,0:T(8,128)(2,1)S(1)}, bf16[144,512]{1,0:T(8,128)(2,1)S(1)}, u32[]{:S(2)}, u32[]{:S(2)}) collective-permute-start(bf16[144,512]{1,0:T(8,128)(2,1)S(1)} %collective-permute-done.8.refs_2_), channel_id=1, source_target_pairs={{0,1},{1,0},{2,3},{3,2},{4,5},{5,4},{6,7},{7,6},{8,9},{9,8},{10,11... | collective-permute-start | bytes 442376 | tf_op jit(solution)/shard_map/ppermute | solution.py:303
  85.6 2.2 %collective-permute-start.7 = (bf16[144,512]{1,0:T(8,128)(2,1)S(1)}, bf16[144,512]{1,0:T(8,128)(2,1)S(1)}, u32[]{:S(2)}, u32[]{:S(2)}) collective-permute-start(bf16[144,512]{1,0:T(8,128)(2,1)S(1)} %collective-permute-done.6.refs_0_), channel_id=1, source_target_pairs={{0,1},{1,0},{2,3},{3,2},{4,5},{5,4},{6,7},{7,6},{8,9},{9,8},{10,11... | collective-permute-start | bytes 442376 | tf_op jit(solution)/shard_map/ppermute | solution.py:303
  112.0 25.1 %all-to-all-start.2 = ((f32[32,8,384]{2,1,0:T(8,128)}), f32[32,8,384]{2,1,0:T(8,128)S(1)}, u32[]{:S(2)}, u32[]{:S(2)}) async-start(f32[32,8,384]{2,1,0:T(8,128)} %get-tuple-element.38), calls=%async_computation.2 | async-start | bytes 786432 | tf_op jit(solution)/shard_map/all_to_all | solution.py:407
  119.7 6.1 %collective-permute-start.15 = (f32[32,8,128]{2,1,0:T(8,128)S(1)}, f32[32,8,128]{2,1,0:T(8,128)S(1)}, u32[]{:S(2)}, u32[]{:S(2)}) collective-permute-start(f32[32,8,128]{2,1,0:T(8,128)S(1)} %get-tuple-element.39.a0), channel_id=1, source_target_pairs={{0,6},{1,7},{2,0},{3,1},{4,2},{5,3},{6,4},{7,5},{8,14},{9,15},{10,... | collective-permute-start | bytes 393224 | tf_op jit(solution)/shard_map/ppermute | solution.py:307
  122.1 6.6 %collective-permute-start.14 = (f32[32,8,128]{2,1,0:T(8,128)S(1)}, f32[32,8,128]{2,1,0:T(8,128)S(1)}, u32[]{:S(2)}, u32[]{:S(2)}) collective-permute-start(f32[32,8,128]{2,1,0:T(8,128)S(1)} %get-tuple-element.39.a0), channel_id=1, source_target_pairs={{0,4},{1,5},{2,6},{3,7},{4,0},{5,1},{6,2},{7,3},{8,12},{9,13},{10,... | collective-permute-start | bytes 393224 | tf_op jit(solution)/shard_map/ppermute | solution.py:307
  122.9 8.1 %collective-permute-start.13 = (f32[32,8,128]{2,1,0:T(8,128)S(1)}, f32[32,8,128]{2,1,0:T(8,128)S(1)}, u32[]{:S(2)}, u32[]{:S(2)}) collective-permute-start(f32[32,8,128]{2,1,0:T(8,128)S(1)} %get-tuple-element.39.a0), channel_id=1, source_target_pairs={{0,2},{1,3},{2,4},{3,5},{4,6},{5,7},{6,0},{7,1},{8,10},{9,11},{10,... | collective-permute-start | bytes 393224 | tf_op jit(solution)/shard_map/ppermute | solution.py:307
  122.9 9.5 %collective-permute-start.16 = (f32[32,8,128]{2,1,0:T(8,128)S(1)}, f32[32,8,128]{2,1,0:T(8,128)S(1)}, u32[]{:S(2)}, u32[]{:S(2)}) collective-permute-start(f32[32,8,128]{2,1,0:T(8,128)S(1)} %get-tuple-element.39.a0), channel_id=1, source_target_pairs={{0,1},{1,0},{2,3},{3,2},{4,5},{5,4},{6,7},{7,6},{8,9},{9,8},{10,11... | collective-permute-start | bytes 393224 | tf_op jit(solution)/shard_map/ppermute | solution.py:303
  125.9 6.5 %collective-permute-start.19 = (f32[32,8,128]{2,1,0:T(8,128)S(1)}, f32[32,8,128]{2,1,0:T(8,128)S(1)}, u32[]{:S(2)}, u32[]{:S(2)}) collective-permute-start(f32[32,8,128]{2,1,0:T(8,128)S(1)} %collective-permute-done.15.a3), channel_id=1, source_target_pairs={{0,1},{1,0},{2,3},{3,2},{4,5},{5,4},{6,7},{7,6},{8,9},{9,8},{10,11... | collective-permute-start | bytes 393224 | tf_op jit(solution)/shard_map/ppermute | solution.py:303
  128.7 3.7 %collective-permute-start.18 = (f32[32,8,128]{2,1,0:T(8,128)S(1)}, f32[32,8,128]{2,1,0:T(8,128)S(1)}, u32[]{:S(2)}, u32[]{:S(2)}) collective-permute-start(f32[32,8,128]{2,1,0:T(8,128)S(1)} %collective-permute-done.14.a2), channel_id=1, source_target_pairs={{0,1},{1,0},{2,3},{3,2},{4,5},{5,4},{6,7},{7,6},{8,9},{9,8},{10,11... | collective-permute-start | bytes 393224 | tf_op jit(solution)/shard_map/ppermute | solution.py:303
  131.0 2.3 %collective-permute-start.17 = (f32[32,8,128]{2,1,0:T(8,128)S(1)}, f32[32,8,128]{2,1,0:T(8,128)S(1)}, u32[]{:S(2)}, u32[]{:S(2)}) collective-permute-start(f32[32,8,128]{2,1,0:T(8,128)S(1)} %collective-permute-done.13.a1), channel_id=1, source_target_pairs={{0,1},{1,0},{2,3},{3,2},{4,5},{5,4},{6,7},{7,6},{8,9},{9,8},{10,11... | collective-permute-start | bytes 393224 | tf_op jit(solution)/shard_map/ppermute | solution.py:303
  137.2 8.3 %collective-permute-start.22 = (f32[24,8,384]{2,1,0:T(8,128)S(1)}, f32[24,8,384]{2,1,0:T(8,128)S(1)}, u32[]{:S(2)}, u32[]{:S(2)}) collective-permute-start(f32[24,8,384]{2,1,0:T(8,128)S(1)} %slice.3.a0), channel_id=1, source_target_pairs={{0,6},{1,7},{2,0},{3,1},{4,2},{5,3},{6,4},{7,5},{8,14},{9,15},{10,... | collective-permute-start | bytes 884744 | tf_op jit(solution)/shard_map/ppermute | solution.py:307
  137.7 9.8 %collective-permute-start.21 = (f32[24,8,384]{2,1,0:T(8,128)S(1)}, f32[24,8,384]{2,1,0:T(8,128)S(1)}, u32[]{:S(2)}, u32[]{:S(2)}) collective-permute-start(f32[24,8,384]{2,1,0:T(8,128)S(1)} %slice.3.a0), channel_id=1, source_target_pairs={{0,4},{1,5},{2,6},{3,7},{4,0},{5,1},{6,2},{7,3},{8,12},{9,13},{10,... | collective-permute-start | bytes 884744 | tf_op jit(solution)/shard_map/ppermute | solution.py:307
  138.3 16.1 %collective-permute-start.20 = (f32[24,8,384]{2,1,0:T(8,128)S(1)}, f32[24,8,384]{2,1,0:T(8,128)S(1)}, u32[]{:S(2)}, u32[]{:S(2)}) collective-permute-start(f32[24,8,384]{2,1,0:T(8,128)S(1)} %slice.3.a0), channel_id=1, source_target_pairs={{0,2},{1,3},{2,4},{3,5},{4,6},{5,7},{6,0},{7,1},{8,10},{9,11},{10,... | collective-permute-start | bytes 884744 | tf_op jit(solution)/shard_map/ppermute | solution.py:307
  138.9 16.0 %collective-permute-start.23 = (f32[24,8,384]{2,1,0:T(8,128)S(1)}, f32[24,8,384]{2,1,0:T(8,128)S(1)}, u32[]{:S(2)}, u32[]{:S(2)}) collective-permute-start(f32[24,8,384]{2,1,0:T(8,128)S(1)} %slice.3.a0), channel_id=1, source_target_pairs={{0,1},{1,0},{2,3},{3,2},{4,5},{5,4},{6,7},{7,6},{8,9},{9,8},{10,11... | collective-permute-start | bytes 884744 | tf_op jit(solution)/shard_map/ppermute | solution.py:303
  145.5 9.4 %collective-permute-start.26 = (f32[24,8,384]{2,1,0:T(8,128)S(1)}, f32[24,8,384]{2,1,0:T(8,128)S(1)}, u32[]{:S(2)}, u32[]{:S(2)}) collective-permute-start(f32[24,8,384]{2,1,0:T(8,128)S(1)} %collective-permute-done.22.a3), channel_id=1, source_target_pairs={{0,1},{1,0},{2,3},{3,2},{4,5},{5,4},{6,7},{7,6},{8,9},{9,8},{10,11... | collective-permute-start | bytes 884744 | tf_op jit(solution)/shard_map/ppermute | solution.py:303
  147.5 7.4 %collective-permute-start.25 = (f32[24,8,384]{2,1,0:T(8,128)S(1)}, f32[24,8,384]{2,1,0:T(8,128)S(1)}, u32[]{:S(2)}, u32[]{:S(2)}) collective-permute-start(f32[24,8,384]{2,1,0:T(8,128)S(1)} %collective-permute-done.21.a2), channel_id=1, source_target_pairs={{0,1},{1,0},{2,3},{3,2},{4,5},{5,4},{6,7},{7,6},{8,9},{9,8},{10,11... | collective-permute-start | bytes 884744 | tf_op jit(solution)/shard_map/ppermute | solution.py:303
  154.4 1.7 %collective-permute-start.24 = (f32[24,8,384]{2,1,0:T(8,128)S(1)}, f32[24,8,384]{2,1,0:T(8,128)S(1)}, u32[]{:S(2)}, u32[]{:S(2)}) collective-permute-start(f32[24,8,384]{2,1,0:T(8,128)S(1)} %collective-permute-done.20.a1), channel_id=1, source_target_pairs={{0,1},{1,0},{2,3},{3,2},{4,5},{5,4},{6,7},{7,6},{8,9},{9,8},{10,11... | collective-permute-start | bytes 884744 | tf_op jit(solution)/shard_map/ppermute | solution.py:303

commit v5 on v4

--- a/solution.py
+++ b/solution.py
@@ -28,7 +28,7 @@
     return lax.dot_general(a, b, (dims, ((), ())), preferred_element_type=F32)
 
 
-def call(body, out_shape, places, args, scratch=(), out_places=None, mib=48):
+def call(body, out_shape, places, args, scratch=(), out_places=None, mib=48, aliases=None):
     if out_places is None:
         out_places = jax.tree.map(lambda _: VM, out_shape)
     return pl.pallas_call(
@@ -37,6 +37,7 @@
         in_specs=list(places) + [VM] * (len(args) - len(places)),
         out_specs=out_places,
         scratch_shapes=list(scratch),
+        input_output_aliases=aliases or {},
         compiler_params=pltpu.CompilerParams(vmem_limit_bytes=mib * 1024 * 1024),
     )(*args)
 
@@ -213,15 +214,23 @@
         out[h : h + 256, :] = mm(pick, hi) + (mm(pick, mid) + mm(pick, low))
 
 
-def update_kernel(ds, last, pos, *refs):
+def update_kernel(ds, done, pos, *refs):
+    last = len(done) > 0
     parts, refs = refs[: 2 * len(ds)], refs[2 * len(ds) :]
     mem, cot, hot_mem, hot_cot, w_in, w_hid = refs[:6]
+    refs = refs[6:]
     if last:
-        own_new, own_hot, own_acc, new, grad, acc = refs[6:]
-        acc[...] = own_acc[...]
-        new[pl.ds(pl.multiple_of(256 * pos[0], 256), 256), :] = own_new[...]
+        olds, (own_hot, old_acc, new, grad, acc) = refs[: len(done)], refs[len(done) :]
+        for d, old in zip(done, olds):
+            chip = (pos[0] - d + 4) & 3
+            new[pl.ds(pl.multiple_of(256 * chip, 256), 256), :] = old[...]
+    elif 0 in ds:
+        new, hot, acc = refs
+        old_acc = None
     else:
-        new, hot, acc = refs[6:]
+        old_acc, new, acc = refs
+    if old_acc is not None:
+        acc[...] = old_acc[...]
     x, core, rep = pos[0], pos[1], pos[2]
     k, q = iota((512, 128), 0), iota((512, 128), 1)
     sel_a = one_hot((k == 64 * rep + q) & (q < 64))
@@ -244,8 +253,9 @@
             new[at, :] = fresh[0:256, :]
         else:
             new[...] = fresh[0:256, :]
-            own = jnp.where(core == 0, fresh[256:264, :], fresh[272:280, :])
-            hot[...] = jnp.concatenate([own[0:4, 0:128], own[0:4, 128:256]], axis=0)
+            if d == 0:
+                own = jnp.where(core == 0, fresh[256:264, :], fresh[272:280, :])
+                hot[...] = jnp.concatenate([own[0:4, 0:128], own[0:4, 128:256]], axis=0)
         g = jnp.where(live, jnp.concatenate([cot[at, :], hot_cot[hot_at, :]], axis=0), 0.0)
         d_cand = g * (1.0 - update) * (1.0 - cand * cand)
         d_upd = g * (m - cand) * update * (1.0 - update)
@@ -256,7 +266,7 @@
             low = (v - hi.astype(F32)).astype(BF16)
             part = mm(left, hi, ((0,), (0,))) + mm(left, low, ((0,), (0,)))
             cols = slice(256 * j, 256 * j + 256)
-            if i == 0 and not last:
+            if i == 0 and old_acc is None:
                 acc[:, cols] = part
             else:
                 acc[:, cols] += part
@@ -279,22 +289,22 @@
         hot[k] = parts[k, :, 384:512]
 
 
-def place_kernel(pos, a0, a1, a2, a3, b0, b1, b2, b3, g_in, g_hid, both, sems):
-    x, core = pos[0], pos[1]
+def place_kernel(other, pos, a0, a1, a2, a3, *refs):
+    g_in, g_hid, both, sems = refs[-4:]
+    x = pos[0]
+    core = 1 - pos[1] if other else pos[1]
     stores = []
-    for group, c in (((a0, a1, a2, a3), core), ((b0, b1, b2, b3), 1 - core)):
-        for d, part in enumerate(group):
-            block = 2 * ((x - d + 4) & 3) + c
-            k = len(stores)
-            for p in range(24):
-                i, j = p // 2, p % 2
-                both[96 * (k // 2) + 8 * i : 96 * (k // 2) + 8 * i + 8, 384 * j : 384 * j + 384] = part[p]
-            for rows, at, dst in (
-                (64, 96 * (k // 2), g_in.at[pl.ds(pl.multiple_of(block * 64, 64), 64)]),
-                (32, 96 * (k // 2) + 64, g_hid.at[pl.ds(pl.multiple_of(block * 32, 32), 32)]),
-            ):
-                stores.append(pltpu.make_async_copy(both.at[at : at + rows], dst, sems.at[len(stores)]))
-                stores[-1].start()
+    for d, part in enumerate((a0, a1, a2, a3)):
+        block = 2 * ((x - d + 4) & 3) + core
+        for p in range(24):
+            i, j = p // 2, p % 2
+            both[96 * d + 8 * i : 96 * d + 8 * i + 8, 384 * j : 384 * j + 384] = part[p]
+        for rows, at, dst in (
+            (64, 96 * d, g_in.at[pl.ds(pl.multiple_of(block * 64, 64), 64)]),
+            (32, 96 * d + 64, g_hid.at[pl.ds(pl.multiple_of(block * 32, 32), 32)]),
+        ):
+            stores.append(pltpu.make_async_copy(both.at[at : at + rows], dst, sems.at[len(stores)]))
+            stores[-1].start()
     for c in stores:
         c.wait()
 
@@ -386,40 +396,57 @@
         (pltpu.VMEM((3, 136, 512), F32), pltpu.VMEM((144, 512), BF16), pltpu.SemaphoreType.DMA((4,))),
         ANY,
     )
-    parts = gather_rep(agg)
+    near, far, back = [shift_x(agg, d) for d in (1, 2, 3)]
     shared = (memory, cot_cold, hot_mem, hot_cot, w_in, w_hid)
-    own = call(
-        functools.partial(update_kernel, (0,), False),
-        (sds((256, 256), F32), sds((8, 128), F32), sds((128, 1024), F32)),
+    rows, sums = sds((256, 256), F32), sds((128, 1024), F32)
+    new_own, hot_own, acc = call(
+        functools.partial(update_kernel, (0,), ()),
+        (rows, sds((8, 128), F32), sums),
         (SM,),
-        (pos, parts[0], parts[4], *shared),
-    )
+        (pos, agg, swap_core(agg), *shared),
+    )
+    new_near, acc = call(
+        functools.partial(update_kernel, (1,), ()),
+        (rows, sums),
+        (SM,),
+        (pos, near, swap_core(near), *shared, acc),
+    )
+    far, new_near = lax.optimization_barrier((far, new_near))
     new_memory, grad = call(
-        functools.partial(update_kernel, (3, 2, 1), True),
+        functools.partial(update_kernel, (3, 2), (0, 1)),
         (sds((1024, 256), F32), sds((32, 8, 512), F32)),
         (SM,),
-        (pos, parts[3], parts[7], parts[2], parts[6], parts[1], parts[5], *shared, *own),
+        (pos, back, swap_core(back), far, swap_core(far), *shared, new_own, new_near, hot_own, acc),
         (pltpu.VMEM((128, 1024), F32),),
     )
 
     grad = lax.all_to_all(grad, "node", split_axis=0, concat_axis=0, tiled=True)
     grad, hot_new = call(piece_kernel, (sds((32, 8, 384), F32), sds((32, 8, 128), F32)), (), (grad,))
     grad = lax.all_to_all(grad, "node", split_axis=0, concat_axis=0, tiled=True)
+    hot_parts = gather_rep(hot_new)
+    grad, hot_parts = lax.optimization_barrier((grad, hot_parts))
     new_hot = call(
         hot_place_kernel,
         sds((1024, 256), F32),
         (SM,),
-        (pos, hot_ids[None, :], *gather_rep(hot_new)),
+        (pos, hot_ids[None, :], *hot_parts),
         (pltpu.VMEM((8, 128, 256), F32),),
     )
-    grad, new_hot = lax.optimization_barrier((grad, new_hot))
+    own = [grad[0:24]] + [shift_x(grad[0:24], d) for d in (1, 2, 3)]
+    own[2], new_hot = lax.optimization_barrier((own[2], new_hot))
+    places = (pltpu.VMEM((384, 768), F32), pltpu.SemaphoreType.DMA((8,)))
+    grads = (sds((512, 768), F32), sds((256, 768), F32))
+    grads = call(
+        functools.partial(place_kernel, False), grads, (SM,), (pos, *own), places, (ANY, ANY)
+    )
     grad_in, grad_hid = call(
-        place_kernel,
-        (sds((512, 768), F32), sds((256, 768), F32)),
-        (SM,),
-        (pos, *gather_rep(grad[0:24])),
-        (pltpu.VMEM((768, 768), F32), pltpu.SemaphoreType.DMA((16,))),
+        functools.partial(place_kernel, True),
+        tuple(sds(g.shape, F32) for g in grads),
+        (SM, VM, VM, VM, VM, ANY, ANY),
+        (pos, *[swap_core(v) for v in own], *grads),
+        places,
         (ANY, ANY),
+        aliases={5: 0, 6: 1},
     )
     return (new_memory, new_hot, grad_in, grad_hid)
 

time: 159 us -> 155 us (0.975)
  waiting for transfers between devices: 53.9 us -> 43.2 us
  starting transfers between devices: 58.8 us -> 64 us
    ppermute x12, waiting for transfers between devices: 25.6 us -> 15.1 us  [shift_x(): return lax.ppermute(v, 'rep', [(k, (k + 2 * d) % 8) for k in range(8)])]
    ppermute x14, starting transfers between devices: 23.4 us -> 29 us  [swap_core(): return lax.ppermute(v, 'rep', [(k, k ^ 1) for k in range(8)])]
    pallas_call x8 -> x10, Pallas kernels: 23.4 us -> 24.9 us  [call(): pl.pallas_call(body, out_shape=out_shape, in_specs=list(places) + [VM] *...]
  transfers between devices with their start and end apart: 29 -> 29, of which waited for: 11 -> 11; matrix products, arithmetic and copies ran while one was open for 2% -> 2% of each run, Pallas kernels for 4% -> 6%
where the time goes in v5:
time: 155 us; the launch traced here: 154 us
  starting transfers between devices  64 us (41%)
  waiting for transfers between devices  43.2 us (28%)
  Pallas kernels  24.9 us (16%)
  blocking collectives  18.2 us (12%)
  local copies, waits for them, and re-layouts  2.8 us (2%)
    ppermute x14, starting transfers between devices, swap_core(): return lax.ppermute(v, 'rep', [(k, k ^ 1) for k in range(8)])  29 us
    pallas_call x10, Pallas kernels, call(): pl.pallas_call(body, out_shape=out_shape, in_specs=list(places) + [VM] *...  24.9 us
    ppermute x1, waiting for transfers between devices, on_device(): spill = lax.ppermute(spill, 'node', [(k, (k + 1) % 32) for k in range(32)])  22.8 us
    all_to_all x1, blocking collectives, on_device(): grad = lax.all_to_all(grad, 'node', split_axis=0, concat_axis=0, tiled=True)  18.2 us
    ppermute x12, waiting for transfers between devices, shift_x(): return lax.ppermute(v, 'rep', [(k, (k + 2 * d) % 8) for k in range(8)])  15.1 us
    ppermute x12, starting transfers between devices, shift_x(): return lax.ppermute(v, 'rep', [(k, (k + 2 * d) % 8) for k in range(8)])  13.1 us
    all_to_all x1, starting transfers between devices, on_device(): recv = lax.all_to_all(send, 'node', split_axis=0, concat_axis=0, tiled=True)  12.2 us
    all_to_all x1, starting transfers between devices, on_device(): grad = lax.all_to_all(grad, 'node', split_axis=0, concat_axis=0, tiled=True)  8.13 us
  transfers between devices with their start and end apart: 29, of which 11 were waited for; matrix products, arithmetic and copies ran while one was open for 2% of the time, Pallas kernels for 6%

profile of v5, /device:TPU:1, one launch (start us, length us, event | category | flops | bytes accessed | tf_op | source)
XLA Modules:
  0.0 154.5 jit_solution(4477788830793408233)
XLA Ops:
  0.6 6.3 %shard_map.192 = (bf16[32,144,128]{2,1,0:T(8,128)(2,1)}, f32[96,512]{1,0:T(8,128)}) custom-call(s32[1]{0:T(128)} %bitcast.3.pos, f32[1024,256]{1,0:T(8,128)} %refs_4_.1, bf16[1024,128]{1,0:T(8,128)(2,1)} %edge_h.1, bf16[512,512]{1,0:T(8,128)(2,1)} %w_h.1, s32[1,1024]{1,0:T(1,128)} %bitcast.17, s32[1,1024]{1,0:T(1,128)} %bitcast.18, s32[1,1024]{1,0:T(1,128)} %bitcast.19, ...), custom_call_target="tpu_custom_call" | custom-call | tf_op jit(solution)/shard_map/pallas_call | solution.py:34
  7.0 0.0 copy-start.6
  7.0 0.0 copy-start.4
  7.0 0.0 copy-start.5
  7.0 12.2 %all-to-all-start = ((bf16[32,144,128]{2,1,0:T(8,128)(2,1)}), bf16[32,144,128]{2,1,0:T(8,128)(2,1)S(1)}, u32[]{:S(2)}, u32[]{:S(2)}) async-start(bf16[32,144,128]{2,1,0:T(8,128)(2,1)} %get-tuple-element.39), calls=%async_computation | async-start | bytes 2359296 | tf_op jit(solution)/shard_map/all_to_all | solution.py:371
  19.2 1.0 collective-permute-start
  20.3 0.2 select_reduce_fusion
  20.5 0.9 collective-permute-done
  21.4 1.6 %collective-permute-start.1 = (f32[16,512]{1,0:T(8,128)S(1)}, f32[16,512]{1,0:T(8,128)S(1)}, u32[]{:S(2)}, u32[]{:S(2)}) collective-permute-start(f32[16,512]{1,0:T(8,128)S(1)} %constant_dynamic-slice_fusion), channel_id=1, source_target_pairs={{0,8},{8,16},{16,24},{24,32},{32,40},{40,48},{48,56},{56,64},{64,7... | collective-permute-start | bytes 98312 | tf_op jit(solution)/shard_map/ppermute | solution.py:375
  23.0 0.8 gather_fusion.1
  23.7 2.0 %gather_fusion = f32[128,256]{1,0:T(8,128)S(1)} fusion(f32[1024,256]{1,0:T(8,128)} %param.18, s32[1024]{0:T(1024)S(1)} %pad_clamp_fusion), kind=kCustom, calls=%fused_computation | custom fusion | bytes 262656 | tf_op jit(solution)/shard_map/jit(_take)/gather | solution.py:379
  25.7 22.8 %collective-permute-done.1 = f32[16,512]{1,0:T(8,128)S(1)} collective-permute-done((f32[16,512]{1,0:T(8,128)S(1)}, f32[16,512]{1,0:T(8,128)S(1)}, u32[]{:S(2)}, u32[]{:S(2)}) %collective-permute-start.1) | collective-permute-done | bytes 32800 | tf_op jit(solution)/shard_map/ppermute | solution.py:375
  48.6 3.6 %collective-permute-start.2 = (bf16[32,144,128]{2,1,0:T(8,128)(2,1)S(1)}, bf16[32,144,128]{2,1,0:T(8,128)(2,1)S(1)}, u32[]{:S(2)}, u32[]{:S(2)}) collective-permute-start(bf16[32,144,128]{2,1,0:T(8,128)(2,1)S(1)} %all-to-all-done.own), channel_id=1, source_target_pairs={{0,1},{1,0},{2,3},{3,2},{4,5},{5,4},{6,7},{7,6},{8,9},{9,8},{10,11... | collective-permute-start | bytes 3538952 | tf_op jit(solution)/shard_map/ppermute | solution.py:313
  52.2 0.1 pad_add_fusion.pos
  52.2 2.4 %collective-permute-done.2.peer = bf16[32,144,128]{2,1,0:T(8,128)(2,1)S(1)} collective-permute-done((bf16[32,144,128]{2,1,0:T(8,128)(2,1)S(1)}, bf16[32,144,128]{2,1,0:T(8,128)(2,1)S(1)}, u32[]{:S(2)}, u32[]{:S(2)}) %collective-permute-start.2) | collective-permute-done | bytes 1179680 | tf_op jit(solution)/shard_map/ppermute | solution.py:313
  54.6 2.4 %shard_map.193 = (f32[136,512]{1,0:T(8,128)S(1)}, f32[136,512]{1,0:T(8,128)S(1)}, f32[136,512]{1,0:T(8,128)S(1)}, f32[136,512]{1,0:T(8,128)S(1)}) custom-call(s32[3]{0:T(128)S(1)} %pad_add_fusion.pos, bf16[32,144,128]{2,1,0:T(8,128)(2,1)S(1)} %all-to-all-done.own, bf16[32,144,128]{2,1,0:T(8,128)(2,1)S(1)} %collective-permute-done.2.peer, ...), custom_call_target="tpu_custom_call" | custom-call | tf_op jit(solution)/shard_map/pallas_call | solution.py:34
  57.0 0.0 copy-start
  57.0 1.3 collective-permute-start.3
  58.3 2.5 %collective-permute-start.4 = (f32[136,512]{1,0:T(8,128)S(1)}, f32[136,512]{1,0:T(8,128)S(1)}, u32[]{:S(2)}, u32[]{:S(2)}) collective-permute-start(f32[136,512]{1,0:T(8,128)S(1)} %get-tuple-element.43), channel_id=1, source_target_pairs={{0,4},{1,5},{2,6},{3,7},{4,0},{5,1},{6,2},{7,3},{8,12},{9,13},{10,... | collective-permute-start | bytes 835592 | tf_op jit(solution)/shard_map/ppermute | solution.py:317
  60.8 1.1 collective-permute-start.5
  61.9 4.3 %collective-permute-done.3.p1_h = f32[136,512]{1,0:T(8,128)S(1)} collective-permute-done((f32[136,512]{1,0:T(8,128)S(1)}, f32[136,512]{1,0:T(8,128)S(1)}, u32[]{:S(2)}, u32[]{:S(2)}) %collective-permute-start.3) | collective-permute-done | bytes 278560 | tf_op jit(solution)/shard_map/ppermute | solution.py:317
  66.2 7.0 %collective-permute-done.4.p2_h = f32[136,512]{1,0:T(8,128)S(1)} collective-permute-done((f32[136,512]{1,0:T(8,128)S(1)}, f32[136,512]{1,0:T(8,128)S(1)}, u32[]{:S(2)}, u32[]{:S(2)}) %collective-permute-start.4) | collective-permute-done | bytes 278560 | tf_op jit(solution)/shard_map/ppermute | solution.py:317
  73.2 0.0 collective-permute-done.5.p3_h
  73.2 0.5 shard_map.194.refs_0_
  73.7 1.1 collective-permute-start.9
  74.8 1.7 %collective-permute-start.6 = (bf16[144,512]{1,0:T(8,128)(2,1)S(1)}, bf16[144,512]{1,0:T(8,128)(2,1)S(1)}, u32[]{:S(2)}, u32[]{:S(2)}) collective-permute-start(bf16[144,512]{1,0:T(8,128)(2,1)S(1)} %shard_map.194.refs_0_), channel_id=1, source_target_pairs={{0,6},{1,7},{2,0},{3,1},{4,2},{5,3},{6,4},{7,5},{8,14},{9,15},{10,... | collective-permute-start | bytes 442376 | tf_op jit(solution)/shard_map/ppermute | solution.py:317
  76.6 1.7 %collective-permute-start.11 = (bf16[144,512]{1,0:T(8,128)(2,1)S(1)}, bf16[144,512]{1,0:T(8,128)(2,1)S(1)}, u32[]{:S(2)}, u32[]{:S(2)}) collective-permute-start(bf16[144,512]{1,0:T(8,128)(2,1)S(1)} %shard_map.194.refs_0_), channel_id=1, source_target_pairs={{0,1},{1,0},{2,3},{3,2},{4,5},{5,4},{6,7},{7,6},{8,9},{9,8},{10,11... | collective-permute-start | bytes 442376 | tf_op jit(solution)/shard_map/ppermute | solution.py:313
  78.2 0.8 collective-permute-done.9.refs_0_
  79.0 2.3 %collective-permute-start.10 = (bf16[144,512]{1,0:T(8,128)(2,1)S(1)}, bf16[144,512]{1,0:T(8,128)(2,1)S(1)}, u32[]{:S(2)}, u32[]{:S(2)}) collective-permute-start(bf16[144,512]{1,0:T(8,128)(2,1)S(1)} %collective-permute-done.9.refs_0_), channel_id=1, source_target_pairs={{0,1},{1,0},{2,3},{3,2},{4,5},{5,4},{6,7},{7,6},{8,9},{9,8},{10,11... | collective-permute-start | bytes 442376 | tf_op jit(solution)/shard_map/ppermute | solution.py:313
  81.3 1.2 collective-permute-start.8
  82.5 0.0 collective-permute-done.6.refs_0_
  82.5 0.3 collective-permute-start.7
  82.8 2.1 %shard_map.195 = (f32[256,256]{1,0:T(8,128)S(1)}, f32[8,128]{1,0:T(8,128)S(1)}, f32[128,1024]{1,0:T(8,128)S(1)}) custom-call(s32[3]{0:T(128)S(1)} %pad_add_fusion.pos, bf16[144,512]{1,0:T(8,128)(2,1)S(1)} %shard_map.194.refs_0_, bf16[144,512]{1,0:T(8,128)(2,1)S(1)} %collective-permute-done.11.refs_1_, f32[1024,256]{1,0:T(8,128)S(1)} %copy-done, ...), custom_call_target="tpu_custom_call" | custom-call | tf_op jit(solution)/shard_map/pallas_call | solution.py:34
  84.9 0.0 collective-permute-done.10.refs_1_
  84.9 2.1 %shard_map.196 = (f32[256,256]{1,0:T(8,128)S(1)}, f32[128,1024]{1,0:T(8,128)S(1)}) custom-call(s32[3]{0:T(128)S(1)} %pad_add_fusion.pos, bf16[144,512]{1,0:T(8,128)(2,1)S(1)} %collective-permute-done.9.refs_0_, bf16[144,512]{1,0:T(8,128)(2,1)S(1)} %collective-permute-done.10.refs_1_, f32[1024,256]{1,0:T(8,128)S(1)} %copy-done, f32[1024,256]{1,0:T(8,128)S(1)} %copy-done.1, ...), custom_call_target="tpu_custom_call" | custom-call | tf_op jit(solution)/shard_map/pallas_call | solution.py:34
  87.0 1.3 collective-permute-done.8.refs_2_
  88.3 0.8 collective-permute-start.12
  89.1 0.0 collective-permute-done.7.refs_1_
  89.1 1.0 collective-permute-done.12.refs_3_
  90.1 3.5 %shard_map.197 = (f32[1024,256]{1,0:T(8,128)}, f32[32,8,512]{2,1,0:T(8,128)S(1)}) custom-call(s32[3]{0:T(128)S(1)} %pad_add_fusion.pos, bf16[144,512]{1,0:T(8,128)(2,1)S(1)} %collective-permute-done.6.refs_0_, bf16[144,512]{1,0:T(8,128)(2,1)S(1)} %collective-permute-done.7.refs_1_, bf16[144,512]{1,0:T(8,128)(2,1)S(1)} %collective-permute-done.8.refs_2_, ...), custom_call_target="tpu_custom_call" | custom-call | tf_op jit(solution)/shard_map/pallas_call | solution.py:34
  93.6 18.2 %all_to_all.15.parts = f32[32,8,512]{2,1,0:T(8,128)S(1)} all-to-all(f32[32,8,512]{2,1,0:T(8,128)S(1)} %get-tuple-element.56), channel_id=1, replica_groups=mesh['node'=32,'rep'=8] {'node'}, dimensions={0} | all-to-all | bytes 1048576 | tf_op jit(solution)/shard_map/all_to_all | solution.py:423
  111.8 0.8 shard_map.198
  112.6 8.1 %all-to-all-start.2 = ((f32[32,8,384]{2,1,0:T(8,128)}), f32[32,8,384]{2,1,0:T(8,128)S(1)}, u32[]{:S(2)}, u32[]{:S(2)}) async-start(f32[32,8,384]{2,1,0:T(8,128)} %get-tuple-element.57), calls=%async_computation.2 | async-start | bytes 786432 | tf_op jit(solution)/shard_map/all_to_all | solution.py:425
  120.8 1.5 collective-permute-start.15
  122.2 0.2 collective-permute-start.14
  122.5 0.4 collective-permute-start.13
  122.9 2.0 %collective-permute-start.16 = (f32[32,8,128]{2,1,0:T(8,128)S(1)}, f32[32,8,128]{2,1,0:T(8,128)S(1)}, u32[]{:S(2)}, u32[]{:S(2)}) collective-permute-start(f32[32,8,128]{2,1,0:T(8,128)S(1)} %get-tuple-element.60.a0), channel_id=1, source_target_pairs={{0,1},{1,0},{2,3},{3,2},{4,5},{5,4},{6,7},{7,6},{8,9},{9,8},{10,11... | collective-permute-start | bytes 393224 | tf_op jit(solution)/shard_map/ppermute | solution.py:313
  124.9 3.3 %collective-permute-start.19 = (f32[32,8,128]{2,1,0:T(8,128)S(1)}, f32[32,8,128]{2,1,0:T(8,128)S(1)}, u32[]{:S(2)}, u32[]{:S(2)}) collective-permute-start(f32[32,8,128]{2,1,0:T(8,128)S(1)} %collective-permute-done.15.a3), channel_id=1, source_target_pairs={{0,1},{1,0},{2,3},{3,2},{4,5},{5,4},{6,7},{7,6},{8,9},{9,8},{10,11... | collective-permute-start | bytes 393224 | tf_op jit(solution)/shard_map/ppermute | solution.py:313
  128.2 0.0 collective-permute-done.14.a2
  128.2 3.0 %collective-permute-start.18 = (f32[32,8,128]{2,1,0:T(8,128)S(1)}, f32[32,8,128]{2,1,0:T(8,128)S(1)}, u32[]{:S(2)}, u32[]{:S(2)}) collective-permute-start(f32[32,8,128]{2,1,0:T(8,128)S(1)} %collective-permute-done.14.a2), channel_id=1, source_target_pairs={{0,1},{1,0},{2,3},{3,2},{4,5},{5,4},{6,7},{7,6},{8,9},{9,8},{10,11... | collective-permute-start | bytes 393224 | tf_op jit(solution)/shard_map/ppermute | solution.py:313
  131.2 0.1 collective-permute-done.13.a1
  131.2 1.2 collective-permute-start.17
  132.4 1.0 collective-permute-done.17.b1
  133.4 0.6 collective-permute-start.20
  134.0 0.9 collective-permute-start.25
  134.9 0.6 collective-permute-start.22
  135.5 4.6 %collective-permute-start.21 = (f32[24,8,384]{2,1,0:T(8,128)S(1)}, f32[24,8,384]{2,1,0:T(8,128)S(1)}, u32[]{:S(2)}, u32[]{:S(2)}) collective-permute-start(f32[24,8,384]{2,1,0:T(8,128)S(1)} %slice.2.a0), channel_id=1, source_target_pairs={{0,1},{1,0},{2,3},{3,2},{4,5},{5,4},{6,7},{7,6},{8,9},{9,8},{10,11... | collective-permute-start | bytes 884744 | tf_op jit(solution)/shard_map/ppermute | solution.py:313
  140.1 3.9 %shard_map.199 = f32[1024,256]{1,0:T(8,128)} custom-call(s32[3]{0:T(128)S(1)} %pad_add_fusion.pos, s32[1,1024]{1,0:T(1,128)S(1)} %bitcast.16, f32[32,8,128]{2,1,0:T(8,128)S(1)} %get-tuple-element.60.a0, f32[32,8,128]{2,1,0:T(8,128)S(1)} %collective-permute-done.13.a1, f32[32,8,128]{2,1,0:T(8,128)S(1)} %collective-permute-done.14.a2, ...), custom_call_target="tpu_custom_call" | custom-call | tf_op jit(solution)/shard_map/pallas_call | solution.py:34
  144.0 1.7 %collective-permute-done.25.a3 = f32[24,8,384]{2,1,0:T(8,128)S(1)} collective-permute-done((f32[24,8,384]{2,1,0:T(8,128)S(1)}, f32[24,8,384]{2,1,0:T(8,128)S(1)}, u32[]{:S(2)}, u32[]{:S(2)}) %collective-permute-start.25) | collective-permute-done | bytes 294944 | tf_op jit(solution)/shard_map/ppermute | solution.py:317
  145.7 3.4 %collective-permute-start.26 = (f32[24,8,384]{2,1,0:T(8,128)S(1)}, f32[24,8,384]{2,1,0:T(8,128)S(1)}, u32[]{:S(2)}, u32[]{:S(2)}) collective-permute-start(f32[24,8,384]{2,1,0:T(8,128)S(1)} %collective-permute-done.25.a3), channel_id=1, source_target_pairs={{0,1},{1,0},{2,3},{3,2},{4,5},{5,4},{6,7},{7,6},{8,9},{9,8},{10,11... | collective-permute-start | bytes 884744 | tf_op jit(solution)/shard_map/ppermute | solution.py:313
  149.1 1.9 %collective-permute-start.23 = (f32[24,8,384]{2,1,0:T(8,128)S(1)}, f32[24,8,384]{2,1,0:T(8,128)S(1)}, u32[]{:S(2)}, u32[]{:S(2)}) collective-permute-start(f32[24,8,384]{2,1,0:T(8,128)S(1)} %collective-permute-done.22.a1), channel_id=1, source_target_pairs={{0,1},{1,0},{2,3},{3,2},{4,5},{5,4},{6,7},{7,6},{8,9},{9,8},{10,11... | collective-permute-start | bytes 884744 | tf_op jit(solution)/shard_map/ppermute | solution.py:313
  151.0 0.0 collective-permute-start.24
  151.0 1.6 %shard_map.200 = (f32[512,768]{1,0:T(8,128)}, f32[256,768]{1,0:T(8,128)}) custom-call(s32[3]{0:T(128)S(1)} %pad_add_fusion.pos, f32[24,8,384]{2,1,0:T(8,128)S(1)} %slice.2.a0, f32[24,8,384]{2,1,0:T(8,128)S(1)} %collective-permute-done.22.a1, f32[24,8,384]{2,1,0:T(8,128)S(1)} %collective-permute-done.20.a2, f32[24,8,384]{2,1,0:T(8,128)S(1)} %collective-permute-done.25.a3), custom_call_target="tpu_custom_call" | custom-call | tf_op jit(solution)/shard_map/pallas_call | solution.py:34
  152.6 1.6 %shard_map.201 = (f32[512,768]{1,0:T(8,128)}, f32[256,768]{1,0:T(8,128)}) custom-call(s32[3]{0:T(128)S(1)} %pad_add_fusion.pos, f32[24,8,384]{2,1,0:T(8,128)S(1)} %collective-permute-done.21.a0, f32[24,8,384]{2,1,0:T(8,128)S(1)} %collective-permute-done.23.a1, ...), custom_call_target="tpu_custom_call", output_to_operand_aliasing={{0}: (5, {}), {1}: (6, {})} | custom-call | tf_op jit(solution)/shard_map/pallas_call | solution.py:34
  (28 shorter events, 0.1 us)
Async XLA Ops:
  7.0 12.2 %copy-start.6 = (f32[96,512]{1,0:T(8,128)S(1)}, f32[96,512]{1,0:T(8,128)}, u32[]{:S(2)}) copy-start(f32[96,512]{1,0:T(8,128)} %get-tuple-element.40) | copy-start | bytes 589828
  7.0 13.3 %copy-start.4 = (s32[1024]{0:T(1024)S(1)}, s32[1024]{0:T(1024)}, u32[]{:S(2)}) copy-start(s32[1024]{0:T(1024)} %param.27) | copy-start | bytes 12292
  7.0 16.0 %copy-start.5 = (f32[1024,256]{1,0:T(8,128)S(1)}, f32[1024,256]{1,0:T(8,128)}, u32[]{:S(2)}) copy-start(f32[1024,256]{1,0:T(8,128)} %param.20) | copy-start | bytes 3145732
  7.0 41.6 %all-to-all-start = ((bf16[32,144,128]{2,1,0:T(8,128)(2,1)}), bf16[32,144,128]{2,1,0:T(8,128)(2,1)S(1)}, u32[]{:S(2)}, u32[]{:S(2)}) async-start(bf16[32,144,128]{2,1,0:T(8,128)(2,1)} %get-tuple-element.39), calls=%async_computation | async-start | bytes 2359296 | tf_op jit(solution)/shard_map/all_to_all | solution.py:371
  19.2 2.1 %collective-permute-start = (f32[96,512]{1,0:T(8,128)S(1)}, f32[96,512]{1,0:T(8,128)S(1)}, u32[]{:S(2)}, u32[]{:S(2)}) collective-permute-start(f32[96,512]{1,0:T(8,128)S(1)} %copy-done.6), channel_id=1, source_target_pairs={{0,1},{1,0},{2,3},{3,2},{4,5},{5,4},{6,7},{7,6},{8,9},{9,8},{10,11... | collective-permute-start | bytes 589832 | tf_op jit(solution)/shard_map/ppermute | solution.py:313
  21.4 27.2 %collective-permute-start.1 = (f32[16,512]{1,0:T(8,128)S(1)}, f32[16,512]{1,0:T(8,128)S(1)}, u32[]{:S(2)}, u32[]{:S(2)}) collective-permute-start(f32[16,512]{1,0:T(8,128)S(1)} %constant_dynamic-slice_fusion), channel_id=1, source_target_pairs={{0,8},{8,16},{16,24},{24,32},{32,40},{40,48},{48,56},{56,64},{64,7... | collective-permute-start | bytes 98312 | tf_op jit(solution)/shard_map/ppermute | solution.py:375
  48.6 6.1 %collective-permute-start.2 = (bf16[32,144,128]{2,1,0:T(8,128)(2,1)S(1)}, bf16[32,144,128]{2,1,0:T(8,128)(2,1)S(1)}, u32[]{:S(2)}, u32[]{:S(2)}) collective-permute-start(bf16[32,144,128]{2,1,0:T(8,128)(2,1)S(1)} %all-to-all-done.own), channel_id=1, source_target_pairs={{0,1},{1,0},{2,3},{3,2},{4,5},{5,4},{6,7},{7,6},{8,9},{9,8},{10,11... | collective-permute-start | bytes 3538952 | tf_op jit(solution)/shard_map/ppermute | solution.py:313
  54.6 28.2 %copy-start.1 = (f32[1024,256]{1,0:T(8,128)S(1)}, f32[1024,256]{1,0:T(8,128)}, u32[]{:S(2)}) copy-start(f32[1024,256]{1,0:T(8,128)} %refs_5_.1) | copy-start | bytes 3145732
  54.6 28.2 %copy-start.2 = (bf16[512,768]{1,0:T(8,128)(2,1)S(1)}, bf16[512,768]{1,0:T(8,128)(2,1)}, u32[]{:S(2)}) copy-start(bf16[512,768]{1,0:T(8,128)(2,1)} %refs_8_.1) | copy-start | bytes 2359300
  54.6 28.2 %copy-start.3 = (bf16[256,768]{1,0:T(8,128)(2,1)S(1)}, bf16[256,768]{1,0:T(8,128)(2,1)}, u32[]{:S(2)}) copy-start(bf16[256,768]{1,0:T(8,128)(2,1)} %refs_9_.1) | copy-start | bytes 1179652
  57.0 25.8 %copy-start = (f32[1024,256]{1,0:T(8,128)S(1)}, f32[1024,256]{1,0:T(8,128)}, u32[]{:S(2)}) copy-start(f32[1024,256]{1,0:T(8,128)} %refs_4_.1) | copy-start | bytes 3145732
  57.0 9.2 %collective-permute-start.3 = (f32[136,512]{1,0:T(8,128)S(1)}, f32[136,512]{1,0:T(8,128)S(1)}, u32[]{:S(2)}, u32[]{:S(2)}) collective-permute-start(f32[136,512]{1,0:T(8,128)S(1)} %get-tuple-element.42), channel_id=1, source_target_pairs={{0,2},{1,3},{2,4},{3,5},{4,6},{5,7},{6,0},{7,1},{8,10},{9,11},{10,... | collective-permute-start | bytes 835592 | tf_op jit(solution)/shard_map/ppermute | solution.py:317
  58.3 14.8 %collective-permute-start.4 = (f32[136,512]{1,0:T(8,128)S(1)}, f32[136,512]{1,0:T(8,128)S(1)}, u32[]{:S(2)}, u32[]{:S(2)}) collective-permute-start(f32[136,512]{1,0:T(8,128)S(1)} %get-tuple-element.43), channel_id=1, source_target_pairs={{0,4},{1,5},{2,6},{3,7},{4,0},{5,1},{6,2},{7,3},{8,12},{9,13},{10,... | collective-permute-start | bytes 835592 | tf_op jit(solution)/shard_map/ppermute | solution.py:317
  60.8 12.4 %collective-permute-start.5 = (f32[136,512]{1,0:T(8,128)S(1)}, f32[136,512]{1,0:T(8,128)S(1)}, u32[]{:S(2)}, u32[]{:S(2)}) collective-permute-start(f32[136,512]{1,0:T(8,128)S(1)} %get-tuple-element.44), channel_id=1, source_target_pairs={{0,6},{1,7},{2,0},{3,1},{4,2},{5,3},{6,4},{7,5},{8,14},{9,15},{10,... | collective-permute-start | bytes 835592 | tf_op jit(solution)/shard_map/ppermute | solution.py:317
  73.7 5.3 %collective-permute-start.9 = (bf16[144,512]{1,0:T(8,128)(2,1)S(1)}, bf16[144,512]{1,0:T(8,128)(2,1)S(1)}, u32[]{:S(2)}, u32[]{:S(2)}) collective-permute-start(bf16[144,512]{1,0:T(8,128)(2,1)S(1)} %shard_map.194.refs_0_), channel_id=1, source_target_pairs={{0,2},{1,3},{2,4},{3,5},{4,6},{5,7},{6,0},{7,1},{8,10},{9,11},{10,... | collective-permute-start | bytes 442376 | tf_op jit(solution)/shard_map/ppermute | solution.py:317
  74.8 7.7 %collective-permute-start.6 = (bf16[144,512]{1,0:T(8,128)(2,1)S(1)}, bf16[144,512]{1,0:T(8,128)(2,1)S(1)}, u32[]{:S(2)}, u32[]{:S(2)}) collective-permute-start(bf16[144,512]{1,0:T(8,128)(2,1)S(1)} %shard_map.194.refs_0_), channel_id=1, source_target_pairs={{0,6},{1,7},{2,0},{3,1},{4,2},{5,3},{6,4},{7,5},{8,14},{9,15},{10,... | collective-permute-start | bytes 442376 | tf_op jit(solution)/shard_map/ppermute | solution.py:317
  76.6 6.2 %collective-permute-start.11 = (bf16[144,512]{1,0:T(8,128)(2,1)S(1)}, bf16[144,512]{1,0:T(8,128)(2,1)S(1)}, u32[]{:S(2)}, u32[]{:S(2)}) collective-permute-start(bf16[144,512]{1,0:T(8,128)(2,1)S(1)} %shard_map.194.refs_0_), channel_id=1, source_target_pairs={{0,1},{1,0},{2,3},{3,2},{4,5},{5,4},{6,7},{7,6},{8,9},{9,8},{10,11... | collective-permute-start | bytes 442376 | tf_op jit(solution)/shard_map/ppermute | solution.py:313
  79.0 5.9 %collective-permute-start.10 = (bf16[144,512]{1,0:T(8,128)(2,1)S(1)}, bf16[144,512]{1,0:T(8,128)(2,1)S(1)}, u32[]{:S(2)}, u32[]{:S(2)}) collective-permute-start(bf16[144,512]{1,0:T(8,128)(2,1)S(1)} %collective-permute-done.9.refs_0_), channel_id=1, source_target_pairs={{0,1},{1,0},{2,3},{3,2},{4,5},{5,4},{6,7},{7,6},{8,9},{9,8},{10,11... | collective-permute-start | bytes 442376 | tf_op jit(solution)/shard_map/ppermute | solution.py:313
  81.3 7.0 %collective-permute-start.8 = (bf16[144,512]{1,0:T(8,128)(2,1)S(1)}, bf16[144,512]{1,0:T(8,128)(2,1)S(1)}, u32[]{:S(2)}, u32[]{:S(2)}) collective-permute-start(bf16[144,512]{1,0:T(8,128)(2,1)S(1)} %shard_map.194.refs_0_), channel_id=1, source_target_pairs={{0,4},{1,5},{2,6},{3,7},{4,0},{5,1},{6,2},{7,3},{8,12},{9,13},{10,... | collective-permute-start | bytes 442376 | tf_op jit(solution)/shard_map/ppermute | solution.py:317
  82.5 6.6 %collective-permute-start.7 = (bf16[144,512]{1,0:T(8,128)(2,1)S(1)}, bf16[144,512]{1,0:T(8,128)(2,1)S(1)}, u32[]{:S(2)}, u32[]{:S(2)}) collective-permute-start(bf16[144,512]{1,0:T(8,128)(2,1)S(1)} %collective-permute-done.6.refs_0_), channel_id=1, source_target_pairs={{0,1},{1,0},{2,3},{3,2},{4,5},{5,4},{6,7},{7,6},{8,9},{9,8},{10,11... | collective-permute-start | bytes 442376 | tf_op jit(solution)/shard_map/ppermute | solution.py:313
  88.3 1.8 %collective-permute-start.12 = (bf16[144,512]{1,0:T(8,128)(2,1)S(1)}, bf16[144,512]{1,0:T(8,128)(2,1)S(1)}, u32[]{:S(2)}, u32[]{:S(2)}) collective-permute-start(bf16[144,512]{1,0:T(8,128)(2,1)S(1)} %collective-permute-done.8.refs_2_), channel_id=1, source_target_pairs={{0,1},{1,0},{2,3},{3,2},{4,5},{5,4},{6,7},{7,6},{8,9},{9,8},{10,11... | collective-permute-start | bytes 442376 | tf_op jit(solution)/shard_map/ppermute | solution.py:313
  112.6 20.8 %all-to-all-start.2 = ((f32[32,8,384]{2,1,0:T(8,128)}), f32[32,8,384]{2,1,0:T(8,128)S(1)}, u32[]{:S(2)}, u32[]{:S(2)}) async-start(f32[32,8,384]{2,1,0:T(8,128)} %get-tuple-element.57), calls=%async_computation.2 | async-start | bytes 786432 | tf_op jit(solution)/shard_map/all_to_all | solution.py:425
  120.8 4.1 %collective-permute-start.15 = (f32[32,8,128]{2,1,0:T(8,128)S(1)}, f32[32,8,128]{2,1,0:T(8,128)S(1)}, u32[]{:S(2)}, u32[]{:S(2)}) collective-permute-start(f32[32,8,128]{2,1,0:T(8,128)S(1)} %get-tuple-element.60.a0), channel_id=1, source_target_pairs={{0,6},{1,7},{2,0},{3,1},{4,2},{5,3},{6,4},{7,5},{8,14},{9,15},{10,... | collective-permute-start | bytes 393224 | tf_op jit(solution)/shard_map/ppermute | solution.py:317
  122.2 5.9 %collective-permute-start.14 = (f32[32,8,128]{2,1,0:T(8,128)S(1)}, f32[32,8,128]{2,1,0:T(8,128)S(1)}, u32[]{:S(2)}, u32[]{:S(2)}) collective-permute-start(f32[32,8,128]{2,1,0:T(8,128)S(1)} %get-tuple-element.60.a0), channel_id=1, source_target_pairs={{0,4},{1,5},{2,6},{3,7},{4,0},{5,1},{6,2},{7,3},{8,12},{9,13},{10,... | collective-permute-start | bytes 393224 | tf_op jit(solution)/shard_map/ppermute | solution.py:317
  122.5 8.8 %collective-permute-start.13 = (f32[32,8,128]{2,1,0:T(8,128)S(1)}, f32[32,8,128]{2,1,0:T(8,128)S(1)}, u32[]{:S(2)}, u32[]{:S(2)}) collective-permute-start(f32[32,8,128]{2,1,0:T(8,128)S(1)} %get-tuple-element.60.a0), channel_id=1, source_target_pairs={{0,2},{1,3},{2,4},{3,5},{4,6},{5,7},{6,0},{7,1},{8,10},{9,11},{10,... | collective-permute-start | bytes 393224 | tf_op jit(solution)/shard_map/ppermute | solution.py:317
  122.9 9.5 %collective-permute-start.16 = (f32[32,8,128]{2,1,0:T(8,128)S(1)}, f32[32,8,128]{2,1,0:T(8,128)S(1)}, u32[]{:S(2)}, u32[]{:S(2)}) collective-permute-start(f32[32,8,128]{2,1,0:T(8,128)S(1)} %get-tuple-element.60.a0), channel_id=1, source_target_pairs={{0,1},{1,0},{2,3},{3,2},{4,5},{5,4},{6,7},{7,6},{8,9},{9,8},{10,11... | collective-permute-start | bytes 393224 | tf_op jit(solution)/shard_map/ppermute | solution.py:313
  124.9 7.5 %collective-permute-start.19 = (f32[32,8,128]{2,1,0:T(8,128)S(1)}, f32[32,8,128]{2,1,0:T(8,128)S(1)}, u32[]{:S(2)}, u32[]{:S(2)}) collective-permute-start(f32[32,8,128]{2,1,0:T(8,128)S(1)} %collective-permute-done.15.a3), channel_id=1, source_target_pairs={{0,1},{1,0},{2,3},{3,2},{4,5},{5,4},{6,7},{7,6},{8,9},{9,8},{10,11... | collective-permute-start | bytes 393224 | tf_op jit(solution)/shard_map/ppermute | solution.py:313
  128.2 4.2 %collective-permute-start.18 = (f32[32,8,128]{2,1,0:T(8,128)S(1)}, f32[32,8,128]{2,1,0:T(8,128)S(1)}, u32[]{:S(2)}, u32[]{:S(2)}) collective-permute-start(f32[32,8,128]{2,1,0:T(8,128)S(1)} %collective-permute-done.14.a2), channel_id=1, source_target_pairs={{0,1},{1,0},{2,3},{3,2},{4,5},{5,4},{6,7},{7,6},{8,9},{9,8},{10,11... | collective-permute-start | bytes 393224 | tf_op jit(solution)/shard_map/ppermute | solution.py:313
  131.2 2.2 %collective-permute-start.17 = (f32[32,8,128]{2,1,0:T(8,128)S(1)}, f32[32,8,128]{2,1,0:T(8,128)S(1)}, u32[]{:S(2)}, u32[]{:S(2)}) collective-permute-start(f32[32,8,128]{2,1,0:T(8,128)S(1)} %collective-permute-done.13.a1), channel_id=1, source_target_pairs={{0,1},{1,0},{2,3},{3,2},{4,5},{5,4},{6,7},{7,6},{8,9},{9,8},{10,11... | collective-permute-start | bytes 393224 | tf_op jit(solution)/shard_map/ppermute | solution.py:313
  133.4 10.5 %collective-permute-start.20 = (f32[24,8,384]{2,1,0:T(8,128)S(1)}, f32[24,8,384]{2,1,0:T(8,128)S(1)}, u32[]{:S(2)}, u32[]{:S(2)}) collective-permute-start(f32[24,8,384]{2,1,0:T(8,128)S(1)} %slice.2.a0), channel_id=1, source_target_pairs={{0,4},{1,5},{2,6},{3,7},{4,0},{5,1},{6,2},{7,3},{8,12},{9,13},{10,... | collective-permute-start | bytes 884744 | tf_op jit(solution)/shard_map/ppermute | solution.py:317
  134.0 11.7 %collective-permute-start.25 = (f32[24,8,384]{2,1,0:T(8,128)S(1)}, f32[24,8,384]{2,1,0:T(8,128)S(1)}, u32[]{:S(2)}, u32[]{:S(2)}) collective-permute-start(f32[24,8,384]{2,1,0:T(8,128)S(1)} %slice.2.a0), channel_id=1, source_target_pairs={{0,6},{1,7},{2,0},{3,1},{4,2},{5,3},{6,4},{7,5},{8,14},{9,15},{10,... | collective-permute-start | bytes 884744 | tf_op jit(solution)/shard_map/ppermute | solution.py:317
  134.9 14.2 %collective-permute-start.22 = (f32[24,8,384]{2,1,0:T(8,128)S(1)}, f32[24,8,384]{2,1,0:T(8,128)S(1)}, u32[]{:S(2)}, u32[]{:S(2)}) collective-permute-start(f32[24,8,384]{2,1,0:T(8,128)S(1)} %slice.2.a0), channel_id=1, source_target_pairs={{0,2},{1,3},{2,4},{3,5},{4,6},{5,7},{6,0},{7,1},{8,10},{9,11},{10,... | collective-permute-start | bytes 884744 | tf_op jit(solution)/shard_map/ppermute | solution.py:317
  135.5 17.1 %collective-permute-start.21 = (f32[24,8,384]{2,1,0:T(8,128)S(1)}, f32[24,8,384]{2,1,0:T(8,128)S(1)}, u32[]{:S(2)}, u32[]{:S(2)}) collective-permute-start(f32[24,8,384]{2,1,0:T(8,128)S(1)} %slice.2.a0), channel_id=1, source_target_pairs={{0,1},{1,0},{2,3},{3,2},{4,5},{5,4},{6,7},{7,6},{8,9},{9,8},{10,11... | collective-permute-start | bytes 884744 | tf_op jit(solution)/shard_map/ppermute | solution.py:313
  145.7 6.9 %collective-permute-start.26 = (f32[24,8,384]{2,1,0:T(8,128)S(1)}, f32[24,8,384]{2,1,0:T(8,128)S(1)}, u32[]{:S(2)}, u32[]{:S(2)}) collective-permute-start(f32[24,8,384]{2,1,0:T(8,128)S(1)} %collective-permute-done.25.a3), channel_id=1, source_target_pairs={{0,1},{1,0},{2,3},{3,2},{4,5},{5,4},{6,7},{7,6},{8,9},{9,8},{10,11... | collective-permute-start | bytes 884744 | tf_op jit(solution)/shard_map/ppermute | solution.py:313
  149.1 3.6 %collective-permute-start.23 = (f32[24,8,384]{2,1,0:T(8,128)S(1)}, f32[24,8,384]{2,1,0:T(8,128)S(1)}, u32[]{:S(2)}, u32[]{:S(2)}) collective-permute-start(f32[24,8,384]{2,1,0:T(8,128)S(1)} %collective-permute-done.22.a1), channel_id=1, source_target_pairs={{0,1},{1,0},{2,3},{3,2},{4,5},{5,4},{6,7},{7,6},{8,9},{9,8},{10,11... | collective-permute-start | bytes 884744 | tf_op jit(solution)/shard_map/ppermute | solution.py:313
  151.0 1.7 %collective-permute-start.24 = (f32[24,8,384]{2,1,0:T(8,128)S(1)}, f32[24,8,384]{2,1,0:T(8,128)S(1)}, u32[]{:S(2)}, u32[]{:S(2)}) collective-permute-start(f32[24,8,384]{2,1,0:T(8,128)S(1)} %collective-permute-done.20.a2), channel_id=1, source_target_pairs={{0,1},{1,0},{2,3},{3,2},{4,5},{5,4},{6,7},{7,6},{8,9},{9,8},{10,11... | collective-permute-start | bytes 884744 | tf_op jit(solution)/shard_map/ppermute | solution.py:313

commit v6 on v5

--- a/solution.py
+++ b/solution.py
@@ -220,10 +220,12 @@
     mem, cot, hot_mem, hot_cot, w_in, w_hid = refs[:6]
     refs = refs[6:]
     if last:
-        olds, (own_hot, old_acc, new, grad, acc) = refs[: len(done)], refs[len(done) :]
+        olds, (own_hot, old_acc, new_h, grad, acc, new, sems) = refs[: len(done)], refs[len(done) :]
+        stores = []
         for d, old in zip(done, olds):
-            chip = (pos[0] - d + 4) & 3
-            new[pl.ds(pl.multiple_of(256 * chip, 256), 256), :] = old[...]
+            at = pl.ds(pl.multiple_of(256 * ((pos[0] - d + 4) & 3), 256), 256)
+            stores.append(pltpu.make_async_copy(old, new_h.at[at], sems.at[d]))
+            stores[-1].start()
     elif 0 in ds:
         new, hot, acc = refs
         old_acc = None
@@ -232,44 +234,51 @@
     if old_acc is not None:
         acc[...] = old_acc[...]
     x, core, rep = pos[0], pos[1], pos[2]
-    k, q = iota((512, 128), 0), iota((512, 128), 1)
+    q, k = iota((128, 512), 0), iota((128, 512), 1)
     sel_a = one_hot((k == 64 * rep + q) & (q < 64))
-    k, q = iota((256, 128), 0), iota((256, 128), 1)
+    q, k = iota((128, 256), 0), iota((128, 256), 1)
     sel_m = one_hot((k == 32 * rep + q - 64) & (q >= 64) & (q < 96))
-    for i, d in enumerate(ds):
-        chip = (x - d + 4) & 3
-        at = pl.ds(pl.multiple_of(256 * chip, 256), 256)
-        hot_at = pl.ds(pl.multiple_of(32 * chip, 32), 32)
+    chips = [(x - d + 4) & 3 for d in ds]
+    ats = [pl.ds(pl.multiple_of(256 * c, 256), 256) for c in chips]
+    hot_ats = [pl.ds(pl.multiple_of(32 * c, 32), 32) for c in chips]
+    rows = []
+    for i in range(len(ds)):
         mine, other = parts[2 * i][...], parts[2 * i + 1][...]
         low = jnp.where(core == 0, mine, other)
         high = jnp.where(core == 0, other, mine)
-        wide = jnp.concatenate([low[0:128], high[0:128], low[128:144], high[128:144]], axis=0).astype(F32)
-        live = wide[:, 0:1] < DEAD * 0.5
-        a = jnp.where(live, wide, 0.0).astype(BF16)
-        m = jnp.concatenate([mem[at, :], hot_mem[hot_at, :]], axis=0)
-        reset, update, cand, hid_cand = gates(a, m, w_in[...], w_hid[...])
-        fresh = jnp.where(live, (1.0 - update) * cand + update * m, m)
+        rows += [low[0:128], high[0:128], low[128:144], high[128:144]]
+    wide = jnp.concatenate(rows, axis=0).astype(F32)
+    live = wide[:, 0:1] < DEAD * 0.5
+    a = jnp.where(live, wide, 0.0).astype(BF16)
+    m = jnp.concatenate([v for h, k in zip(ats, hot_ats) for v in (mem[h, :], hot_mem[k, :])], axis=0)
+    g = jnp.concatenate([v for h, k in zip(ats, hot_ats) for v in (cot[h, :], hot_cot[k, :])], axis=0)
+    reset, update, cand, hid_cand = gates(a, m, w_in[...], w_hid[...])
+    fresh = jnp.where(live, (1.0 - update) * cand + update * m, m)
+    for i, d in enumerate(ds):
+        part = fresh[288 * i : 288 * i + 256, :]
         if last:
-            new[at, :] = fresh[0:256, :]
+            new[256 * i : 256 * i + 256, :] = part
+            stores.append(pltpu.make_async_copy(new.at[256 * i : 256 * i + 256], new_h.at[ats[i]], sems.at[d]))
+            stores[-1].start()
         else:
-            new[...] = fresh[0:256, :]
+            new[...] = part
             if d == 0:
                 own = jnp.where(core == 0, fresh[256:264, :], fresh[272:280, :])
                 hot[...] = jnp.concatenate([own[0:4, 0:128], own[0:4, 128:256]], axis=0)
-        g = jnp.where(live, jnp.concatenate([cot[at, :], hot_cot[hot_at, :]], axis=0), 0.0)
-        d_cand = g * (1.0 - update) * (1.0 - cand * cand)
-        d_upd = g * (m - cand) * update * (1.0 - update)
-        d_reset = d_cand * hid_cand * reset * (1.0 - reset)
-        left = (mm(a, sel_a) + mm(m.astype(BF16), sel_m)).astype(BF16)
-        for j, v in enumerate((d_reset, d_upd, d_cand, d_cand * reset)):
-            hi = v.astype(BF16)
-            low = (v - hi.astype(F32)).astype(BF16)
-            part = mm(left, hi, ((0,), (0,))) + mm(left, low, ((0,), (0,)))
-            cols = slice(256 * j, 256 * j + 256)
-            if i == 0 and old_acc is None:
-                acc[:, cols] = part
-            else:
-                acc[:, cols] += part
+    g = jnp.where(live, g, 0.0)
+    d_cand = g * (1.0 - update) * (1.0 - cand * cand)
+    d_upd = g * (m - cand) * update * (1.0 - update)
+    d_reset = d_cand * hid_cand * reset * (1.0 - reset)
+    left = (mm(sel_a, a, ((1,), (1,))) + mm(sel_m, m.astype(BF16), ((1,), (1,)))).astype(BF16)
+    for j, v in enumerate((d_reset, d_upd, d_cand, d_cand * reset)):
+        hi = v.astype(BF16)
+        low = (v - hi.astype(F32)).astype(BF16)
+        part = mm(left, hi) + mm(left, low)
+        cols = slice(256 * j, 256 * j + 256)
+        if old_acc is None:
+            acc[:, cols] = part
+        else:
+            acc[:, cols] += part
     if last:
         total = acc[...] * GRAD_SCALE
         third = jnp.where(iota((128, 256), 0) < 64, total[:, 512:768], total[:, 768:1024])
@@ -278,6 +287,8 @@
             i, j = p // 2, p % 2
             grad[p, :, 0:384] = total[8 * i : 8 * i + 8, 384 * j : 384 * j + 384]
             grad[p, :, 384:512] = own_hot[...]
+        for c in stores:
+            c.wait()
 
 
 def piece_kernel(parts, out, hot):
@@ -320,6 +331,39 @@
 def gather_rep(v):
     own = [v] + [shift_x(v, d) for d in (1, 2, 3)]
     return own + [swap_core(u) for u in own]
+
+
+def message_call(*args):
+    sds = jax.ShapeDtypeStruct
+    return call(
+        message_kernel,
+        (sds((32, 144, 128), BF16), sds((96, 512), F32)),
+        (SM,) + (HB,) * 11,
+        args,
+        (
+            pltpu.VMEM((1024, 256), F32), pltpu.VMEM((1024, 128), BF16), pltpu.VMEM((512, 512), BF16),
+            pltpu.VMEM((1, 1024), I32), pltpu.VMEM((1, 1024), I32), pltpu.VMEM((1, 1024), I32),
+            pltpu.VMEM((32, 32), I32), pltpu.VMEM((1, 32), I32), pltpu.VMEM((1, 128), F32),
+            pltpu.VMEM((1, 128), F32), pltpu.VMEM((1, 512), F32),
+            pltpu.VMEM((1024, 128), BF16), pltpu.VMEM((1024, 512), BF16), pltpu.VMEM((32, 144, 128), BF16),
+            pltpu.VMEM((1024, 8), I32),
+            pltpu.SemaphoreType.DMA((15,)),
+        ),
+        (ANY, VM),
+        63,
+    )
+
+
+def last_update(pos, parts, shared, olds, hot_own, acc):
+    sds = jax.ShapeDtypeStruct
+    return call(
+        functools.partial(update_kernel, (3, 2, 1), (0,)),
+        (sds((1024, 256), F32), sds((32, 8, 512), F32)),
+        (SM,),
+        (pos, *parts, *shared, *olds, hot_own, acc),
+        (pltpu.VMEM((128, 1024), F32), pltpu.VMEM((768, 256), F32), pltpu.SemaphoreType.DMA((4,))),
+        (ANY, VM),
+    )
 
 
 def on_device(
@@ -347,26 +391,10 @@
     sds = jax.ShapeDtypeStruct
 
     chip, core = rep // 2, rep % 2
-    send, hot = call(
-        message_kernel,
-        (sds((32, 144, 128), BF16), sds((96, 512), F32)),
-        (SM,) + (HB,) * 11,
-        (
-            node.astype(I32)[None], memory, edge_feat, w_msg, src_local[None, :], times[None, :],
-            dst_ids[None, :], cold_list, cold_count[None, :], time_freq[None, :], time_phase[None, :],
-            b_msg[None, :],
-        ),
-        (
-            pltpu.VMEM((1024, 256), F32), pltpu.VMEM((1024, 128), BF16), pltpu.VMEM((512, 512), BF16),
-            pltpu.VMEM((1, 1024), I32), pltpu.VMEM((1, 1024), I32), pltpu.VMEM((1, 1024), I32),
-            pltpu.VMEM((32, 32), I32), pltpu.VMEM((1, 32), I32), pltpu.VMEM((1, 128), F32),
-            pltpu.VMEM((1, 128), F32), pltpu.VMEM((1, 512), F32),
-            pltpu.VMEM((1024, 128), BF16), pltpu.VMEM((1024, 512), BF16), pltpu.VMEM((32, 144, 128), BF16),
-            pltpu.VMEM((1024, 8), I32),
-            pltpu.SemaphoreType.DMA((15,)),
-        ),
-        (ANY, VM),
-        63,
+    send, hot = message_call(
+        node.astype(I32)[None], memory, edge_feat, w_msg, src_local[None, :], times[None, :],
+        dst_ids[None, :], cold_list, cold_count[None, :], time_freq[None, :], time_phase[None, :],
+        b_msg[None, :],
     )
     recv = lax.all_to_all(send, "node", split_axis=0, concat_axis=0, tiled=True)
 
@@ -405,20 +433,9 @@
         (SM,),
         (pos, agg, swap_core(agg), *shared),
     )
-    new_near, acc = call(
-        functools.partial(update_kernel, (1,), ()),
-        (rows, sums),
-        (SM,),
-        (pos, near, swap_core(near), *shared, acc),
-    )
-    far, new_near = lax.optimization_barrier((far, new_near))
-    new_memory, grad = call(
-        functools.partial(update_kernel, (3, 2), (0, 1)),
-        (sds((1024, 256), F32), sds((32, 8, 512), F32)),
-        (SM,),
-        (pos, back, swap_core(back), far, swap_core(far), *shared, new_own, new_near, hot_own, acc),
-        (pltpu.VMEM((128, 1024), F32),),
-    )
+    near, far, back, new_own = lax.optimization_barrier((near, far, back, new_own))
+    parts = (back, swap_core(back), far, swap_core(far), near, swap_core(near))
+    new_memory, grad = last_update(pos, parts, shared, (new_own,), hot_own, acc)
 
     grad = lax.all_to_all(grad, "node", split_axis=0, concat_axis=0, tiled=True)
     grad, hot_new = call(piece_kernel, (sds((32, 8, 384), F32), sds((32, 8, 128), F32)), (), (grad,))

time: 155 us -> 154 us (level)
  waiting for transfers between devices: 43.2 us -> 48.6 us
  starting transfers between devices: 64 us -> 59.3 us
  Pallas kernels: 24.9 us -> 23.2 us
    ppermute x12, waiting for transfers between devices: 15.1 us -> 20.4 us  [shift_x(): return lax.ppermute(v, 'rep', [(k, (k + 2 * d) % 8) for k in range(8)])]
    ppermute x14, starting transfers between devices: 29 us -> 24.7 us  [swap_core(): return lax.ppermute(v, 'rep', [(k, k ^ 1) for k in range(8)])]
    pallas_call x10 -> x9, Pallas kernels: 24.9 us -> 23.2 us  [call(): pl.pallas_call(body, out_shape=out_shape, in_specs=list(places) + [VM] *...]
  transfers between devices with their start and end apart: 29 -> 29, of which waited for: 11 -> 14; matrix products, arithmetic and copies ran while one was open for 2% -> 2% of each run, Pallas kernels for 6% -> 5%
where the time goes in v6:
time: 154 us; the launch traced here: 153 us
  starting transfers between devices  59.3 us (39%)
  waiting for transfers between devices  48.6 us (32%)
  Pallas kernels  23.2 us (15%)
  blocking collectives  18.1 us (12%)
  local copies, waits for them, and re-layouts  2.8 us (2%)
    ppermute x14, starting transfers between devices, swap_core(): return lax.ppermute(v, 'rep', [(k, k ^ 1) for k in range(8)])  24.7 us
    pallas_call x9, Pallas kernels, call(): pl.pallas_call(body, out_shape=out_shape, in_specs=list(places) + [VM] *...  23.2 us
    ppermute x1, waiting for transfers between devices, on_device(): spill = lax.ppermute(spill, 'node', [(k, (k + 1) % 32) for k in range(32)])  22.9 us
    ppermute x12, waiting for transfers between devices, shift_x(): return lax.ppermute(v, 'rep', [(k, (k + 2 * d) % 8) for k in range(8)])  20.4 us
    all_to_all x1, blocking collectives, on_device(): grad = lax.all_to_all(grad, 'node', split_axis=0, concat_axis=0, tiled=True)  18.1 us
    ppermute x12, starting transfers between devices, shift_x(): return lax.ppermute(v, 'rep', [(k, (k + 2 * d) % 8) for k in range(8)])  12.6 us
    all_to_all x1, starting transfers between devices, on_device(): recv = lax.all_to_all(send, 'node', split_axis=0, concat_axis=0, tiled=True)  12.2 us
    all_to_all x1, starting transfers between devices, on_device(): grad = lax.all_to_all(grad, 'node', split_axis=0, concat_axis=0, tiled=True)  8.26 us
  transfers between devices with their start and end apart: 29, of which 14 were waited for; matrix products, arithmetic and copies ran while one was open for 2% of the time, Pallas kernels for 5%

profile of v6, /device:TPU:1, one launch (start us, length us, event | category | flops | bytes accessed | tf_op | source)
XLA Modules:
  0.0 153.3 jit_solution(15958667433205015088)
XLA Ops:
  0.6 6.3 %shard_map.192 = (bf16[32,144,128]{2,1,0:T(8,128)(2,1)}, f32[96,512]{1,0:T(8,128)}) custom-call(s32[1]{0:T(128)} %bitcast.3.pos, f32[1024,256]{1,0:T(8,128)} %refs_6_.3, bf16[1024,128]{1,0:T(8,128)(2,1)} %edge_h.1, bf16[512,512]{1,0:T(8,128)(2,1)} %w_h.1, s32[1,1024]{1,0:T(1,128)} %bitcast.17, s32[1,1024]{1,0:T(1,128)} %bitcast.18, s32[1,1024]{1,0:T(1,128)} %bitcast.19, ...), custom_call_target="tpu_custom_call" | custom-call | tf_op jit(solution)/shard_map/pallas_call | solution.py:34
  7.0 0.0 copy-start.6
  7.0 0.0 copy-start.4
  7.0 0.0 copy-start.5
  7.0 12.2 %all-to-all-start = ((bf16[32,144,128]{2,1,0:T(8,128)(2,1)}), bf16[32,144,128]{2,1,0:T(8,128)(2,1)S(1)}, u32[]{:S(2)}, u32[]{:S(2)}) async-start(bf16[32,144,128]{2,1,0:T(8,128)(2,1)} %get-tuple-element.39), calls=%async_computation | async-start | bytes 2359296 | tf_op jit(solution)/shard_map/all_to_all | solution.py:399
  19.2 1.0 collective-permute-start
  20.3 0.2 select_reduce_fusion
  20.5 0.9 collective-permute-done
  21.4 1.6 %collective-permute-start.1 = (f32[16,512]{1,0:T(8,128)S(1)}, f32[16,512]{1,0:T(8,128)S(1)}, u32[]{:S(2)}, u32[]{:S(2)}) collective-permute-start(f32[16,512]{1,0:T(8,128)S(1)} %constant_dynamic-slice_fusion), channel_id=1, source_target_pairs={{0,8},{8,16},{16,24},{24,32},{32,40},{40,48},{48,56},{56,64},{64,7... | collective-permute-start | bytes 98312 | tf_op jit(solution)/shard_map/ppermute | solution.py:403
  23.0 0.8 gather_fusion.1
  23.7 2.0 %gather_fusion = f32[128,256]{1,0:T(8,128)S(1)} fusion(f32[1024,256]{1,0:T(8,128)} %param.18, s32[1024]{0:T(1024)S(1)} %pad_clamp_fusion), kind=kCustom, calls=%fused_computation | custom fusion | bytes 262656 | tf_op jit(solution)/shard_map/jit(_take)/gather | solution.py:407
  25.7 22.9 %collective-permute-done.1 = f32[16,512]{1,0:T(8,128)S(1)} collective-permute-done((f32[16,512]{1,0:T(8,128)S(1)}, f32[16,512]{1,0:T(8,128)S(1)}, u32[]{:S(2)}, u32[]{:S(2)}) %collective-permute-start.1) | collective-permute-done | bytes 32800 | tf_op jit(solution)/shard_map/ppermute | solution.py:403
  48.6 3.6 %collective-permute-start.2 = (bf16[32,144,128]{2,1,0:T(8,128)(2,1)S(1)}, bf16[32,144,128]{2,1,0:T(8,128)(2,1)S(1)}, u32[]{:S(2)}, u32[]{:S(2)}) collective-permute-start(bf16[32,144,128]{2,1,0:T(8,128)(2,1)S(1)} %all-to-all-done.own), channel_id=1, source_target_pairs={{0,1},{1,0},{2,3},{3,2},{4,5},{5,4},{6,7},{7,6},{8,9},{9,8},{10,11... | collective-permute-start | bytes 3538952 | tf_op jit(solution)/shard_map/ppermute | solution.py:324
  52.2 0.1 pad_add_fusion.pos
  52.2 2.4 %collective-permute-done.2.peer = bf16[32,144,128]{2,1,0:T(8,128)(2,1)S(1)} collective-permute-done((bf16[32,144,128]{2,1,0:T(8,128)(2,1)S(1)}, bf16[32,144,128]{2,1,0:T(8,128)(2,1)S(1)}, u32[]{:S(2)}, u32[]{:S(2)}) %collective-permute-start.2) | collective-permute-done | bytes 1179680 | tf_op jit(solution)/shard_map/ppermute | solution.py:324
  54.6 2.4 %shard_map.193 = (f32[136,512]{1,0:T(8,128)S(1)}, f32[136,512]{1,0:T(8,128)S(1)}, f32[136,512]{1,0:T(8,128)S(1)}, f32[136,512]{1,0:T(8,128)S(1)}) custom-call(s32[3]{0:T(128)S(1)} %pad_add_fusion.pos, bf16[32,144,128]{2,1,0:T(8,128)(2,1)S(1)} %all-to-all-done.own, bf16[32,144,128]{2,1,0:T(8,128)(2,1)S(1)} %collective-permute-done.2.peer, ...), custom_call_target="tpu_custom_call" | custom-call | tf_op jit(solution)/shard_map/pallas_call | solution.py:34
  57.0 0.0 copy-start
  57.0 1.3 collective-permute-start.3
  58.3 2.5 %collective-permute-start.4 = (f32[136,512]{1,0:T(8,128)S(1)}, f32[136,512]{1,0:T(8,128)S(1)}, u32[]{:S(2)}, u32[]{:S(2)}) collective-permute-start(f32[136,512]{1,0:T(8,128)S(1)} %get-tuple-element.43), channel_id=1, source_target_pairs={{0,4},{1,5},{2,6},{3,7},{4,0},{5,1},{6,2},{7,3},{8,12},{9,13},{10,... | collective-permute-start | bytes 835592 | tf_op jit(solution)/shard_map/ppermute | solution.py:328
  60.8 1.1 collective-permute-start.5
  61.9 4.3 %collective-permute-done.3.p1_h = f32[136,512]{1,0:T(8,128)S(1)} collective-permute-done((f32[136,512]{1,0:T(8,128)S(1)}, f32[136,512]{1,0:T(8,128)S(1)}, u32[]{:S(2)}, u32[]{:S(2)}) %collective-permute-start.3) | collective-permute-done | bytes 278560 | tf_op jit(solution)/shard_map/ppermute | solution.py:328
  66.2 7.0 %collective-permute-done.4.p2_h = f32[136,512]{1,0:T(8,128)S(1)} collective-permute-done((f32[136,512]{1,0:T(8,128)S(1)}, f32[136,512]{1,0:T(8,128)S(1)}, u32[]{:S(2)}, u32[]{:S(2)}) %collective-permute-start.4) | collective-permute-done | bytes 278560 | tf_op jit(solution)/shard_map/ppermute | solution.py:328
  73.1 0.6 shard_map.194.refs_0_
  73.7 1.3 collective-permute-start.9
  75.0 2.0 %collective-permute-start.8 = (bf16[144,512]{1,0:T(8,128)(2,1)S(1)}, bf16[144,512]{1,0:T(8,128)(2,1)S(1)}, u32[]{:S(2)}, u32[]{:S(2)}) collective-permute-start(bf16[144,512]{1,0:T(8,128)(2,1)S(1)} %shard_map.194.refs_0_), channel_id=1, source_target_pairs={{0,6},{1,7},{2,0},{3,1},{4,2},{5,3},{6,4},{7,5},{8,14},{9,15},{10,... | collective-permute-start | bytes 442376 | tf_op jit(solution)/shard_map/ppermute | solution.py:328
  77.0 0.9 collective-permute-start.7
  77.9 0.4 collective-permute-start.6
  78.3 2.1 %shard_map.195 = (f32[256,256]{1,0:T(8,128)S(1)}, f32[8,128]{1,0:T(8,128)S(1)}, f32[128,1024]{1,0:T(8,128)S(1)}) custom-call(s32[3]{0:T(128)S(1)} %pad_add_fusion.pos, bf16[144,512]{1,0:T(8,128)(2,1)S(1)} %shard_map.194.refs_0_, bf16[144,512]{1,0:T(8,128)(2,1)S(1)} %collective-permute-done.9.refs_1_, f32[1024,256]{1,0:T(8,128)S(1)} %copy-done, ...), custom_call_target="tpu_custom_call" | custom-call | tf_op jit(solution)/shard_map/pallas_call | solution.py:34
  80.4 0.1 collective-permute-done.8.refs_0_
  80.5 3.1 %collective-permute-done.7.refs_2_ = bf16[144,512]{1,0:T(8,128)(2,1)S(1)} collective-permute-done((bf16[144,512]{1,0:T(8,128)(2,1)S(1)}, bf16[144,512]{1,0:T(8,128)(2,1)S(1)}, u32[]{:S(2)}, u32[]{:S(2)}) %collective-permute-start.7) | collective-permute-done | bytes 147488 | tf_op jit(solution)/shard_map/ppermute | solution.py:328
  83.6 3.8 %collective-permute-done.6.refs_4_ = bf16[144,512]{1,0:T(8,128)(2,1)S(1)} collective-permute-done((bf16[144,512]{1,0:T(8,128)(2,1)S(1)}, bf16[144,512]{1,0:T(8,128)(2,1)S(1)}, u32[]{:S(2)}, u32[]{:S(2)}) %collective-permute-start.6) | collective-permute-done | bytes 147488 | tf_op jit(solution)/shard_map/ppermute | solution.py:328
  87.4 0.5 collective-permute-start.10
  87.9 0.0 collective-permute-start.11
  87.9 0.5 collective-permute-start.12
  88.4 0.5 collective-permute-done.10.refs_1_
  88.9 0.4 collective-permute-done.11.refs_3_
  89.3 0.2 collective-permute-done.12.refs_5_
  89.5 4.0 %shard_map.196 = (f32[1024,256]{1,0:T(8,128)}, f32[32,8,512]{2,1,0:T(8,128)S(1)}) custom-call(s32[3]{0:T(128)S(1)} %pad_add_fusion.pos, bf16[144,512]{1,0:T(8,128)(2,1)S(1)} %collective-permute-done.8.refs_0_, bf16[144,512]{1,0:T(8,128)(2,1)S(1)} %collective-permute-done.10.refs_1_, bf16[144,512]{1,0:T(8,128)(2,1)S(1)} %collective-permute-done.7.refs_2_, ...), custom_call_target="tpu_custom_call" | custom-call | tf_op jit(solution)/shard_map/pallas_call | solution.py:34
  93.5 18.1 %all_to_all.15.parts = f32[32,8,512]{2,1,0:T(8,128)S(1)} all-to-all(f32[32,8,512]{2,1,0:T(8,128)S(1)} %get-tuple-element.56), channel_id=1, replica_groups=mesh['node'=32,'rep'=8] {'node'}, dimensions={0} | all-to-all | bytes 1048576 | tf_op jit(solution)/shard_map/all_to_all | solution.py:440
  111.6 0.8 shard_map.197
  112.4 8.3 %all-to-all-start.2 = ((f32[32,8,384]{2,1,0:T(8,128)}), f32[32,8,384]{2,1,0:T(8,128)S(1)}, u32[]{:S(2)}, u32[]{:S(2)}) async-start(f32[32,8,384]{2,1,0:T(8,128)} %get-tuple-element.57), calls=%async_computation.2 | async-start | bytes 786432 | tf_op jit(solution)/shard_map/all_to_all | solution.py:442
  120.6 0.4 collective-permute-start.15
  121.0 0.9 collective-permute-start.14
  121.9 0.5 collective-permute-start.13
  122.4 2.0 %collective-permute-start.16 = (f32[32,8,128]{2,1,0:T(8,128)S(1)}, f32[32,8,128]{2,1,0:T(8,128)S(1)}, u32[]{:S(2)}, u32[]{:S(2)}) collective-permute-start(f32[32,8,128]{2,1,0:T(8,128)S(1)} %get-tuple-element.60.a0), channel_id=1, source_target_pairs={{0,1},{1,0},{2,3},{3,2},{4,5},{5,4},{6,7},{7,6},{8,9},{9,8},{10,11... | collective-permute-start | bytes 393224 | tf_op jit(solution)/shard_map/ppermute | solution.py:324
  124.4 0.1 collective-permute-done.15.a3
  124.5 3.5 %collective-permute-start.19 = (f32[32,8,128]{2,1,0:T(8,128)S(1)}, f32[32,8,128]{2,1,0:T(8,128)S(1)}, u32[]{:S(2)}, u32[]{:S(2)}) collective-permute-start(f32[32,8,128]{2,1,0:T(8,128)S(1)} %collective-permute-done.15.a3), channel_id=1, source_target_pairs={{0,1},{1,0},{2,3},{3,2},{4,5},{5,4},{6,7},{7,6},{8,9},{9,8},{10,11... | collective-permute-start | bytes 393224 | tf_op jit(solution)/shard_map/ppermute | solution.py:324
  128.0 0.0 collective-permute-done.14.a2
  128.0 2.2 %collective-permute-start.18 = (f32[32,8,128]{2,1,0:T(8,128)S(1)}, f32[32,8,128]{2,1,0:T(8,128)S(1)}, u32[]{:S(2)}, u32[]{:S(2)}) collective-permute-start(f32[32,8,128]{2,1,0:T(8,128)S(1)} %collective-permute-done.14.a2), channel_id=1, source_target_pairs={{0,1},{1,0},{2,3},{3,2},{4,5},{5,4},{6,7},{7,6},{8,9},{9,8},{10,11... | collective-permute-start | bytes 393224 | tf_op jit(solution)/shard_map/ppermute | solution.py:324
  130.2 0.0 collective-permute-done.13.a1
  130.2 1.0 collective-permute-start.17
  131.3 0.0 collective-permute-done.19.b3
  131.3 1.0 collective-permute-done.17.b1
  132.3 1.2 collective-permute-start.20
  133.4 0.9 collective-permute-start.25
  134.3 0.6 collective-permute-start.22
  134.9 4.8 %collective-permute-start.21 = (f32[24,8,384]{2,1,0:T(8,128)S(1)}, f32[24,8,384]{2,1,0:T(8,128)S(1)}, u32[]{:S(2)}, u32[]{:S(2)}) collective-permute-start(f32[24,8,384]{2,1,0:T(8,128)S(1)} %slice.2.a0), channel_id=1, source_target_pairs={{0,1},{1,0},{2,3},{3,2},{4,5},{5,4},{6,7},{7,6},{8,9},{9,8},{10,11... | collective-permute-start | bytes 884744 | tf_op jit(solution)/shard_map/ppermute | solution.py:324
  139.7 3.9 %shard_map.198 = f32[1024,256]{1,0:T(8,128)} custom-call(s32[3]{0:T(128)S(1)} %pad_add_fusion.pos, s32[1,1024]{1,0:T(1,128)S(1)} %bitcast.16, f32[32,8,128]{2,1,0:T(8,128)S(1)} %get-tuple-element.60.a0, f32[32,8,128]{2,1,0:T(8,128)S(1)} %collective-permute-done.13.a1, f32[32,8,128]{2,1,0:T(8,128)S(1)} %collective-permute-done.14.a2, ...), custom_call_target="tpu_custom_call" | custom-call | tf_op jit(solution)/shard_map/pallas_call | solution.py:34
  143.5 2.0 %collective-permute-done.25.a3 = f32[24,8,384]{2,1,0:T(8,128)S(1)} collective-permute-done((f32[24,8,384]{2,1,0:T(8,128)S(1)}, f32[24,8,384]{2,1,0:T(8,128)S(1)}, u32[]{:S(2)}, u32[]{:S(2)}) %collective-permute-start.25) | collective-permute-done | bytes 294944 | tf_op jit(solution)/shard_map/ppermute | solution.py:328
  145.5 2.9 %collective-permute-start.26 = (f32[24,8,384]{2,1,0:T(8,128)S(1)}, f32[24,8,384]{2,1,0:T(8,128)S(1)}, u32[]{:S(2)}, u32[]{:S(2)}) collective-permute-start(f32[24,8,384]{2,1,0:T(8,128)S(1)} %collective-permute-done.25.a3), channel_id=1, source_target_pairs={{0,1},{1,0},{2,3},{3,2},{4,5},{5,4},{6,7},{7,6},{8,9},{9,8},{10,11... | collective-permute-start | bytes 884744 | tf_op jit(solution)/shard_map/ppermute | solution.py:324
  148.4 1.4 collective-permute-start.23
  149.8 0.0 collective-permute-start.24
  149.8 1.6 %shard_map.199 = (f32[512,768]{1,0:T(8,128)}, f32[256,768]{1,0:T(8,128)}) custom-call(s32[3]{0:T(128)S(1)} %pad_add_fusion.pos, f32[24,8,384]{2,1,0:T(8,128)S(1)} %slice.2.a0, f32[24,8,384]{2,1,0:T(8,128)S(1)} %collective-permute-done.22.a1, f32[24,8,384]{2,1,0:T(8,128)S(1)} %collective-permute-done.20.a2, f32[24,8,384]{2,1,0:T(8,128)S(1)} %collective-permute-done.25.a3), custom_call_target="tpu_custom_call" | custom-call | tf_op jit(solution)/shard_map/pallas_call | solution.py:34
  151.5 1.6 %shard_map.200 = (f32[512,768]{1,0:T(8,128)}, f32[256,768]{1,0:T(8,128)}) custom-call(s32[3]{0:T(128)S(1)} %pad_add_fusion.pos, f32[24,8,384]{2,1,0:T(8,128)S(1)} %collective-permute-done.21.a0, f32[24,8,384]{2,1,0:T(8,128)S(1)} %collective-permute-done.23.a1, ...), custom_call_target="tpu_custom_call", output_to_operand_aliasing={{0}: (5, {}), {1}: (6, {})} | custom-call | tf_op jit(solution)/shard_map/pallas_call | solution.py:34
  (27 shorter events, 0.1 us)
Async XLA Ops:
  7.0 12.2 %copy-start.6 = (f32[96,512]{1,0:T(8,128)S(1)}, f32[96,512]{1,0:T(8,128)}, u32[]{:S(2)}) copy-start(f32[96,512]{1,0:T(8,128)} %get-tuple-element.40) | copy-start | bytes 589828
  7.0 13.3 %copy-start.4 = (s32[1024]{0:T(1024)S(1)}, s32[1024]{0:T(1024)}, u32[]{:S(2)}) copy-start(s32[1024]{0:T(1024)} %param.27) | copy-start | bytes 12292
  7.0 16.0 %copy-start.5 = (f32[1024,256]{1,0:T(8,128)S(1)}, f32[1024,256]{1,0:T(8,128)}, u32[]{:S(2)}) copy-start(f32[1024,256]{1,0:T(8,128)} %param.20) | copy-start | bytes 3145732
  7.0 41.6 %all-to-all-start = ((bf16[32,144,128]{2,1,0:T(8,128)(2,1)}), bf16[32,144,128]{2,1,0:T(8,128)(2,1)S(1)}, u32[]{:S(2)}, u32[]{:S(2)}) async-start(bf16[32,144,128]{2,1,0:T(8,128)(2,1)} %get-tuple-element.39), calls=%async_computation | async-start | bytes 2359296 | tf_op jit(solution)/shard_map/all_to_all | solution.py:399
  19.2 2.1 %collective-permute-start = (f32[96,512]{1,0:T(8,128)S(1)}, f32[96,512]{1,0:T(8,128)S(1)}, u32[]{:S(2)}, u32[]{:S(2)}) collective-permute-start(f32[96,512]{1,0:T(8,128)S(1)} %copy-done.6), channel_id=1, source_target_pairs={{0,1},{1,0},{2,3},{3,2},{4,5},{5,4},{6,7},{7,6},{8,9},{9,8},{10,11... | collective-permute-start | bytes 589832 | tf_op jit(solution)/shard_map/ppermute | solution.py:324
  21.4 27.2 %collective-permute-start.1 = (f32[16,512]{1,0:T(8,128)S(1)}, f32[16,512]{1,0:T(8,128)S(1)}, u32[]{:S(2)}, u32[]{:S(2)}) collective-permute-start(f32[16,512]{1,0:T(8,128)S(1)} %constant_dynamic-slice_fusion), channel_id=1, source_target_pairs={{0,8},{8,16},{16,24},{24,32},{32,40},{40,48},{48,56},{56,64},{64,7... | collective-permute-start | bytes 98312 | tf_op jit(solution)/shard_map/ppermute | solution.py:403
  48.6 6.1 %collective-permute-start.2 = (bf16[32,144,128]{2,1,0:T(8,128)(2,1)S(1)}, bf16[32,144,128]{2,1,0:T(8,128)(2,1)S(1)}, u32[]{:S(2)}, u32[]{:S(2)}) collective-permute-start(bf16[32,144,128]{2,1,0:T(8,128)(2,1)S(1)} %all-to-all-done.own), channel_id=1, source_target_pairs={{0,1},{1,0},{2,3},{3,2},{4,5},{5,4},{6,7},{7,6},{8,9},{9,8},{10,11... | collective-permute-start | bytes 3538952 | tf_op jit(solution)/shard_map/ppermute | solution.py:324
  54.6 23.6 %copy-start.1 = (f32[1024,256]{1,0:T(8,128)S(1)}, f32[1024,256]{1,0:T(8,128)}, u32[]{:S(2)}) copy-start(f32[1024,256]{1,0:T(8,128)} %refs_7_.3) | copy-start | bytes 3145732
  54.6 23.6 %copy-start.2 = (bf16[512,768]{1,0:T(8,128)(2,1)S(1)}, bf16[512,768]{1,0:T(8,128)(2,1)}, u32[]{:S(2)}) copy-start(bf16[512,768]{1,0:T(8,128)(2,1)} %refs_10_.1) | copy-start | bytes 2359300
  54.6 23.6 %copy-start.3 = (bf16[256,768]{1,0:T(8,128)(2,1)S(1)}, bf16[256,768]{1,0:T(8,128)(2,1)}, u32[]{:S(2)}) copy-start(bf16[256,768]{1,0:T(8,128)(2,1)} %refs_11_.1) | copy-start | bytes 1179652
  57.0 21.3 %copy-start = (f32[1024,256]{1,0:T(8,128)S(1)}, f32[1024,256]{1,0:T(8,128)}, u32[]{:S(2)}) copy-start(f32[1024,256]{1,0:T(8,128)} %refs_6_.3) | copy-start | bytes 3145732
  57.0 9.2 %collective-permute-start.3 = (f32[136,512]{1,0:T(8,128)S(1)}, f32[136,512]{1,0:T(8,128)S(1)}, u32[]{:S(2)}, u32[]{:S(2)}) collective-permute-start(f32[136,512]{1,0:T(8,128)S(1)} %get-tuple-element.42), channel_id=1, source_target_pairs={{0,2},{1,3},{2,4},{3,5},{4,6},{5,7},{6,0},{7,1},{8,10},{9,11},{10,... | collective-permute-start | bytes 835592 | tf_op jit(solution)/shard_map/ppermute | solution.py:328
  58.3 14.8 %collective-permute-start.4 = (f32[136,512]{1,0:T(8,128)S(1)}, f32[136,512]{1,0:T(8,128)S(1)}, u32[]{:S(2)}, u32[]{:S(2)}) collective-permute-start(f32[136,512]{1,0:T(8,128)S(1)} %get-tuple-element.43), channel_id=1, source_target_pairs={{0,4},{1,5},{2,6},{3,7},{4,0},{5,1},{6,2},{7,3},{8,12},{9,13},{10,... | collective-permute-start | bytes 835592 | tf_op jit(solution)/shard_map/ppermute | solution.py:328
  60.8 12.4 %collective-permute-start.5 = (f32[136,512]{1,0:T(8,128)S(1)}, f32[136,512]{1,0:T(8,128)S(1)}, u32[]{:S(2)}, u32[]{:S(2)}) collective-permute-start(f32[136,512]{1,0:T(8,128)S(1)} %get-tuple-element.44), channel_id=1, source_target_pairs={{0,6},{1,7},{2,0},{3,1},{4,2},{5,3},{6,4},{7,5},{8,14},{9,15},{10,... | collective-permute-start | bytes 835592 | tf_op jit(solution)/shard_map/ppermute | solution.py:328
  73.7 4.5 %collective-permute-start.9 = (bf16[144,512]{1,0:T(8,128)(2,1)S(1)}, bf16[144,512]{1,0:T(8,128)(2,1)S(1)}, u32[]{:S(2)}, u32[]{:S(2)}) collective-permute-start(bf16[144,512]{1,0:T(8,128)(2,1)S(1)} %shard_map.194.refs_0_), channel_id=1, source_target_pairs={{0,1},{1,0},{2,3},{3,2},{4,5},{5,4},{6,7},{7,6},{8,9},{9,8},{10,11... | collective-permute-start | bytes 442376 | tf_op jit(solution)/shard_map/ppermute | solution.py:324
  75.0 5.5 %collective-permute-start.8 = (bf16[144,512]{1,0:T(8,128)(2,1)S(1)}, bf16[144,512]{1,0:T(8,128)(2,1)S(1)}, u32[]{:S(2)}, u32[]{:S(2)}) collective-permute-start(bf16[144,512]{1,0:T(8,128)(2,1)S(1)} %shard_map.194.refs_0_), channel_id=1, source_target_pairs={{0,6},{1,7},{2,0},{3,1},{4,2},{5,3},{6,4},{7,5},{8,14},{9,15},{10,... | collective-permute-start | bytes 442376 | tf_op jit(solution)/shard_map/ppermute | solution.py:328
  77.0 6.6 %collective-permute-start.7 = (bf16[144,512]{1,0:T(8,128)(2,1)S(1)}, bf16[144,512]{1,0:T(8,128)(2,1)S(1)}, u32[]{:S(2)}, u32[]{:S(2)}) collective-permute-start(bf16[144,512]{1,0:T(8,128)(2,1)S(1)} %shard_map.194.refs_0_), channel_id=1, source_target_pairs={{0,4},{1,5},{2,6},{3,7},{4,0},{5,1},{6,2},{7,3},{8,12},{9,13},{10,... | collective-permute-start | bytes 442376 | tf_op jit(solution)/shard_map/ppermute | solution.py:328
  77.9 9.6 %collective-permute-start.6 = (bf16[144,512]{1,0:T(8,128)(2,1)S(1)}, bf16[144,512]{1,0:T(8,128)(2,1)S(1)}, u32[]{:S(2)}, u32[]{:S(2)}) collective-permute-start(bf16[144,512]{1,0:T(8,128)(2,1)S(1)} %shard_map.194.refs_0_), channel_id=1, source_target_pairs={{0,2},{1,3},{2,4},{3,5},{4,6},{5,7},{6,0},{7,1},{8,10},{9,11},{10,... | collective-permute-start | bytes 442376 | tf_op jit(solution)/shard_map/ppermute | solution.py:328
  87.4 1.5 collective-permute-start.10
  87.9 1.4 collective-permute-start.11
  87.9 1.6 %collective-permute-start.12 = (bf16[144,512]{1,0:T(8,128)(2,1)S(1)}, bf16[144,512]{1,0:T(8,128)(2,1)S(1)}, u32[]{:S(2)}, u32[]{:S(2)}) collective-permute-start(bf16[144,512]{1,0:T(8,128)(2,1)S(1)} %collective-permute-done.6.refs_4_), channel_id=1, source_target_pairs={{0,1},{1,0},{2,3},{3,2},{4,5},{5,4},{6,7},{7,6},{8,9},{9,8},{10,11... | collective-permute-start | bytes 442376 | tf_op jit(solution)/shard_map/ppermute | solution.py:324
  112.4 19.9 %all-to-all-start.2 = ((f32[32,8,384]{2,1,0:T(8,128)}), f32[32,8,384]{2,1,0:T(8,128)S(1)}, u32[]{:S(2)}, u32[]{:S(2)}) async-start(f32[32,8,384]{2,1,0:T(8,128)} %get-tuple-element.57), calls=%async_computation.2 | async-start | bytes 786432 | tf_op jit(solution)/shard_map/all_to_all | solution.py:442
  120.6 3.9 %collective-permute-start.15 = (f32[32,8,128]{2,1,0:T(8,128)S(1)}, f32[32,8,128]{2,1,0:T(8,128)S(1)}, u32[]{:S(2)}, u32[]{:S(2)}) collective-permute-start(f32[32,8,128]{2,1,0:T(8,128)S(1)} %get-tuple-element.60.a0), channel_id=1, source_target_pairs={{0,6},{1,7},{2,0},{3,1},{4,2},{5,3},{6,4},{7,5},{8,14},{9,15},{10,... | collective-permute-start | bytes 393224 | tf_op jit(solution)/shard_map/ppermute | solution.py:328
  121.0 7.0 %collective-permute-start.14 = (f32[32,8,128]{2,1,0:T(8,128)S(1)}, f32[32,8,128]{2,1,0:T(8,128)S(1)}, u32[]{:S(2)}, u32[]{:S(2)}) collective-permute-start(f32[32,8,128]{2,1,0:T(8,128)S(1)} %get-tuple-element.60.a0), channel_id=1, source_target_pairs={{0,4},{1,5},{2,6},{3,7},{4,0},{5,1},{6,2},{7,3},{8,12},{9,13},{10,... | collective-permute-start | bytes 393224 | tf_op jit(solution)/shard_map/ppermute | solution.py:328
  121.9 8.3 %collective-permute-start.13 = (f32[32,8,128]{2,1,0:T(8,128)S(1)}, f32[32,8,128]{2,1,0:T(8,128)S(1)}, u32[]{:S(2)}, u32[]{:S(2)}) collective-permute-start(f32[32,8,128]{2,1,0:T(8,128)S(1)} %get-tuple-element.60.a0), channel_id=1, source_target_pairs={{0,2},{1,3},{2,4},{3,5},{4,6},{5,7},{6,0},{7,1},{8,10},{9,11},{10,... | collective-permute-start | bytes 393224 | tf_op jit(solution)/shard_map/ppermute | solution.py:328
  122.4 8.8 %collective-permute-start.16 = (f32[32,8,128]{2,1,0:T(8,128)S(1)}, f32[32,8,128]{2,1,0:T(8,128)S(1)}, u32[]{:S(2)}, u32[]{:S(2)}) collective-permute-start(f32[32,8,128]{2,1,0:T(8,128)S(1)} %get-tuple-element.60.a0), channel_id=1, source_target_pairs={{0,1},{1,0},{2,3},{3,2},{4,5},{5,4},{6,7},{7,6},{8,9},{9,8},{10,11... | collective-permute-start | bytes 393224 | tf_op jit(solution)/shard_map/ppermute | solution.py:324
  124.5 6.7 %collective-permute-start.19 = (f32[32,8,128]{2,1,0:T(8,128)S(1)}, f32[32,8,128]{2,1,0:T(8,128)S(1)}, u32[]{:S(2)}, u32[]{:S(2)}) collective-permute-start(f32[32,8,128]{2,1,0:T(8,128)S(1)} %collective-permute-done.15.a3), channel_id=1, source_target_pairs={{0,1},{1,0},{2,3},{3,2},{4,5},{5,4},{6,7},{7,6},{8,9},{9,8},{10,11... | collective-permute-start | bytes 393224 | tf_op jit(solution)/shard_map/ppermute | solution.py:324
  128.0 3.2 %collective-permute-start.18 = (f32[32,8,128]{2,1,0:T(8,128)S(1)}, f32[32,8,128]{2,1,0:T(8,128)S(1)}, u32[]{:S(2)}, u32[]{:S(2)}) collective-permute-start(f32[32,8,128]{2,1,0:T(8,128)S(1)} %collective-permute-done.14.a2), channel_id=1, source_target_pairs={{0,1},{1,0},{2,3},{3,2},{4,5},{5,4},{6,7},{7,6},{8,9},{9,8},{10,11... | collective-permute-start | bytes 393224 | tf_op jit(solution)/shard_map/ppermute | solution.py:324
  130.2 2.0 %collective-permute-start.17 = (f32[32,8,128]{2,1,0:T(8,128)S(1)}, f32[32,8,128]{2,1,0:T(8,128)S(1)}, u32[]{:S(2)}, u32[]{:S(2)}) collective-permute-start(f32[32,8,128]{2,1,0:T(8,128)S(1)} %collective-permute-done.13.a1), channel_id=1, source_target_pairs={{0,1},{1,0},{2,3},{3,2},{4,5},{5,4},{6,7},{7,6},{8,9},{9,8},{10,11... | collective-permute-start | bytes 393224 | tf_op jit(solution)/shard_map/ppermute | solution.py:324
  132.3 11.3 %collective-permute-start.20 = (f32[24,8,384]{2,1,0:T(8,128)S(1)}, f32[24,8,384]{2,1,0:T(8,128)S(1)}, u32[]{:S(2)}, u32[]{:S(2)}) collective-permute-start(f32[24,8,384]{2,1,0:T(8,128)S(1)} %slice.2.a0), channel_id=1, source_target_pairs={{0,4},{1,5},{2,6},{3,7},{4,0},{5,1},{6,2},{7,3},{8,12},{9,13},{10,... | collective-permute-start | bytes 884744 | tf_op jit(solution)/shard_map/ppermute | solution.py:328
  133.4 12.1 %collective-permute-start.25 = (f32[24,8,384]{2,1,0:T(8,128)S(1)}, f32[24,8,384]{2,1,0:T(8,128)S(1)}, u32[]{:S(2)}, u32[]{:S(2)}) collective-permute-start(f32[24,8,384]{2,1,0:T(8,128)S(1)} %slice.2.a0), channel_id=1, source_target_pairs={{0,6},{1,7},{2,0},{3,1},{4,2},{5,3},{6,4},{7,5},{8,14},{9,15},{10,... | collective-permute-start | bytes 884744 | tf_op jit(solution)/shard_map/ppermute | solution.py:328
  134.3 14.1 %collective-permute-start.22 = (f32[24,8,384]{2,1,0:T(8,128)S(1)}, f32[24,8,384]{2,1,0:T(8,128)S(1)}, u32[]{:S(2)}, u32[]{:S(2)}) collective-permute-start(f32[24,8,384]{2,1,0:T(8,128)S(1)} %slice.2.a0), channel_id=1, source_target_pairs={{0,2},{1,3},{2,4},{3,5},{4,6},{5,7},{6,0},{7,1},{8,10},{9,11},{10,... | collective-permute-start | bytes 884744 | tf_op jit(solution)/shard_map/ppermute | solution.py:328
  134.9 16.6 %collective-permute-start.21 = (f32[24,8,384]{2,1,0:T(8,128)S(1)}, f32[24,8,384]{2,1,0:T(8,128)S(1)}, u32[]{:S(2)}, u32[]{:S(2)}) collective-permute-start(f32[24,8,384]{2,1,0:T(8,128)S(1)} %slice.2.a0), channel_id=1, source_target_pairs={{0,1},{1,0},{2,3},{3,2},{4,5},{5,4},{6,7},{7,6},{8,9},{9,8},{10,11... | collective-permute-start | bytes 884744 | tf_op jit(solution)/shard_map/ppermute | solution.py:324
  145.5 6.0 %collective-permute-start.26 = (f32[24,8,384]{2,1,0:T(8,128)S(1)}, f32[24,8,384]{2,1,0:T(8,128)S(1)}, u32[]{:S(2)}, u32[]{:S(2)}) collective-permute-start(f32[24,8,384]{2,1,0:T(8,128)S(1)} %collective-permute-done.25.a3), channel_id=1, source_target_pairs={{0,1},{1,0},{2,3},{3,2},{4,5},{5,4},{6,7},{7,6},{8,9},{9,8},{10,11... | collective-permute-start | bytes 884744 | tf_op jit(solution)/shard_map/ppermute | solution.py:324
  148.4 3.1 %collective-permute-start.23 = (f32[24,8,384]{2,1,0:T(8,128)S(1)}, f32[24,8,384]{2,1,0:T(8,128)S(1)}, u32[]{:S(2)}, u32[]{:S(2)}) collective-permute-start(f32[24,8,384]{2,1,0:T(8,128)S(1)} %collective-permute-done.22.a1), channel_id=1, source_target_pairs={{0,1},{1,0},{2,3},{3,2},{4,5},{5,4},{6,7},{7,6},{8,9},{9,8},{10,11... | collective-permute-start | bytes 884744 | tf_op jit(solution)/shard_map/ppermute | solution.py:324
  149.8 1.7 %collective-permute-start.24 = (f32[24,8,384]{2,1,0:T(8,128)S(1)}, f32[24,8,384]{2,1,0:T(8,128)S(1)}, u32[]{:S(2)}, u32[]{:S(2)}) collective-permute-start(f32[24,8,384]{2,1,0:T(8,128)S(1)} %collective-permute-done.20.a2), channel_id=1, source_target_pairs={{0,1},{1,0},{2,3},{3,2},{4,5},{5,4},{6,7},{7,6},{8,9},{9,8},{10,11... | collective-permute-start | bytes 884744 | tf_op jit(solution)/shard_map/ppermute | solution.py:324

commit v7 on v6

--- a/solution.py
+++ b/solution.py
@@ -200,8 +200,8 @@
         for d, part in enumerate(group):
             block = 2 * ((x - d + 4) & 3) + c
             for n in range(32):
-                rows[block, 4 * n : 4 * n + 4, 0:128] = part[n, 0:4, :]
-                rows[block, 4 * n : 4 * n + 4, 128:256] = part[n, 4:8, :]
+                rows[block, 4 * n : 4 * n + 4, 0:128] = part[n, 0]
+                rows[block, 4 * n : 4 * n + 4, 128:256] = part[n, 1]
     name = column(ids[...]) - 32768
     at = 128 * ((name >> 2) & 7) + 4 * (name >> 5) + (name & 3)
     full = rows[...].reshape(1024, 256)
@@ -220,7 +220,7 @@
     mem, cot, hot_mem, hot_cot, w_in, w_hid = refs[:6]
     refs = refs[6:]
     if last:
-        olds, (own_hot, old_acc, new_h, grad, acc, new, sems) = refs[: len(done)], refs[len(done) :]
+        olds, (own_hot, old_acc, new_h, grad, acc, new, flat, sems) = refs[: len(done)], refs[len(done) :]
         stores = []
         for d, old in zip(done, olds):
             at = pl.ds(pl.multiple_of(256 * ((pos[0] - d + 4) & 3), 256), 256)
@@ -283,21 +283,27 @@
         total = acc[...] * GRAD_SCALE
         third = jnp.where(iota((128, 256), 0) < 64, total[:, 512:768], total[:, 768:1024])
         total = jnp.concatenate([total[:, 0:512], third], axis=1)
+        for c in range(6):
+            flat[96 * c : 96 * c + 96, :] = total[0:96, 128 * c : 128 * c + 128]
+        flat[576:640, :] = jnp.zeros((64, 128), F32)
         for p in range(32):
-            i, j = p // 2, p % 2
-            grad[p, :, 0:384] = total[8 * i : 8 * i + 8, 384 * j : 384 * j + 384]
-            grad[p, :, 384:512] = own_hot[...]
+            for j in range(5):
+                grad[p, j] = flat[20 * p + 4 * j : 20 * p + 4 * j + 4, :]
+            for j in range(2):
+                grad[p, 5 + j] = own_hot[4 * j : 4 * j + 4, :]
         for c in stores:
             c.wait()
 
 
 def piece_kernel(parts, out, hot):
-    total = parts[0, :, 0:384]
-    for k in range(1, 32):
-        total = total + parts[k, :, 0:384]
+    for j in range(5):
+        total = parts[0, j]
+        for k in range(1, 32):
+            total = total + parts[k, j]
+        for k in range(32):
+            out[k, j] = total
     for k in range(32):
-        out[k] = total
-        hot[k] = parts[k, :, 384:512]
+        hot[k] = parts[k, 5:7]
 
 
 def place_kernel(other, pos, a0, a1, a2, a3, *refs):
@@ -307,9 +313,9 @@
     stores = []
     for d, part in enumerate((a0, a1, a2, a3)):
         block = 2 * ((x - d + 4) & 3) + core
-        for p in range(24):
-            i, j = p // 2, p % 2
-            both[96 * d + 8 * i : 96 * d + 8 * i + 8, 384 * j : 384 * j + 384] = part[p]
+        for k in range(144):
+            i, c = 4 * k % 96, 4 * k // 96
+            both[96 * d + i : 96 * d + i + 4, 128 * c : 128 * c + 128] = part[k // 5, k % 5]
         for rows, at, dst in (
             (64, 96 * d, g_in.at[pl.ds(pl.multiple_of(block * 64, 64), 64)]),
             (32, 96 * d + 64, g_hid.at[pl.ds(pl.multiple_of(block * 32, 32), 32)]),
@@ -358,10 +364,13 @@
     sds = jax.ShapeDtypeStruct
     return call(
         functools.partial(update_kernel, (3, 2, 1), (0,)),
-        (sds((1024, 256), F32), sds((32, 8, 512), F32)),
+        (sds((1024, 256), F32), sds((32, 7, 4, 128), F32)),
         (SM,),
         (pos, *parts, *shared, *olds, hot_own, acc),
-        (pltpu.VMEM((128, 1024), F32), pltpu.VMEM((768, 256), F32), pltpu.SemaphoreType.DMA((4,))),
+        (
+            pltpu.VMEM((128, 1024), F32), pltpu.VMEM((768, 256), F32), pltpu.VMEM((640, 128), F32),
+            pltpu.SemaphoreType.DMA((4,)),
+        ),
         (ANY, VM),
     )
 
@@ -420,7 +429,7 @@
         agg_kernel,
         sds((144, 512), BF16),
         (ANY, ANY, ANY),
-        (*parts[1:], parts[0]),
+        (parts[2], parts[3], parts[1], parts[0]),
         (pltpu.VMEM((3, 136, 512), F32), pltpu.VMEM((144, 512), BF16), pltpu.SemaphoreType.DMA((4,))),
         ANY,
     )
@@ -433,12 +442,12 @@
         (SM,),
         (pos, agg, swap_core(agg), *shared),
     )
-    near, far, back, new_own = lax.optimization_barrier((near, far, back, new_own))
+    far, back, near, new_own = lax.optimization_barrier((far, back, near, new_own))
     parts = (back, swap_core(back), far, swap_core(far), near, swap_core(near))
     new_memory, grad = last_update(pos, parts, shared, (new_own,), hot_own, acc)
 
     grad = lax.all_to_all(grad, "node", split_axis=0, concat_axis=0, tiled=True)
-    grad, hot_new = call(piece_kernel, (sds((32, 8, 384), F32), sds((32, 8, 128), F32)), (), (grad,))
+    grad, hot_new = call(piece_kernel, (sds((32, 5, 4, 128), F32), sds((32, 2, 4, 128), F32)), (), (grad,))
     grad = lax.all_to_all(grad, "node", split_axis=0, concat_axis=0, tiled=True)
     hot_parts = gather_rep(hot_new)
     grad, hot_parts = lax.optimization_barrier((grad, hot_parts))
@@ -449,7 +458,7 @@
         (pos, hot_ids[None, :], *hot_parts),
         (pltpu.VMEM((8, 128, 256), F32),),
     )
-    own = [grad[0:24]] + [shift_x(grad[0:24], d) for d in (1, 2, 3)]
+    own = [grad[0:29]] + [shift_x(grad[0:29], d) for d in (1, 2, 3)]
     own[2], new_hot = lax.optimization_barrier((own[2], new_hot))
     places = (pltpu.VMEM((384, 768), F32), pltpu.SemaphoreType.DMA((8,)))
     grads = (sds((512, 768), F32), sds((256, 768), F32))

time: 154 us -> 152 us (0.987)
  starting transfers between devices: 59.3 us -> 56.9 us
    ppermute x14, starting transfers between devices: 24.7 us -> 21.7 us  [swap_core(): return lax.ppermute(v, 'rep', [(k, k ^ 1) for k in range(8)])]
  transfers between devices with their start and end apart: 29 -> 29, of which waited for: 14 -> 15; matrix products, arithmetic and copies ran while one was open for 2% -> 2% of each run, Pallas kernels for 5% -> 5%
where the time goes in v7:
time: 152 us
  starting transfers between devices  56.9 us (37%)
  waiting for transfers between devices  50 us (33%)
  Pallas kernels  23.3 us (15%)
  blocking collectives  17.2 us (11%)
  local copies, waits for them, and re-layouts  2.81 us (2%)
    pallas_call x9, Pallas kernels, call(): pl.pallas_call(body, out_shape=out_shape, in_specs=list(places) + [VM] *...  23.3 us
    ppermute x1, waiting for transfers between devices, on_device(): spill = lax.ppermute(spill, 'node', [(k, (k + 1) % 32) for k in range(32)])  22.9 us
    ppermute x12, waiting for transfers between devices, shift_x(): return lax.ppermute(v, 'rep', [(k, (k + 2 * d) % 8) for k in range(8)])  21.9 us
    ppermute x14, starting transfers between devices, swap_core(): return lax.ppermute(v, 'rep', [(k, k ^ 1) for k in range(8)])  21.7 us
    all_to_all x1, blocking collectives, on_device(): grad = lax.all_to_all(grad, 'node', split_axis=0, concat_axis=0, tiled=True)  17.2 us
    ppermute x12, starting transfers between devices, shift_x(): return lax.ppermute(v, 'rep', [(k, (k + 2 * d) % 8) for k in range(8)])  13.7 us
    all_to_all x1, starting transfers between devices, on_device(): recv = lax.all_to_all(send, 'node', split_axis=0, concat_axis=0, tiled=True)  12.2 us
    all_to_all x1, starting transfers between devices, on_device(): grad = lax.all_to_all(grad, 'node', split_axis=0, concat_axis=0, tiled=True)  7.72 us
  transfers between devices with their start and end apart: 29, of which 15 were waited for; matrix products, arithmetic and copies ran while one was open for 2% of the time, Pallas kernels for 5%

profile of v7, /device:TPU:1, one launch (start us, length us, event | category | flops | bytes accessed | tf_op | source)
XLA Modules:
  0.0 151.6 jit_solution(18324263747395850957)
XLA Ops:
  0.6 6.3 %shard_map.192 = (bf16[32,144,128]{2,1,0:T(8,128)(2,1)}, f32[96,512]{1,0:T(8,128)}) custom-call(s32[1]{0:T(128)} %bitcast.3.pos, f32[1024,256]{1,0:T(8,128)} %refs_6_.3, bf16[1024,128]{1,0:T(8,128)(2,1)} %edge_h.1, bf16[512,512]{1,0:T(8,128)(2,1)} %w_h.1, s32[1,1024]{1,0:T(1,128)} %bitcast.17, s32[1,1024]{1,0:T(1,128)} %bitcast.18, s32[1,1024]{1,0:T(1,128)} %bitcast.19, ...), custom_call_target="tpu_custom_call" | custom-call | tf_op jit(solution)/shard_map/pallas_call | solution.py:34
  7.0 0.0 copy-start.6
  7.0 0.0 copy-start.4
  7.0 0.0 copy-start.5
  7.0 12.2 %all-to-all-start = ((bf16[32,144,128]{2,1,0:T(8,128)(2,1)}), bf16[32,144,128]{2,1,0:T(8,128)(2,1)S(1)}, u32[]{:S(2)}, u32[]{:S(2)}) async-start(bf16[32,144,128]{2,1,0:T(8,128)(2,1)} %get-tuple-element.39), calls=%async_computation | async-start | bytes 2359296 | tf_op jit(solution)/shard_map/all_to_all | solution.py:408
  19.2 1.0 collective-permute-start
  20.3 0.2 select_reduce_fusion
  20.5 0.9 collective-permute-done
  21.4 1.6 %collective-permute-start.1 = (f32[16,512]{1,0:T(8,128)S(1)}, f32[16,512]{1,0:T(8,128)S(1)}, u32[]{:S(2)}, u32[]{:S(2)}) collective-permute-start(f32[16,512]{1,0:T(8,128)S(1)} %constant_dynamic-slice_fusion), channel_id=1, source_target_pairs={{0,8},{8,16},{16,24},{24,32},{32,40},{40,48},{48,56},{56,64},{64,7... | collective-permute-start | bytes 98312 | tf_op jit(solution)/shard_map/ppermute | solution.py:412
  23.0 0.8 gather_fusion.1
  23.7 2.0 %gather_fusion = f32[128,256]{1,0:T(8,128)S(1)} fusion(f32[1024,256]{1,0:T(8,128)} %param.18, s32[1024]{0:T(1024)S(1)} %pad_clamp_fusion), kind=kCustom, calls=%fused_computation | custom fusion | bytes 262656 | tf_op jit(solution)/shard_map/jit(_take)/gather | solution.py:416
  25.7 22.9 %collective-permute-done.1 = f32[16,512]{1,0:T(8,128)S(1)} collective-permute-done((f32[16,512]{1,0:T(8,128)S(1)}, f32[16,512]{1,0:T(8,128)S(1)}, u32[]{:S(2)}, u32[]{:S(2)}) %collective-permute-start.1) | collective-permute-done | bytes 32800 | tf_op jit(solution)/shard_map/ppermute | solution.py:412
  48.6 3.6 %collective-permute-start.2 = (bf16[32,144,128]{2,1,0:T(8,128)(2,1)S(1)}, bf16[32,144,128]{2,1,0:T(8,128)(2,1)S(1)}, u32[]{:S(2)}, u32[]{:S(2)}) collective-permute-start(bf16[32,144,128]{2,1,0:T(8,128)(2,1)S(1)} %all-to-all-done.own), channel_id=1, source_target_pairs={{0,1},{1,0},{2,3},{3,2},{4,5},{5,4},{6,7},{7,6},{8,9},{9,8},{10,11... | collective-permute-start | bytes 3538952 | tf_op jit(solution)/shard_map/ppermute | solution.py:330
  52.2 0.1 pad_add_fusion.pos
  52.2 2.4 %collective-permute-done.2.peer = bf16[32,144,128]{2,1,0:T(8,128)(2,1)S(1)} collective-permute-done((bf16[32,144,128]{2,1,0:T(8,128)(2,1)S(1)}, bf16[32,144,128]{2,1,0:T(8,128)(2,1)S(1)}, u32[]{:S(2)}, u32[]{:S(2)}) %collective-permute-start.2) | collective-permute-done | bytes 1179680 | tf_op jit(solution)/shard_map/ppermute | solution.py:330
  54.6 2.4 %shard_map.193 = (f32[136,512]{1,0:T(8,128)S(1)}, f32[136,512]{1,0:T(8,128)S(1)}, f32[136,512]{1,0:T(8,128)S(1)}, f32[136,512]{1,0:T(8,128)S(1)}) custom-call(s32[3]{0:T(128)S(1)} %pad_add_fusion.pos, bf16[32,144,128]{2,1,0:T(8,128)(2,1)S(1)} %all-to-all-done.own, bf16[32,144,128]{2,1,0:T(8,128)(2,1)S(1)} %collective-permute-done.2.peer, ...), custom_call_target="tpu_custom_call" | custom-call | tf_op jit(solution)/shard_map/pallas_call | solution.py:34
  57.0 0.0 copy-start
  57.0 2.8 %collective-permute-start.3 = (f32[136,512]{1,0:T(8,128)S(1)}, f32[136,512]{1,0:T(8,128)S(1)}, u32[]{:S(2)}, u32[]{:S(2)}) collective-permute-start(f32[136,512]{1,0:T(8,128)S(1)} %get-tuple-element.42), channel_id=1, source_target_pairs={{0,4},{1,5},{2,6},{3,7},{4,0},{5,1},{6,2},{7,3},{8,12},{9,13},{10,... | collective-permute-start | bytes 835592 | tf_op jit(solution)/shard_map/ppermute | solution.py:334
  59.9 0.9 collective-permute-start.4
  60.7 0.6 collective-permute-start.5
  61.3 5.2 %collective-permute-done.3.p1_h = f32[136,512]{1,0:T(8,128)S(1)} collective-permute-done((f32[136,512]{1,0:T(8,128)S(1)}, f32[136,512]{1,0:T(8,128)S(1)}, u32[]{:S(2)}, u32[]{:S(2)}) %collective-permute-start.3) | collective-permute-done | bytes 278560 | tf_op jit(solution)/shard_map/ppermute | solution.py:334
  66.5 6.1 %collective-permute-done.4.p2_h = f32[136,512]{1,0:T(8,128)S(1)} collective-permute-done((f32[136,512]{1,0:T(8,128)S(1)}, f32[136,512]{1,0:T(8,128)S(1)}, u32[]{:S(2)}, u32[]{:S(2)}) %collective-permute-start.4) | collective-permute-done | bytes 278560 | tf_op jit(solution)/shard_map/ppermute | solution.py:334
  72.6 0.6 collective-permute-done.5.p3_h
  73.2 0.6 shard_map.194.refs_0_
  73.7 0.7 collective-permute-start.9
  74.4 1.2 collective-permute-start.8
  75.6 1.5 %collective-permute-start.7 = (bf16[144,512]{1,0:T(8,128)(2,1)S(1)}, bf16[144,512]{1,0:T(8,128)(2,1)S(1)}, u32[]{:S(2)}, u32[]{:S(2)}) collective-permute-start(bf16[144,512]{1,0:T(8,128)(2,1)S(1)} %shard_map.194.refs_0_), channel_id=1, source_target_pairs={{0,6},{1,7},{2,0},{3,1},{4,2},{5,3},{6,4},{7,5},{8,14},{9,15},{10,... | collective-permute-start | bytes 442376 | tf_op jit(solution)/shard_map/ppermute | solution.py:334
  77.1 1.4 collective-permute-start.6
  78.6 2.1 %shard_map.195 = (f32[256,256]{1,0:T(8,128)S(1)}, f32[8,128]{1,0:T(8,128)S(1)}, f32[128,1024]{1,0:T(8,128)S(1)}) custom-call(s32[3]{0:T(128)S(1)} %pad_add_fusion.pos, bf16[144,512]{1,0:T(8,128)(2,1)S(1)} %shard_map.194.refs_0_, bf16[144,512]{1,0:T(8,128)(2,1)S(1)} %collective-permute-done.9.refs_1_, f32[1024,256]{1,0:T(8,128)S(1)} %copy-done, ...), custom_call_target="tpu_custom_call" | custom-call | tf_op jit(solution)/shard_map/pallas_call | solution.py:34
  80.6 0.4 collective-permute-done.8.refs_4_
  81.1 4.0 %collective-permute-done.6.refs_2_ = bf16[144,512]{1,0:T(8,128)(2,1)S(1)} collective-permute-done((bf16[144,512]{1,0:T(8,128)(2,1)S(1)}, bf16[144,512]{1,0:T(8,128)(2,1)S(1)}, u32[]{:S(2)}, u32[]{:S(2)}) %collective-permute-start.6) | collective-permute-done | bytes 147488 | tf_op jit(solution)/shard_map/ppermute | solution.py:334
  85.1 0.9 collective-permute-start.10
  86.0 0.0 collective-permute-start.11
  86.0 0.5 collective-permute-start.12
  86.5 0.5 collective-permute-done.10.refs_1_
  87.0 0.4 collective-permute-done.11.refs_3_
  87.3 0.2 collective-permute-done.12.refs_5_
  87.5 3.9 %shard_map.196 = (f32[1024,256]{1,0:T(8,128)}, f32[32,7,4,128]{3,2,1,0:T(4,128)S(1)}) custom-call(s32[3]{0:T(128)S(1)} %pad_add_fusion.pos, bf16[144,512]{1,0:T(8,128)(2,1)S(1)} %collective-permute-done.7.refs_0_, bf16[144,512]{1,0:T(8,128)(2,1)S(1)} %collective-permute-done.10.refs_1_, bf16[144,512]{1,0:T(8,128)(2,1)S(1)} %collective-permute-done.6.refs_2_, ...), custom_call_target="tpu_custom_call" | custom-call | tf_op jit(solution)/shard_map/pallas_call | solution.py:34
  91.5 17.2 %all_to_all.15.parts = f32[32,7,4,128]{3,2,1,0:T(4,128)S(1)} all-to-all(f32[32,7,4,128]{3,2,1,0:T(4,128)S(1)} %get-tuple-element.56), channel_id=1, replica_groups=mesh['node'=32,'rep'=8] {'node'}, dimensions={0} | all-to-all | bytes 917504 | tf_op jit(solution)/shard_map/all_to_all | solution.py:449
  108.7 0.8 shard_map.197
  109.5 7.7 %all-to-all-start.2 = ((f32[32,5,4,128]{3,2,1,0:T(4,128)}), f32[32,5,4,128]{3,2,1,0:T(4,128)S(1)}, u32[]{:S(2)}, u32[]{:S(2)}) async-start(f32[32,5,4,128]{3,2,1,0:T(4,128)} %get-tuple-element.57), calls=%async_computation.2 | async-start | bytes 655360 | tf_op jit(solution)/shard_map/all_to_all | solution.py:451
  117.2 1.9 %collective-permute-start.15 = (f32[32,2,4,128]{3,2,1,0:T(4,128)S(1)}, f32[32,2,4,128]{3,2,1,0:T(4,128)S(1)}, u32[]{:S(2)}, u32[]{:S(2)}) collective-permute-start(f32[32,2,4,128]{3,2,1,0:T(4,128)S(1)} %get-tuple-element.60.a0), channel_id=1, source_target_pairs={{0,6},{1,7},{2,0},{3,1},{4,2},{5,3},{6,4},{7,5},{8,14},{9,15},{10,... | collective-permute-start | bytes 393224 | tf_op jit(solution)/shard_map/ppermute | solution.py:334
  119.1 0.8 collective-permute-start.14
  120.0 0.0 collective-permute-start.13
  120.0 1.7 %collective-permute-start.16 = (f32[32,2,4,128]{3,2,1,0:T(4,128)S(1)}, f32[32,2,4,128]{3,2,1,0:T(4,128)S(1)}, u32[]{:S(2)}, u32[]{:S(2)}) collective-permute-start(f32[32,2,4,128]{3,2,1,0:T(4,128)S(1)} %get-tuple-element.60.a0), channel_id=1, source_target_pairs={{0,1},{1,0},{2,3},{3,2},{4,5},{5,4},{6,7},{7,6},{8,9},{9,8},{10,11... | collective-permute-start | bytes 393224 | tf_op jit(solution)/shard_map/ppermute | solution.py:330
  121.7 0.3 collective-permute-done.15.a3
  122.0 3.7 %collective-permute-start.19 = (f32[32,2,4,128]{3,2,1,0:T(4,128)S(1)}, f32[32,2,4,128]{3,2,1,0:T(4,128)S(1)}, u32[]{:S(2)}, u32[]{:S(2)}) collective-permute-start(f32[32,2,4,128]{3,2,1,0:T(4,128)S(1)} %collective-permute-done.15.a3), channel_id=1, source_target_pairs={{0,1},{1,0},{2,3},{3,2},{4,5},{5,4},{6,7},{7,6},{8,9},{9,8},{10,11... | collective-permute-start | bytes 393224 | tf_op jit(solution)/shard_map/ppermute | solution.py:330
  125.7 2.3 %collective-permute-start.18 = (f32[32,2,4,128]{3,2,1,0:T(4,128)S(1)}, f32[32,2,4,128]{3,2,1,0:T(4,128)S(1)}, u32[]{:S(2)}, u32[]{:S(2)}) collective-permute-start(f32[32,2,4,128]{3,2,1,0:T(4,128)S(1)} %collective-permute-done.14.a2), channel_id=1, source_target_pairs={{0,1},{1,0},{2,3},{3,2},{4,5},{5,4},{6,7},{7,6},{8,9},{9,8},{10,11... | collective-permute-start | bytes 393224 | tf_op jit(solution)/shard_map/ppermute | solution.py:330
  128.0 1.3 collective-permute-start.17
  129.4 0.0 collective-permute-done.16.b0
  129.4 0.0 collective-permute-done.19.b3
  129.4 1.0 collective-permute-done.17.b1
  130.4 1.1 collective-permute-start.20
  131.5 0.9 collective-permute-start.25
  132.4 0.6 collective-permute-start.22
  133.0 2.8 %collective-permute-start.21 = (f32[29,5,4,128]{3,2,1,0:T(4,128)S(1)}, f32[29,5,4,128]{3,2,1,0:T(4,128)S(1)}, u32[]{:S(2)}, u32[]{:S(2)}) collective-permute-start(f32[29,5,4,128]{3,2,1,0:T(4,128)S(1)} %slice.2.a0), channel_id=1, source_target_pairs={{0,1},{1,0},{2,3},{3,2},{4,5},{5,4},{6,7},{7,6},{8,9},{9,8},{10,11... | collective-permute-start | bytes 890888 | tf_op jit(solution)/shard_map/ppermute | solution.py:330
  135.8 3.9 %shard_map.198 = f32[1024,256]{1,0:T(8,128)} custom-call(s32[3]{0:T(128)S(1)} %pad_add_fusion.pos, s32[1,1024]{1,0:T(1,128)S(1)} %bitcast.16, f32[32,2,4,128]{3,2,1,0:T(4,128)S(1)} %get-tuple-element.60.a0, f32[32,2,4,128]{3,2,1,0:T(4,128)S(1)} %collective-permute-done.13.a1, f32[32,2,4,128]{3,2,1,0:T(4,128)S(1)} %collective-permute-done.14.a2, ...), custom_call_target="tpu_custom_call" | custom-call | tf_op jit(solution)/shard_map/pallas_call | solution.py:34
  139.6 4.0 %collective-permute-done.25.a3 = f32[29,5,4,128]{3,2,1,0:T(4,128)S(1)} collective-permute-done((f32[29,5,4,128]{3,2,1,0:T(4,128)S(1)}, f32[29,5,4,128]{3,2,1,0:T(4,128)S(1)}, u32[]{:S(2)}, u32[]{:S(2)}) %collective-permute-start.25) | collective-permute-done | bytes 296992 | tf_op jit(solution)/shard_map/ppermute | solution.py:334
  143.6 2.4 %collective-permute-start.26 = (f32[29,5,4,128]{3,2,1,0:T(4,128)S(1)}, f32[29,5,4,128]{3,2,1,0:T(4,128)S(1)}, u32[]{:S(2)}, u32[]{:S(2)}) collective-permute-start(f32[29,5,4,128]{3,2,1,0:T(4,128)S(1)} %collective-permute-done.25.a3), channel_id=1, source_target_pairs={{0,1},{1,0},{2,3},{3,2},{4,5},{5,4},{6,7},{7,6},{8,9},{9,8},{10,11... | collective-permute-start | bytes 890888 | tf_op jit(solution)/shard_map/ppermute | solution.py:330
  146.0 1.2 collective-permute-done.22.a1
  147.2 0.8 collective-permute-start.23
  148.0 0.0 collective-permute-start.24
  148.0 1.7 %shard_map.199 = (f32[512,768]{1,0:T(8,128)}, f32[256,768]{1,0:T(8,128)}) custom-call(s32[3]{0:T(128)S(1)} %pad_add_fusion.pos, f32[29,5,4,128]{3,2,1,0:T(4,128)S(1)} %slice.2.a0, f32[29,5,4,128]{3,2,1,0:T(4,128)S(1)} %collective-permute-done.22.a1, f32[29,5,4,128]{3,2,1,0:T(4,128)S(1)} %collective-permute-done.20.a2, ...), custom_call_target="tpu_custom_call" | custom-call | tf_op jit(solution)/shard_map/pallas_call | solution.py:34
  149.8 1.7 %shard_map.200 = (f32[512,768]{1,0:T(8,128)}, f32[256,768]{1,0:T(8,128)}) custom-call(s32[3]{0:T(128)S(1)} %pad_add_fusion.pos, f32[29,5,4,128]{3,2,1,0:T(4,128)S(1)} %collective-permute-done.21.a0, f32[29,5,4,128]{3,2,1,0:T(4,128)S(1)} %collective-permute-done.23.a1, ...), custom_call_target="tpu_custom_call", output_to_operand_aliasing={{0}: (5, {}), {1}: (6, {})} | custom-call | tf_op jit(solution)/shard_map/pallas_call | solution.py:34
  (27 shorter events, 0.1 us)
Async XLA Ops:
  7.0 12.2 %copy-start.6 = (f32[96,512]{1,0:T(8,128)S(1)}, f32[96,512]{1,0:T(8,128)}, u32[]{:S(2)}) copy-start(f32[96,512]{1,0:T(8,128)} %get-tuple-element.40) | copy-start | bytes 589828
  7.0 13.3 %copy-start.4 = (s32[1024]{0:T(1024)S(1)}, s32[1024]{0:T(1024)}, u32[]{:S(2)}) copy-start(s32[1024]{0:T(1024)} %param.27) | copy-start | bytes 12292
  7.0 16.0 %copy-start.5 = (f32[1024,256]{1,0:T(8,128)S(1)}, f32[1024,256]{1,0:T(8,128)}, u32[]{:S(2)}) copy-start(f32[1024,256]{1,0:T(8,128)} %param.20) | copy-start | bytes 3145732
  7.0 41.6 %all-to-all-start = ((bf16[32,144,128]{2,1,0:T(8,128)(2,1)}), bf16[32,144,128]{2,1,0:T(8,128)(2,1)S(1)}, u32[]{:S(2)}, u32[]{:S(2)}) async-start(bf16[32,144,128]{2,1,0:T(8,128)(2,1)} %get-tuple-element.39), calls=%async_computation | async-start | bytes 2359296 | tf_op jit(solution)/shard_map/all_to_all | solution.py:408
  19.2 2.1 %collective-permute-start = (f32[96,512]{1,0:T(8,128)S(1)}, f32[96,512]{1,0:T(8,128)S(1)}, u32[]{:S(2)}, u32[]{:S(2)}) collective-permute-start(f32[96,512]{1,0:T(8,128)S(1)} %copy-done.6), channel_id=1, source_target_pairs={{0,1},{1,0},{2,3},{3,2},{4,5},{5,4},{6,7},{7,6},{8,9},{9,8},{10,11... | collective-permute-start | bytes 589832 | tf_op jit(solution)/shard_map/ppermute | solution.py:330
  21.4 27.2 %collective-permute-start.1 = (f32[16,512]{1,0:T(8,128)S(1)}, f32[16,512]{1,0:T(8,128)S(1)}, u32[]{:S(2)}, u32[]{:S(2)}) collective-permute-start(f32[16,512]{1,0:T(8,128)S(1)} %constant_dynamic-slice_fusion), channel_id=1, source_target_pairs={{0,8},{8,16},{16,24},{24,32},{32,40},{40,48},{48,56},{56,64},{64,7... | collective-permute-start | bytes 98312 | tf_op jit(solution)/shard_map/ppermute | solution.py:412
  48.6 6.1 %collective-permute-start.2 = (bf16[32,144,128]{2,1,0:T(8,128)(2,1)S(1)}, bf16[32,144,128]{2,1,0:T(8,128)(2,1)S(1)}, u32[]{:S(2)}, u32[]{:S(2)}) collective-permute-start(bf16[32,144,128]{2,1,0:T(8,128)(2,1)S(1)} %all-to-all-done.own), channel_id=1, source_target_pairs={{0,1},{1,0},{2,3},{3,2},{4,5},{5,4},{6,7},{7,6},{8,9},{9,8},{10,11... | collective-permute-start | bytes 3538952 | tf_op jit(solution)/shard_map/ppermute | solution.py:330
  54.6 23.9 %copy-start.1 = (f32[1024,256]{1,0:T(8,128)S(1)}, f32[1024,256]{1,0:T(8,128)}, u32[]{:S(2)}) copy-start(f32[1024,256]{1,0:T(8,128)} %refs_7_.3) | copy-start | bytes 3145732
  54.6 23.9 %copy-start.2 = (bf16[512,768]{1,0:T(8,128)(2,1)S(1)}, bf16[512,768]{1,0:T(8,128)(2,1)}, u32[]{:S(2)}) copy-start(bf16[512,768]{1,0:T(8,128)(2,1)} %refs_10_.1) | copy-start | bytes 2359300
  54.6 23.9 %copy-start.3 = (bf16[256,768]{1,0:T(8,128)(2,1)S(1)}, bf16[256,768]{1,0:T(8,128)(2,1)}, u32[]{:S(2)}) copy-start(bf16[256,768]{1,0:T(8,128)(2,1)} %refs_11_.1) | copy-start | bytes 1179652
  57.0 21.5 %copy-start = (f32[1024,256]{1,0:T(8,128)S(1)}, f32[1024,256]{1,0:T(8,128)}, u32[]{:S(2)}) copy-start(f32[1024,256]{1,0:T(8,128)} %refs_6_.3) | copy-start | bytes 3145732
  57.0 9.5 %collective-permute-start.3 = (f32[136,512]{1,0:T(8,128)S(1)}, f32[136,512]{1,0:T(8,128)S(1)}, u32[]{:S(2)}, u32[]{:S(2)}) collective-permute-start(f32[136,512]{1,0:T(8,128)S(1)} %get-tuple-element.42), channel_id=1, source_target_pairs={{0,4},{1,5},{2,6},{3,7},{4,0},{5,1},{6,2},{7,3},{8,12},{9,13},{10,... | collective-permute-start | bytes 835592 | tf_op jit(solution)/shard_map/ppermute | solution.py:334
  59.9 12.7 %collective-permute-start.4 = (f32[136,512]{1,0:T(8,128)S(1)}, f32[136,512]{1,0:T(8,128)S(1)}, u32[]{:S(2)}, u32[]{:S(2)}) collective-permute-start(f32[136,512]{1,0:T(8,128)S(1)} %get-tuple-element.43), channel_id=1, source_target_pairs={{0,6},{1,7},{2,0},{3,1},{4,2},{5,3},{6,4},{7,5},{8,14},{9,15},{10,... | collective-permute-start | bytes 835592 | tf_op jit(solution)/shard_map/ppermute | solution.py:334
  60.7 12.4 %collective-permute-start.5 = (f32[136,512]{1,0:T(8,128)S(1)}, f32[136,512]{1,0:T(8,128)S(1)}, u32[]{:S(2)}, u32[]{:S(2)}) collective-permute-start(f32[136,512]{1,0:T(8,128)S(1)} %get-tuple-element.44), channel_id=1, source_target_pairs={{0,2},{1,3},{2,4},{3,5},{4,6},{5,7},{6,0},{7,1},{8,10},{9,11},{10,... | collective-permute-start | bytes 835592 | tf_op jit(solution)/shard_map/ppermute | solution.py:334
  73.7 4.8 %collective-permute-start.9 = (bf16[144,512]{1,0:T(8,128)(2,1)S(1)}, bf16[144,512]{1,0:T(8,128)(2,1)S(1)}, u32[]{:S(2)}, u32[]{:S(2)}) collective-permute-start(bf16[144,512]{1,0:T(8,128)(2,1)S(1)} %shard_map.194.refs_0_), channel_id=1, source_target_pairs={{0,1},{1,0},{2,3},{3,2},{4,5},{5,4},{6,7},{7,6},{8,9},{9,8},{10,11... | collective-permute-start | bytes 442376 | tf_op jit(solution)/shard_map/ppermute | solution.py:330
  74.4 6.6 %collective-permute-start.8 = (bf16[144,512]{1,0:T(8,128)(2,1)S(1)}, bf16[144,512]{1,0:T(8,128)(2,1)S(1)}, u32[]{:S(2)}, u32[]{:S(2)}) collective-permute-start(bf16[144,512]{1,0:T(8,128)(2,1)S(1)} %shard_map.194.refs_0_), channel_id=1, source_target_pairs={{0,2},{1,3},{2,4},{3,5},{4,6},{5,7},{6,0},{7,1},{8,10},{9,11},{10,... | collective-permute-start | bytes 442376 | tf_op jit(solution)/shard_map/ppermute | solution.py:334
  75.6 5.5 %collective-permute-start.7 = (bf16[144,512]{1,0:T(8,128)(2,1)S(1)}, bf16[144,512]{1,0:T(8,128)(2,1)S(1)}, u32[]{:S(2)}, u32[]{:S(2)}) collective-permute-start(bf16[144,512]{1,0:T(8,128)(2,1)S(1)} %shard_map.194.refs_0_), channel_id=1, source_target_pairs={{0,6},{1,7},{2,0},{3,1},{4,2},{5,3},{6,4},{7,5},{8,14},{9,15},{10,... | collective-permute-start | bytes 442376 | tf_op jit(solution)/shard_map/ppermute | solution.py:334
  77.1 7.9 %collective-permute-start.6 = (bf16[144,512]{1,0:T(8,128)(2,1)S(1)}, bf16[144,512]{1,0:T(8,128)(2,1)S(1)}, u32[]{:S(2)}, u32[]{:S(2)}) collective-permute-start(bf16[144,512]{1,0:T(8,128)(2,1)S(1)} %shard_map.194.refs_0_), channel_id=1, source_target_pairs={{0,4},{1,5},{2,6},{3,7},{4,0},{5,1},{6,2},{7,3},{8,12},{9,13},{10,... | collective-permute-start | bytes 442376 | tf_op jit(solution)/shard_map/ppermute | solution.py:334
  85.1 1.9 %collective-permute-start.10 = (bf16[144,512]{1,0:T(8,128)(2,1)S(1)}, bf16[144,512]{1,0:T(8,128)(2,1)S(1)}, u32[]{:S(2)}, u32[]{:S(2)}) collective-permute-start(bf16[144,512]{1,0:T(8,128)(2,1)S(1)} %collective-permute-done.7.refs_0_), channel_id=1, source_target_pairs={{0,1},{1,0},{2,3},{3,2},{4,5},{5,4},{6,7},{7,6},{8,9},{9,8},{10,11... | collective-permute-start | bytes 442376 | tf_op jit(solution)/shard_map/ppermute | solution.py:330
  86.0 1.4 collective-permute-start.11
  86.0 1.6 %collective-permute-start.12 = (bf16[144,512]{1,0:T(8,128)(2,1)S(1)}, bf16[144,512]{1,0:T(8,128)(2,1)S(1)}, u32[]{:S(2)}, u32[]{:S(2)}) collective-permute-start(bf16[144,512]{1,0:T(8,128)(2,1)S(1)} %collective-permute-done.8.refs_4_), channel_id=1, source_target_pairs={{0,1},{1,0},{2,3},{3,2},{4,5},{5,4},{6,7},{7,6},{8,9},{9,8},{10,11... | collective-permute-start | bytes 442376 | tf_op jit(solution)/shard_map/ppermute | solution.py:330
  109.5 20.8 %all-to-all-start.2 = ((f32[32,5,4,128]{3,2,1,0:T(4,128)}), f32[32,5,4,128]{3,2,1,0:T(4,128)S(1)}, u32[]{:S(2)}, u32[]{:S(2)}) async-start(f32[32,5,4,128]{3,2,1,0:T(4,128)} %get-tuple-element.57), calls=%async_computation.2 | async-start | bytes 655360 | tf_op jit(solution)/shard_map/all_to_all | solution.py:451
  117.2 4.8 %collective-permute-start.15 = (f32[32,2,4,128]{3,2,1,0:T(4,128)S(1)}, f32[32,2,4,128]{3,2,1,0:T(4,128)S(1)}, u32[]{:S(2)}, u32[]{:S(2)}) collective-permute-start(f32[32,2,4,128]{3,2,1,0:T(4,128)S(1)} %get-tuple-element.60.a0), channel_id=1, source_target_pairs={{0,6},{1,7},{2,0},{3,1},{4,2},{5,3},{6,4},{7,5},{8,14},{9,15},{10,... | collective-permute-start | bytes 393224 | tf_op jit(solution)/shard_map/ppermute | solution.py:334
  119.1 6.6 %collective-permute-start.14 = (f32[32,2,4,128]{3,2,1,0:T(4,128)S(1)}, f32[32,2,4,128]{3,2,1,0:T(4,128)S(1)}, u32[]{:S(2)}, u32[]{:S(2)}) collective-permute-start(f32[32,2,4,128]{3,2,1,0:T(4,128)S(1)} %get-tuple-element.60.a0), channel_id=1, source_target_pairs={{0,4},{1,5},{2,6},{3,7},{4,0},{5,1},{6,2},{7,3},{8,12},{9,13},{10,... | collective-permute-start | bytes 393224 | tf_op jit(solution)/shard_map/ppermute | solution.py:334
  120.0 8.1 %collective-permute-start.13 = (f32[32,2,4,128]{3,2,1,0:T(4,128)S(1)}, f32[32,2,4,128]{3,2,1,0:T(4,128)S(1)}, u32[]{:S(2)}, u32[]{:S(2)}) collective-permute-start(f32[32,2,4,128]{3,2,1,0:T(4,128)S(1)} %get-tuple-element.60.a0), channel_id=1, source_target_pairs={{0,2},{1,3},{2,4},{3,5},{4,6},{5,7},{6,0},{7,1},{8,10},{9,11},{10,... | collective-permute-start | bytes 393224 | tf_op jit(solution)/shard_map/ppermute | solution.py:334
  120.0 9.4 %collective-permute-start.16 = (f32[32,2,4,128]{3,2,1,0:T(4,128)S(1)}, f32[32,2,4,128]{3,2,1,0:T(4,128)S(1)}, u32[]{:S(2)}, u32[]{:S(2)}) collective-permute-start(f32[32,2,4,128]{3,2,1,0:T(4,128)S(1)} %get-tuple-element.60.a0), channel_id=1, source_target_pairs={{0,1},{1,0},{2,3},{3,2},{4,5},{5,4},{6,7},{7,6},{8,9},{9,8},{10,11... | collective-permute-start | bytes 393224 | tf_op jit(solution)/shard_map/ppermute | solution.py:330
  122.0 7.4 %collective-permute-start.19 = (f32[32,2,4,128]{3,2,1,0:T(4,128)S(1)}, f32[32,2,4,128]{3,2,1,0:T(4,128)S(1)}, u32[]{:S(2)}, u32[]{:S(2)}) collective-permute-start(f32[32,2,4,128]{3,2,1,0:T(4,128)S(1)} %collective-permute-done.15.a3), channel_id=1, source_target_pairs={{0,1},{1,0},{2,3},{3,2},{4,5},{5,4},{6,7},{7,6},{8,9},{9,8},{10,11... | collective-permute-start | bytes 393224 | tf_op jit(solution)/shard_map/ppermute | solution.py:330
  125.7 3.7 %collective-permute-start.18 = (f32[32,2,4,128]{3,2,1,0:T(4,128)S(1)}, f32[32,2,4,128]{3,2,1,0:T(4,128)S(1)}, u32[]{:S(2)}, u32[]{:S(2)}) collective-permute-start(f32[32,2,4,128]{3,2,1,0:T(4,128)S(1)} %collective-permute-done.14.a2), channel_id=1, source_target_pairs={{0,1},{1,0},{2,3},{3,2},{4,5},{5,4},{6,7},{7,6},{8,9},{9,8},{10,11... | collective-permute-start | bytes 393224 | tf_op jit(solution)/shard_map/ppermute | solution.py:330
  128.0 2.3 %collective-permute-start.17 = (f32[32,2,4,128]{3,2,1,0:T(4,128)S(1)}, f32[32,2,4,128]{3,2,1,0:T(4,128)S(1)}, u32[]{:S(2)}, u32[]{:S(2)}) collective-permute-start(f32[32,2,4,128]{3,2,1,0:T(4,128)S(1)} %collective-permute-done.13.a1), channel_id=1, source_target_pairs={{0,1},{1,0},{2,3},{3,2},{4,5},{5,4},{6,7},{7,6},{8,9},{9,8},{10,11... | collective-permute-start | bytes 393224 | tf_op jit(solution)/shard_map/ppermute | solution.py:330
  130.4 9.3 %collective-permute-start.20 = (f32[29,5,4,128]{3,2,1,0:T(4,128)S(1)}, f32[29,5,4,128]{3,2,1,0:T(4,128)S(1)}, u32[]{:S(2)}, u32[]{:S(2)}) collective-permute-start(f32[29,5,4,128]{3,2,1,0:T(4,128)S(1)} %slice.2.a0), channel_id=1, source_target_pairs={{0,4},{1,5},{2,6},{3,7},{4,0},{5,1},{6,2},{7,3},{8,12},{9,13},{10,... | collective-permute-start | bytes 890888 | tf_op jit(solution)/shard_map/ppermute | solution.py:334
  131.5 12.1 %collective-permute-start.25 = (f32[29,5,4,128]{3,2,1,0:T(4,128)S(1)}, f32[29,5,4,128]{3,2,1,0:T(4,128)S(1)}, u32[]{:S(2)}, u32[]{:S(2)}) collective-permute-start(f32[29,5,4,128]{3,2,1,0:T(4,128)S(1)} %slice.2.a0), channel_id=1, source_target_pairs={{0,6},{1,7},{2,0},{3,1},{4,2},{5,3},{6,4},{7,5},{8,14},{9,15},{10,... | collective-permute-start | bytes 890888 | tf_op jit(solution)/shard_map/ppermute | solution.py:334
  132.4 14.8 %collective-permute-start.22 = (f32[29,5,4,128]{3,2,1,0:T(4,128)S(1)}, f32[29,5,4,128]{3,2,1,0:T(4,128)S(1)}, u32[]{:S(2)}, u32[]{:S(2)}) collective-permute-start(f32[29,5,4,128]{3,2,1,0:T(4,128)S(1)} %slice.2.a0), channel_id=1, source_target_pairs={{0,2},{1,3},{2,4},{3,5},{4,6},{5,7},{6,0},{7,1},{8,10},{9,11},{10,... | collective-permute-start | bytes 890888 | tf_op jit(solution)/shard_map/ppermute | solution.py:334
  133.0 16.7 %collective-permute-start.21 = (f32[29,5,4,128]{3,2,1,0:T(4,128)S(1)}, f32[29,5,4,128]{3,2,1,0:T(4,128)S(1)}, u32[]{:S(2)}, u32[]{:S(2)}) collective-permute-start(f32[29,5,4,128]{3,2,1,0:T(4,128)S(1)} %slice.2.a0), channel_id=1, source_target_pairs={{0,1},{1,0},{2,3},{3,2},{4,5},{5,4},{6,7},{7,6},{8,9},{9,8},{10,11... | collective-permute-start | bytes 890888 | tf_op jit(solution)/shard_map/ppermute | solution.py:330
  143.6 6.1 %collective-permute-start.26 = (f32[29,5,4,128]{3,2,1,0:T(4,128)S(1)}, f32[29,5,4,128]{3,2,1,0:T(4,128)S(1)}, u32[]{:S(2)}, u32[]{:S(2)}) collective-permute-start(f32[29,5,4,128]{3,2,1,0:T(4,128)S(1)} %collective-permute-done.25.a3), channel_id=1, source_target_pairs={{0,1},{1,0},{2,3},{3,2},{4,5},{5,4},{6,7},{7,6},{8,9},{9,8},{10,11... | collective-permute-start | bytes 890888 | tf_op jit(solution)/shard_map/ppermute | solution.py:330
  147.2 2.5 %collective-permute-start.23 = (f32[29,5,4,128]{3,2,1,0:T(4,128)S(1)}, f32[29,5,4,128]{3,2,1,0:T(4,128)S(1)}, u32[]{:S(2)}, u32[]{:S(2)}) collective-permute-start(f32[29,5,4,128]{3,2,1,0:T(4,128)S(1)} %collective-permute-done.22.a1), channel_id=1, source_target_pairs={{0,1},{1,0},{2,3},{3,2},{4,5},{5,4},{6,7},{7,6},{8,9},{9,8},{10,11... | collective-permute-start | bytes 890888 | tf_op jit(solution)/shard_map/ppermute | solution.py:330
  148.0 1.7 %collective-permute-start.24 = (f32[29,5,4,128]{3,2,1,0:T(4,128)S(1)}, f32[29,5,4,128]{3,2,1,0:T(4,128)S(1)}, u32[]{:S(2)}, u32[]{:S(2)}) collective-permute-start(f32[29,5,4,128]{3,2,1,0:T(4,128)S(1)} %collective-permute-done.20.a2), channel_id=1, source_target_pairs={{0,1},{1,0},{2,3},{3,2},{4,5},{5,4},{6,7},{7,6},{8,9},{9,8},{10,11... | collective-permute-start | bytes 890888 | tf_op jit(solution)/shard_map/ppermute | solution.py:330

commit v8 on v7

--- a/solution.py
+++ b/solution.py
@@ -131,31 +131,37 @@
         c.wait()
 
 
-def cold_kernel(pos, own, peer, hot, spill, o0, o1, o2, o3):
+def cold_hits(pos, got):
     q = iota((512, 128), 0)
     want = (q & 127) + 256 * ((pos[0] + (q >> 7)) & 3) + 128 * pos[1]
     hits = []
-    for got in (own, peer):
-        for g in range(8):
-            tail = got[4 * g, 128:144, :].astype(F32)
-            for i in range(1, 4):
-                tail = tail + got[4 * g + i, 128:144, :].astype(F32)
-            row = jnp.where(tail[2:3, :] > 0.5, tail[0:1, :] * 32.0 + tail[1:2, :], -1.0).astype(I32)
-            hits.append(one_hot(want == row))
-    hit = jnp.concatenate(hits, axis=1)
-    count = mm(jnp.ones((8, 2048), BF16), hit, ((1,), (1,)))
+    for g in range(8):
+        tail = got[4 * g, 128:144, :].astype(F32)
+        for i in range(1, 4):
+            tail = tail + got[4 * g + i, 128:144, :].astype(F32)
+        row = jnp.where(tail[2:3, :] > 0.5, tail[0:1, :] * 32.0 + tail[1:2, :], -1.0).astype(I32)
+        hits.append(one_hot(want == row))
+    return jnp.concatenate(hits, axis=1)
+
+
+def cold_sums(hit, got, n):
+    msgs = [got[:, 32 * k : 32 * k + 32, :].reshape(1024, 128) for k in (2 * n, 2 * n + 1)]
+    return mm(hit, jnp.concatenate(msgs, axis=1))
+
+
+def own_cold_kernel(pos, own, sums, counts):
+    hit = cold_hits(pos, own)
+    counts[...] = mm(jnp.ones((8, 1024), BF16), hit, ((1,), (1,)))
+    for n in range(2):
+        sums[:, 256 * n : 256 * n + 256] = cold_sums(hit, own, n)
+
+
+def cold_kernel(pos, peer, sums, counts, hot, spill, o0, o1, o2, o3):
+    hit = cold_hits(pos, peer)
+    count = counts[...] + mm(jnp.ones((8, 1024), BF16), hit, ((1,), (1,)))
     for n in range(2):
         cols = slice(256 * n, 256 * n + 256)
-        msgs = jnp.concatenate(
-            [
-                jnp.concatenate(
-                    [got[:, 32 * k : 32 * k + 32, :].reshape(1024, 128) for k in (2 * n, 2 * n + 1)], axis=1
-                )
-                for got in (own, peer)
-            ],
-            axis=0,
-        )
-        total = mm(hit, msgs)
+        total = sums[:, cols] + cold_sums(hit, peer, n)
         for d, to in enumerate((o0, o1, o2, o3)):
             here = slice(128 * d, 128 * d + 128)
             to[0:128, cols] = total[here, :]
@@ -306,19 +312,17 @@
         hot[k] = parts[k, 5:7]
 
 
-def place_kernel(other, pos, a0, a1, a2, a3, *refs):
-    g_in, g_hid, both, sems = refs[-4:]
-    x = pos[0]
-    core = 1 - pos[1] if other else pos[1]
+def place_kernel(blocks, pos, *refs):
+    parts, (g_in, g_hid, both, sems) = refs[: len(blocks)], refs[-4:]
     stores = []
-    for d, part in enumerate((a0, a1, a2, a3)):
-        block = 2 * ((x - d + 4) & 3) + core
+    for n, ((d, other), part) in enumerate(zip(blocks, parts)):
+        block = 2 * ((pos[0] - d + 4) & 3) + (1 - pos[1] if other else pos[1])
         for k in range(144):
             i, c = 4 * k % 96, 4 * k // 96
-            both[96 * d + i : 96 * d + i + 4, 128 * c : 128 * c + 128] = part[k // 5, k % 5]
+            both[96 * n + i : 96 * n + i + 4, 128 * c : 128 * c + 128] = part[k // 5, k % 5]
         for rows, at, dst in (
-            (64, 96 * d, g_in.at[pl.ds(pl.multiple_of(block * 64, 64), 64)]),
-            (32, 96 * d + 64, g_hid.at[pl.ds(pl.multiple_of(block * 32, 32), 32)]),
+            (64, 96 * n, g_in.at[pl.ds(pl.multiple_of(block * 64, 64), 64)]),
+            (32, 96 * n + 64, g_hid.at[pl.ds(pl.multiple_of(block * 32, 32), 32)]),
         ):
             stores.append(pltpu.make_async_copy(both.at[at : at + rows], dst, sems.at[len(stores)]))
             stores[-1].start()
@@ -418,11 +422,13 @@
 
     recv, hot_mem, hot_cot, _ = lax.optimization_barrier((recv, hot_mem, hot_cot, spill))
     block = sds((136, 512), F32)
+    peer = swap_core(recv)
+    sums = call(own_cold_kernel, (sds((512, 512), F32), sds((8, 512), F32)), (SM,), (pos, recv))
     parts = call(
         cold_kernel,
         (block,) * 4,
         (SM,),
-        (pos, recv, swap_core(recv), hot.reshape(12, 8, 512), spill.reshape(2, 8, 512)),
+        (pos, peer, *sums, hot.reshape(12, 8, 512), spill.reshape(2, 8, 512)),
     )
     parts = [parts[0]] + [shift_x(parts[d], d) for d in (1, 2, 3)]
     agg = call(
@@ -442,7 +448,7 @@
         (SM,),
         (pos, agg, swap_core(agg), *shared),
     )
-    far, back, near, new_own = lax.optimization_barrier((far, back, near, new_own))
+    near, back, far, new_own = lax.optimization_barrier((near, back, far, new_own))
     parts = (back, swap_core(back), far, swap_core(far), near, swap_core(near))
     new_memory, grad = last_update(pos, parts, shared, (new_own,), hot_own, acc)
 
@@ -459,21 +465,24 @@
         (pltpu.VMEM((8, 128, 256), F32),),
     )
     own = [grad[0:29]] + [shift_x(grad[0:29], d) for d in (1, 2, 3)]
-    own[2], new_hot = lax.optimization_barrier((own[2], new_hot))
-    places = (pltpu.VMEM((384, 768), F32), pltpu.SemaphoreType.DMA((8,)))
-    grads = (sds((512, 768), F32), sds((256, 768), F32))
-    grads = call(
-        functools.partial(place_kernel, False), grads, (SM,), (pos, *own), places, (ANY, ANY)
-    )
-    grad_in, grad_hid = call(
-        functools.partial(place_kernel, True),
-        tuple(sds(g.shape, F32) for g in grads),
-        (SM, VM, VM, VM, VM, ANY, ANY),
-        (pos, *[swap_core(v) for v in own], *grads),
-        places,
-        (ANY, ANY),
-        aliases={5: 0, 6: 1},
-    )
+    grads = ()
+    for blocks in (((0, False), (0, True)), tuple((d, False) for d in (2, 3, 1)), tuple((d, True) for d in (2, 3, 1))):
+        parts = [swap_core(own[d]) if other else own[d] for d, other in blocks]
+        n = len(parts)
+        grads = call(
+            functools.partial(place_kernel, blocks),
+            (sds((512, 768), F32), sds((256, 768), F32)),
+            (SM,) + (VM,) * n + (ANY,) * len(grads),
+            (pos, *parts, *grads),
+            (pltpu.VMEM((96 * n, 768), F32), pltpu.SemaphoreType.DMA((2 * n,))),
+            (ANY, ANY),
+            aliases={n + 1: 0, n + 2: 1} if grads else {},
+        )
+        if n == 2:
+            own[2], own[3], own[1], new_hot, *grads = lax.optimization_barrier(
+                (own[2], own[3], own[1], new_hot, *grads)
+            )
+    grad_in, grad_hid = grads
     return (new_memory, new_hot, grad_in, grad_hid)
 
 

time: 152 us -> 153 us (level)
  starting transfers between devices: 56.9 us -> 54.4 us
  Pallas kernels: 23.3 us -> 25.1 us
    ppermute x14, starting transfers between devices: 21.7 us -> 17.9 us  [swap_core(): return lax.ppermute(v, 'rep', [(k, k ^ 1) for k in range(8)])]
    ppermute x12, waiting for transfers between devices: 21.9 us -> 24.6 us  [shift_x(): return lax.ppermute(v, 'rep', [(k, (k + 2 * d) % 8) for k in range(8)])]
    pallas_call x9 -> x11, Pallas kernels: 23.3 us -> 25.1 us  [call(): pl.pallas_call(body, out_shape=out_shape, in_specs=list(places) + [VM] *...]
  transfers between devices with their start and end apart: 29 -> 29, of which waited for: 15 -> 16; matrix products, arithmetic and copies ran while one was open for 2% -> 2% of each run, Pallas kernels for 5% -> 7%
where the time goes in v8:
time: 153 us; the launch traced here: 152 us
  starting transfers between devices  54.4 us (36%)
  waiting for transfers between devices  51.3 us (34%)
  Pallas kernels  25.1 us (16%)
  blocking collectives  17.2 us (11%)
  local copies, waits for them, and re-layouts  2.81 us (2%)
    pallas_call x11, Pallas kernels, call(): pl.pallas_call(body, out_shape=out_shape, in_specs=list(places) + [VM] *...  25.1 us
    ppermute x12, waiting for transfers between devices, shift_x(): return lax.ppermute(v, 'rep', [(k, (k + 2 * d) % 8) for k in range(8)])  24.6 us
    ppermute x1, waiting for transfers between devices, on_device(): spill = lax.ppermute(spill, 'node', [(k, (k + 1) % 32) for k in range(32)])  22.8 us
    ppermute x14, starting transfers between devices, swap_core(): return lax.ppermute(v, 'rep', [(k, k ^ 1) for k in range(8)])  17.9 us
    all_to_all x1, blocking collectives, on_device(): grad = lax.all_to_all(grad, 'node', split_axis=0, concat_axis=0, tiled=True)  17.2 us
    ppermute x12, starting transfers between devices, shift_x(): return lax.ppermute(v, 'rep', [(k, (k + 2 * d) % 8) for k in range(8)])  15.1 us
    all_to_all x1, starting transfers between devices, on_device(): recv = lax.all_to_all(send, 'node', split_axis=0, concat_axis=0, tiled=True)  12.2 us
    all_to_all x1, starting transfers between devices, on_device(): grad = lax.all_to_all(grad, 'node', split_axis=0, concat_axis=0, tiled=True)  7.72 us
  transfers between devices with their start and end apart: 29, of which 16 were waited for; matrix products, arithmetic and copies ran while one was open for 2% of the time, Pallas kernels for 7%

profile of v8, /device:TPU:1, one launch (start us, length us, event | category | flops | bytes accessed | tf_op | source)
XLA Modules:
  0.0 152.2 jit_solution(15525343086774795908)
XLA Ops:
  0.6 6.3 %shard_map.192 = (bf16[32,144,128]{2,1,0:T(8,128)(2,1)}, f32[96,512]{1,0:T(8,128)}) custom-call(s32[1]{0:T(128)} %bitcast.3.pos, f32[1024,256]{1,0:T(8,128)} %refs_6_.3, bf16[1024,128]{1,0:T(8,128)(2,1)} %edge_h.1, bf16[512,512]{1,0:T(8,128)(2,1)} %w_h.1, s32[1,1024]{1,0:T(1,128)} %bitcast.17, s32[1,1024]{1,0:T(1,128)} %bitcast.18, s32[1,1024]{1,0:T(1,128)} %bitcast.19, ...), custom_call_target="tpu_custom_call" | custom-call | tf_op jit(solution)/shard_map/pallas_call | solution.py:34
  7.0 0.0 copy-start.6
  7.0 0.0 copy-start.4
  7.0 0.0 copy-start.5
  7.0 12.2 %all-to-all-start = ((bf16[32,144,128]{2,1,0:T(8,128)(2,1)}), bf16[32,144,128]{2,1,0:T(8,128)(2,1)S(1)}, u32[]{:S(2)}, u32[]{:S(2)}) async-start(bf16[32,144,128]{2,1,0:T(8,128)(2,1)} %get-tuple-element.47), calls=%async_computation | async-start | bytes 2359296 | tf_op jit(solution)/shard_map/all_to_all | solution.py:412
  19.2 1.0 collective-permute-start
  20.3 0.2 select_reduce_fusion
  20.5 0.9 collective-permute-done
  21.4 1.6 %collective-permute-start.1 = (f32[16,512]{1,0:T(8,128)S(1)}, f32[16,512]{1,0:T(8,128)S(1)}, u32[]{:S(2)}, u32[]{:S(2)}) collective-permute-start(f32[16,512]{1,0:T(8,128)S(1)} %constant_dynamic-slice_fusion), channel_id=1, source_target_pairs={{0,8},{8,16},{16,24},{24,32},{32,40},{40,48},{48,56},{56,64},{64,7... | collective-permute-start | bytes 98312 | tf_op jit(solution)/shard_map/ppermute | solution.py:416
  23.0 0.8 gather_fusion
  23.7 2.0 %gather_fusion.1 = f32[128,256]{1,0:T(8,128)S(1)} fusion(f32[1024,256]{1,0:T(8,128)} %param.20, s32[1024]{0:T(1024)S(1)} %pad_clamp_fusion), kind=kCustom, calls=%fused_computation.1 | custom fusion | bytes 262656 | tf_op jit(solution)/shard_map/jit(_take)/gather | solution.py:421
  25.7 22.8 %collective-permute-done.1 = f32[16,512]{1,0:T(8,128)S(1)} collective-permute-done((f32[16,512]{1,0:T(8,128)S(1)}, f32[16,512]{1,0:T(8,128)S(1)}, u32[]{:S(2)}, u32[]{:S(2)}) %collective-permute-start.1) | collective-permute-done | bytes 32800 | tf_op jit(solution)/shard_map/ppermute | solution.py:416
  48.6 3.6 %collective-permute-start.2 = (bf16[32,144,128]{2,1,0:T(8,128)(2,1)S(1)}, bf16[32,144,128]{2,1,0:T(8,128)(2,1)S(1)}, u32[]{:S(2)}, u32[]{:S(2)}) collective-permute-start(bf16[32,144,128]{2,1,0:T(8,128)(2,1)S(1)} %all-to-all-done.own), channel_id=1, source_target_pairs={{0,1},{1,0},{2,3},{3,2},{4,5},{5,4},{6,7},{7,6},{8,9},{9,8},{10,11... | collective-permute-start | bytes 3538952 | tf_op jit(solution)/shard_map/ppermute | solution.py:334
  52.2 0.1 pad_add_fusion.pos
  52.2 1.6 %shard_map.193 = (f32[512,512]{1,0:T(8,128)S(1)}, f32[8,512]{1,0:T(8,128)S(1)}) custom-call(s32[3]{0:T(128)S(1)} %pad_add_fusion.pos, bf16[32,144,128]{2,1,0:T(8,128)(2,1)S(1)} %all-to-all-done.own), custom_call_target="tpu_custom_call" | custom-call | tf_op jit(solution)/shard_map/pallas_call | solution.py:34
  53.8 0.8 collective-permute-done.2.peer
  54.6 1.6 %shard_map.194 = (f32[136,512]{1,0:T(8,128)S(1)}, f32[136,512]{1,0:T(8,128)S(1)}, f32[136,512]{1,0:T(8,128)S(1)}, f32[136,512]{1,0:T(8,128)S(1)}) custom-call(s32[3]{0:T(128)S(1)} %pad_add_fusion.pos, bf16[32,144,128]{2,1,0:T(8,128)(2,1)S(1)} %collective-permute-done.2.peer, f32[512,512]{1,0:T(8,128)S(1)} %get-tuple-element.50.sums, ...), custom_call_target="tpu_custom_call" | custom-call | tf_op jit(solution)/shard_map/pallas_call | solution.py:34
  56.2 2.8 %collective-permute-start.3 = (f32[136,512]{1,0:T(8,128)S(1)}, f32[136,512]{1,0:T(8,128)S(1)}, u32[]{:S(2)}, u32[]{:S(2)}) collective-permute-start(f32[136,512]{1,0:T(8,128)S(1)} %get-tuple-element.52), channel_id=1, source_target_pairs={{0,4},{1,5},{2,6},{3,7},{4,0},{5,1},{6,2},{7,3},{8,12},{9,13},{10,... | collective-permute-start | bytes 835592 | tf_op jit(solution)/shard_map/ppermute | solution.py:338
  59.0 0.9 collective-permute-start.4
  59.9 0.6 collective-permute-start.5
  60.5 5.2 %collective-permute-done.3.p1_h = f32[136,512]{1,0:T(8,128)S(1)} collective-permute-done((f32[136,512]{1,0:T(8,128)S(1)}, f32[136,512]{1,0:T(8,128)S(1)}, u32[]{:S(2)}, u32[]{:S(2)}) %collective-permute-start.3) | collective-permute-done | bytes 278560 | tf_op jit(solution)/shard_map/ppermute | solution.py:338
  65.7 6.1 %collective-permute-done.4.p2_h = f32[136,512]{1,0:T(8,128)S(1)} collective-permute-done((f32[136,512]{1,0:T(8,128)S(1)}, f32[136,512]{1,0:T(8,128)S(1)}, u32[]{:S(2)}, u32[]{:S(2)}) %collective-permute-start.4) | collective-permute-done | bytes 278560 | tf_op jit(solution)/shard_map/ppermute | solution.py:338
  71.8 0.6 collective-permute-done.5.p3_h
  72.3 0.6 shard_map.195.refs_0_
  72.9 0.7 collective-permute-start.9
  73.6 1.2 collective-permute-start.6
  74.8 1.5 %collective-permute-start.7 = (bf16[144,512]{1,0:T(8,128)(2,1)S(1)}, bf16[144,512]{1,0:T(8,128)(2,1)S(1)}, u32[]{:S(2)}, u32[]{:S(2)}) collective-permute-start(bf16[144,512]{1,0:T(8,128)(2,1)S(1)} %shard_map.195.refs_0_), channel_id=1, source_target_pairs={{0,6},{1,7},{2,0},{3,1},{4,2},{5,3},{6,4},{7,5},{8,14},{9,15},{10,... | collective-permute-start | bytes 442376 | tf_op jit(solution)/shard_map/ppermute | solution.py:338
  76.3 1.4 collective-permute-start.8
  77.7 0.0 collective-permute-done.9.refs_1_
  77.7 2.0 %shard_map.196 = (f32[256,256]{1,0:T(8,128)S(1)}, f32[8,128]{1,0:T(8,128)S(1)}, f32[128,1024]{1,0:T(8,128)S(1)}) custom-call(s32[3]{0:T(128)S(1)} %pad_add_fusion.pos, bf16[144,512]{1,0:T(8,128)(2,1)S(1)} %shard_map.195.refs_0_, bf16[144,512]{1,0:T(8,128)(2,1)S(1)} %collective-permute-done.9.refs_1_, f32[1024,256]{1,0:T(8,128)S(1)} %copy-done, ...), custom_call_target="tpu_custom_call" | custom-call | tf_op jit(solution)/shard_map/pallas_call | solution.py:34
  79.8 0.5 collective-permute-done.6.refs_4_
  80.2 4.0 %collective-permute-done.8.refs_2_ = bf16[144,512]{1,0:T(8,128)(2,1)S(1)} collective-permute-done((bf16[144,512]{1,0:T(8,128)(2,1)S(1)}, bf16[144,512]{1,0:T(8,128)(2,1)S(1)}, u32[]{:S(2)}, u32[]{:S(2)}) %collective-permute-start.8) | collective-permute-done | bytes 147488 | tf_op jit(solution)/shard_map/ppermute | solution.py:338
  84.3 0.9 collective-permute-start.10
  85.1 0.0 collective-permute-start.11
  85.1 0.5 collective-permute-start.12
  85.6 0.5 collective-permute-done.10.refs_1_
  86.1 0.4 collective-permute-done.11.refs_3_
  86.5 0.2 collective-permute-done.12.refs_5_
  86.7 3.8 %shard_map.197 = (f32[1024,256]{1,0:T(8,128)}, f32[32,7,4,128]{3,2,1,0:T(4,128)S(1)}) custom-call(s32[3]{0:T(128)S(1)} %pad_add_fusion.pos, bf16[144,512]{1,0:T(8,128)(2,1)S(1)} %collective-permute-done.7.refs_0_, bf16[144,512]{1,0:T(8,128)(2,1)S(1)} %collective-permute-done.10.refs_1_, bf16[144,512]{1,0:T(8,128)(2,1)S(1)} %collective-permute-done.8.refs_2_, ...), custom_call_target="tpu_custom_call" | custom-call | tf_op jit(solution)/shard_map/pallas_call | solution.py:34
  90.5 17.2 %all_to_all.15.parts = f32[32,7,4,128]{3,2,1,0:T(4,128)S(1)} all-to-all(f32[32,7,4,128]{3,2,1,0:T(4,128)S(1)} %get-tuple-element.66), channel_id=1, replica_groups=mesh['node'=32,'rep'=8] {'node'}, dimensions={0} | all-to-all | bytes 917504 | tf_op jit(solution)/shard_map/all_to_all | solution.py:455
  107.7 0.8 shard_map.198
  108.5 7.7 %all-to-all-start.2 = ((f32[32,5,4,128]{3,2,1,0:T(4,128)}), f32[32,5,4,128]{3,2,1,0:T(4,128)S(1)}, u32[]{:S(2)}, u32[]{:S(2)}) async-start(f32[32,5,4,128]{3,2,1,0:T(4,128)} %get-tuple-element.67), calls=%async_computation.2 | async-start | bytes 655360 | tf_op jit(solution)/shard_map/all_to_all | solution.py:457
  116.3 0.9 collective-permute-start.13
  117.2 2.1 %collective-permute-start.14 = (f32[32,2,4,128]{3,2,1,0:T(4,128)S(1)}, f32[32,2,4,128]{3,2,1,0:T(4,128)S(1)}, u32[]{:S(2)}, u32[]{:S(2)}) collective-permute-start(f32[32,2,4,128]{3,2,1,0:T(4,128)S(1)} %get-tuple-element.70.a0), channel_id=1, source_target_pairs={{0,4},{1,5},{2,6},{3,7},{4,0},{5,1},{6,2},{7,3},{8,12},{9,13},{10,... | collective-permute-start | bytes 393224 | tf_op jit(solution)/shard_map/ppermute | solution.py:338
  119.3 0.3 collective-permute-start.15
  119.7 1.7 %collective-permute-start.16 = (f32[32,2,4,128]{3,2,1,0:T(4,128)S(1)}, f32[32,2,4,128]{3,2,1,0:T(4,128)S(1)}, u32[]{:S(2)}, u32[]{:S(2)}) collective-permute-start(f32[32,2,4,128]{3,2,1,0:T(4,128)S(1)} %get-tuple-element.70.a0), channel_id=1, source_target_pairs={{0,1},{1,0},{2,3},{3,2},{4,5},{5,4},{6,7},{7,6},{8,9},{9,8},{10,11... | collective-permute-start | bytes 393224 | tf_op jit(solution)/shard_map/ppermute | solution.py:334
  121.4 3.7 %collective-permute-start.17 = (f32[32,2,4,128]{3,2,1,0:T(4,128)S(1)}, f32[32,2,4,128]{3,2,1,0:T(4,128)S(1)}, u32[]{:S(2)}, u32[]{:S(2)}) collective-permute-start(f32[32,2,4,128]{3,2,1,0:T(4,128)S(1)} %collective-permute-done.13.a1), channel_id=1, source_target_pairs={{0,1},{1,0},{2,3},{3,2},{4,5},{5,4},{6,7},{7,6},{8,9},{9,8},{10,11... | collective-permute-start | bytes 393224 | tf_op jit(solution)/shard_map/ppermute | solution.py:334
  125.1 1.5 %collective-permute-start.18 = (f32[32,2,4,128]{3,2,1,0:T(4,128)S(1)}, f32[32,2,4,128]{3,2,1,0:T(4,128)S(1)}, u32[]{:S(2)}, u32[]{:S(2)}) collective-permute-start(f32[32,2,4,128]{3,2,1,0:T(4,128)S(1)} %collective-permute-done.14.a2), channel_id=1, source_target_pairs={{0,1},{1,0},{2,3},{3,2},{4,5},{5,4},{6,7},{7,6},{8,9},{9,8},{10,11... | collective-permute-start | bytes 393224 | tf_op jit(solution)/shard_map/ppermute | solution.py:334
  126.6 0.2 collective-permute-start.19
  126.8 0.7 collective-permute-done.18.b2
  127.6 0.4 collective-permute-done.19.b3
  128.0 3.0 %collective-permute-start.23 = (f32[29,5,4,128]{3,2,1,0:T(4,128)S(1)}, f32[29,5,4,128]{3,2,1,0:T(4,128)S(1)}, u32[]{:S(2)}, u32[]{:S(2)}) collective-permute-start(f32[29,5,4,128]{3,2,1,0:T(4,128)S(1)} %slice.2.refs_0_), channel_id=1, source_target_pairs={{0,1},{1,0},{2,3},{3,2},{4,5},{5,4},{6,7},{7,6},{8,9},{9,8},{10,11... | collective-permute-start | bytes 890888 | tf_op jit(solution)/shard_map/ppermute | solution.py:334
  131.0 0.6 collective-permute-start.20
  131.6 2.7 %collective-permute-start.21 = (f32[29,5,4,128]{3,2,1,0:T(4,128)S(1)}, f32[29,5,4,128]{3,2,1,0:T(4,128)S(1)}, u32[]{:S(2)}, u32[]{:S(2)}) collective-permute-start(f32[29,5,4,128]{3,2,1,0:T(4,128)S(1)} %slice.2.refs_0_), channel_id=1, source_target_pairs={{0,6},{1,7},{2,0},{3,1},{4,2},{5,3},{6,4},{7,5},{8,14},{9,15},{10,... | collective-permute-start | bytes 890888 | tf_op jit(solution)/shard_map/ppermute | solution.py:338
  134.3 3.9 %shard_map.199 = f32[1024,256]{1,0:T(8,128)} custom-call(s32[3]{0:T(128)S(1)} %pad_add_fusion.pos, s32[1,1024]{1,0:T(1,128)S(1)} %bitcast.16, f32[32,2,4,128]{3,2,1,0:T(4,128)S(1)} %get-tuple-element.70.a0, f32[32,2,4,128]{3,2,1,0:T(4,128)S(1)} %collective-permute-done.13.a1, f32[32,2,4,128]{3,2,1,0:T(4,128)S(1)} %collective-permute-done.14.a2, ...), custom_call_target="tpu_custom_call" | custom-call | tf_op jit(solution)/shard_map/pallas_call | solution.py:34
  138.1 1.4 shard_map.200
  139.6 1.6 %collective-permute-done.20.refs_0_ = f32[29,5,4,128]{3,2,1,0:T(4,128)S(1)} collective-permute-done((f32[29,5,4,128]{3,2,1,0:T(4,128)S(1)}, f32[29,5,4,128]{3,2,1,0:T(4,128)S(1)}, u32[]{:S(2)}, u32[]{:S(2)}) %collective-permute-start.20) | collective-permute-done | bytes 296992 | tf_op jit(solution)/shard_map/ppermute | solution.py:338
  141.1 5.8 %collective-permute-done.21.refs_1_ = f32[29,5,4,128]{3,2,1,0:T(4,128)S(1)} collective-permute-done((f32[29,5,4,128]{3,2,1,0:T(4,128)S(1)}, f32[29,5,4,128]{3,2,1,0:T(4,128)S(1)}, u32[]{:S(2)}, u32[]{:S(2)}) %collective-permute-start.21) | collective-permute-done | bytes 296992 | tf_op jit(solution)/shard_map/ppermute | solution.py:338
  146.9 0.9 collective-permute-done.22.refs_2_
  147.8 0.5 collective-permute-start.24
  148.3 0.0 collective-permute-start.25
  148.3 0.5 collective-permute-start.26
  148.8 1.6 %shard_map.201 = (f32[512,768]{1,0:T(8,128)}, f32[256,768]{1,0:T(8,128)}) custom-call(s32[3]{0:T(128)S(1)} %pad_add_fusion.pos, f32[29,5,4,128]{3,2,1,0:T(4,128)S(1)} %collective-permute-done.20.refs_0_, f32[29,5,4,128]{3,2,1,0:T(4,128)S(1)} %collective-permute-done.21.refs_1_, ...), custom_call_target="tpu_custom_call", output_to_operand_aliasing={{0}: (4, {}), {1}: (5, {})} | custom-call | tf_op jit(solution)/shard_map/pallas_call | solution.py:34
  150.4 1.6 %shard_map.202 = (f32[512,768]{1,0:T(8,128)}, f32[256,768]{1,0:T(8,128)}) custom-call(s32[3]{0:T(128)S(1)} %pad_add_fusion.pos, f32[29,5,4,128]{3,2,1,0:T(4,128)S(1)} %collective-permute-done.24.refs_0_, f32[29,5,4,128]{3,2,1,0:T(4,128)S(1)} %collective-permute-done.25.refs_1_, ...), custom_call_target="tpu_custom_call", output_to_operand_aliasing={{0}: (4, {}), {1}: (5, {})} | custom-call | tf_op jit(solution)/shard_map/pallas_call | solution.py:34
  (29 shorter events, 0.1 us)
Async XLA Ops:
  7.0 12.2 %copy-start.6 = (f32[96,512]{1,0:T(8,128)S(1)}, f32[96,512]{1,0:T(8,128)}, u32[]{:S(2)}) copy-start(f32[96,512]{1,0:T(8,128)} %get-tuple-element.48) | copy-start | bytes 589828
  7.0 13.3 %copy-start.4 = (s32[1024]{0:T(1024)S(1)}, s32[1024]{0:T(1024)}, u32[]{:S(2)}) copy-start(s32[1024]{0:T(1024)} %param.27) | copy-start | bytes 12292
  7.0 16.0 %copy-start.5 = (f32[1024,256]{1,0:T(8,128)S(1)}, f32[1024,256]{1,0:T(8,128)}, u32[]{:S(2)}) copy-start(f32[1024,256]{1,0:T(8,128)} %param.18) | copy-start | bytes 3145732
  7.0 41.6 %all-to-all-start = ((bf16[32,144,128]{2,1,0:T(8,128)(2,1)}), bf16[32,144,128]{2,1,0:T(8,128)(2,1)S(1)}, u32[]{:S(2)}, u32[]{:S(2)}) async-start(bf16[32,144,128]{2,1,0:T(8,128)(2,1)} %get-tuple-element.47), calls=%async_computation | async-start | bytes 2359296 | tf_op jit(solution)/shard_map/all_to_all | solution.py:412
  19.2 2.1 %collective-permute-start = (f32[96,512]{1,0:T(8,128)S(1)}, f32[96,512]{1,0:T(8,128)S(1)}, u32[]{:S(2)}, u32[]{:S(2)}) collective-permute-start(f32[96,512]{1,0:T(8,128)S(1)} %copy-done.6), channel_id=1, source_target_pairs={{0,1},{1,0},{2,3},{3,2},{4,5},{5,4},{6,7},{7,6},{8,9},{9,8},{10,11... | collective-permute-start | bytes 589832 | tf_op jit(solution)/shard_map/ppermute | solution.py:334
  21.4 27.2 %collective-permute-start.1 = (f32[16,512]{1,0:T(8,128)S(1)}, f32[16,512]{1,0:T(8,128)S(1)}, u32[]{:S(2)}, u32[]{:S(2)}) collective-permute-start(f32[16,512]{1,0:T(8,128)S(1)} %constant_dynamic-slice_fusion), channel_id=1, source_target_pairs={{0,8},{8,16},{16,24},{24,32},{32,40},{40,48},{48,56},{56,64},{64,7... | collective-permute-start | bytes 98312 | tf_op jit(solution)/shard_map/ppermute | solution.py:416
  48.6 6.1 %collective-permute-start.2 = (bf16[32,144,128]{2,1,0:T(8,128)(2,1)S(1)}, bf16[32,144,128]{2,1,0:T(8,128)(2,1)S(1)}, u32[]{:S(2)}, u32[]{:S(2)}) collective-permute-start(bf16[32,144,128]{2,1,0:T(8,128)(2,1)S(1)} %all-to-all-done.own), channel_id=1, source_target_pairs={{0,1},{1,0},{2,3},{3,2},{4,5},{5,4},{6,7},{7,6},{8,9},{9,8},{10,11... | collective-permute-start | bytes 3538952 | tf_op jit(solution)/shard_map/ppermute | solution.py:334
  54.6 23.1 %copy-start = (f32[1024,256]{1,0:T(8,128)S(1)}, f32[1024,256]{1,0:T(8,128)}, u32[]{:S(2)}) copy-start(f32[1024,256]{1,0:T(8,128)} %refs_6_.3) | copy-start | bytes 3145732
  54.6 23.1 %copy-start.1 = (f32[1024,256]{1,0:T(8,128)S(1)}, f32[1024,256]{1,0:T(8,128)}, u32[]{:S(2)}) copy-start(f32[1024,256]{1,0:T(8,128)} %refs_7_.3) | copy-start | bytes 3145732
  54.6 23.1 %copy-start.2 = (bf16[512,768]{1,0:T(8,128)(2,1)S(1)}, bf16[512,768]{1,0:T(8,128)(2,1)}, u32[]{:S(2)}) copy-start(bf16[512,768]{1,0:T(8,128)(2,1)} %refs_10_.1) | copy-start | bytes 2359300
  54.6 23.1 %copy-start.3 = (bf16[256,768]{1,0:T(8,128)(2,1)S(1)}, bf16[256,768]{1,0:T(8,128)(2,1)}, u32[]{:S(2)}) copy-start(bf16[256,768]{1,0:T(8,128)(2,1)} %refs_11_.1) | copy-start | bytes 1179652
  56.2 9.5 %collective-permute-start.3 = (f32[136,512]{1,0:T(8,128)S(1)}, f32[136,512]{1,0:T(8,128)S(1)}, u32[]{:S(2)}, u32[]{:S(2)}) collective-permute-start(f32[136,512]{1,0:T(8,128)S(1)} %get-tuple-element.52), channel_id=1, source_target_pairs={{0,4},{1,5},{2,6},{3,7},{4,0},{5,1},{6,2},{7,3},{8,12},{9,13},{10,... | collective-permute-start | bytes 835592 | tf_op jit(solution)/shard_map/ppermute | solution.py:338
  59.0 12.7 %collective-permute-start.4 = (f32[136,512]{1,0:T(8,128)S(1)}, f32[136,512]{1,0:T(8,128)S(1)}, u32[]{:S(2)}, u32[]{:S(2)}) collective-permute-start(f32[136,512]{1,0:T(8,128)S(1)} %get-tuple-element.53), channel_id=1, source_target_pairs={{0,6},{1,7},{2,0},{3,1},{4,2},{5,3},{6,4},{7,5},{8,14},{9,15},{10,... | collective-permute-start | bytes 835592 | tf_op jit(solution)/shard_map/ppermute | solution.py:338
  59.9 12.5 %collective-permute-start.5 = (f32[136,512]{1,0:T(8,128)S(1)}, f32[136,512]{1,0:T(8,128)S(1)}, u32[]{:S(2)}, u32[]{:S(2)}) collective-permute-start(f32[136,512]{1,0:T(8,128)S(1)} %get-tuple-element.54), channel_id=1, source_target_pairs={{0,2},{1,3},{2,4},{3,5},{4,6},{5,7},{6,0},{7,1},{8,10},{9,11},{10,... | collective-permute-start | bytes 835592 | tf_op jit(solution)/shard_map/ppermute | solution.py:338
  72.9 4.8 %collective-permute-start.9 = (bf16[144,512]{1,0:T(8,128)(2,1)S(1)}, bf16[144,512]{1,0:T(8,128)(2,1)S(1)}, u32[]{:S(2)}, u32[]{:S(2)}) collective-permute-start(bf16[144,512]{1,0:T(8,128)(2,1)S(1)} %shard_map.195.refs_0_), channel_id=1, source_target_pairs={{0,1},{1,0},{2,3},{3,2},{4,5},{5,4},{6,7},{7,6},{8,9},{9,8},{10,11... | collective-permute-start | bytes 442376 | tf_op jit(solution)/shard_map/ppermute | solution.py:334
  73.6 6.6 %collective-permute-start.6 = (bf16[144,512]{1,0:T(8,128)(2,1)S(1)}, bf16[144,512]{1,0:T(8,128)(2,1)S(1)}, u32[]{:S(2)}, u32[]{:S(2)}) collective-permute-start(bf16[144,512]{1,0:T(8,128)(2,1)S(1)} %shard_map.195.refs_0_), channel_id=1, source_target_pairs={{0,2},{1,3},{2,4},{3,5},{4,6},{5,7},{6,0},{7,1},{8,10},{9,11},{10,... | collective-permute-start | bytes 442376 | tf_op jit(solution)/shard_map/ppermute | solution.py:338
  74.8 5.5 %collective-permute-start.7 = (bf16[144,512]{1,0:T(8,128)(2,1)S(1)}, bf16[144,512]{1,0:T(8,128)(2,1)S(1)}, u32[]{:S(2)}, u32[]{:S(2)}) collective-permute-start(bf16[144,512]{1,0:T(8,128)(2,1)S(1)} %shard_map.195.refs_0_), channel_id=1, source_target_pairs={{0,6},{1,7},{2,0},{3,1},{4,2},{5,3},{6,4},{7,5},{8,14},{9,15},{10,... | collective-permute-start | bytes 442376 | tf_op jit(solution)/shard_map/ppermute | solution.py:338
  76.3 7.9 %collective-permute-start.8 = (bf16[144,512]{1,0:T(8,128)(2,1)S(1)}, bf16[144,512]{1,0:T(8,128)(2,1)S(1)}, u32[]{:S(2)}, u32[]{:S(2)}) collective-permute-start(bf16[144,512]{1,0:T(8,128)(2,1)S(1)} %shard_map.195.refs_0_), channel_id=1, source_target_pairs={{0,4},{1,5},{2,6},{3,7},{4,0},{5,1},{6,2},{7,3},{8,12},{9,13},{10,... | collective-permute-start | bytes 442376 | tf_op jit(solution)/shard_map/ppermute | solution.py:338
  84.3 1.9 %collective-permute-start.10 = (bf16[144,512]{1,0:T(8,128)(2,1)S(1)}, bf16[144,512]{1,0:T(8,128)(2,1)S(1)}, u32[]{:S(2)}, u32[]{:S(2)}) collective-permute-start(bf16[144,512]{1,0:T(8,128)(2,1)S(1)} %collective-permute-done.7.refs_0_), channel_id=1, source_target_pairs={{0,1},{1,0},{2,3},{3,2},{4,5},{5,4},{6,7},{7,6},{8,9},{9,8},{10,11... | collective-permute-start | bytes 442376 | tf_op jit(solution)/shard_map/ppermute | solution.py:334
  85.1 1.4 collective-permute-start.11
  85.1 1.6 %collective-permute-start.12 = (bf16[144,512]{1,0:T(8,128)(2,1)S(1)}, bf16[144,512]{1,0:T(8,128)(2,1)S(1)}, u32[]{:S(2)}, u32[]{:S(2)}) collective-permute-start(bf16[144,512]{1,0:T(8,128)(2,1)S(1)} %collective-permute-done.6.refs_4_), channel_id=1, source_target_pairs={{0,1},{1,0},{2,3},{3,2},{4,5},{5,4},{6,7},{7,6},{8,9},{9,8},{10,11... | collective-permute-start | bytes 442376 | tf_op jit(solution)/shard_map/ppermute | solution.py:334
  108.5 19.4 %all-to-all-start.2 = ((f32[32,5,4,128]{3,2,1,0:T(4,128)}), f32[32,5,4,128]{3,2,1,0:T(4,128)S(1)}, u32[]{:S(2)}, u32[]{:S(2)}) async-start(f32[32,5,4,128]{3,2,1,0:T(4,128)} %get-tuple-element.67), calls=%async_computation.2 | async-start | bytes 655360 | tf_op jit(solution)/shard_map/all_to_all | solution.py:457
  116.3 5.1 %collective-permute-start.13 = (f32[32,2,4,128]{3,2,1,0:T(4,128)S(1)}, f32[32,2,4,128]{3,2,1,0:T(4,128)S(1)}, u32[]{:S(2)}, u32[]{:S(2)}) collective-permute-start(f32[32,2,4,128]{3,2,1,0:T(4,128)S(1)} %get-tuple-element.70.a0), channel_id=1, source_target_pairs={{0,2},{1,3},{2,4},{3,5},{4,6},{5,7},{6,0},{7,1},{8,10},{9,11},{10,... | collective-permute-start | bytes 393224 | tf_op jit(solution)/shard_map/ppermute | solution.py:338
  117.2 7.9 %collective-permute-start.14 = (f32[32,2,4,128]{3,2,1,0:T(4,128)S(1)}, f32[32,2,4,128]{3,2,1,0:T(4,128)S(1)}, u32[]{:S(2)}, u32[]{:S(2)}) collective-permute-start(f32[32,2,4,128]{3,2,1,0:T(4,128)S(1)} %get-tuple-element.70.a0), channel_id=1, source_target_pairs={{0,4},{1,5},{2,6},{3,7},{4,0},{5,1},{6,2},{7,3},{8,12},{9,13},{10,... | collective-permute-start | bytes 393224 | tf_op jit(solution)/shard_map/ppermute | solution.py:338
  119.3 7.3 %collective-permute-start.15 = (f32[32,2,4,128]{3,2,1,0:T(4,128)S(1)}, f32[32,2,4,128]{3,2,1,0:T(4,128)S(1)}, u32[]{:S(2)}, u32[]{:S(2)}) collective-permute-start(f32[32,2,4,128]{3,2,1,0:T(4,128)S(1)} %get-tuple-element.70.a0), channel_id=1, source_target_pairs={{0,6},{1,7},{2,0},{3,1},{4,2},{5,3},{6,4},{7,5},{8,14},{9,15},{10,... | collective-permute-start | bytes 393224 | tf_op jit(solution)/shard_map/ppermute | solution.py:338
  119.7 7.2 %collective-permute-start.16 = (f32[32,2,4,128]{3,2,1,0:T(4,128)S(1)}, f32[32,2,4,128]{3,2,1,0:T(4,128)S(1)}, u32[]{:S(2)}, u32[]{:S(2)}) collective-permute-start(f32[32,2,4,128]{3,2,1,0:T(4,128)S(1)} %get-tuple-element.70.a0), channel_id=1, source_target_pairs={{0,1},{1,0},{2,3},{3,2},{4,5},{5,4},{6,7},{7,6},{8,9},{9,8},{10,11... | collective-permute-start | bytes 393224 | tf_op jit(solution)/shard_map/ppermute | solution.py:334
  121.4 5.5 %collective-permute-start.17 = (f32[32,2,4,128]{3,2,1,0:T(4,128)S(1)}, f32[32,2,4,128]{3,2,1,0:T(4,128)S(1)}, u32[]{:S(2)}, u32[]{:S(2)}) collective-permute-start(f32[32,2,4,128]{3,2,1,0:T(4,128)S(1)} %collective-permute-done.13.a1), channel_id=1, source_target_pairs={{0,1},{1,0},{2,3},{3,2},{4,5},{5,4},{6,7},{7,6},{8,9},{9,8},{10,11... | collective-permute-start | bytes 393224 | tf_op jit(solution)/shard_map/ppermute | solution.py:334
  125.1 2.5 %collective-permute-start.18 = (f32[32,2,4,128]{3,2,1,0:T(4,128)S(1)}, f32[32,2,4,128]{3,2,1,0:T(4,128)S(1)}, u32[]{:S(2)}, u32[]{:S(2)}) collective-permute-start(f32[32,2,4,128]{3,2,1,0:T(4,128)S(1)} %collective-permute-done.14.a2), channel_id=1, source_target_pairs={{0,1},{1,0},{2,3},{3,2},{4,5},{5,4},{6,7},{7,6},{8,9},{9,8},{10,11... | collective-permute-start | bytes 393224 | tf_op jit(solution)/shard_map/ppermute | solution.py:334
  126.6 1.3 collective-permute-start.19
  128.0 10.1 %collective-permute-start.23 = (f32[29,5,4,128]{3,2,1,0:T(4,128)S(1)}, f32[29,5,4,128]{3,2,1,0:T(4,128)S(1)}, u32[]{:S(2)}, u32[]{:S(2)}) collective-permute-start(f32[29,5,4,128]{3,2,1,0:T(4,128)S(1)} %slice.2.refs_0_), channel_id=1, source_target_pairs={{0,1},{1,0},{2,3},{3,2},{4,5},{5,4},{6,7},{7,6},{8,9},{9,8},{10,11... | collective-permute-start | bytes 890888 | tf_op jit(solution)/shard_map/ppermute | solution.py:334
  131.0 10.2 %collective-permute-start.20 = (f32[29,5,4,128]{3,2,1,0:T(4,128)S(1)}, f32[29,5,4,128]{3,2,1,0:T(4,128)S(1)}, u32[]{:S(2)}, u32[]{:S(2)}) collective-permute-start(f32[29,5,4,128]{3,2,1,0:T(4,128)S(1)} %slice.2.refs_0_), channel_id=1, source_target_pairs={{0,4},{1,5},{2,6},{3,7},{4,0},{5,1},{6,2},{7,3},{8,12},{9,13},{10,... | collective-permute-start | bytes 890888 | tf_op jit(solution)/shard_map/ppermute | solution.py:338
  131.6 15.3 %collective-permute-start.21 = (f32[29,5,4,128]{3,2,1,0:T(4,128)S(1)}, f32[29,5,4,128]{3,2,1,0:T(4,128)S(1)}, u32[]{:S(2)}, u32[]{:S(2)}) collective-permute-start(f32[29,5,4,128]{3,2,1,0:T(4,128)S(1)} %slice.2.refs_0_), channel_id=1, source_target_pairs={{0,6},{1,7},{2,0},{3,1},{4,2},{5,3},{6,4},{7,5},{8,14},{9,15},{10,... | collective-permute-start | bytes 890888 | tf_op jit(solution)/shard_map/ppermute | solution.py:338
  134.2 13.6 %collective-permute-start.22 = (f32[29,5,4,128]{3,2,1,0:T(4,128)S(1)}, f32[29,5,4,128]{3,2,1,0:T(4,128)S(1)}, u32[]{:S(2)}, u32[]{:S(2)}) collective-permute-start(f32[29,5,4,128]{3,2,1,0:T(4,128)S(1)} %slice.2.refs_0_), channel_id=1, source_target_pairs={{0,2},{1,3},{2,4},{3,5},{4,6},{5,7},{6,0},{7,1},{8,10},{9,11},{10,... | collective-permute-start | bytes 890888 | tf_op jit(solution)/shard_map/ppermute | solution.py:338
  147.8 2.6 %collective-permute-start.24 = (f32[29,5,4,128]{3,2,1,0:T(4,128)S(1)}, f32[29,5,4,128]{3,2,1,0:T(4,128)S(1)}, u32[]{:S(2)}, u32[]{:S(2)}) collective-permute-start(f32[29,5,4,128]{3,2,1,0:T(4,128)S(1)} %collective-permute-done.20.refs_0_), channel_id=1, source_target_pairs={{0,1},{1,0},{2,3},{3,2},{4,5},{5,4},{6,7},{7,6},{8,9},{9,8},{10,11... | collective-permute-start | bytes 890888 | tf_op jit(solution)/shard_map/ppermute | solution.py:334
  148.3 2.1 %collective-permute-start.25 = (f32[29,5,4,128]{3,2,1,0:T(4,128)S(1)}, f32[29,5,4,128]{3,2,1,0:T(4,128)S(1)}, u32[]{:S(2)}, u32[]{:S(2)}) collective-permute-start(f32[29,5,4,128]{3,2,1,0:T(4,128)S(1)} %collective-permute-done.21.refs_1_), channel_id=1, source_target_pairs={{0,1},{1,0},{2,3},{3,2},{4,5},{5,4},{6,7},{7,6},{8,9},{9,8},{10,11... | collective-permute-start | bytes 890888 | tf_op jit(solution)/shard_map/ppermute | solution.py:334
  148.3 2.1 %collective-permute-start.26 = (f32[29,5,4,128]{3,2,1,0:T(4,128)S(1)}, f32[29,5,4,128]{3,2,1,0:T(4,128)S(1)}, u32[]{:S(2)}, u32[]{:S(2)}) collective-permute-start(f32[29,5,4,128]{3,2,1,0:T(4,128)S(1)} %collective-permute-done.22.refs_2_), channel_id=1, source_target_pairs={{0,1},{1,0},{2,3},{3,2},{4,5},{5,4},{6,7},{7,6},{8,9},{9,8},{10,11... | collective-permute-start | bytes 890888 | tf_op jit(solution)/shard_map/ppermute | solution.py:334

commit v9 on v8

--- a/solution.py
+++ b/solution.py
@@ -448,7 +448,7 @@
         (SM,),
         (pos, agg, swap_core(agg), *shared),
     )
-    near, back, far, new_own = lax.optimization_barrier((near, back, far, new_own))
+    far, back, near, new_own = lax.optimization_barrier((far, back, near, new_own))
     parts = (back, swap_core(back), far, swap_core(far), near, swap_core(near))
     new_memory, grad = last_update(pos, parts, shared, (new_own,), hot_own, acc)
 
@@ -465,23 +465,18 @@
         (pltpu.VMEM((8, 128, 256), F32),),
     )
     own = [grad[0:29]] + [shift_x(grad[0:29], d) for d in (1, 2, 3)]
+    own[2], new_hot = lax.optimization_barrier((own[2], new_hot))
     grads = ()
-    for blocks in (((0, False), (0, True)), tuple((d, False) for d in (2, 3, 1)), tuple((d, True) for d in (2, 3, 1))):
-        parts = [swap_core(own[d]) if other else own[d] for d, other in blocks]
-        n = len(parts)
+    for other in (False, True):
         grads = call(
-            functools.partial(place_kernel, blocks),
+            functools.partial(place_kernel, tuple((d, other) for d in range(4))),
             (sds((512, 768), F32), sds((256, 768), F32)),
-            (SM,) + (VM,) * n + (ANY,) * len(grads),
-            (pos, *parts, *grads),
-            (pltpu.VMEM((96 * n, 768), F32), pltpu.SemaphoreType.DMA((2 * n,))),
+            (SM, VM, VM, VM, VM) + (ANY,) * len(grads),
+            (pos, *[swap_core(v) if other else v for v in own], *grads),
+            (pltpu.VMEM((384, 768), F32), pltpu.SemaphoreType.DMA((8,))),
             (ANY, ANY),
-            aliases={n + 1: 0, n + 2: 1} if grads else {},
+            aliases={5: 0, 6: 1} if grads else {},
         )
-        if n == 2:
-            own[2], own[3], own[1], new_hot, *grads = lax.optimization_barrier(
-                (own[2], own[3], own[1], new_hot, *grads)
-            )
     grad_in, grad_hid = grads
     return (new_memory, new_hot, grad_in, grad_hid)
 

time: 153 us -> 151 us (0.987)
  waiting for transfers between devices: 51.3 us -> 48.6 us
  starting transfers between devices: 54.4 us -> 56.9 us
    ppermute x14, starting transfers between devices: 17.9 us -> 21.7 us  [swap_core(): return lax.ppermute(v, 'rep', [(k, k ^ 1) for k in range(8)])]
    ppermute x12, waiting for transfers between devices: 24.6 us -> 21.9 us  [shift_x(): return lax.ppermute(v, 'rep', [(k, (k + 2 * d) % 8) for k in range(8)])]
    pallas_call x11 -> x10, Pallas kernels: 25.1 us -> 23.9 us  [call(): pl.pallas_call(body, out_shape=out_shape, in_specs=list(places) + [VM] *...]
  transfers between devices with their start and end apart: 29 -> 29, of which waited for: 16 -> 15; matrix products, arithmetic and copies ran while one was open for 2% -> 2% of each run, Pallas kernels for 7% -> 6%
where the time goes in v9:
time: 151 us
  starting transfers between devices  56.9 us (38%)
  waiting for transfers between devices  48.6 us (32%)
  Pallas kernels  23.9 us (16%)
  blocking collectives  17.2 us (11%)
  local copies, waits for them, and re-layouts  2.81 us (2%)
    pallas_call x10, Pallas kernels, call(): pl.pallas_call(body, out_shape=out_shape, in_specs=list(places) + [VM] *...  23.9 us
    ppermute x1, waiting for transfers between devices, on_device(): spill = lax.ppermute(spill, 'node', [(k, (k + 1) % 32) for k in range(32)])  22.8 us
    ppermute x12, waiting for transfers between devices, shift_x(): return lax.ppermute(v, 'rep', [(k, (k + 2 * d) % 8) for k in range(8)])  21.9 us
    ppermute x14, starting transfers between devices, swap_core(): return lax.ppermute(v, 'rep', [(k, k ^ 1) for k in range(8)])  21.7 us
    all_to_all x1, blocking collectives, on_device(): grad = lax.all_to_all(grad, 'node', split_axis=0, concat_axis=0, tiled=True)  17.2 us
    ppermute x12, starting transfers between devices, shift_x(): return lax.ppermute(v, 'rep', [(k, (k + 2 * d) % 8) for k in range(8)])  13.7 us
    all_to_all x1, starting transfers between devices, on_device(): recv = lax.all_to_all(send, 'node', split_axis=0, concat_axis=0, tiled=True)  12.2 us
    all_to_all x1, starting transfers between devices, on_device(): grad = lax.all_to_all(grad, 'node', split_axis=0, concat_axis=0, tiled=True)  7.72 us
  transfers between devices with their start and end apart: 29, of which 15 were waited for; matrix products, arithmetic and copies ran while one was open for 2% of the time, Pallas kernels for 6%

profile of v9, /device:TPU:1, one launch (start us, length us, event | category | flops | bytes accessed | tf_op | source)
XLA Modules:
  0.0 150.6 jit_solution(7935781807982259453)
XLA Ops:
  0.6 6.3 %shard_map.192 = (bf16[32,144,128]{2,1,0:T(8,128)(2,1)}, f32[96,512]{1,0:T(8,128)}) custom-call(s32[1]{0:T(128)} %bitcast.3.pos, f32[1024,256]{1,0:T(8,128)} %refs_6_.3, bf16[1024,128]{1,0:T(8,128)(2,1)} %edge_h.1, bf16[512,512]{1,0:T(8,128)(2,1)} %w_h.1, s32[1,1024]{1,0:T(1,128)} %bitcast.17, s32[1,1024]{1,0:T(1,128)} %bitcast.18, s32[1,1024]{1,0:T(1,128)} %bitcast.19, ...), custom_call_target="tpu_custom_call" | custom-call | tf_op jit(solution)/shard_map/pallas_call | solution.py:34
  7.0 0.0 copy-start.6
  7.0 0.0 copy-start.4
  7.0 0.0 copy-start.5
  7.0 12.2 %all-to-all-start = ((bf16[32,144,128]{2,1,0:T(8,128)(2,1)}), bf16[32,144,128]{2,1,0:T(8,128)(2,1)S(1)}, u32[]{:S(2)}, u32[]{:S(2)}) async-start(bf16[32,144,128]{2,1,0:T(8,128)(2,1)} %get-tuple-element.41), calls=%async_computation | async-start | bytes 2359296 | tf_op jit(solution)/shard_map/all_to_all | solution.py:412
  19.2 1.0 collective-permute-start
  20.3 0.2 select_reduce_fusion
  20.5 0.9 collective-permute-done
  21.4 1.6 %collective-permute-start.1 = (f32[16,512]{1,0:T(8,128)S(1)}, f32[16,512]{1,0:T(8,128)S(1)}, u32[]{:S(2)}, u32[]{:S(2)}) collective-permute-start(f32[16,512]{1,0:T(8,128)S(1)} %constant_dynamic-slice_fusion), channel_id=1, source_target_pairs={{0,8},{8,16},{16,24},{24,32},{32,40},{40,48},{48,56},{56,64},{64,7... | collective-permute-start | bytes 98312 | tf_op jit(solution)/shard_map/ppermute | solution.py:416
  23.0 0.8 gather_fusion.1
  23.7 2.0 %gather_fusion = f32[128,256]{1,0:T(8,128)S(1)} fusion(f32[1024,256]{1,0:T(8,128)} %param.18, s32[1024]{0:T(1024)S(1)} %pad_clamp_fusion), kind=kCustom, calls=%fused_computation | custom fusion | bytes 262656 | tf_op jit(solution)/shard_map/jit(_take)/gather | solution.py:420
  25.7 22.8 %collective-permute-done.1 = f32[16,512]{1,0:T(8,128)S(1)} collective-permute-done((f32[16,512]{1,0:T(8,128)S(1)}, f32[16,512]{1,0:T(8,128)S(1)}, u32[]{:S(2)}, u32[]{:S(2)}) %collective-permute-start.1) | collective-permute-done | bytes 32800 | tf_op jit(solution)/shard_map/ppermute | solution.py:416
  48.6 3.6 %collective-permute-start.2 = (bf16[32,144,128]{2,1,0:T(8,128)(2,1)S(1)}, bf16[32,144,128]{2,1,0:T(8,128)(2,1)S(1)}, u32[]{:S(2)}, u32[]{:S(2)}) collective-permute-start(bf16[32,144,128]{2,1,0:T(8,128)(2,1)S(1)} %all-to-all-done.own), channel_id=1, source_target_pairs={{0,1},{1,0},{2,3},{3,2},{4,5},{5,4},{6,7},{7,6},{8,9},{9,8},{10,11... | collective-permute-start | bytes 3538952 | tf_op jit(solution)/shard_map/ppermute | solution.py:334
  52.2 0.1 pad_add_fusion.pos
  52.2 1.6 %shard_map.193 = (f32[512,512]{1,0:T(8,128)S(1)}, f32[8,512]{1,0:T(8,128)S(1)}) custom-call(s32[3]{0:T(128)S(1)} %pad_add_fusion.pos, bf16[32,144,128]{2,1,0:T(8,128)(2,1)S(1)} %all-to-all-done.own), custom_call_target="tpu_custom_call" | custom-call | tf_op jit(solution)/shard_map/pallas_call | solution.py:34
  53.8 0.8 collective-permute-done.2.peer
  54.6 1.5 %shard_map.194 = (f32[136,512]{1,0:T(8,128)S(1)}, f32[136,512]{1,0:T(8,128)S(1)}, f32[136,512]{1,0:T(8,128)S(1)}, f32[136,512]{1,0:T(8,128)S(1)}) custom-call(s32[3]{0:T(128)S(1)} %pad_add_fusion.pos, bf16[32,144,128]{2,1,0:T(8,128)(2,1)S(1)} %collective-permute-done.2.peer, f32[512,512]{1,0:T(8,128)S(1)} %get-tuple-element.44.sums, ...), custom_call_target="tpu_custom_call" | custom-call | tf_op jit(solution)/shard_map/pallas_call | solution.py:34
  56.2 0.0 copy-start
  56.2 2.8 %collective-permute-start.3 = (f32[136,512]{1,0:T(8,128)S(1)}, f32[136,512]{1,0:T(8,128)S(1)}, u32[]{:S(2)}, u32[]{:S(2)}) collective-permute-start(f32[136,512]{1,0:T(8,128)S(1)} %get-tuple-element.46), channel_id=1, source_target_pairs={{0,4},{1,5},{2,6},{3,7},{4,0},{5,1},{6,2},{7,3},{8,12},{9,13},{10,... | collective-permute-start | bytes 835592 | tf_op jit(solution)/shard_map/ppermute | solution.py:338
  59.0 0.9 collective-permute-start.4
  59.9 0.6 collective-permute-start.5
  60.5 5.2 %collective-permute-done.3.p1_h = f32[136,512]{1,0:T(8,128)S(1)} collective-permute-done((f32[136,512]{1,0:T(8,128)S(1)}, f32[136,512]{1,0:T(8,128)S(1)}, u32[]{:S(2)}, u32[]{:S(2)}) %collective-permute-start.3) | collective-permute-done | bytes 278560 | tf_op jit(solution)/shard_map/ppermute | solution.py:338
  65.7 6.1 %collective-permute-done.4.p2_h = f32[136,512]{1,0:T(8,128)S(1)} collective-permute-done((f32[136,512]{1,0:T(8,128)S(1)}, f32[136,512]{1,0:T(8,128)S(1)}, u32[]{:S(2)}, u32[]{:S(2)}) %collective-permute-start.4) | collective-permute-done | bytes 278560 | tf_op jit(solution)/shard_map/ppermute | solution.py:338
  71.8 0.6 collective-permute-done.5.p3_h
  72.3 0.6 shard_map.195.refs_0_
  72.9 0.7 collective-permute-start.9
  73.6 1.2 collective-permute-start.8
  74.8 1.5 %collective-permute-start.7 = (bf16[144,512]{1,0:T(8,128)(2,1)S(1)}, bf16[144,512]{1,0:T(8,128)(2,1)S(1)}, u32[]{:S(2)}, u32[]{:S(2)}) collective-permute-start(bf16[144,512]{1,0:T(8,128)(2,1)S(1)} %shard_map.195.refs_0_), channel_id=1, source_target_pairs={{0,6},{1,7},{2,0},{3,1},{4,2},{5,3},{6,4},{7,5},{8,14},{9,15},{10,... | collective-permute-start | bytes 442376 | tf_op jit(solution)/shard_map/ppermute | solution.py:338
  76.3 1.4 collective-permute-start.6
  77.7 0.0 collective-permute-done.9.refs_1_
  77.7 2.0 %shard_map.196 = (f32[256,256]{1,0:T(8,128)S(1)}, f32[8,128]{1,0:T(8,128)S(1)}, f32[128,1024]{1,0:T(8,128)S(1)}) custom-call(s32[3]{0:T(128)S(1)} %pad_add_fusion.pos, bf16[144,512]{1,0:T(8,128)(2,1)S(1)} %shard_map.195.refs_0_, bf16[144,512]{1,0:T(8,128)(2,1)S(1)} %collective-permute-done.9.refs_1_, f32[1024,256]{1,0:T(8,128)S(1)} %copy-done, ...), custom_call_target="tpu_custom_call" | custom-call | tf_op jit(solution)/shard_map/pallas_call | solution.py:34
  79.8 0.5 collective-permute-done.8.refs_4_
  80.2 0.0 collective-permute-done.7.refs_0_
  80.2 4.0 %collective-permute-done.6.refs_2_ = bf16[144,512]{1,0:T(8,128)(2,1)S(1)} collective-permute-done((bf16[144,512]{1,0:T(8,128)(2,1)S(1)}, bf16[144,512]{1,0:T(8,128)(2,1)S(1)}, u32[]{:S(2)}, u32[]{:S(2)}) %collective-permute-start.6) | collective-permute-done | bytes 147488 | tf_op jit(solution)/shard_map/ppermute | solution.py:338
  84.3 0.9 collective-permute-start.10
  85.1 0.0 collective-permute-start.11
  85.1 0.5 collective-permute-start.12
  85.6 0.5 collective-permute-done.10.refs_1_
  86.1 0.4 collective-permute-done.11.refs_3_
  86.5 0.2 collective-permute-done.12.refs_5_
  86.7 3.8 %shard_map.197 = (f32[1024,256]{1,0:T(8,128)}, f32[32,7,4,128]{3,2,1,0:T(4,128)S(1)}) custom-call(s32[3]{0:T(128)S(1)} %pad_add_fusion.pos, bf16[144,512]{1,0:T(8,128)(2,1)S(1)} %collective-permute-done.7.refs_0_, bf16[144,512]{1,0:T(8,128)(2,1)S(1)} %collective-permute-done.10.refs_1_, bf16[144,512]{1,0:T(8,128)(2,1)S(1)} %collective-permute-done.6.refs_2_, ...), custom_call_target="tpu_custom_call" | custom-call | tf_op jit(solution)/shard_map/pallas_call | solution.py:34
  90.5 17.2 %all_to_all.15.parts = f32[32,7,4,128]{3,2,1,0:T(4,128)S(1)} all-to-all(f32[32,7,4,128]{3,2,1,0:T(4,128)S(1)} %get-tuple-element.60), channel_id=1, replica_groups=mesh['node'=32,'rep'=8] {'node'}, dimensions={0} | all-to-all | bytes 917504 | tf_op jit(solution)/shard_map/all_to_all | solution.py:455
  107.7 0.8 shard_map.198
  108.5 7.7 %all-to-all-start.2 = ((f32[32,5,4,128]{3,2,1,0:T(4,128)}), f32[32,5,4,128]{3,2,1,0:T(4,128)S(1)}, u32[]{:S(2)}, u32[]{:S(2)}) async-start(f32[32,5,4,128]{3,2,1,0:T(4,128)} %get-tuple-element.61), calls=%async_computation.2 | async-start | bytes 655360 | tf_op jit(solution)/shard_map/all_to_all | solution.py:457
  116.3 1.9 %collective-permute-start.15 = (f32[32,2,4,128]{3,2,1,0:T(4,128)S(1)}, f32[32,2,4,128]{3,2,1,0:T(4,128)S(1)}, u32[]{:S(2)}, u32[]{:S(2)}) collective-permute-start(f32[32,2,4,128]{3,2,1,0:T(4,128)S(1)} %get-tuple-element.64.a0), channel_id=1, source_target_pairs={{0,6},{1,7},{2,0},{3,1},{4,2},{5,3},{6,4},{7,5},{8,14},{9,15},{10,... | collective-permute-start | bytes 393224 | tf_op jit(solution)/shard_map/ppermute | solution.py:338
  118.2 0.8 collective-permute-start.14
  119.0 1.7 %collective-permute-start.16 = (f32[32,2,4,128]{3,2,1,0:T(4,128)S(1)}, f32[32,2,4,128]{3,2,1,0:T(4,128)S(1)}, u32[]{:S(2)}, u32[]{:S(2)}) collective-permute-start(f32[32,2,4,128]{3,2,1,0:T(4,128)S(1)} %get-tuple-element.64.a0), channel_id=1, source_target_pairs={{0,1},{1,0},{2,3},{3,2},{4,5},{5,4},{6,7},{7,6},{8,9},{9,8},{10,11... | collective-permute-start | bytes 393224 | tf_op jit(solution)/shard_map/ppermute | solution.py:334
  120.7 0.4 collective-permute-done.15.a3
  121.1 3.6 %collective-permute-start.19 = (f32[32,2,4,128]{3,2,1,0:T(4,128)S(1)}, f32[32,2,4,128]{3,2,1,0:T(4,128)S(1)}, u32[]{:S(2)}, u32[]{:S(2)}) collective-permute-start(f32[32,2,4,128]{3,2,1,0:T(4,128)S(1)} %collective-permute-done.15.a3), channel_id=1, source_target_pairs={{0,1},{1,0},{2,3},{3,2},{4,5},{5,4},{6,7},{7,6},{8,9},{9,8},{10,11... | collective-permute-start | bytes 393224 | tf_op jit(solution)/shard_map/ppermute | solution.py:334
  124.7 2.3 %collective-permute-start.18 = (f32[32,2,4,128]{3,2,1,0:T(4,128)S(1)}, f32[32,2,4,128]{3,2,1,0:T(4,128)S(1)}, u32[]{:S(2)}, u32[]{:S(2)}) collective-permute-start(f32[32,2,4,128]{3,2,1,0:T(4,128)S(1)} %collective-permute-done.14.a2), channel_id=1, source_target_pairs={{0,1},{1,0},{2,3},{3,2},{4,5},{5,4},{6,7},{7,6},{8,9},{9,8},{10,11... | collective-permute-start | bytes 393224 | tf_op jit(solution)/shard_map/ppermute | solution.py:334
  127.1 1.3 collective-permute-start.17
  128.4 1.0 collective-permute-done.17.b1
  129.4 1.1 collective-permute-start.20
  130.5 0.9 collective-permute-start.25
  131.4 0.6 collective-permute-start.22
  132.0 2.8 %collective-permute-start.21 = (f32[29,5,4,128]{3,2,1,0:T(4,128)S(1)}, f32[29,5,4,128]{3,2,1,0:T(4,128)S(1)}, u32[]{:S(2)}, u32[]{:S(2)}) collective-permute-start(f32[29,5,4,128]{3,2,1,0:T(4,128)S(1)} %slice.2.refs_0_), channel_id=1, source_target_pairs={{0,1},{1,0},{2,3},{3,2},{4,5},{5,4},{6,7},{7,6},{8,9},{9,8},{10,11... | collective-permute-start | bytes 890888 | tf_op jit(solution)/shard_map/ppermute | solution.py:334
  134.8 3.9 %shard_map.199 = f32[1024,256]{1,0:T(8,128)} custom-call(s32[3]{0:T(128)S(1)} %pad_add_fusion.pos, s32[1,1024]{1,0:T(1,128)S(1)} %bitcast.16, f32[32,2,4,128]{3,2,1,0:T(4,128)S(1)} %get-tuple-element.64.a0, f32[32,2,4,128]{3,2,1,0:T(4,128)S(1)} %collective-permute-done.13.a1, f32[32,2,4,128]{3,2,1,0:T(4,128)S(1)} %collective-permute-done.14.a2, ...), custom_call_target="tpu_custom_call" | custom-call | tf_op jit(solution)/shard_map/pallas_call | solution.py:34
  138.7 4.0 %collective-permute-done.25.refs_3_ = f32[29,5,4,128]{3,2,1,0:T(4,128)S(1)} collective-permute-done((f32[29,5,4,128]{3,2,1,0:T(4,128)S(1)}, f32[29,5,4,128]{3,2,1,0:T(4,128)S(1)}, u32[]{:S(2)}, u32[]{:S(2)}) %collective-permute-start.25) | collective-permute-done | bytes 296992 | tf_op jit(solution)/shard_map/ppermute | solution.py:338
  142.6 2.3 %collective-permute-start.26 = (f32[29,5,4,128]{3,2,1,0:T(4,128)S(1)}, f32[29,5,4,128]{3,2,1,0:T(4,128)S(1)}, u32[]{:S(2)}, u32[]{:S(2)}) collective-permute-start(f32[29,5,4,128]{3,2,1,0:T(4,128)S(1)} %collective-permute-done.25.refs_3_), channel_id=1, source_target_pairs={{0,1},{1,0},{2,3},{3,2},{4,5},{5,4},{6,7},{7,6},{8,9},{9,8},{10,11... | collective-permute-start | bytes 890888 | tf_op jit(solution)/shard_map/ppermute | solution.py:334
  145.0 1.3 collective-permute-done.22.refs_1_
  146.2 0.8 collective-permute-start.23
  147.1 0.0 collective-permute-start.24
  147.1 1.7 %shard_map.200 = (f32[512,768]{1,0:T(8,128)}, f32[256,768]{1,0:T(8,128)}) custom-call(s32[3]{0:T(128)S(1)} %pad_add_fusion.pos, f32[29,5,4,128]{3,2,1,0:T(4,128)S(1)} %slice.2.refs_0_, f32[29,5,4,128]{3,2,1,0:T(4,128)S(1)} %collective-permute-done.22.refs_1_, f32[29,5,4,128]{3,2,1,0:T(4,128)S(1)} %collective-permute-done.20.refs_2_, ...), custom_call_target="tpu_custom_call" | custom-call | tf_op jit(solution)/shard_map/pallas_call | solution.py:34
  148.8 1.7 %shard_map.201 = (f32[512,768]{1,0:T(8,128)}, f32[256,768]{1,0:T(8,128)}) custom-call(s32[3]{0:T(128)S(1)} %pad_add_fusion.pos, f32[29,5,4,128]{3,2,1,0:T(4,128)S(1)} %collective-permute-done.21.refs_0_, f32[29,5,4,128]{3,2,1,0:T(4,128)S(1)} %collective-permute-done.23.refs_1_, ...), custom_call_target="tpu_custom_call", output_to_operand_aliasing={{0}: (5, {}), {1}: (6, {})} | custom-call | tf_op jit(solution)/shard_map/pallas_call | solution.py:34
  (28 shorter events, 0.1 us)
Async XLA Ops:
  7.0 12.2 %copy-start.6 = (f32[96,512]{1,0:T(8,128)S(1)}, f32[96,512]{1,0:T(8,128)}, u32[]{:S(2)}) copy-start(f32[96,512]{1,0:T(8,128)} %get-tuple-element.42) | copy-start | bytes 589828
  7.0 13.3 %copy-start.4 = (s32[1024]{0:T(1024)S(1)}, s32[1024]{0:T(1024)}, u32[]{:S(2)}) copy-start(s32[1024]{0:T(1024)} %param.27) | copy-start | bytes 12292
  7.0 16.0 %copy-start.5 = (f32[1024,256]{1,0:T(8,128)S(1)}, f32[1024,256]{1,0:T(8,128)}, u32[]{:S(2)}) copy-start(f32[1024,256]{1,0:T(8,128)} %param.20) | copy-start | bytes 3145732
  7.0 41.6 %all-to-all-start = ((bf16[32,144,128]{2,1,0:T(8,128)(2,1)}), bf16[32,144,128]{2,1,0:T(8,128)(2,1)S(1)}, u32[]{:S(2)}, u32[]{:S(2)}) async-start(bf16[32,144,128]{2,1,0:T(8,128)(2,1)} %get-tuple-element.41), calls=%async_computation | async-start | bytes 2359296 | tf_op jit(solution)/shard_map/all_to_all | solution.py:412
  19.2 2.1 %collective-permute-start = (f32[96,512]{1,0:T(8,128)S(1)}, f32[96,512]{1,0:T(8,128)S(1)}, u32[]{:S(2)}, u32[]{:S(2)}) collective-permute-start(f32[96,512]{1,0:T(8,128)S(1)} %copy-done.6), channel_id=1, source_target_pairs={{0,1},{1,0},{2,3},{3,2},{4,5},{5,4},{6,7},{7,6},{8,9},{9,8},{10,11... | collective-permute-start | bytes 589832 | tf_op jit(solution)/shard_map/ppermute | solution.py:334
  21.4 27.2 %collective-permute-start.1 = (f32[16,512]{1,0:T(8,128)S(1)}, f32[16,512]{1,0:T(8,128)S(1)}, u32[]{:S(2)}, u32[]{:S(2)}) collective-permute-start(f32[16,512]{1,0:T(8,128)S(1)} %constant_dynamic-slice_fusion), channel_id=1, source_target_pairs={{0,8},{8,16},{16,24},{24,32},{32,40},{40,48},{48,56},{56,64},{64,7... | collective-permute-start | bytes 98312 | tf_op jit(solution)/shard_map/ppermute | solution.py:416
  48.6 6.1 %collective-permute-start.2 = (bf16[32,144,128]{2,1,0:T(8,128)(2,1)S(1)}, bf16[32,144,128]{2,1,0:T(8,128)(2,1)S(1)}, u32[]{:S(2)}, u32[]{:S(2)}) collective-permute-start(bf16[32,144,128]{2,1,0:T(8,128)(2,1)S(1)} %all-to-all-done.own), channel_id=1, source_target_pairs={{0,1},{1,0},{2,3},{3,2},{4,5},{5,4},{6,7},{7,6},{8,9},{9,8},{10,11... | collective-permute-start | bytes 3538952 | tf_op jit(solution)/shard_map/ppermute | solution.py:334
  54.6 23.1 %copy-start.1 = (f32[1024,256]{1,0:T(8,128)S(1)}, f32[1024,256]{1,0:T(8,128)}, u32[]{:S(2)}) copy-start(f32[1024,256]{1,0:T(8,128)} %refs_7_.3) | copy-start | bytes 3145732
  54.6 23.1 %copy-start.2 = (bf16[512,768]{1,0:T(8,128)(2,1)S(1)}, bf16[512,768]{1,0:T(8,128)(2,1)}, u32[]{:S(2)}) copy-start(bf16[512,768]{1,0:T(8,128)(2,1)} %refs_10_.1) | copy-start | bytes 2359300
  54.6 23.1 %copy-start.3 = (bf16[256,768]{1,0:T(8,128)(2,1)S(1)}, bf16[256,768]{1,0:T(8,128)(2,1)}, u32[]{:S(2)}) copy-start(bf16[256,768]{1,0:T(8,128)(2,1)} %refs_11_.1) | copy-start | bytes 1179652
  56.2 21.5 %copy-start = (f32[1024,256]{1,0:T(8,128)S(1)}, f32[1024,256]{1,0:T(8,128)}, u32[]{:S(2)}) copy-start(f32[1024,256]{1,0:T(8,128)} %refs_6_.3) | copy-start | bytes 3145732
  56.2 9.5 %collective-permute-start.3 = (f32[136,512]{1,0:T(8,128)S(1)}, f32[136,512]{1,0:T(8,128)S(1)}, u32[]{:S(2)}, u32[]{:S(2)}) collective-permute-start(f32[136,512]{1,0:T(8,128)S(1)} %get-tuple-element.46), channel_id=1, source_target_pairs={{0,4},{1,5},{2,6},{3,7},{4,0},{5,1},{6,2},{7,3},{8,12},{9,13},{10,... | collective-permute-start | bytes 835592 | tf_op jit(solution)/shard_map/ppermute | solution.py:338
  59.0 12.7 %collective-permute-start.4 = (f32[136,512]{1,0:T(8,128)S(1)}, f32[136,512]{1,0:T(8,128)S(1)}, u32[]{:S(2)}, u32[]{:S(2)}) collective-permute-start(f32[136,512]{1,0:T(8,128)S(1)} %get-tuple-element.47), channel_id=1, source_target_pairs={{0,6},{1,7},{2,0},{3,1},{4,2},{5,3},{6,4},{7,5},{8,14},{9,15},{10,... | collective-permute-start | bytes 835592 | tf_op jit(solution)/shard_map/ppermute | solution.py:338
  59.9 12.4 %collective-permute-start.5 = (f32[136,512]{1,0:T(8,128)S(1)}, f32[136,512]{1,0:T(8,128)S(1)}, u32[]{:S(2)}, u32[]{:S(2)}) collective-permute-start(f32[136,512]{1,0:T(8,128)S(1)} %get-tuple-element.48), channel_id=1, source_target_pairs={{0,2},{1,3},{2,4},{3,5},{4,6},{5,7},{6,0},{7,1},{8,10},{9,11},{10,... | collective-permute-start | bytes 835592 | tf_op jit(solution)/shard_map/ppermute | solution.py:338
  72.9 4.8 %collective-permute-start.9 = (bf16[144,512]{1,0:T(8,128)(2,1)S(1)}, bf16[144,512]{1,0:T(8,128)(2,1)S(1)}, u32[]{:S(2)}, u32[]{:S(2)}) collective-permute-start(bf16[144,512]{1,0:T(8,128)(2,1)S(1)} %shard_map.195.refs_0_), channel_id=1, source_target_pairs={{0,1},{1,0},{2,3},{3,2},{4,5},{5,4},{6,7},{7,6},{8,9},{9,8},{10,11... | collective-permute-start | bytes 442376 | tf_op jit(solution)/shard_map/ppermute | solution.py:334
  73.6 6.6 %collective-permute-start.8 = (bf16[144,512]{1,0:T(8,128)(2,1)S(1)}, bf16[144,512]{1,0:T(8,128)(2,1)S(1)}, u32[]{:S(2)}, u32[]{:S(2)}) collective-permute-start(bf16[144,512]{1,0:T(8,128)(2,1)S(1)} %shard_map.195.refs_0_), channel_id=1, source_target_pairs={{0,2},{1,3},{2,4},{3,5},{4,6},{5,7},{6,0},{7,1},{8,10},{9,11},{10,... | collective-permute-start | bytes 442376 | tf_op jit(solution)/shard_map/ppermute | solution.py:338
  74.8 5.5 %collective-permute-start.7 = (bf16[144,512]{1,0:T(8,128)(2,1)S(1)}, bf16[144,512]{1,0:T(8,128)(2,1)S(1)}, u32[]{:S(2)}, u32[]{:S(2)}) collective-permute-start(bf16[144,512]{1,0:T(8,128)(2,1)S(1)} %shard_map.195.refs_0_), channel_id=1, source_target_pairs={{0,6},{1,7},{2,0},{3,1},{4,2},{5,3},{6,4},{7,5},{8,14},{9,15},{10,... | collective-permute-start | bytes 442376 | tf_op jit(solution)/shard_map/ppermute | solution.py:338
  76.3 7.9 %collective-permute-start.6 = (bf16[144,512]{1,0:T(8,128)(2,1)S(1)}, bf16[144,512]{1,0:T(8,128)(2,1)S(1)}, u32[]{:S(2)}, u32[]{:S(2)}) collective-permute-start(bf16[144,512]{1,0:T(8,128)(2,1)S(1)} %shard_map.195.refs_0_), channel_id=1, source_target_pairs={{0,4},{1,5},{2,6},{3,7},{4,0},{5,1},{6,2},{7,3},{8,12},{9,13},{10,... | collective-permute-start | bytes 442376 | tf_op jit(solution)/shard_map/ppermute | solution.py:338
  84.3 1.9 %collective-permute-start.10 = (bf16[144,512]{1,0:T(8,128)(2,1)S(1)}, bf16[144,512]{1,0:T(8,128)(2,1)S(1)}, u32[]{:S(2)}, u32[]{:S(2)}) collective-permute-start(bf16[144,512]{1,0:T(8,128)(2,1)S(1)} %collective-permute-done.7.refs_0_), channel_id=1, source_target_pairs={{0,1},{1,0},{2,3},{3,2},{4,5},{5,4},{6,7},{7,6},{8,9},{9,8},{10,11... | collective-permute-start | bytes 442376 | tf_op jit(solution)/shard_map/ppermute | solution.py:334
  85.1 1.4 collective-permute-start.11
  85.1 1.6 %collective-permute-start.12 = (bf16[144,512]{1,0:T(8,128)(2,1)S(1)}, bf16[144,512]{1,0:T(8,128)(2,1)S(1)}, u32[]{:S(2)}, u32[]{:S(2)}) collective-permute-start(bf16[144,512]{1,0:T(8,128)(2,1)S(1)} %collective-permute-done.8.refs_4_), channel_id=1, source_target_pairs={{0,1},{1,0},{2,3},{3,2},{4,5},{5,4},{6,7},{7,6},{8,9},{9,8},{10,11... | collective-permute-start | bytes 442376 | tf_op jit(solution)/shard_map/ppermute | solution.py:334
  108.5 20.9 %all-to-all-start.2 = ((f32[32,5,4,128]{3,2,1,0:T(4,128)}), f32[32,5,4,128]{3,2,1,0:T(4,128)S(1)}, u32[]{:S(2)}, u32[]{:S(2)}) async-start(f32[32,5,4,128]{3,2,1,0:T(4,128)} %get-tuple-element.61), calls=%async_computation.2 | async-start | bytes 655360 | tf_op jit(solution)/shard_map/all_to_all | solution.py:457
  116.3 4.8 %collective-permute-start.15 = (f32[32,2,4,128]{3,2,1,0:T(4,128)S(1)}, f32[32,2,4,128]{3,2,1,0:T(4,128)S(1)}, u32[]{:S(2)}, u32[]{:S(2)}) collective-permute-start(f32[32,2,4,128]{3,2,1,0:T(4,128)S(1)} %get-tuple-element.64.a0), channel_id=1, source_target_pairs={{0,6},{1,7},{2,0},{3,1},{4,2},{5,3},{6,4},{7,5},{8,14},{9,15},{10,... | collective-permute-start | bytes 393224 | tf_op jit(solution)/shard_map/ppermute | solution.py:338
  118.2 6.6 %collective-permute-start.14 = (f32[32,2,4,128]{3,2,1,0:T(4,128)S(1)}, f32[32,2,4,128]{3,2,1,0:T(4,128)S(1)}, u32[]{:S(2)}, u32[]{:S(2)}) collective-permute-start(f32[32,2,4,128]{3,2,1,0:T(4,128)S(1)} %get-tuple-element.64.a0), channel_id=1, source_target_pairs={{0,4},{1,5},{2,6},{3,7},{4,0},{5,1},{6,2},{7,3},{8,12},{9,13},{10,... | collective-permute-start | bytes 393224 | tf_op jit(solution)/shard_map/ppermute | solution.py:338
  119.0 8.1 %collective-permute-start.13 = (f32[32,2,4,128]{3,2,1,0:T(4,128)S(1)}, f32[32,2,4,128]{3,2,1,0:T(4,128)S(1)}, u32[]{:S(2)}, u32[]{:S(2)}) collective-permute-start(f32[32,2,4,128]{3,2,1,0:T(4,128)S(1)} %get-tuple-element.64.a0), channel_id=1, source_target_pairs={{0,2},{1,3},{2,4},{3,5},{4,6},{5,7},{6,0},{7,1},{8,10},{9,11},{10,... | collective-permute-start | bytes 393224 | tf_op jit(solution)/shard_map/ppermute | solution.py:338
  119.0 9.4 %collective-permute-start.16 = (f32[32,2,4,128]{3,2,1,0:T(4,128)S(1)}, f32[32,2,4,128]{3,2,1,0:T(4,128)S(1)}, u32[]{:S(2)}, u32[]{:S(2)}) collective-permute-start(f32[32,2,4,128]{3,2,1,0:T(4,128)S(1)} %get-tuple-element.64.a0), channel_id=1, source_target_pairs={{0,1},{1,0},{2,3},{3,2},{4,5},{5,4},{6,7},{7,6},{8,9},{9,8},{10,11... | collective-permute-start | bytes 393224 | tf_op jit(solution)/shard_map/ppermute | solution.py:334
  121.1 7.3 %collective-permute-start.19 = (f32[32,2,4,128]{3,2,1,0:T(4,128)S(1)}, f32[32,2,4,128]{3,2,1,0:T(4,128)S(1)}, u32[]{:S(2)}, u32[]{:S(2)}) collective-permute-start(f32[32,2,4,128]{3,2,1,0:T(4,128)S(1)} %collective-permute-done.15.a3), channel_id=1, source_target_pairs={{0,1},{1,0},{2,3},{3,2},{4,5},{5,4},{6,7},{7,6},{8,9},{9,8},{10,11... | collective-permute-start | bytes 393224 | tf_op jit(solution)/shard_map/ppermute | solution.py:334
  124.7 3.7 %collective-permute-start.18 = (f32[32,2,4,128]{3,2,1,0:T(4,128)S(1)}, f32[32,2,4,128]{3,2,1,0:T(4,128)S(1)}, u32[]{:S(2)}, u32[]{:S(2)}) collective-permute-start(f32[32,2,4,128]{3,2,1,0:T(4,128)S(1)} %collective-permute-done.14.a2), channel_id=1, source_target_pairs={{0,1},{1,0},{2,3},{3,2},{4,5},{5,4},{6,7},{7,6},{8,9},{9,8},{10,11... | collective-permute-start | bytes 393224 | tf_op jit(solution)/shard_map/ppermute | solution.py:334
  127.1 2.3 %collective-permute-start.17 = (f32[32,2,4,128]{3,2,1,0:T(4,128)S(1)}, f32[32,2,4,128]{3,2,1,0:T(4,128)S(1)}, u32[]{:S(2)}, u32[]{:S(2)}) collective-permute-start(f32[32,2,4,128]{3,2,1,0:T(4,128)S(1)} %collective-permute-done.13.a1), channel_id=1, source_target_pairs={{0,1},{1,0},{2,3},{3,2},{4,5},{5,4},{6,7},{7,6},{8,9},{9,8},{10,11... | collective-permute-start | bytes 393224 | tf_op jit(solution)/shard_map/ppermute | solution.py:334
  129.4 9.2 %collective-permute-start.20 = (f32[29,5,4,128]{3,2,1,0:T(4,128)S(1)}, f32[29,5,4,128]{3,2,1,0:T(4,128)S(1)}, u32[]{:S(2)}, u32[]{:S(2)}) collective-permute-start(f32[29,5,4,128]{3,2,1,0:T(4,128)S(1)} %slice.2.refs_0_), channel_id=1, source_target_pairs={{0,4},{1,5},{2,6},{3,7},{4,0},{5,1},{6,2},{7,3},{8,12},{9,13},{10,... | collective-permute-start | bytes 890888 | tf_op jit(solution)/shard_map/ppermute | solution.py:338
  130.5 12.1 %collective-permute-start.25 = (f32[29,5,4,128]{3,2,1,0:T(4,128)S(1)}, f32[29,5,4,128]{3,2,1,0:T(4,128)S(1)}, u32[]{:S(2)}, u32[]{:S(2)}) collective-permute-start(f32[29,5,4,128]{3,2,1,0:T(4,128)S(1)} %slice.2.refs_0_), channel_id=1, source_target_pairs={{0,6},{1,7},{2,0},{3,1},{4,2},{5,3},{6,4},{7,5},{8,14},{9,15},{10,... | collective-permute-start | bytes 890888 | tf_op jit(solution)/shard_map/ppermute | solution.py:338
  131.4 14.8 %collective-permute-start.22 = (f32[29,5,4,128]{3,2,1,0:T(4,128)S(1)}, f32[29,5,4,128]{3,2,1,0:T(4,128)S(1)}, u32[]{:S(2)}, u32[]{:S(2)}) collective-permute-start(f32[29,5,4,128]{3,2,1,0:T(4,128)S(1)} %slice.2.refs_0_), channel_id=1, source_target_pairs={{0,2},{1,3},{2,4},{3,5},{4,6},{5,7},{6,0},{7,1},{8,10},{9,11},{10,... | collective-permute-start | bytes 890888 | tf_op jit(solution)/shard_map/ppermute | solution.py:338
  132.0 16.7 %collective-permute-start.21 = (f32[29,5,4,128]{3,2,1,0:T(4,128)S(1)}, f32[29,5,4,128]{3,2,1,0:T(4,128)S(1)}, u32[]{:S(2)}, u32[]{:S(2)}) collective-permute-start(f32[29,5,4,128]{3,2,1,0:T(4,128)S(1)} %slice.2.refs_0_), channel_id=1, source_target_pairs={{0,1},{1,0},{2,3},{3,2},{4,5},{5,4},{6,7},{7,6},{8,9},{9,8},{10,11... | collective-permute-start | bytes 890888 | tf_op jit(solution)/shard_map/ppermute | solution.py:334
  142.6 6.1 %collective-permute-start.26 = (f32[29,5,4,128]{3,2,1,0:T(4,128)S(1)}, f32[29,5,4,128]{3,2,1,0:T(4,128)S(1)}, u32[]{:S(2)}, u32[]{:S(2)}) collective-permute-start(f32[29,5,4,128]{3,2,1,0:T(4,128)S(1)} %collective-permute-done.25.refs_3_), channel_id=1, source_target_pairs={{0,1},{1,0},{2,3},{3,2},{4,5},{5,4},{6,7},{7,6},{8,9},{9,8},{10,11... | collective-permute-start | bytes 890888 | tf_op jit(solution)/shard_map/ppermute | solution.py:334
  146.2 2.5 %collective-permute-start.23 = (f32[29,5,4,128]{3,2,1,0:T(4,128)S(1)}, f32[29,5,4,128]{3,2,1,0:T(4,128)S(1)}, u32[]{:S(2)}, u32[]{:S(2)}) collective-permute-start(f32[29,5,4,128]{3,2,1,0:T(4,128)S(1)} %collective-permute-done.22.refs_1_), channel_id=1, source_target_pairs={{0,1},{1,0},{2,3},{3,2},{4,5},{5,4},{6,7},{7,6},{8,9},{9,8},{10,11... | collective-permute-start | bytes 890888 | tf_op jit(solution)/shard_map/ppermute | solution.py:334
  147.1 1.7 %collective-permute-start.24 = (f32[29,5,4,128]{3,2,1,0:T(4,128)S(1)}, f32[29,5,4,128]{3,2,1,0:T(4,128)S(1)}, u32[]{:S(2)}, u32[]{:S(2)}) collective-permute-start(f32[29,5,4,128]{3,2,1,0:T(4,128)S(1)} %collective-permute-done.20.refs_2_), channel_id=1, source_target_pairs={{0,1},{1,0},{2,3},{3,2},{4,5},{5,4},{6,7},{7,6},{8,9},{9,8},{10,11... | collective-permute-start | bytes 890888 | tf_op jit(solution)/shard_map/ppermute | solution.py:334

commit v10 on v9

--- a/solution.py
+++ b/solution.py
@@ -367,12 +367,12 @@
 def last_update(pos, parts, shared, olds, hot_own, acc):
     sds = jax.ShapeDtypeStruct
     return call(
-        functools.partial(update_kernel, (3, 2, 1), (0,)),
+        functools.partial(update_kernel, (3, 2), (0, 1)),
         (sds((1024, 256), F32), sds((32, 7, 4, 128), F32)),
         (SM,),
         (pos, *parts, *shared, *olds, hot_own, acc),
         (
-            pltpu.VMEM((128, 1024), F32), pltpu.VMEM((768, 256), F32), pltpu.VMEM((640, 128), F32),
+            pltpu.VMEM((128, 1024), F32), pltpu.VMEM((512, 256), F32), pltpu.VMEM((640, 128), F32),
             pltpu.SemaphoreType.DMA((4,)),
         ),
         (ANY, VM),
@@ -448,9 +448,17 @@
         (SM,),
         (pos, agg, swap_core(agg), *shared),
     )
-    far, back, near, new_own = lax.optimization_barrier((far, back, near, new_own))
-    parts = (back, swap_core(back), far, swap_core(far), near, swap_core(near))
-    new_memory, grad = last_update(pos, parts, shared, (new_own,), hot_own, acc)
+    near_swap = swap_core(near)
+    far, near_swap = lax.optimization_barrier((far, near_swap))
+    back, new_own = lax.optimization_barrier((back, new_own))
+    new_near, acc = call(
+        functools.partial(update_kernel, (1,), ()),
+        (rows, sums),
+        (SM,),
+        (pos, near, near_swap, *shared, acc),
+    )
+    parts = (back, swap_core(back), far, swap_core(far))
+    new_memory, grad = last_update(pos, parts, shared, (new_own, new_near), hot_own, acc)
 
     grad = lax.all_to_all(grad, "node", split_axis=0, concat_axis=0, tiled=True)
     grad, hot_new = call(piece_kernel, (sds((32, 5, 4, 128), F32), sds((32, 2, 4, 128), F32)), (), (grad,))

time: 151 us -> 151 us (level)
  waiting for transfers between devices: 48.6 us -> 44.2 us
  starting transfers between devices: 56.9 us -> 58.9 us
    ppermute x12, waiting for transfers between devices: 21.9 us -> 18.6 us  [shift_x(): return lax.ppermute(v, 'rep', [(k, (k + 2 * d) % 8) for k in range(8)])]
    ppermute x14, starting transfers between devices: 21.7 us -> 23.5 us  [swap_core(): return lax.ppermute(v, 'rep', [(k, k ^ 1) for k in range(8)])]
    pallas_call x10 -> x11, Pallas kernels: 23.9 us -> 25.2 us  [call(): pl.pallas_call(body, out_shape=out_shape, in_specs=list(places) + [VM] *...]
  transfers between devices with their start and end apart: 29 -> 29, of which waited for: 15 -> 12; matrix products, arithmetic and copies ran while one was open for 2% -> 2% of each run, Pallas kernels for 6% -> 7%
where the time goes in v10:
time: 151 us; the launch traced here: 150 us
  starting transfers between devices  58.9 us (39%)
  waiting for transfers between devices  44.2 us (29%)
  Pallas kernels  25.2 us (17%)
  blocking collectives  18 us (12%)
  local copies, waits for them, and re-layouts  2.81 us (2%)
    pallas_call x11, Pallas kernels, call(): pl.pallas_call(body, out_shape=out_shape, in_specs=list(places) + [VM] *...  25.2 us
    ppermute x14, starting transfers between devices, swap_core(): return lax.ppermute(v, 'rep', [(k, k ^ 1) for k in range(8)])  23.5 us
    ppermute x1, waiting for transfers between devices, on_device(): spill = lax.ppermute(spill, 'node', [(k, (k + 1) % 32) for k in range(32)])  22.8 us
    ppermute x12, waiting for transfers between devices, shift_x(): return lax.ppermute(v, 'rep', [(k, (k + 2 * d) % 8) for k in range(8)])  18.6 us
    all_to_all x1, blocking collectives, on_device(): grad = lax.all_to_all(grad, 'node', split_axis=0, concat_axis=0, tiled=True)  18 us
    ppermute x12, starting transfers between devices, shift_x(): return lax.ppermute(v, 'rep', [(k, (k + 2 * d) % 8) for k in range(8)])  14.5 us
    all_to_all x1, starting transfers between devices, on_device(): recv = lax.all_to_all(send, 'node', split_axis=0, concat_axis=0, tiled=True)  12.2 us
    all_to_all x1, starting transfers between devices, on_device(): grad = lax.all_to_all(grad, 'node', split_axis=0, concat_axis=0, tiled=True)  7.05 us
  transfers between devices with their start and end apart: 29, of which 12 were waited for; matrix products, arithmetic and copies ran while one was open for 2% of the time, Pallas kernels for 7%

profile of v10, /device:TPU:1, one launch (start us, length us, event | category | flops | bytes accessed | tf_op | source)
XLA Modules:
  0.0 150.4 jit_solution(9369504419105118876)
XLA Ops:
  0.6 6.3 %shard_map.192 = (bf16[32,144,128]{2,1,0:T(8,128)(2,1)}, f32[96,512]{1,0:T(8,128)}) custom-call(s32[1]{0:T(128)} %bitcast.3.pos, f32[1024,256]{1,0:T(8,128)} %refs_4_.1, bf16[1024,128]{1,0:T(8,128)(2,1)} %edge_h.1, bf16[512,512]{1,0:T(8,128)(2,1)} %w_h.1, s32[1,1024]{1,0:T(1,128)} %bitcast.17, s32[1,1024]{1,0:T(1,128)} %bitcast.18, s32[1,1024]{1,0:T(1,128)} %bitcast.19, ...), custom_call_target="tpu_custom_call" | custom-call | tf_op jit(solution)/shard_map/pallas_call | solution.py:34
  7.0 0.0 copy-start.6
  7.0 0.0 copy-start.4
  7.0 0.0 copy-start.5
  7.0 12.2 %all-to-all-start = ((bf16[32,144,128]{2,1,0:T(8,128)(2,1)}), bf16[32,144,128]{2,1,0:T(8,128)(2,1)S(1)}, u32[]{:S(2)}, u32[]{:S(2)}) async-start(bf16[32,144,128]{2,1,0:T(8,128)(2,1)} %get-tuple-element.43), calls=%async_computation | async-start | bytes 2359296 | tf_op jit(solution)/shard_map/all_to_all | solution.py:412
  19.2 1.0 collective-permute-start
  20.3 0.2 select_reduce_fusion
  20.5 0.9 collective-permute-done
  21.4 1.6 %collective-permute-start.1 = (f32[16,512]{1,0:T(8,128)S(1)}, f32[16,512]{1,0:T(8,128)S(1)}, u32[]{:S(2)}, u32[]{:S(2)}) collective-permute-start(f32[16,512]{1,0:T(8,128)S(1)} %constant_dynamic-slice_fusion), channel_id=1, source_target_pairs={{0,8},{8,16},{16,24},{24,32},{32,40},{40,48},{48,56},{56,64},{64,7... | collective-permute-start | bytes 98312 | tf_op jit(solution)/shard_map/ppermute | solution.py:416
  23.0 0.8 gather_fusion.1
  23.7 2.0 %gather_fusion = f32[128,256]{1,0:T(8,128)S(1)} fusion(f32[1024,256]{1,0:T(8,128)} %param.18, s32[1024]{0:T(1024)S(1)} %pad_clamp_fusion), kind=kCustom, calls=%fused_computation | custom fusion | bytes 262656 | tf_op jit(solution)/shard_map/jit(_take)/gather | solution.py:420
  25.7 22.8 %collective-permute-done.1 = f32[16,512]{1,0:T(8,128)S(1)} collective-permute-done((f32[16,512]{1,0:T(8,128)S(1)}, f32[16,512]{1,0:T(8,128)S(1)}, u32[]{:S(2)}, u32[]{:S(2)}) %collective-permute-start.1) | collective-permute-done | bytes 32800 | tf_op jit(solution)/shard_map/ppermute | solution.py:416
  48.6 0.0 all-to-all-done.own
  48.6 3.6 %collective-permute-start.2 = (bf16[32,144,128]{2,1,0:T(8,128)(2,1)S(1)}, bf16[32,144,128]{2,1,0:T(8,128)(2,1)S(1)}, u32[]{:S(2)}, u32[]{:S(2)}) collective-permute-start(bf16[32,144,128]{2,1,0:T(8,128)(2,1)S(1)} %all-to-all-done.own), channel_id=1, source_target_pairs={{0,1},{1,0},{2,3},{3,2},{4,5},{5,4},{6,7},{7,6},{8,9},{9,8},{10,11... | collective-permute-start | bytes 3538952 | tf_op jit(solution)/shard_map/ppermute | solution.py:334
  52.2 0.1 pad_add_fusion.pos
  52.2 1.6 %shard_map.193 = (f32[512,512]{1,0:T(8,128)S(1)}, f32[8,512]{1,0:T(8,128)S(1)}) custom-call(s32[3]{0:T(128)S(1)} %pad_add_fusion.pos, bf16[32,144,128]{2,1,0:T(8,128)(2,1)S(1)} %all-to-all-done.own), custom_call_target="tpu_custom_call" | custom-call | tf_op jit(solution)/shard_map/pallas_call | solution.py:34
  53.8 0.8 collective-permute-done.2.peer
  54.6 1.5 %shard_map.194 = (f32[136,512]{1,0:T(8,128)S(1)}, f32[136,512]{1,0:T(8,128)S(1)}, f32[136,512]{1,0:T(8,128)S(1)}, f32[136,512]{1,0:T(8,128)S(1)}) custom-call(s32[3]{0:T(128)S(1)} %pad_add_fusion.pos, bf16[32,144,128]{2,1,0:T(8,128)(2,1)S(1)} %collective-permute-done.2.peer, f32[512,512]{1,0:T(8,128)S(1)} %get-tuple-element.46.sums, ...), custom_call_target="tpu_custom_call" | custom-call | tf_op jit(solution)/shard_map/pallas_call | solution.py:34
  56.2 0.0 copy-start
  56.2 2.8 %collective-permute-start.3 = (f32[136,512]{1,0:T(8,128)S(1)}, f32[136,512]{1,0:T(8,128)S(1)}, u32[]{:S(2)}, u32[]{:S(2)}) collective-permute-start(f32[136,512]{1,0:T(8,128)S(1)} %get-tuple-element.48), channel_id=1, source_target_pairs={{0,4},{1,5},{2,6},{3,7},{4,0},{5,1},{6,2},{7,3},{8,12},{9,13},{10,... | collective-permute-start | bytes 835592 | tf_op jit(solution)/shard_map/ppermute | solution.py:338
  59.0 0.9 collective-permute-start.4
  59.9 0.6 collective-permute-start.5
  60.5 5.2 %collective-permute-done.3.p1_h = f32[136,512]{1,0:T(8,128)S(1)} collective-permute-done((f32[136,512]{1,0:T(8,128)S(1)}, f32[136,512]{1,0:T(8,128)S(1)}, u32[]{:S(2)}, u32[]{:S(2)}) %collective-permute-start.3) | collective-permute-done | bytes 278560 | tf_op jit(solution)/shard_map/ppermute | solution.py:338
  65.7 6.1 %collective-permute-done.4.p2_h = f32[136,512]{1,0:T(8,128)S(1)} collective-permute-done((f32[136,512]{1,0:T(8,128)S(1)}, f32[136,512]{1,0:T(8,128)S(1)}, u32[]{:S(2)}, u32[]{:S(2)}) %collective-permute-start.4) | collective-permute-done | bytes 278560 | tf_op jit(solution)/shard_map/ppermute | solution.py:338
  71.8 0.6 collective-permute-done.5.p3_h
  72.3 0.5 shard_map.195.refs_0_
  72.9 1.3 collective-permute-start.10
  74.2 0.8 collective-permute-start.7
  75.0 1.5 %collective-permute-start.6 = (bf16[144,512]{1,0:T(8,128)(2,1)S(1)}, bf16[144,512]{1,0:T(8,128)(2,1)S(1)}, u32[]{:S(2)}, u32[]{:S(2)}) collective-permute-start(bf16[144,512]{1,0:T(8,128)(2,1)S(1)} %shard_map.195.refs_0_), channel_id=1, source_target_pairs={{0,6},{1,7},{2,0},{3,1},{4,2},{5,3},{6,4},{7,5},{8,14},{9,15},{10,... | collective-permute-start | bytes 442376 | tf_op jit(solution)/shard_map/ppermute | solution.py:338
  76.6 1.4 collective-permute-start.9
  77.9 1.0 collective-permute-done.10.refs_0_
  78.9 1.5 collective-permute-start.11
  80.5 2.1 %shard_map.196 = (f32[256,256]{1,0:T(8,128)S(1)}, f32[8,128]{1,0:T(8,128)S(1)}, f32[128,1024]{1,0:T(8,128)S(1)}) custom-call(s32[3]{0:T(128)S(1)} %pad_add_fusion.pos, bf16[144,512]{1,0:T(8,128)(2,1)S(1)} %shard_map.195.refs_0_, bf16[144,512]{1,0:T(8,128)(2,1)S(1)} %collective-permute-done.7.refs_1_, f32[1024,256]{1,0:T(8,128)S(1)} %copy-done, ...), custom_call_target="tpu_custom_call" | custom-call | tf_op jit(solution)/shard_map/pallas_call | solution.py:34
  82.5 0.0 collective-permute-done.6.refs_0_
  82.5 1.3 collective-permute-start.8
  83.8 0.0 collective-permute-done.9.refs_2_
  83.8 0.0 collective-permute-done.11.refs_1_
  83.8 0.8 collective-permute-start.12
  84.6 2.0 %shard_map.197 = (f32[256,256]{1,0:T(8,128)S(1)}, f32[128,1024]{1,0:T(8,128)S(1)}) custom-call(s32[3]{0:T(128)S(1)} %pad_add_fusion.pos, bf16[144,512]{1,0:T(8,128)(2,1)S(1)} %collective-permute-done.10.refs_0_, bf16[144,512]{1,0:T(8,128)(2,1)S(1)} %collective-permute-done.11.refs_1_, f32[1024,256]{1,0:T(8,128)S(1)} %copy-done, f32[1024,256]{1,0:T(8,128)S(1)} %copy-done.1, ...), custom_call_target="tpu_custom_call" | custom-call | tf_op jit(solution)/shard_map/pallas_call | solution.py:34
  86.7 3.1 %shard_map.198 = (f32[1024,256]{1,0:T(8,128)}, f32[32,7,4,128]{3,2,1,0:T(4,128)S(1)}) custom-call(s32[3]{0:T(128)S(1)} %pad_add_fusion.pos, bf16[144,512]{1,0:T(8,128)(2,1)S(1)} %collective-permute-done.6.refs_0_, bf16[144,512]{1,0:T(8,128)(2,1)S(1)} %collective-permute-done.8.refs_1_, bf16[144,512]{1,0:T(8,128)(2,1)S(1)} %collective-permute-done.9.refs_2_, ...), custom_call_target="tpu_custom_call" | custom-call | tf_op jit(solution)/shard_map/pallas_call | solution.py:34
  89.8 18.0 %all_to_all.15.parts = f32[32,7,4,128]{3,2,1,0:T(4,128)S(1)} all-to-all(f32[32,7,4,128]{3,2,1,0:T(4,128)S(1)} %get-tuple-element.64), channel_id=1, replica_groups=mesh['node'=32,'rep'=8] {'node'}, dimensions={0} | all-to-all | bytes 917504 | tf_op jit(solution)/shard_map/all_to_all | solution.py:463
  107.7 0.8 shard_map.199
  108.5 7.0 %all-to-all-start.2 = ((f32[32,5,4,128]{3,2,1,0:T(4,128)}), f32[32,5,4,128]{3,2,1,0:T(4,128)S(1)}, u32[]{:S(2)}, u32[]{:S(2)}) async-start(f32[32,5,4,128]{3,2,1,0:T(4,128)} %get-tuple-element.65), calls=%async_computation.2 | async-start | bytes 655360 | tf_op jit(solution)/shard_map/all_to_all | solution.py:465
  115.6 2.5 %collective-permute-start.15 = (f32[32,2,4,128]{3,2,1,0:T(4,128)S(1)}, f32[32,2,4,128]{3,2,1,0:T(4,128)S(1)}, u32[]{:S(2)}, u32[]{:S(2)}) collective-permute-start(f32[32,2,4,128]{3,2,1,0:T(4,128)S(1)} %get-tuple-element.68.a0), channel_id=1, source_target_pairs={{0,6},{1,7},{2,0},{3,1},{4,2},{5,3},{6,4},{7,5},{8,14},{9,15},{10,... | collective-permute-start | bytes 393224 | tf_op jit(solution)/shard_map/ppermute | solution.py:338
  118.1 0.9 collective-permute-start.14
  119.1 1.6 %collective-permute-start.16 = (f32[32,2,4,128]{3,2,1,0:T(4,128)S(1)}, f32[32,2,4,128]{3,2,1,0:T(4,128)S(1)}, u32[]{:S(2)}, u32[]{:S(2)}) collective-permute-start(f32[32,2,4,128]{3,2,1,0:T(4,128)S(1)} %get-tuple-element.68.a0), channel_id=1, source_target_pairs={{0,1},{1,0},{2,3},{3,2},{4,5},{5,4},{6,7},{7,6},{8,9},{9,8},{10,11... | collective-permute-start | bytes 393224 | tf_op jit(solution)/shard_map/ppermute | solution.py:334
  120.7 0.3 collective-permute-done.15.a3
  121.1 3.6 %collective-permute-start.19 = (f32[32,2,4,128]{3,2,1,0:T(4,128)S(1)}, f32[32,2,4,128]{3,2,1,0:T(4,128)S(1)}, u32[]{:S(2)}, u32[]{:S(2)}) collective-permute-start(f32[32,2,4,128]{3,2,1,0:T(4,128)S(1)} %collective-permute-done.15.a3), channel_id=1, source_target_pairs={{0,1},{1,0},{2,3},{3,2},{4,5},{5,4},{6,7},{7,6},{8,9},{9,8},{10,11... | collective-permute-start | bytes 393224 | tf_op jit(solution)/shard_map/ppermute | solution.py:334
  124.7 2.3 %collective-permute-start.18 = (f32[32,2,4,128]{3,2,1,0:T(4,128)S(1)}, f32[32,2,4,128]{3,2,1,0:T(4,128)S(1)}, u32[]{:S(2)}, u32[]{:S(2)}) collective-permute-start(f32[32,2,4,128]{3,2,1,0:T(4,128)S(1)} %collective-permute-done.14.a2), channel_id=1, source_target_pairs={{0,1},{1,0},{2,3},{3,2},{4,5},{5,4},{6,7},{7,6},{8,9},{9,8},{10,11... | collective-permute-start | bytes 393224 | tf_op jit(solution)/shard_map/ppermute | solution.py:334
  127.0 1.3 collective-permute-start.17
  128.4 1.0 collective-permute-done.17.b1
  129.4 1.0 collective-permute-start.20
  130.4 0.9 collective-permute-start.25
  131.3 0.6 collective-permute-start.22
  131.9 2.8 %collective-permute-start.21 = (f32[29,5,4,128]{3,2,1,0:T(4,128)S(1)}, f32[29,5,4,128]{3,2,1,0:T(4,128)S(1)}, u32[]{:S(2)}, u32[]{:S(2)}) collective-permute-start(f32[29,5,4,128]{3,2,1,0:T(4,128)S(1)} %slice.2.refs_0_), channel_id=1, source_target_pairs={{0,1},{1,0},{2,3},{3,2},{4,5},{5,4},{6,7},{7,6},{8,9},{9,8},{10,11... | collective-permute-start | bytes 890888 | tf_op jit(solution)/shard_map/ppermute | solution.py:334
  134.7 3.9 %shard_map.200 = f32[1024,256]{1,0:T(8,128)} custom-call(s32[3]{0:T(128)S(1)} %pad_add_fusion.pos, s32[1,1024]{1,0:T(1,128)S(1)} %bitcast.16, f32[32,2,4,128]{3,2,1,0:T(4,128)S(1)} %get-tuple-element.68.a0, f32[32,2,4,128]{3,2,1,0:T(4,128)S(1)} %collective-permute-done.13.a1, f32[32,2,4,128]{3,2,1,0:T(4,128)S(1)} %collective-permute-done.14.a2, ...), custom_call_target="tpu_custom_call" | custom-call | tf_op jit(solution)/shard_map/pallas_call | solution.py:34
  138.5 0.5 collective-permute-done.20.refs_2_
  139.0 3.5 %collective-permute-done.25.refs_3_ = f32[29,5,4,128]{3,2,1,0:T(4,128)S(1)} collective-permute-done((f32[29,5,4,128]{3,2,1,0:T(4,128)S(1)}, f32[29,5,4,128]{3,2,1,0:T(4,128)S(1)}, u32[]{:S(2)}, u32[]{:S(2)}) %collective-permute-start.25) | collective-permute-done | bytes 296992 | tf_op jit(solution)/shard_map/ppermute | solution.py:338
  142.5 2.3 %collective-permute-start.26 = (f32[29,5,4,128]{3,2,1,0:T(4,128)S(1)}, f32[29,5,4,128]{3,2,1,0:T(4,128)S(1)}, u32[]{:S(2)}, u32[]{:S(2)}) collective-permute-start(f32[29,5,4,128]{3,2,1,0:T(4,128)S(1)} %collective-permute-done.25.refs_3_), channel_id=1, source_target_pairs={{0,1},{1,0},{2,3},{3,2},{4,5},{5,4},{6,7},{7,6},{8,9},{9,8},{10,11... | collective-permute-start | bytes 890888 | tf_op jit(solution)/shard_map/ppermute | solution.py:334
  144.9 1.5 collective-permute-done.22.refs_1_
  146.3 0.5 collective-permute-start.23
  146.8 0.0 collective-permute-start.24
  146.8 1.7 %shard_map.201 = (f32[512,768]{1,0:T(8,128)}, f32[256,768]{1,0:T(8,128)}) custom-call(s32[3]{0:T(128)S(1)} %pad_add_fusion.pos, f32[29,5,4,128]{3,2,1,0:T(4,128)S(1)} %slice.2.refs_0_, f32[29,5,4,128]{3,2,1,0:T(4,128)S(1)} %collective-permute-done.22.refs_1_, f32[29,5,4,128]{3,2,1,0:T(4,128)S(1)} %collective-permute-done.20.refs_2_, ...), custom_call_target="tpu_custom_call" | custom-call | tf_op jit(solution)/shard_map/pallas_call | solution.py:34
  148.6 1.7 %shard_map.202 = (f32[512,768]{1,0:T(8,128)}, f32[256,768]{1,0:T(8,128)}) custom-call(s32[3]{0:T(128)S(1)} %pad_add_fusion.pos, f32[29,5,4,128]{3,2,1,0:T(4,128)S(1)} %collective-permute-done.21.refs_0_, f32[29,5,4,128]{3,2,1,0:T(4,128)S(1)} %collective-permute-done.23.refs_1_, ...), custom_call_target="tpu_custom_call", output_to_operand_aliasing={{0}: (5, {}), {1}: (6, {})} | custom-call | tf_op jit(solution)/shard_map/pallas_call | solution.py:34
  (29 shorter events, 0.1 us)
Async XLA Ops:
  7.0 12.2 %copy-start.6 = (f32[96,512]{1,0:T(8,128)S(1)}, f32[96,512]{1,0:T(8,128)}, u32[]{:S(2)}) copy-start(f32[96,512]{1,0:T(8,128)} %get-tuple-element.44) | copy-start | bytes 589828
  7.0 13.3 %copy-start.4 = (s32[1024]{0:T(1024)S(1)}, s32[1024]{0:T(1024)}, u32[]{:S(2)}) copy-start(s32[1024]{0:T(1024)} %param.27) | copy-start | bytes 12292
  7.0 16.0 %copy-start.5 = (f32[1024,256]{1,0:T(8,128)S(1)}, f32[1024,256]{1,0:T(8,128)}, u32[]{:S(2)}) copy-start(f32[1024,256]{1,0:T(8,128)} %param.20) | copy-start | bytes 3145732
  7.0 41.6 %all-to-all-start = ((bf16[32,144,128]{2,1,0:T(8,128)(2,1)}), bf16[32,144,128]{2,1,0:T(8,128)(2,1)S(1)}, u32[]{:S(2)}, u32[]{:S(2)}) async-start(bf16[32,144,128]{2,1,0:T(8,128)(2,1)} %get-tuple-element.43), calls=%async_computation | async-start | bytes 2359296 | tf_op jit(solution)/shard_map/all_to_all | solution.py:412
  19.2 2.1 %collective-permute-start = (f32[96,512]{1,0:T(8,128)S(1)}, f32[96,512]{1,0:T(8,128)S(1)}, u32[]{:S(2)}, u32[]{:S(2)}) collective-permute-start(f32[96,512]{1,0:T(8,128)S(1)} %copy-done.6), channel_id=1, source_target_pairs={{0,1},{1,0},{2,3},{3,2},{4,5},{5,4},{6,7},{7,6},{8,9},{9,8},{10,11... | collective-permute-start | bytes 589832 | tf_op jit(solution)/shard_map/ppermute | solution.py:334
  21.4 27.2 %collective-permute-start.1 = (f32[16,512]{1,0:T(8,128)S(1)}, f32[16,512]{1,0:T(8,128)S(1)}, u32[]{:S(2)}, u32[]{:S(2)}) collective-permute-start(f32[16,512]{1,0:T(8,128)S(1)} %constant_dynamic-slice_fusion), channel_id=1, source_target_pairs={{0,8},{8,16},{16,24},{24,32},{32,40},{40,48},{48,56},{56,64},{64,7... | collective-permute-start | bytes 98312 | tf_op jit(solution)/shard_map/ppermute | solution.py:416
  48.6 6.1 %collective-permute-start.2 = (bf16[32,144,128]{2,1,0:T(8,128)(2,1)S(1)}, bf16[32,144,128]{2,1,0:T(8,128)(2,1)S(1)}, u32[]{:S(2)}, u32[]{:S(2)}) collective-permute-start(bf16[32,144,128]{2,1,0:T(8,128)(2,1)S(1)} %all-to-all-done.own), channel_id=1, source_target_pairs={{0,1},{1,0},{2,3},{3,2},{4,5},{5,4},{6,7},{7,6},{8,9},{9,8},{10,11... | collective-permute-start | bytes 3538952 | tf_op jit(solution)/shard_map/ppermute | solution.py:334
  54.6 25.8 %copy-start.1 = (f32[1024,256]{1,0:T(8,128)S(1)}, f32[1024,256]{1,0:T(8,128)}, u32[]{:S(2)}) copy-start(f32[1024,256]{1,0:T(8,128)} %refs_5_.1) | copy-start | bytes 3145732
  54.6 25.8 %copy-start.2 = (bf16[512,768]{1,0:T(8,128)(2,1)S(1)}, bf16[512,768]{1,0:T(8,128)(2,1)}, u32[]{:S(2)}) copy-start(bf16[512,768]{1,0:T(8,128)(2,1)} %refs_8_.1) | copy-start | bytes 2359300
  54.6 25.8 %copy-start.3 = (bf16[256,768]{1,0:T(8,128)(2,1)S(1)}, bf16[256,768]{1,0:T(8,128)(2,1)}, u32[]{:S(2)}) copy-start(bf16[256,768]{1,0:T(8,128)(2,1)} %refs_9_.1) | copy-start | bytes 1179652
  56.2 24.3 %copy-start = (f32[1024,256]{1,0:T(8,128)S(1)}, f32[1024,256]{1,0:T(8,128)}, u32[]{:S(2)}) copy-start(f32[1024,256]{1,0:T(8,128)} %refs_4_.1) | copy-start | bytes 3145732
  56.2 9.5 %collective-permute-start.3 = (f32[136,512]{1,0:T(8,128)S(1)}, f32[136,512]{1,0:T(8,128)S(1)}, u32[]{:S(2)}, u32[]{:S(2)}) collective-permute-start(f32[136,512]{1,0:T(8,128)S(1)} %get-tuple-element.48), channel_id=1, source_target_pairs={{0,4},{1,5},{2,6},{3,7},{4,0},{5,1},{6,2},{7,3},{8,12},{9,13},{10,... | collective-permute-start | bytes 835592 | tf_op jit(solution)/shard_map/ppermute | solution.py:338
  59.0 12.7 %collective-permute-start.4 = (f32[136,512]{1,0:T(8,128)S(1)}, f32[136,512]{1,0:T(8,128)S(1)}, u32[]{:S(2)}, u32[]{:S(2)}) collective-permute-start(f32[136,512]{1,0:T(8,128)S(1)} %get-tuple-element.49), channel_id=1, source_target_pairs={{0,6},{1,7},{2,0},{3,1},{4,2},{5,3},{6,4},{7,5},{8,14},{9,15},{10,... | collective-permute-start | bytes 835592 | tf_op jit(solution)/shard_map/ppermute | solution.py:338
  59.9 12.4 %collective-permute-start.5 = (f32[136,512]{1,0:T(8,128)S(1)}, f32[136,512]{1,0:T(8,128)S(1)}, u32[]{:S(2)}, u32[]{:S(2)}) collective-permute-start(f32[136,512]{1,0:T(8,128)S(1)} %get-tuple-element.50), channel_id=1, source_target_pairs={{0,2},{1,3},{2,4},{3,5},{4,6},{5,7},{6,0},{7,1},{8,10},{9,11},{10,... | collective-permute-start | bytes 835592 | tf_op jit(solution)/shard_map/ppermute | solution.py:338
  72.9 6.1 %collective-permute-start.10 = (bf16[144,512]{1,0:T(8,128)(2,1)S(1)}, bf16[144,512]{1,0:T(8,128)(2,1)S(1)}, u32[]{:S(2)}, u32[]{:S(2)}) collective-permute-start(bf16[144,512]{1,0:T(8,128)(2,1)S(1)} %shard_map.195.refs_0_), channel_id=1, source_target_pairs={{0,2},{1,3},{2,4},{3,5},{4,6},{5,7},{6,0},{7,1},{8,10},{9,11},{10,... | collective-permute-start | bytes 442376 | tf_op jit(solution)/shard_map/ppermute | solution.py:338
  74.2 6.3 %collective-permute-start.7 = (bf16[144,512]{1,0:T(8,128)(2,1)S(1)}, bf16[144,512]{1,0:T(8,128)(2,1)S(1)}, u32[]{:S(2)}, u32[]{:S(2)}) collective-permute-start(bf16[144,512]{1,0:T(8,128)(2,1)S(1)} %shard_map.195.refs_0_), channel_id=1, source_target_pairs={{0,1},{1,0},{2,3},{3,2},{4,5},{5,4},{6,7},{7,6},{8,9},{9,8},{10,11... | collective-permute-start | bytes 442376 | tf_op jit(solution)/shard_map/ppermute | solution.py:334
  75.0 7.5 %collective-permute-start.6 = (bf16[144,512]{1,0:T(8,128)(2,1)S(1)}, bf16[144,512]{1,0:T(8,128)(2,1)S(1)}, u32[]{:S(2)}, u32[]{:S(2)}) collective-permute-start(bf16[144,512]{1,0:T(8,128)(2,1)S(1)} %shard_map.195.refs_0_), channel_id=1, source_target_pairs={{0,6},{1,7},{2,0},{3,1},{4,2},{5,3},{6,4},{7,5},{8,14},{9,15},{10,... | collective-permute-start | bytes 442376 | tf_op jit(solution)/shard_map/ppermute | solution.py:338
  76.6 7.3 %collective-permute-start.9 = (bf16[144,512]{1,0:T(8,128)(2,1)S(1)}, bf16[144,512]{1,0:T(8,128)(2,1)S(1)}, u32[]{:S(2)}, u32[]{:S(2)}) collective-permute-start(bf16[144,512]{1,0:T(8,128)(2,1)S(1)} %shard_map.195.refs_0_), channel_id=1, source_target_pairs={{0,4},{1,5},{2,6},{3,7},{4,0},{5,1},{6,2},{7,3},{8,12},{9,13},{10,... | collective-permute-start | bytes 442376 | tf_op jit(solution)/shard_map/ppermute | solution.py:338
  78.9 4.9 %collective-permute-start.11 = (bf16[144,512]{1,0:T(8,128)(2,1)S(1)}, bf16[144,512]{1,0:T(8,128)(2,1)S(1)}, u32[]{:S(2)}, u32[]{:S(2)}) collective-permute-start(bf16[144,512]{1,0:T(8,128)(2,1)S(1)} %collective-permute-done.10.refs_0_), channel_id=1, source_target_pairs={{0,1},{1,0},{2,3},{3,2},{4,5},{5,4},{6,7},{7,6},{8,9},{9,8},{10,11... | collective-permute-start | bytes 442376 | tf_op jit(solution)/shard_map/ppermute | solution.py:334
  82.5 4.1 %collective-permute-start.8 = (bf16[144,512]{1,0:T(8,128)(2,1)S(1)}, bf16[144,512]{1,0:T(8,128)(2,1)S(1)}, u32[]{:S(2)}, u32[]{:S(2)}) collective-permute-start(bf16[144,512]{1,0:T(8,128)(2,1)S(1)} %collective-permute-done.6.refs_0_), channel_id=1, source_target_pairs={{0,1},{1,0},{2,3},{3,2},{4,5},{5,4},{6,7},{7,6},{8,9},{9,8},{10,11... | collective-permute-start | bytes 442376 | tf_op jit(solution)/shard_map/ppermute | solution.py:334
  83.8 2.8 %collective-permute-start.12 = (bf16[144,512]{1,0:T(8,128)(2,1)S(1)}, bf16[144,512]{1,0:T(8,128)(2,1)S(1)}, u32[]{:S(2)}, u32[]{:S(2)}) collective-permute-start(bf16[144,512]{1,0:T(8,128)(2,1)S(1)} %collective-permute-done.9.refs_2_), channel_id=1, source_target_pairs={{0,1},{1,0},{2,3},{3,2},{4,5},{5,4},{6,7},{7,6},{8,9},{9,8},{10,11... | collective-permute-start | bytes 442376 | tf_op jit(solution)/shard_map/ppermute | solution.py:334
  108.5 20.8 %all-to-all-start.2 = ((f32[32,5,4,128]{3,2,1,0:T(4,128)}), f32[32,5,4,128]{3,2,1,0:T(4,128)S(1)}, u32[]{:S(2)}, u32[]{:S(2)}) async-start(f32[32,5,4,128]{3,2,1,0:T(4,128)} %get-tuple-element.65), calls=%async_computation.2 | async-start | bytes 655360 | tf_op jit(solution)/shard_map/all_to_all | solution.py:465
  115.6 5.5 %collective-permute-start.15 = (f32[32,2,4,128]{3,2,1,0:T(4,128)S(1)}, f32[32,2,4,128]{3,2,1,0:T(4,128)S(1)}, u32[]{:S(2)}, u32[]{:S(2)}) collective-permute-start(f32[32,2,4,128]{3,2,1,0:T(4,128)S(1)} %get-tuple-element.68.a0), channel_id=1, source_target_pairs={{0,6},{1,7},{2,0},{3,1},{4,2},{5,3},{6,4},{7,5},{8,14},{9,15},{10,... | collective-permute-start | bytes 393224 | tf_op jit(solution)/shard_map/ppermute | solution.py:338
  118.1 6.6 %collective-permute-start.14 = (f32[32,2,4,128]{3,2,1,0:T(4,128)S(1)}, f32[32,2,4,128]{3,2,1,0:T(4,128)S(1)}, u32[]{:S(2)}, u32[]{:S(2)}) collective-permute-start(f32[32,2,4,128]{3,2,1,0:T(4,128)S(1)} %get-tuple-element.68.a0), channel_id=1, source_target_pairs={{0,4},{1,5},{2,6},{3,7},{4,0},{5,1},{6,2},{7,3},{8,12},{9,13},{10,... | collective-permute-start | bytes 393224 | tf_op jit(solution)/shard_map/ppermute | solution.py:338
  119.1 7.9 %collective-permute-start.13 = (f32[32,2,4,128]{3,2,1,0:T(4,128)S(1)}, f32[32,2,4,128]{3,2,1,0:T(4,128)S(1)}, u32[]{:S(2)}, u32[]{:S(2)}) collective-permute-start(f32[32,2,4,128]{3,2,1,0:T(4,128)S(1)} %get-tuple-element.68.a0), channel_id=1, source_target_pairs={{0,2},{1,3},{2,4},{3,5},{4,6},{5,7},{6,0},{7,1},{8,10},{9,11},{10,... | collective-permute-start | bytes 393224 | tf_op jit(solution)/shard_map/ppermute | solution.py:338
  119.1 9.3 %collective-permute-start.16 = (f32[32,2,4,128]{3,2,1,0:T(4,128)S(1)}, f32[32,2,4,128]{3,2,1,0:T(4,128)S(1)}, u32[]{:S(2)}, u32[]{:S(2)}) collective-permute-start(f32[32,2,4,128]{3,2,1,0:T(4,128)S(1)} %get-tuple-element.68.a0), channel_id=1, source_target_pairs={{0,1},{1,0},{2,3},{3,2},{4,5},{5,4},{6,7},{7,6},{8,9},{9,8},{10,11... | collective-permute-start | bytes 393224 | tf_op jit(solution)/shard_map/ppermute | solution.py:334
  121.1 7.3 %collective-permute-start.19 = (f32[32,2,4,128]{3,2,1,0:T(4,128)S(1)}, f32[32,2,4,128]{3,2,1,0:T(4,128)S(1)}, u32[]{:S(2)}, u32[]{:S(2)}) collective-permute-start(f32[32,2,4,128]{3,2,1,0:T(4,128)S(1)} %collective-permute-done.15.a3), channel_id=1, source_target_pairs={{0,1},{1,0},{2,3},{3,2},{4,5},{5,4},{6,7},{7,6},{8,9},{9,8},{10,11... | collective-permute-start | bytes 393224 | tf_op jit(solution)/shard_map/ppermute | solution.py:334
  124.7 3.7 %collective-permute-start.18 = (f32[32,2,4,128]{3,2,1,0:T(4,128)S(1)}, f32[32,2,4,128]{3,2,1,0:T(4,128)S(1)}, u32[]{:S(2)}, u32[]{:S(2)}) collective-permute-start(f32[32,2,4,128]{3,2,1,0:T(4,128)S(1)} %collective-permute-done.14.a2), channel_id=1, source_target_pairs={{0,1},{1,0},{2,3},{3,2},{4,5},{5,4},{6,7},{7,6},{8,9},{9,8},{10,11... | collective-permute-start | bytes 393224 | tf_op jit(solution)/shard_map/ppermute | solution.py:334
  127.0 2.3 %collective-permute-start.17 = (f32[32,2,4,128]{3,2,1,0:T(4,128)S(1)}, f32[32,2,4,128]{3,2,1,0:T(4,128)S(1)}, u32[]{:S(2)}, u32[]{:S(2)}) collective-permute-start(f32[32,2,4,128]{3,2,1,0:T(4,128)S(1)} %collective-permute-done.13.a1), channel_id=1, source_target_pairs={{0,1},{1,0},{2,3},{3,2},{4,5},{5,4},{6,7},{7,6},{8,9},{9,8},{10,11... | collective-permute-start | bytes 393224 | tf_op jit(solution)/shard_map/ppermute | solution.py:334
  129.4 9.6 %collective-permute-start.20 = (f32[29,5,4,128]{3,2,1,0:T(4,128)S(1)}, f32[29,5,4,128]{3,2,1,0:T(4,128)S(1)}, u32[]{:S(2)}, u32[]{:S(2)}) collective-permute-start(f32[29,5,4,128]{3,2,1,0:T(4,128)S(1)} %slice.2.refs_0_), channel_id=1, source_target_pairs={{0,4},{1,5},{2,6},{3,7},{4,0},{5,1},{6,2},{7,3},{8,12},{9,13},{10,... | collective-permute-start | bytes 890888 | tf_op jit(solution)/shard_map/ppermute | solution.py:338
  130.4 12.1 %collective-permute-start.25 = (f32[29,5,4,128]{3,2,1,0:T(4,128)S(1)}, f32[29,5,4,128]{3,2,1,0:T(4,128)S(1)}, u32[]{:S(2)}, u32[]{:S(2)}) collective-permute-start(f32[29,5,4,128]{3,2,1,0:T(4,128)S(1)} %slice.2.refs_0_), channel_id=1, source_target_pairs={{0,6},{1,7},{2,0},{3,1},{4,2},{5,3},{6,4},{7,5},{8,14},{9,15},{10,... | collective-permute-start | bytes 890888 | tf_op jit(solution)/shard_map/ppermute | solution.py:338
  131.3 15.0 %collective-permute-start.22 = (f32[29,5,4,128]{3,2,1,0:T(4,128)S(1)}, f32[29,5,4,128]{3,2,1,0:T(4,128)S(1)}, u32[]{:S(2)}, u32[]{:S(2)}) collective-permute-start(f32[29,5,4,128]{3,2,1,0:T(4,128)S(1)} %slice.2.refs_0_), channel_id=1, source_target_pairs={{0,2},{1,3},{2,4},{3,5},{4,6},{5,7},{6,0},{7,1},{8,10},{9,11},{10,... | collective-permute-start | bytes 890888 | tf_op jit(solution)/shard_map/ppermute | solution.py:338
  131.9 16.6 %collective-permute-start.21 = (f32[29,5,4,128]{3,2,1,0:T(4,128)S(1)}, f32[29,5,4,128]{3,2,1,0:T(4,128)S(1)}, u32[]{:S(2)}, u32[]{:S(2)}) collective-permute-start(f32[29,5,4,128]{3,2,1,0:T(4,128)S(1)} %slice.2.refs_0_), channel_id=1, source_target_pairs={{0,1},{1,0},{2,3},{3,2},{4,5},{5,4},{6,7},{7,6},{8,9},{9,8},{10,11... | collective-permute-start | bytes 890888 | tf_op jit(solution)/shard_map/ppermute | solution.py:334
  142.5 6.0 %collective-permute-start.26 = (f32[29,5,4,128]{3,2,1,0:T(4,128)S(1)}, f32[29,5,4,128]{3,2,1,0:T(4,128)S(1)}, u32[]{:S(2)}, u32[]{:S(2)}) collective-permute-start(f32[29,5,4,128]{3,2,1,0:T(4,128)S(1)} %collective-permute-done.25.refs_3_), channel_id=1, source_target_pairs={{0,1},{1,0},{2,3},{3,2},{4,5},{5,4},{6,7},{7,6},{8,9},{9,8},{10,11... | collective-permute-start | bytes 890888 | tf_op jit(solution)/shard_map/ppermute | solution.py:334
  146.3 2.2 %collective-permute-start.23 = (f32[29,5,4,128]{3,2,1,0:T(4,128)S(1)}, f32[29,5,4,128]{3,2,1,0:T(4,128)S(1)}, u32[]{:S(2)}, u32[]{:S(2)}) collective-permute-start(f32[29,5,4,128]{3,2,1,0:T(4,128)S(1)} %collective-permute-done.22.refs_1_), channel_id=1, source_target_pairs={{0,1},{1,0},{2,3},{3,2},{4,5},{5,4},{6,7},{7,6},{8,9},{9,8},{10,11... | collective-permute-start | bytes 890888 | tf_op jit(solution)/shard_map/ppermute | solution.py:334
  146.8 1.7 %collective-permute-start.24 = (f32[29,5,4,128]{3,2,1,0:T(4,128)S(1)}, f32[29,5,4,128]{3,2,1,0:T(4,128)S(1)}, u32[]{:S(2)}, u32[]{:S(2)}) collective-permute-start(f32[29,5,4,128]{3,2,1,0:T(4,128)S(1)} %collective-permute-done.20.refs_2_), channel_id=1, source_target_pairs={{0,1},{1,0},{2,3},{3,2},{4,5},{5,4},{6,7},{7,6},{8,9},{9,8},{10,11... | collective-permute-start | bytes 890888 | tf_op jit(solution)/shard_map/ppermute | solution.py:334

commit v11 on v10

--- a/solution.py
+++ b/solution.py
@@ -473,18 +473,20 @@
         (pltpu.VMEM((8, 128, 256), F32),),
     )
     own = [grad[0:29]] + [shift_x(grad[0:29], d) for d in (1, 2, 3)]
-    own[2], new_hot = lax.optimization_barrier((own[2], new_hot))
     grads = ()
-    for other in (False, True):
+    for blocks in (((0, False),), ((1, False), (2, False), (3, False)), tuple((d, True) for d in range(4))):
+        n = len(blocks)
         grads = call(
-            functools.partial(place_kernel, tuple((d, other) for d in range(4))),
+            functools.partial(place_kernel, blocks),
             (sds((512, 768), F32), sds((256, 768), F32)),
-            (SM, VM, VM, VM, VM) + (ANY,) * len(grads),
-            (pos, *[swap_core(v) if other else v for v in own], *grads),
-            (pltpu.VMEM((384, 768), F32), pltpu.SemaphoreType.DMA((8,))),
+            (SM,) + (VM,) * n + (ANY,) * len(grads),
+            (pos, *[swap_core(own[d]) if other else own[d] for d, other in blocks], *grads),
+            (pltpu.VMEM((96 * n, 768), F32), pltpu.SemaphoreType.DMA((2 * n,))),
             (ANY, ANY),
-            aliases={5: 0, 6: 1} if grads else {},
+            aliases={n + 1: 0, n + 2: 1} if grads else {},
         )
+        if n == 1:
+            own[2], new_hot, *grads = lax.optimization_barrier((own[2], new_hot, *grads))
     grad_in, grad_hid = grads
     return (new_memory, new_hot, grad_in, grad_hid)
 

time: 151 us -> 149 us (0.987)
  waiting for transfers between devices: 44.2 us -> 42.5 us
    ppermute x14, starting transfers between devices: 23.5 us -> 20.3 us  [swap_core(): return lax.ppermute(v, 'rep', [(k, k ^ 1) for k in range(8)])]
    ppermute x12, starting transfers between devices: 14.5 us -> 16.8 us  [shift_x(): return lax.ppermute(v, 'rep', [(k, (k + 2 * d) % 8) for k in range(8)])]
    ppermute x12, waiting for transfers between devices: 18.6 us -> 16.6 us  [shift_x(): return lax.ppermute(v, 'rep', [(k, (k + 2 * d) % 8) for k in range(8)])]
    pallas_call x11 -> x12, Pallas kernels: 25.2 us -> 26.5 us  [call(): pl.pallas_call(body, out_shape=out_shape, in_specs=list(places) + [VM] *...]
  transfers between devices with their start and end apart: 29 -> 29, of which waited for: 12 -> 11; matrix products, arithmetic and copies ran while one was open for 2% -> 2% of each run, Pallas kernels for 7% -> 8%
where the time goes in v11:
time: 149 us
  starting transfers between devices  57.8 us (39%)
  waiting for transfers between devices  42.5 us (29%)
  Pallas kernels  26.5 us (18%)
  blocking collectives  18 us (12%)
  local copies, waits for them, and re-layouts  2.81 us (2%)
    pallas_call x12, Pallas kernels, call(): pl.pallas_call(body, out_shape=out_shape, in_specs=list(places) + [VM] *...  26.5 us
    ppermute x1, waiting for transfers between devices, on_device(): spill = lax.ppermute(spill, 'node', [(k, (k + 1) % 32) for k in range(32)])  22.8 us
    ppermute x14, starting transfers between devices, swap_core(): return lax.ppermute(v, 'rep', [(k, k ^ 1) for k in range(8)])  20.3 us
    all_to_all x1, blocking collectives, on_device(): grad = lax.all_to_all(grad, 'node', split_axis=0, concat_axis=0, tiled=True)  18 us
    ppermute x12, starting transfers between devices, shift_x(): return lax.ppermute(v, 'rep', [(k, (k + 2 * d) % 8) for k in range(8)])  16.8 us
    ppermute x12, waiting for transfers between devices, shift_x(): return lax.ppermute(v, 'rep', [(k, (k + 2 * d) % 8) for k in range(8)])  16.6 us
    all_to_all x1, starting transfers between devices, on_device(): recv = lax.all_to_all(send, 'node', split_axis=0, concat_axis=0, tiled=True)  12.2 us
    all_to_all x1, starting transfers between devices, on_device(): grad = lax.all_to_all(grad, 'node', split_axis=0, concat_axis=0, tiled=True)  7.02 us
  transfers between devices with their start and end apart: 29, of which 11 were waited for; matrix products, arithmetic and copies ran while one was open for 2% of the time, Pallas kernels for 8%

profile of v11, /device:TPU:1, one launch (start us, length us, event | category | flops | bytes accessed | tf_op | source)
XLA Modules:
  0.0 149.0 jit_solution(16059635548347289581)
XLA Ops:
  0.6 6.3 %shard_map.192 = (bf16[32,144,128]{2,1,0:T(8,128)(2,1)}, f32[96,512]{1,0:T(8,128)}) custom-call(s32[1]{0:T(128)} %bitcast.3.pos, f32[1024,256]{1,0:T(8,128)} %refs_4_.1, bf16[1024,128]{1,0:T(8,128)(2,1)} %edge_h.1, bf16[512,512]{1,0:T(8,128)(2,1)} %w_h.1, s32[1,1024]{1,0:T(1,128)} %bitcast.17, s32[1,1024]{1,0:T(1,128)} %bitcast.18, s32[1,1024]{1,0:T(1,128)} %bitcast.19, ...), custom_call_target="tpu_custom_call" | custom-call | tf_op jit(solution)/shard_map/pallas_call | solution.py:34
  7.0 0.0 copy-start.6
  7.0 0.0 copy-start.4
  7.0 0.0 copy-start.5
  7.0 12.2 %all-to-all-start = ((bf16[32,144,128]{2,1,0:T(8,128)(2,1)}), bf16[32,144,128]{2,1,0:T(8,128)(2,1)S(1)}, u32[]{:S(2)}, u32[]{:S(2)}) async-start(bf16[32,144,128]{2,1,0:T(8,128)(2,1)} %get-tuple-element.47), calls=%async_computation | async-start | bytes 2359296 | tf_op jit(solution)/shard_map/all_to_all | solution.py:412
  19.2 1.0 collective-permute-start
  20.3 0.2 select_reduce_fusion
  20.5 0.9 collective-permute-done
  21.4 1.6 %collective-permute-start.1 = (f32[16,512]{1,0:T(8,128)S(1)}, f32[16,512]{1,0:T(8,128)S(1)}, u32[]{:S(2)}, u32[]{:S(2)}) collective-permute-start(f32[16,512]{1,0:T(8,128)S(1)} %constant_dynamic-slice_fusion), channel_id=1, source_target_pairs={{0,8},{8,16},{16,24},{24,32},{32,40},{40,48},{48,56},{56,64},{64,7... | collective-permute-start | bytes 98312 | tf_op jit(solution)/shard_map/ppermute | solution.py:416
  23.0 0.8 gather_fusion
  23.7 2.0 %gather_fusion.1 = f32[128,256]{1,0:T(8,128)S(1)} fusion(f32[1024,256]{1,0:T(8,128)} %param.20, s32[1024]{0:T(1024)S(1)} %pad_clamp_fusion), kind=kCustom, calls=%fused_computation.1 | custom fusion | bytes 262656 | tf_op jit(solution)/shard_map/jit(_take)/gather | solution.py:421
  25.7 22.8 %collective-permute-done.1 = f32[16,512]{1,0:T(8,128)S(1)} collective-permute-done((f32[16,512]{1,0:T(8,128)S(1)}, f32[16,512]{1,0:T(8,128)S(1)}, u32[]{:S(2)}, u32[]{:S(2)}) %collective-permute-start.1) | collective-permute-done | bytes 32800 | tf_op jit(solution)/shard_map/ppermute | solution.py:416
  48.6 3.6 %collective-permute-start.2 = (bf16[32,144,128]{2,1,0:T(8,128)(2,1)S(1)}, bf16[32,144,128]{2,1,0:T(8,128)(2,1)S(1)}, u32[]{:S(2)}, u32[]{:S(2)}) collective-permute-start(bf16[32,144,128]{2,1,0:T(8,128)(2,1)S(1)} %all-to-all-done.own), channel_id=1, source_target_pairs={{0,1},{1,0},{2,3},{3,2},{4,5},{5,4},{6,7},{7,6},{8,9},{9,8},{10,11... | collective-permute-start | bytes 3538952 | tf_op jit(solution)/shard_map/ppermute | solution.py:334
  52.2 0.1 pad_add_fusion.pos
  52.2 1.6 %shard_map.193 = (f32[512,512]{1,0:T(8,128)S(1)}, f32[8,512]{1,0:T(8,128)S(1)}) custom-call(s32[3]{0:T(128)S(1)} %pad_add_fusion.pos, bf16[32,144,128]{2,1,0:T(8,128)(2,1)S(1)} %all-to-all-done.own), custom_call_target="tpu_custom_call" | custom-call | tf_op jit(solution)/shard_map/pallas_call | solution.py:34
  53.8 0.8 collective-permute-done.2.peer
  54.6 1.5 %shard_map.194 = (f32[136,512]{1,0:T(8,128)S(1)}, f32[136,512]{1,0:T(8,128)S(1)}, f32[136,512]{1,0:T(8,128)S(1)}, f32[136,512]{1,0:T(8,128)S(1)}) custom-call(s32[3]{0:T(128)S(1)} %pad_add_fusion.pos, bf16[32,144,128]{2,1,0:T(8,128)(2,1)S(1)} %collective-permute-done.2.peer, f32[512,512]{1,0:T(8,128)S(1)} %get-tuple-element.50.sums, ...), custom_call_target="tpu_custom_call" | custom-call | tf_op jit(solution)/shard_map/pallas_call | solution.py:34
  56.2 2.8 %collective-permute-start.3 = (f32[136,512]{1,0:T(8,128)S(1)}, f32[136,512]{1,0:T(8,128)S(1)}, u32[]{:S(2)}, u32[]{:S(2)}) collective-permute-start(f32[136,512]{1,0:T(8,128)S(1)} %get-tuple-element.52), channel_id=1, source_target_pairs={{0,4},{1,5},{2,6},{3,7},{4,0},{5,1},{6,2},{7,3},{8,12},{9,13},{10,... | collective-permute-start | bytes 835592 | tf_op jit(solution)/shard_map/ppermute | solution.py:338
  59.0 0.9 collective-permute-start.4
  59.9 0.6 collective-permute-start.5
  60.5 5.2 %collective-permute-done.3.p1_h = f32[136,512]{1,0:T(8,128)S(1)} collective-permute-done((f32[136,512]{1,0:T(8,128)S(1)}, f32[136,512]{1,0:T(8,128)S(1)}, u32[]{:S(2)}, u32[]{:S(2)}) %collective-permute-start.3) | collective-permute-done | bytes 278560 | tf_op jit(solution)/shard_map/ppermute | solution.py:338
  65.7 6.1 %collective-permute-done.4.p2_h = f32[136,512]{1,0:T(8,128)S(1)} collective-permute-done((f32[136,512]{1,0:T(8,128)S(1)}, f32[136,512]{1,0:T(8,128)S(1)}, u32[]{:S(2)}, u32[]{:S(2)}) %collective-permute-start.4) | collective-permute-done | bytes 278560 | tf_op jit(solution)/shard_map/ppermute | solution.py:338
  71.7 0.6 collective-permute-done.5.p3_h
  72.3 0.6 shard_map.195.refs_0_
  72.9 1.3 collective-permute-start.10
  74.2 0.8 collective-permute-start.7
  75.0 1.5 %collective-permute-start.6 = (bf16[144,512]{1,0:T(8,128)(2,1)S(1)}, bf16[144,512]{1,0:T(8,128)(2,1)S(1)}, u32[]{:S(2)}, u32[]{:S(2)}) collective-permute-start(bf16[144,512]{1,0:T(8,128)(2,1)S(1)} %shard_map.195.refs_0_), channel_id=1, source_target_pairs={{0,6},{1,7},{2,0},{3,1},{4,2},{5,3},{6,4},{7,5},{8,14},{9,15},{10,... | collective-permute-start | bytes 442376 | tf_op jit(solution)/shard_map/ppermute | solution.py:338
  76.6 1.4 collective-permute-start.9
  78.0 1.0 collective-permute-done.10.refs_0_
  79.0 1.5 %collective-permute-start.11 = (bf16[144,512]{1,0:T(8,128)(2,1)S(1)}, bf16[144,512]{1,0:T(8,128)(2,1)S(1)}, u32[]{:S(2)}, u32[]{:S(2)}) collective-permute-start(bf16[144,512]{1,0:T(8,128)(2,1)S(1)} %collective-permute-done.10.refs_0_), channel_id=1, source_target_pairs={{0,1},{1,0},{2,3},{3,2},{4,5},{5,4},{6,7},{7,6},{8,9},{9,8},{10,11... | collective-permute-start | bytes 442376 | tf_op jit(solution)/shard_map/ppermute | solution.py:334
  80.5 2.1 %shard_map.196 = (f32[256,256]{1,0:T(8,128)S(1)}, f32[8,128]{1,0:T(8,128)S(1)}, f32[128,1024]{1,0:T(8,128)S(1)}) custom-call(s32[3]{0:T(128)S(1)} %pad_add_fusion.pos, bf16[144,512]{1,0:T(8,128)(2,1)S(1)} %shard_map.195.refs_0_, bf16[144,512]{1,0:T(8,128)(2,1)S(1)} %collective-permute-done.7.refs_1_, f32[1024,256]{1,0:T(8,128)S(1)} %copy-done, ...), custom_call_target="tpu_custom_call" | custom-call | tf_op jit(solution)/shard_map/pallas_call | solution.py:34
  82.6 0.0 collective-permute-done.6.refs_0_
  82.6 1.2 collective-permute-start.8
  83.8 0.8 collective-permute-start.12
  84.6 2.1 %shard_map.197 = (f32[256,256]{1,0:T(8,128)S(1)}, f32[128,1024]{1,0:T(8,128)S(1)}) custom-call(s32[3]{0:T(128)S(1)} %pad_add_fusion.pos, bf16[144,512]{1,0:T(8,128)(2,1)S(1)} %collective-permute-done.10.refs_0_, bf16[144,512]{1,0:T(8,128)(2,1)S(1)} %collective-permute-done.11.refs_1_, f32[1024,256]{1,0:T(8,128)S(1)} %copy-done, f32[1024,256]{1,0:T(8,128)S(1)} %copy-done.1, ...), custom_call_target="tpu_custom_call" | custom-call | tf_op jit(solution)/shard_map/pallas_call | solution.py:34
  86.7 0.0 collective-permute-done.8.refs_1_
  86.7 0.0 collective-permute-done.12.refs_3_
  86.7 3.2 %shard_map.198 = (f32[1024,256]{1,0:T(8,128)}, f32[32,7,4,128]{3,2,1,0:T(4,128)S(1)}) custom-call(s32[3]{0:T(128)S(1)} %pad_add_fusion.pos, bf16[144,512]{1,0:T(8,128)(2,1)S(1)} %collective-permute-done.6.refs_0_, bf16[144,512]{1,0:T(8,128)(2,1)S(1)} %collective-permute-done.8.refs_1_, bf16[144,512]{1,0:T(8,128)(2,1)S(1)} %collective-permute-done.9.refs_2_, ...), custom_call_target="tpu_custom_call" | custom-call | tf_op jit(solution)/shard_map/pallas_call | solution.py:34
  89.9 18.0 %all_to_all.15.parts = f32[32,7,4,128]{3,2,1,0:T(4,128)S(1)} all-to-all(f32[32,7,4,128]{3,2,1,0:T(4,128)S(1)} %get-tuple-element.68), channel_id=1, replica_groups=mesh['node'=32,'rep'=8] {'node'}, dimensions={0} | all-to-all | bytes 917504 | tf_op jit(solution)/shard_map/all_to_all | solution.py:463
  107.9 0.8 shard_map.199
  108.7 7.0 %all-to-all-start.2 = ((f32[32,5,4,128]{3,2,1,0:T(4,128)}), f32[32,5,4,128]{3,2,1,0:T(4,128)S(1)}, u32[]{:S(2)}, u32[]{:S(2)}) async-start(f32[32,5,4,128]{3,2,1,0:T(4,128)} %get-tuple-element.69), calls=%async_computation.2 | async-start | bytes 655360 | tf_op jit(solution)/shard_map/all_to_all | solution.py:465
  115.7 1.7 %collective-permute-start.13 = (f32[32,2,4,128]{3,2,1,0:T(4,128)S(1)}, f32[32,2,4,128]{3,2,1,0:T(4,128)S(1)}, u32[]{:S(2)}, u32[]{:S(2)}) collective-permute-start(f32[32,2,4,128]{3,2,1,0:T(4,128)S(1)} %get-tuple-element.72.a0), channel_id=1, source_target_pairs={{0,2},{1,3},{2,4},{3,5},{4,6},{5,7},{6,0},{7,1},{8,10},{9,11},{10,... | collective-permute-start | bytes 393224 | tf_op jit(solution)/shard_map/ppermute | solution.py:338
  117.4 2.0 %collective-permute-start.14 = (f32[32,2,4,128]{3,2,1,0:T(4,128)S(1)}, f32[32,2,4,128]{3,2,1,0:T(4,128)S(1)}, u32[]{:S(2)}, u32[]{:S(2)}) collective-permute-start(f32[32,2,4,128]{3,2,1,0:T(4,128)S(1)} %get-tuple-element.72.a0), channel_id=1, source_target_pairs={{0,4},{1,5},{2,6},{3,7},{4,0},{5,1},{6,2},{7,3},{8,12},{9,13},{10,... | collective-permute-start | bytes 393224 | tf_op jit(solution)/shard_map/ppermute | solution.py:338
  119.4 0.5 collective-permute-start.15
  119.9 1.6 %collective-permute-start.16 = (f32[32,2,4,128]{3,2,1,0:T(4,128)S(1)}, f32[32,2,4,128]{3,2,1,0:T(4,128)S(1)}, u32[]{:S(2)}, u32[]{:S(2)}) collective-permute-start(f32[32,2,4,128]{3,2,1,0:T(4,128)S(1)} %get-tuple-element.72.a0), channel_id=1, source_target_pairs={{0,1},{1,0},{2,3},{3,2},{4,5},{5,4},{6,7},{7,6},{8,9},{9,8},{10,11... | collective-permute-start | bytes 393224 | tf_op jit(solution)/shard_map/ppermute | solution.py:334
  121.5 2.5 %collective-permute-start.17 = (f32[32,2,4,128]{3,2,1,0:T(4,128)S(1)}, f32[32,2,4,128]{3,2,1,0:T(4,128)S(1)}, u32[]{:S(2)}, u32[]{:S(2)}) collective-permute-start(f32[32,2,4,128]{3,2,1,0:T(4,128)S(1)} %collective-permute-done.13.a1), channel_id=1, source_target_pairs={{0,1},{1,0},{2,3},{3,2},{4,5},{5,4},{6,7},{7,6},{8,9},{9,8},{10,11... | collective-permute-start | bytes 393224 | tf_op jit(solution)/shard_map/ppermute | solution.py:334
  124.0 0.4 collective-permute-done.14.a2
  124.5 2.2 %collective-permute-start.18 = (f32[32,2,4,128]{3,2,1,0:T(4,128)S(1)}, f32[32,2,4,128]{3,2,1,0:T(4,128)S(1)}, u32[]{:S(2)}, u32[]{:S(2)}) collective-permute-start(f32[32,2,4,128]{3,2,1,0:T(4,128)S(1)} %collective-permute-done.14.a2), channel_id=1, source_target_pairs={{0,1},{1,0},{2,3},{3,2},{4,5},{5,4},{6,7},{7,6},{8,9},{9,8},{10,11... | collective-permute-start | bytes 393224 | tf_op jit(solution)/shard_map/ppermute | solution.py:334
  126.7 0.0 collective-permute-start.19
  126.7 1.0 collective-permute-done.18.b2
  127.7 0.4 collective-permute-done.19.b3
  128.1 1.4 collective-permute-start.20
  129.4 0.9 collective-permute-start.22
  130.4 1.8 %collective-permute-start.25 = (f32[29,5,4,128]{3,2,1,0:T(4,128)S(1)}, f32[29,5,4,128]{3,2,1,0:T(4,128)S(1)}, u32[]{:S(2)}, u32[]{:S(2)}) collective-permute-start(f32[29,5,4,128]{3,2,1,0:T(4,128)S(1)} %slice.2.refs_0_), channel_id=1, source_target_pairs={{0,6},{1,7},{2,0},{3,1},{4,2},{5,3},{6,4},{7,5},{8,14},{9,15},{10,... | collective-permute-start | bytes 890888 | tf_op jit(solution)/shard_map/ppermute | solution.py:338
  132.1 1.3 shard_map.201
  133.4 2.8 %collective-permute-start.21 = (f32[29,5,4,128]{3,2,1,0:T(4,128)S(1)}, f32[29,5,4,128]{3,2,1,0:T(4,128)S(1)}, u32[]{:S(2)}, u32[]{:S(2)}) collective-permute-start(f32[29,5,4,128]{3,2,1,0:T(4,128)S(1)} %slice.2.refs_0_), channel_id=1, source_target_pairs={{0,1},{1,0},{2,3},{3,2},{4,5},{5,4},{6,7},{7,6},{8,9},{9,8},{10,11... | collective-permute-start | bytes 890888 | tf_op jit(solution)/shard_map/ppermute | solution.py:334
  136.2 3.9 %shard_map.200 = f32[1024,256]{1,0:T(8,128)} custom-call(s32[3]{0:T(128)S(1)} %pad_add_fusion.pos, s32[1,1024]{1,0:T(1,128)S(1)} %bitcast.16, f32[32,2,4,128]{3,2,1,0:T(4,128)S(1)} %get-tuple-element.72.a0, f32[32,2,4,128]{3,2,1,0:T(4,128)S(1)} %collective-permute-done.13.a1, f32[32,2,4,128]{3,2,1,0:T(4,128)S(1)} %collective-permute-done.14.a2, ...), custom_call_target="tpu_custom_call" | custom-call | tf_op jit(solution)/shard_map/pallas_call | solution.py:34
  140.1 1.6 %collective-permute-start.24 = (f32[29,5,4,128]{3,2,1,0:T(4,128)S(1)}, f32[29,5,4,128]{3,2,1,0:T(4,128)S(1)}, u32[]{:S(2)}, u32[]{:S(2)}) collective-permute-start(f32[29,5,4,128]{3,2,1,0:T(4,128)S(1)} %collective-permute-done.20.refs_1_), channel_id=1, source_target_pairs={{0,1},{1,0},{2,3},{3,2},{4,5},{5,4},{6,7},{7,6},{8,9},{9,8},{10,11... | collective-permute-start | bytes 890888 | tf_op jit(solution)/shard_map/ppermute | solution.py:334
  141.7 3.3 %collective-permute-done.22.refs_0_ = f32[29,5,4,128]{3,2,1,0:T(4,128)S(1)} collective-permute-done((f32[29,5,4,128]{3,2,1,0:T(4,128)S(1)}, f32[29,5,4,128]{3,2,1,0:T(4,128)S(1)}, u32[]{:S(2)}, u32[]{:S(2)}) %collective-permute-start.22) | collective-permute-done | bytes 296992 | tf_op jit(solution)/shard_map/ppermute | solution.py:338
  145.0 0.5 collective-permute-start.23
  145.5 0.0 collective-permute-start.26
  145.5 1.6 %shard_map.202 = (f32[512,768]{1,0:T(8,128)}, f32[256,768]{1,0:T(8,128)}) custom-call(s32[3]{0:T(128)S(1)} %pad_add_fusion.pos, f32[29,5,4,128]{3,2,1,0:T(4,128)S(1)} %collective-permute-done.22.refs_0_, f32[29,5,4,128]{3,2,1,0:T(4,128)S(1)} %collective-permute-done.20.refs_1_, ...), custom_call_target="tpu_custom_call", output_to_operand_aliasing={{0}: (4, {}), {1}: (5, {})} | custom-call | tf_op jit(solution)/shard_map/pallas_call | solution.py:34
  147.1 0.0 collective-permute-done.26.refs_3_
  147.1 1.7 %shard_map.203 = (f32[512,768]{1,0:T(8,128)}, f32[256,768]{1,0:T(8,128)}) custom-call(s32[3]{0:T(128)S(1)} %pad_add_fusion.pos, f32[29,5,4,128]{3,2,1,0:T(4,128)S(1)} %collective-permute-done.21.refs_0_, f32[29,5,4,128]{3,2,1,0:T(4,128)S(1)} %collective-permute-done.23.refs_1_, ...), custom_call_target="tpu_custom_call", output_to_operand_aliasing={{0}: (5, {}), {1}: (6, {})} | custom-call | tf_op jit(solution)/shard_map/pallas_call | solution.py:34
  (30 shorter events, 0.1 us)
Async XLA Ops:
  7.0 12.2 %copy-start.6 = (f32[96,512]{1,0:T(8,128)S(1)}, f32[96,512]{1,0:T(8,128)}, u32[]{:S(2)}) copy-start(f32[96,512]{1,0:T(8,128)} %get-tuple-element.48) | copy-start | bytes 589828
  7.0 13.3 %copy-start.4 = (s32[1024]{0:T(1024)S(1)}, s32[1024]{0:T(1024)}, u32[]{:S(2)}) copy-start(s32[1024]{0:T(1024)} %param.27) | copy-start | bytes 12292
  7.0 16.0 %copy-start.5 = (f32[1024,256]{1,0:T(8,128)S(1)}, f32[1024,256]{1,0:T(8,128)}, u32[]{:S(2)}) copy-start(f32[1024,256]{1,0:T(8,128)} %param.18) | copy-start | bytes 3145732
  7.0 41.6 %all-to-all-start = ((bf16[32,144,128]{2,1,0:T(8,128)(2,1)}), bf16[32,144,128]{2,1,0:T(8,128)(2,1)S(1)}, u32[]{:S(2)}, u32[]{:S(2)}) async-start(bf16[32,144,128]{2,1,0:T(8,128)(2,1)} %get-tuple-element.47), calls=%async_computation | async-start | bytes 2359296 | tf_op jit(solution)/shard_map/all_to_all | solution.py:412
  19.2 2.1 %collective-permute-start = (f32[96,512]{1,0:T(8,128)S(1)}, f32[96,512]{1,0:T(8,128)S(1)}, u32[]{:S(2)}, u32[]{:S(2)}) collective-permute-start(f32[96,512]{1,0:T(8,128)S(1)} %copy-done.6), channel_id=1, source_target_pairs={{0,1},{1,0},{2,3},{3,2},{4,5},{5,4},{6,7},{7,6},{8,9},{9,8},{10,11... | collective-permute-start | bytes 589832 | tf_op jit(solution)/shard_map/ppermute | solution.py:334
  21.4 27.2 %collective-permute-start.1 = (f32[16,512]{1,0:T(8,128)S(1)}, f32[16,512]{1,0:T(8,128)S(1)}, u32[]{:S(2)}, u32[]{:S(2)}) collective-permute-start(f32[16,512]{1,0:T(8,128)S(1)} %constant_dynamic-slice_fusion), channel_id=1, source_target_pairs={{0,8},{8,16},{16,24},{24,32},{32,40},{40,48},{48,56},{56,64},{64,7... | collective-permute-start | bytes 98312 | tf_op jit(solution)/shard_map/ppermute | solution.py:416
  48.6 6.1 %collective-permute-start.2 = (bf16[32,144,128]{2,1,0:T(8,128)(2,1)S(1)}, bf16[32,144,128]{2,1,0:T(8,128)(2,1)S(1)}, u32[]{:S(2)}, u32[]{:S(2)}) collective-permute-start(bf16[32,144,128]{2,1,0:T(8,128)(2,1)S(1)} %all-to-all-done.own), channel_id=1, source_target_pairs={{0,1},{1,0},{2,3},{3,2},{4,5},{5,4},{6,7},{7,6},{8,9},{9,8},{10,11... | collective-permute-start | bytes 3538952 | tf_op jit(solution)/shard_map/ppermute | solution.py:334
  54.6 25.8 %copy-start = (f32[1024,256]{1,0:T(8,128)S(1)}, f32[1024,256]{1,0:T(8,128)}, u32[]{:S(2)}) copy-start(f32[1024,256]{1,0:T(8,128)} %refs_4_.1) | copy-start | bytes 3145732
  54.6 25.8 %copy-start.1 = (f32[1024,256]{1,0:T(8,128)S(1)}, f32[1024,256]{1,0:T(8,128)}, u32[]{:S(2)}) copy-start(f32[1024,256]{1,0:T(8,128)} %refs_5_.1) | copy-start | bytes 3145732
  54.6 25.8 %copy-start.2 = (bf16[512,768]{1,0:T(8,128)(2,1)S(1)}, bf16[512,768]{1,0:T(8,128)(2,1)}, u32[]{:S(2)}) copy-start(bf16[512,768]{1,0:T(8,128)(2,1)} %refs_8_.1) | copy-start | bytes 2359300
  54.6 25.8 %copy-start.3 = (bf16[256,768]{1,0:T(8,128)(2,1)S(1)}, bf16[256,768]{1,0:T(8,128)(2,1)}, u32[]{:S(2)}) copy-start(bf16[256,768]{1,0:T(8,128)(2,1)} %refs_9_.1) | copy-start | bytes 1179652
  56.2 9.5 %collective-permute-start.3 = (f32[136,512]{1,0:T(8,128)S(1)}, f32[136,512]{1,0:T(8,128)S(1)}, u32[]{:S(2)}, u32[]{:S(2)}) collective-permute-start(f32[136,512]{1,0:T(8,128)S(1)} %get-tuple-element.52), channel_id=1, source_target_pairs={{0,4},{1,5},{2,6},{3,7},{4,0},{5,1},{6,2},{7,3},{8,12},{9,13},{10,... | collective-permute-start | bytes 835592 | tf_op jit(solution)/shard_map/ppermute | solution.py:338
  59.0 12.7 %collective-permute-start.4 = (f32[136,512]{1,0:T(8,128)S(1)}, f32[136,512]{1,0:T(8,128)S(1)}, u32[]{:S(2)}, u32[]{:S(2)}) collective-permute-start(f32[136,512]{1,0:T(8,128)S(1)} %get-tuple-element.53), channel_id=1, source_target_pairs={{0,6},{1,7},{2,0},{3,1},{4,2},{5,3},{6,4},{7,5},{8,14},{9,15},{10,... | collective-permute-start | bytes 835592 | tf_op jit(solution)/shard_map/ppermute | solution.py:338
  59.9 12.4 %collective-permute-start.5 = (f32[136,512]{1,0:T(8,128)S(1)}, f32[136,512]{1,0:T(8,128)S(1)}, u32[]{:S(2)}, u32[]{:S(2)}) collective-permute-start(f32[136,512]{1,0:T(8,128)S(1)} %get-tuple-element.54), channel_id=1, source_target_pairs={{0,2},{1,3},{2,4},{3,5},{4,6},{5,7},{6,0},{7,1},{8,10},{9,11},{10,... | collective-permute-start | bytes 835592 | tf_op jit(solution)/shard_map/ppermute | solution.py:338
  72.9 6.1 %collective-permute-start.10 = (bf16[144,512]{1,0:T(8,128)(2,1)S(1)}, bf16[144,512]{1,0:T(8,128)(2,1)S(1)}, u32[]{:S(2)}, u32[]{:S(2)}) collective-permute-start(bf16[144,512]{1,0:T(8,128)(2,1)S(1)} %shard_map.195.refs_0_), channel_id=1, source_target_pairs={{0,2},{1,3},{2,4},{3,5},{4,6},{5,7},{6,0},{7,1},{8,10},{9,11},{10,... | collective-permute-start | bytes 442376 | tf_op jit(solution)/shard_map/ppermute | solution.py:338
  74.2 6.3 %collective-permute-start.7 = (bf16[144,512]{1,0:T(8,128)(2,1)S(1)}, bf16[144,512]{1,0:T(8,128)(2,1)S(1)}, u32[]{:S(2)}, u32[]{:S(2)}) collective-permute-start(bf16[144,512]{1,0:T(8,128)(2,1)S(1)} %shard_map.195.refs_0_), channel_id=1, source_target_pairs={{0,1},{1,0},{2,3},{3,2},{4,5},{5,4},{6,7},{7,6},{8,9},{9,8},{10,11... | collective-permute-start | bytes 442376 | tf_op jit(solution)/shard_map/ppermute | solution.py:334
  75.0 7.5 %collective-permute-start.6 = (bf16[144,512]{1,0:T(8,128)(2,1)S(1)}, bf16[144,512]{1,0:T(8,128)(2,1)S(1)}, u32[]{:S(2)}, u32[]{:S(2)}) collective-permute-start(bf16[144,512]{1,0:T(8,128)(2,1)S(1)} %shard_map.195.refs_0_), channel_id=1, source_target_pairs={{0,6},{1,7},{2,0},{3,1},{4,2},{5,3},{6,4},{7,5},{8,14},{9,15},{10,... | collective-permute-start | bytes 442376 | tf_op jit(solution)/shard_map/ppermute | solution.py:338
  76.6 7.3 %collective-permute-start.9 = (bf16[144,512]{1,0:T(8,128)(2,1)S(1)}, bf16[144,512]{1,0:T(8,128)(2,1)S(1)}, u32[]{:S(2)}, u32[]{:S(2)}) collective-permute-start(bf16[144,512]{1,0:T(8,128)(2,1)S(1)} %shard_map.195.refs_0_), channel_id=1, source_target_pairs={{0,4},{1,5},{2,6},{3,7},{4,0},{5,1},{6,2},{7,3},{8,12},{9,13},{10,... | collective-permute-start | bytes 442376 | tf_op jit(solution)/shard_map/ppermute | solution.py:338
  79.0 4.9 %collective-permute-start.11 = (bf16[144,512]{1,0:T(8,128)(2,1)S(1)}, bf16[144,512]{1,0:T(8,128)(2,1)S(1)}, u32[]{:S(2)}, u32[]{:S(2)}) collective-permute-start(bf16[144,512]{1,0:T(8,128)(2,1)S(1)} %collective-permute-done.10.refs_0_), channel_id=1, source_target_pairs={{0,1},{1,0},{2,3},{3,2},{4,5},{5,4},{6,7},{7,6},{8,9},{9,8},{10,11... | collective-permute-start | bytes 442376 | tf_op jit(solution)/shard_map/ppermute | solution.py:334
  82.6 4.1 %collective-permute-start.8 = (bf16[144,512]{1,0:T(8,128)(2,1)S(1)}, bf16[144,512]{1,0:T(8,128)(2,1)S(1)}, u32[]{:S(2)}, u32[]{:S(2)}) collective-permute-start(bf16[144,512]{1,0:T(8,128)(2,1)S(1)} %collective-permute-done.6.refs_0_), channel_id=1, source_target_pairs={{0,1},{1,0},{2,3},{3,2},{4,5},{5,4},{6,7},{7,6},{8,9},{9,8},{10,11... | collective-permute-start | bytes 442376 | tf_op jit(solution)/shard_map/ppermute | solution.py:334
  83.8 2.9 %collective-permute-start.12 = (bf16[144,512]{1,0:T(8,128)(2,1)S(1)}, bf16[144,512]{1,0:T(8,128)(2,1)S(1)}, u32[]{:S(2)}, u32[]{:S(2)}) collective-permute-start(bf16[144,512]{1,0:T(8,128)(2,1)S(1)} %collective-permute-done.9.refs_2_), channel_id=1, source_target_pairs={{0,1},{1,0},{2,3},{3,2},{4,5},{5,4},{6,7},{7,6},{8,9},{9,8},{10,11... | collective-permute-start | bytes 442376 | tf_op jit(solution)/shard_map/ppermute | solution.py:334
  108.7 19.4 %all-to-all-start.2 = ((f32[32,5,4,128]{3,2,1,0:T(4,128)}), f32[32,5,4,128]{3,2,1,0:T(4,128)S(1)}, u32[]{:S(2)}, u32[]{:S(2)}) async-start(f32[32,5,4,128]{3,2,1,0:T(4,128)} %get-tuple-element.69), calls=%async_computation.2 | async-start | bytes 655360 | tf_op jit(solution)/shard_map/all_to_all | solution.py:465
  115.7 5.9 %collective-permute-start.13 = (f32[32,2,4,128]{3,2,1,0:T(4,128)S(1)}, f32[32,2,4,128]{3,2,1,0:T(4,128)S(1)}, u32[]{:S(2)}, u32[]{:S(2)}) collective-permute-start(f32[32,2,4,128]{3,2,1,0:T(4,128)S(1)} %get-tuple-element.72.a0), channel_id=1, source_target_pairs={{0,2},{1,3},{2,4},{3,5},{4,6},{5,7},{6,0},{7,1},{8,10},{9,11},{10,... | collective-permute-start | bytes 393224 | tf_op jit(solution)/shard_map/ppermute | solution.py:338
  117.4 7.1 %collective-permute-start.14 = (f32[32,2,4,128]{3,2,1,0:T(4,128)S(1)}, f32[32,2,4,128]{3,2,1,0:T(4,128)S(1)}, u32[]{:S(2)}, u32[]{:S(2)}) collective-permute-start(f32[32,2,4,128]{3,2,1,0:T(4,128)S(1)} %get-tuple-element.72.a0), channel_id=1, source_target_pairs={{0,4},{1,5},{2,6},{3,7},{4,0},{5,1},{6,2},{7,3},{8,12},{9,13},{10,... | collective-permute-start | bytes 393224 | tf_op jit(solution)/shard_map/ppermute | solution.py:338
  119.4 7.3 %collective-permute-start.15 = (f32[32,2,4,128]{3,2,1,0:T(4,128)S(1)}, f32[32,2,4,128]{3,2,1,0:T(4,128)S(1)}, u32[]{:S(2)}, u32[]{:S(2)}) collective-permute-start(f32[32,2,4,128]{3,2,1,0:T(4,128)S(1)} %get-tuple-element.72.a0), channel_id=1, source_target_pairs={{0,6},{1,7},{2,0},{3,1},{4,2},{5,3},{6,4},{7,5},{8,14},{9,15},{10,... | collective-permute-start | bytes 393224 | tf_op jit(solution)/shard_map/ppermute | solution.py:338
  119.9 6.8 %collective-permute-start.16 = (f32[32,2,4,128]{3,2,1,0:T(4,128)S(1)}, f32[32,2,4,128]{3,2,1,0:T(4,128)S(1)}, u32[]{:S(2)}, u32[]{:S(2)}) collective-permute-start(f32[32,2,4,128]{3,2,1,0:T(4,128)S(1)} %get-tuple-element.72.a0), channel_id=1, source_target_pairs={{0,1},{1,0},{2,3},{3,2},{4,5},{5,4},{6,7},{7,6},{8,9},{9,8},{10,11... | collective-permute-start | bytes 393224 | tf_op jit(solution)/shard_map/ppermute | solution.py:334
  121.5 5.2 %collective-permute-start.17 = (f32[32,2,4,128]{3,2,1,0:T(4,128)S(1)}, f32[32,2,4,128]{3,2,1,0:T(4,128)S(1)}, u32[]{:S(2)}, u32[]{:S(2)}) collective-permute-start(f32[32,2,4,128]{3,2,1,0:T(4,128)S(1)} %collective-permute-done.13.a1), channel_id=1, source_target_pairs={{0,1},{1,0},{2,3},{3,2},{4,5},{5,4},{6,7},{7,6},{8,9},{9,8},{10,11... | collective-permute-start | bytes 393224 | tf_op jit(solution)/shard_map/ppermute | solution.py:334
  124.5 3.2 %collective-permute-start.18 = (f32[32,2,4,128]{3,2,1,0:T(4,128)S(1)}, f32[32,2,4,128]{3,2,1,0:T(4,128)S(1)}, u32[]{:S(2)}, u32[]{:S(2)}) collective-permute-start(f32[32,2,4,128]{3,2,1,0:T(4,128)S(1)} %collective-permute-done.14.a2), channel_id=1, source_target_pairs={{0,1},{1,0},{2,3},{3,2},{4,5},{5,4},{6,7},{7,6},{8,9},{9,8},{10,11... | collective-permute-start | bytes 393224 | tf_op jit(solution)/shard_map/ppermute | solution.py:334
  126.7 1.3 collective-permute-start.19
  128.1 12.0 %collective-permute-start.20 = (f32[29,5,4,128]{3,2,1,0:T(4,128)S(1)}, f32[29,5,4,128]{3,2,1,0:T(4,128)S(1)}, u32[]{:S(2)}, u32[]{:S(2)}) collective-permute-start(f32[29,5,4,128]{3,2,1,0:T(4,128)S(1)} %slice.2.refs_0_), channel_id=1, source_target_pairs={{0,4},{1,5},{2,6},{3,7},{4,0},{5,1},{6,2},{7,3},{8,12},{9,13},{10,... | collective-permute-start | bytes 890888 | tf_op jit(solution)/shard_map/ppermute | solution.py:338
  129.4 15.6 %collective-permute-start.22 = (f32[29,5,4,128]{3,2,1,0:T(4,128)S(1)}, f32[29,5,4,128]{3,2,1,0:T(4,128)S(1)}, u32[]{:S(2)}, u32[]{:S(2)}) collective-permute-start(f32[29,5,4,128]{3,2,1,0:T(4,128)S(1)} %slice.2.refs_0_), channel_id=1, source_target_pairs={{0,2},{1,3},{2,4},{3,5},{4,6},{5,7},{6,0},{7,1},{8,10},{9,11},{10,... | collective-permute-start | bytes 890888 | tf_op jit(solution)/shard_map/ppermute | solution.py:338
  130.4 15.1 %collective-permute-start.25 = (f32[29,5,4,128]{3,2,1,0:T(4,128)S(1)}, f32[29,5,4,128]{3,2,1,0:T(4,128)S(1)}, u32[]{:S(2)}, u32[]{:S(2)}) collective-permute-start(f32[29,5,4,128]{3,2,1,0:T(4,128)S(1)} %slice.2.refs_0_), channel_id=1, source_target_pairs={{0,6},{1,7},{2,0},{3,1},{4,2},{5,3},{6,4},{7,5},{8,14},{9,15},{10,... | collective-permute-start | bytes 890888 | tf_op jit(solution)/shard_map/ppermute | solution.py:338
  133.4 13.6 %collective-permute-start.21 = (f32[29,5,4,128]{3,2,1,0:T(4,128)S(1)}, f32[29,5,4,128]{3,2,1,0:T(4,128)S(1)}, u32[]{:S(2)}, u32[]{:S(2)}) collective-permute-start(f32[29,5,4,128]{3,2,1,0:T(4,128)S(1)} %slice.2.refs_0_), channel_id=1, source_target_pairs={{0,1},{1,0},{2,3},{3,2},{4,5},{5,4},{6,7},{7,6},{8,9},{9,8},{10,11... | collective-permute-start | bytes 890888 | tf_op jit(solution)/shard_map/ppermute | solution.py:334
  140.1 7.0 %collective-permute-start.24 = (f32[29,5,4,128]{3,2,1,0:T(4,128)S(1)}, f32[29,5,4,128]{3,2,1,0:T(4,128)S(1)}, u32[]{:S(2)}, u32[]{:S(2)}) collective-permute-start(f32[29,5,4,128]{3,2,1,0:T(4,128)S(1)} %collective-permute-done.20.refs_1_), channel_id=1, source_target_pairs={{0,1},{1,0},{2,3},{3,2},{4,5},{5,4},{6,7},{7,6},{8,9},{9,8},{10,11... | collective-permute-start | bytes 890888 | tf_op jit(solution)/shard_map/ppermute | solution.py:334
  145.0 2.1 %collective-permute-start.23 = (f32[29,5,4,128]{3,2,1,0:T(4,128)S(1)}, f32[29,5,4,128]{3,2,1,0:T(4,128)S(1)}, u32[]{:S(2)}, u32[]{:S(2)}) collective-permute-start(f32[29,5,4,128]{3,2,1,0:T(4,128)S(1)} %collective-permute-done.22.refs_0_), channel_id=1, source_target_pairs={{0,1},{1,0},{2,3},{3,2},{4,5},{5,4},{6,7},{7,6},{8,9},{9,8},{10,11... | collective-permute-start | bytes 890888 | tf_op jit(solution)/shard_map/ppermute | solution.py:334
  145.5 1.6 %collective-permute-start.26 = (f32[29,5,4,128]{3,2,1,0:T(4,128)S(1)}, f32[29,5,4,128]{3,2,1,0:T(4,128)S(1)}, u32[]{:S(2)}, u32[]{:S(2)}) collective-permute-start(f32[29,5,4,128]{3,2,1,0:T(4,128)S(1)} %collective-permute-done.25.refs_2_), channel_id=1, source_target_pairs={{0,1},{1,0},{2,3},{3,2},{4,5},{5,4},{6,7},{7,6},{8,9},{9,8},{10,11... | collective-permute-start | bytes 890888 | tf_op jit(solution)/shard_map/ppermute | solution.py:334
